TPU v7x, 32 devices: a whole 2x2x4 slice. The times are simulated.
32 devices in a mesh: expert: 8 (over z, x), shard: 4 (over y, core).
Axes of the slice: x: 2, y: 2, z: 4, core: 2. Of those that a mesh axis runs over, the one named last changes fastest.
Arguments:
- tokens: bfloat16 [8192, 2048], P(('expert', 'shard')), may hold values from -16 to 16
- cotangent: bfloat16 [8192, 2048], P(('expert', 'shard')), may hold values from -6 to 6
- segments: int32 [32, 256], P(('expert', 'shard')), may hold values from 0 to 2, never falling along the last dimension, each value on 1 to 160 neighbouring positions
- routes: int32 [8192, 8], P(('expert', 'shard')), may hold values from 0 to 15, as said below
- tile_counts: int32 [16], replicated, may hold values from 8 to 16
- norm_one: bfloat16 [2048], P('shard'), may hold values from 0.25 to 1.75
- norm_query: bfloat16 [2048], P('shard'), may hold values from 0.25 to 1.75
- norm_key: bfloat16 [2048], P('shard'), may hold values from 0.25 to 1.75
- norm_two: bfloat16 [2048], P('shard'), may hold values from 0.25 to 1.75
- qkv_weight: bfloat16 [2048, 6144], P('shard'), may hold values from -0.125 to 0.125
- out_weight: bfloat16 [2048, 2048], P('shard'), may hold values from -0.5 to 0.5
- router_weight: bfloat16 [2048, 16], P('shard'), may hold values from -0.125 to 0.125
- gate_up_weight: bfloat16 [16, 2048, 2048], P('expert'), may hold values from -0.125 to 0.125
- down_weight: bfloat16 [16, 1024, 2048], P('expert'), may hold values from -1 to 1
Outputs:
- block_out: bfloat16 [8192, 2048], P(('expert', 'shard'))
- grad_tokens: float32 [8192, 2048], P(('expert', 'shard'))
- grad_norm_one: float32 [2048], P('shard')
- grad_norm_query: float32 [2048], P('shard')
- grad_norm_key: float32 [2048], P('shard')
- grad_norm_two: float32 [2048], P('shard')
- grad_qkv_weight: float32 [2048, 6144], P('shard')
- grad_out_weight: float32 [2048, 2048], P('shard')
- grad_router_weight: float32 [2048, 16], P('shard')
- grad_gate_up_weight: float32 [16, 2048, 2048], P('expert', 'shard')
- grad_down_weight: float32 [16, 1024, 2048], P('expert', None, 'shard')
Inputs may be any that keep to these rules, and one draw needn't show every extreme that they name: `routes`: each row names 8 different experts. In every sequence one expert, the same for all sequences, is named by 192 rows or more, and its tile count is 16. `segments`: segment numbers start at 0 in every sequence.
All inputs are finite; a program needn't handle non-finite values.
Results may differ from a plain program's by a relative error of at most 0.015.
Values may be sent and summed in bfloat16 or wider, within the bound.
A program may use at most 320 MiB of HBM per device.

v0:
```python
import jax
import jax.numpy as jnp
from jax import lax
from jax.sharding import PartitionSpec as P

HEADS = 16
HEAD_DIM = 128
TOP = 8
TILE = 8


epsilon = 1e-05
rope_base = 10000.0


def rms_scale(values, scale_gain):
    return (
        values * lax.rsqrt(jnp.mean(values * values, axis=-1, keepdims=True) + epsilon) * scale_gain
    )


def rotary_tables(length):
    half_dim = HEAD_DIM // 2
    position = jnp.arange(length, dtype=jnp.float32)[:, None]
    frequency = rope_base ** (-jnp.arange(half_dim, dtype=jnp.float32) * 2.0 / HEAD_DIM)
    angles = position * frequency[None, :]
    angles = jnp.concatenate([angles, angles], axis=-1)
    return (jnp.cos(angles)[:, None, :], jnp.sin(angles)[:, None, :])


def rotate(vectors, cosine, sine_table):
    half_dim = vectors.shape[-1] // 2
    turned = jnp.concatenate([-vectors[..., half_dim:], vectors[..., :half_dim]], axis=-1)
    return vectors * cosine + turned * sine_table


def query_key(raw_query, raw_key, query_gain, key_gain, cosine, sine_table):
    length = raw_query.shape[0]
    queries = rms_scale(raw_query, query_gain).reshape(length, HEADS, HEAD_DIM)
    keys_rot = rms_scale(raw_key, key_gain).reshape(length, HEADS, HEAD_DIM)
    return (rotate(queries, cosine, sine_table), rotate(keys_rot, cosine, sine_table))


def swiglu(gate_up):
    half_dim = gate_up.shape[-1] // 2
    gate_part = gate_up[..., :half_dim]
    return gate_part / (1.0 + jnp.exp(-gate_part)) * gate_up[..., half_dim:]


def softmax_rows(logits):
    largest = jnp.max(logits, axis=-1, keepdims=True)
    raised = jnp.exp(logits - largest)
    return raised / jnp.sum(raised, axis=-1, keepdims=True)


def reorder_features(values, shard_group, expert_group):
    leading = values.shape[:-1]
    features = values.shape[-1]
    grouped = values.reshape(
        leading + (shard_group, expert_group, features // (shard_group * expert_group))
    )
    return jnp.swapaxes(grouped, -2, -3).reshape(leading + (features,))


def body(
    tokens,
    cotangent,
    segments,
    routes,
    tile_counts,
    norm_one,
    norm_query,
    norm_key,
    norm_two,
    qkv_weight,
    out_weight,
    router_weight,
    gate_up_weight,
    down_weight,
):
    length, model_width = tokens.shape
    experts_all = tile_counts.shape[0]
    local_experts = gate_up_weight.shape[0]
    expert_group = lax.axis_size("expert")
    shard_group = lax.axis_size("shard")
    capacity = length * TOP // (experts_all * TILE) * TILE
    slots_all = experts_all * capacity
    pair_count = length * TOP
    score_scale = HEAD_DIM ** (-0.5)
    gathered = (
        lax.all_gather(norm_one, "shard", axis=0, tiled=True),
        lax.all_gather(norm_query, "shard", axis=0, tiled=True),
        lax.all_gather(norm_key, "shard", axis=0, tiled=True),
        lax.all_gather(norm_two, "shard", axis=0, tiled=True),
        lax.all_gather(qkv_weight, "shard", axis=0, tiled=True),
        lax.all_gather(out_weight, "shard", axis=0, tiled=True),
        lax.all_gather(router_weight, "shard", axis=0, tiled=True),
    )
    gain_one = gathered[0].astype(jnp.float32)
    gain_query = gathered[1].astype(jnp.float32)
    gain_key = gathered[2].astype(jnp.float32)
    gain_two = gathered[3].astype(jnp.float32)
    inputs = tokens.astype(jnp.float32)
    scaled_one, first_pull = jax.vjp(rms_scale, inputs, gain_one)
    hidden_one = scaled_one.astype(jnp.bfloat16)
    projected = jnp.dot(hidden_one, gathered[4], preferred_element_type=jnp.float32)
    cosine, sine_table = rotary_tables(length)

    def query_key_local(raw_query, raw_key, query_gain, key_gain):
        return query_key(raw_query, raw_key, query_gain, key_gain, cosine, sine_table)

    rotated, rotary_pull = jax.vjp(
        query_key_local,
        projected[:, :model_width],
        projected[:, model_width : 2 * model_width],
        gain_query,
        gain_key,
    )
    query_low = rotated[0].astype(jnp.bfloat16)
    key_low = rotated[1].astype(jnp.bfloat16)
    value_low = (
        projected[:, 2 * model_width :].astype(jnp.bfloat16).reshape(length, HEADS, HEAD_DIM)
    )
    position = jnp.arange(length, dtype=jnp.int32)
    allowed = (position[:, None] >= position[None, :]) & (
        segments[0][:, None] == segments[0][None, :]
    )
    masked = jnp.where(
        allowed[None],
        jnp.einsum("qhd,khd->hqk", query_low, key_low, preferred_element_type=jnp.float32)
        * score_scale,
        -1e30,
    )
    largest = jnp.max(masked, axis=-1, keepdims=True)
    raised = jnp.exp(masked - largest)
    totals = jnp.sum(raised, axis=-1, keepdims=True)
    log_total = largest + jnp.log(totals)
    probs_low = (raised / totals).astype(jnp.bfloat16)
    attended_low = (
        jnp.einsum("hqk,khd->qhd", probs_low, value_low, preferred_element_type=jnp.float32)
        .reshape(length, model_width)
        .astype(jnp.bfloat16)
    )
    middle = inputs + jnp.dot(attended_low, gathered[5], preferred_element_type=jnp.float32)
    scaled_two, second_pull = jax.vjp(rms_scale, middle, gain_two)
    hidden_two = scaled_two.astype(jnp.bfloat16)
    router = softmax_rows(jnp.dot(hidden_two, gathered[6], preferred_element_type=jnp.float32))
    flat_expert = routes.reshape(pair_count)
    chosen = (flat_expert[:, None] == jnp.arange(experts_all, dtype=jnp.int32)[None, :]).astype(
        jnp.int32
    )
    before = jnp.cumsum(chosen, axis=0) - chosen
    rank_pair = jnp.sum(before * chosen, axis=1)
    capacity_pair = jnp.sum(chosen * tile_counts[None, :], axis=1) * TILE
    kept_pair = rank_pair < capacity_pair
    owner_index = flat_expert // local_experts
    local_index = flat_expert % local_experts
    slot_index = jnp.where(
        kept_pair, (local_index * expert_group + owner_index) * capacity + rank_pair, slots_all
    )
    slot_pair = (
        jnp.full((slots_all,), pair_count, jnp.int32)
        .at[slot_index]
        .set(jnp.arange(pair_count, dtype=jnp.int32), mode="drop")
    )
    slot_token = slot_pair // TOP
    zero_row = jnp.zeros((1, model_width), jnp.bfloat16)
    send_rows = jnp.concatenate([hidden_two, zero_row], axis=0)[slot_token].reshape(
        local_experts, expert_group, capacity, model_width
    )
    expert_rows = lax.all_to_all(
        send_rows, "expert", split_axis=1, concat_axis=1, tiled=True
    ).reshape(local_experts, expert_group * capacity, model_width)
    gate_up = jnp.einsum(
        "erd,edf->erf", expert_rows, gate_up_weight, preferred_element_type=jnp.float32
    )
    activated_full, swiglu_pull = jax.vjp(swiglu, gate_up)
    activated = activated_full.astype(jnp.bfloat16)
    expert_out = jnp.einsum(
        "erf,efd->erd", activated, down_weight, preferred_element_type=jnp.float32
    ).astype(jnp.bfloat16)
    returned = lax.all_to_all(
        expert_out.reshape(local_experts, expert_group, capacity, model_width),
        "expert",
        split_axis=1,
        concat_axis=1,
        tiled=True,
    )
    pair_out = jnp.concatenate([returned.reshape(slots_all, model_width), zero_row], axis=0)[
        slot_index
    ].reshape(length, TOP, model_width)
    chosen_float = chosen.astype(jnp.float32).reshape(length, TOP, experts_all)
    kept_float = kept_pair.reshape(length, TOP).astype(jnp.float32)
    pair_prob = jnp.sum(chosen_float * router[:, None, :], axis=-1) * kept_float
    mixture = jnp.sum(pair_prob[:, :, None] * pair_out.astype(jnp.float32), axis=1)
    block_out = (middle + mixture).astype(jnp.bfloat16)
    upstream = cotangent.astype(jnp.float32)
    qkv_back, out_back, router_back = (
        lax.all_gather(qkv_weight, "shard", axis=0, tiled=True),
        lax.all_gather(out_weight, "shard", axis=0, tiled=True),
        lax.all_gather(router_weight, "shard", axis=0, tiled=True),
    )
    prob_padded = jnp.concatenate([pair_prob.reshape(pair_count), jnp.zeros((1,), jnp.float32)])
    upstream_padded = jnp.concatenate([upstream, jnp.zeros((1, model_width), jnp.float32)], axis=0)
    send_grads = (prob_padded[slot_pair][:, None] * upstream_padded[slot_token]).astype(
        jnp.bfloat16
    )
    grad_rows_out = lax.all_to_all(
        send_grads.reshape(local_experts, expert_group, capacity, model_width),
        "expert",
        split_axis=1,
        concat_axis=1,
        tiled=True,
    ).reshape(local_experts, expert_group * capacity, model_width)
    grad_activated = jnp.einsum(
        "erd,efd->erf", grad_rows_out, down_weight, preferred_element_type=jnp.float32
    )
    grad_down_full = jnp.einsum(
        "erf,erd->efd", activated, grad_rows_out, preferred_element_type=jnp.float32
    )
    grad_gate_up_low = swiglu_pull(grad_activated)[0].astype(jnp.bfloat16)
    grad_gate_up_full = jnp.einsum(
        "erd,erf->edf", expert_rows, grad_gate_up_low, preferred_element_type=jnp.float32
    )
    grad_rows_in = jnp.einsum(
        "erf,edf->erd", grad_gate_up_low, gate_up_weight, preferred_element_type=jnp.float32
    ).astype(jnp.bfloat16)
    grad_gate_up_weight, grad_down_weight = (
        lax.psum_scatter(
            grad_gate_up_full.astype(jnp.bfloat16), "shard", scatter_dimension=1, tiled=True
        ).astype(jnp.float32),
        lax.psum_scatter(
            grad_down_full.astype(jnp.bfloat16), "shard", scatter_dimension=2, tiled=True
        ).astype(jnp.float32),
    )
    grad_back = lax.all_to_all(
        grad_rows_in.reshape(local_experts, expert_group, capacity, model_width),
        "expert",
        split_axis=1,
        concat_axis=1,
        tiled=True,
    )
    grad_pairs = jnp.concatenate([grad_back.reshape(slots_all, model_width), zero_row], axis=0)[
        slot_index
    ].reshape(length, TOP, model_width)
    grad_pair_prob = (
        jnp.sum(upstream[:, None, :] * pair_out.astype(jnp.float32), axis=-1) * kept_float
    )
    grad_router = jnp.sum(chosen_float * grad_pair_prob[:, :, None], axis=1)
    grad_logits = (
        router * (grad_router - jnp.sum(router * grad_router, axis=-1, keepdims=True))
    ).astype(jnp.bfloat16)
    grad_hidden_two = jnp.sum(grad_pairs.astype(jnp.float32), axis=1) + jnp.einsum(
        "te,de->td", grad_logits, router_back, preferred_element_type=jnp.float32
    )
    grad_middle_norm, grad_gain_two = second_pull(grad_hidden_two)
    grad_middle = upstream + grad_middle_norm
    grad_branch_low = grad_middle.astype(jnp.bfloat16)
    grad_attended_low = (
        jnp.einsum("te,de->td", grad_branch_low, out_back, preferred_element_type=jnp.float32)
        .astype(jnp.bfloat16)
        .reshape(length, HEADS, HEAD_DIM)
    )
    masked_again = jnp.where(
        allowed[None],
        jnp.einsum("qhd,khd->hqk", query_low, key_low, preferred_element_type=jnp.float32)
        * score_scale,
        -1e30,
    )
    probs_again = jnp.exp(masked_again - log_total)
    grad_probs = jnp.einsum(
        "qhd,khd->hqk", grad_attended_low, value_low, preferred_element_type=jnp.float32
    )
    grad_scores_low = (
        probs_again * (grad_probs - jnp.sum(probs_again * grad_probs, axis=-1, keepdims=True))
    ).astype(jnp.bfloat16)
    grad_queries = (
        jnp.einsum("hqk,khd->qhd", grad_scores_low, key_low, preferred_element_type=jnp.float32)
        * score_scale
    )
    grad_keys = (
        jnp.einsum("hqk,qhd->khd", grad_scores_low, query_low, preferred_element_type=jnp.float32)
        * score_scale
    )
    grad_values = jnp.einsum(
        "hqk,qhd->khd",
        probs_again.astype(jnp.bfloat16),
        grad_attended_low,
        preferred_element_type=jnp.float32,
    )
    grad_raw_query, grad_raw_key, grad_gain_query, grad_gain_key = rotary_pull(
        (grad_queries, grad_keys)
    )
    grad_projected_low = jnp.concatenate(
        [grad_raw_query, grad_raw_key, grad_values.reshape(length, model_width)], axis=-1
    ).astype(jnp.bfloat16)
    grad_hidden_one = jnp.einsum(
        "te,de->td", grad_projected_low, qkv_back, preferred_element_type=jnp.float32
    )
    grad_inputs_norm, grad_gain_one = first_pull(grad_hidden_one)
    grad_tokens = grad_middle + grad_inputs_norm

    def arrange(values):
        return reorder_features(values, shard_group, expert_group)

    grad_qkv_full = jnp.einsum(
        "td,te->de", arrange(hidden_one), grad_projected_low, preferred_element_type=jnp.float32
    )
    grad_out_full = jnp.einsum(
        "td,te->de", arrange(attended_low), grad_branch_low, preferred_element_type=jnp.float32
    )
    grad_router_full = jnp.einsum(
        "td,te->de", arrange(hidden_two), grad_logits, preferred_element_type=jnp.float32
    )
    gain_one_term = arrange(grad_gain_one)
    gain_query_term = arrange(grad_gain_query)
    gain_key_term = arrange(grad_gain_key)
    gain_two_term = arrange(grad_gain_two)
    pieces = (
        lax.psum_scatter(gain_one_term, ("expert", "shard"), scatter_dimension=0, tiled=True),
        lax.psum_scatter(gain_query_term, ("expert", "shard"), scatter_dimension=0, tiled=True),
        lax.psum_scatter(gain_key_term, ("expert", "shard"), scatter_dimension=0, tiled=True),
        lax.psum_scatter(gain_two_term, ("expert", "shard"), scatter_dimension=0, tiled=True),
        lax.psum_scatter(grad_qkv_full, ("expert", "shard"), scatter_dimension=0, tiled=True),
        lax.psum_scatter(grad_out_full, ("expert", "shard"), scatter_dimension=0, tiled=True),
        lax.psum_scatter(grad_router_full, ("expert", "shard"), scatter_dimension=0, tiled=True),
    )
    summed = (
        lax.all_gather(pieces[0].astype(jnp.bfloat16), "expert", axis=0, tiled=True).astype(
            jnp.float32
        ),
        lax.all_gather(pieces[1].astype(jnp.bfloat16), "expert", axis=0, tiled=True).astype(
            jnp.float32
        ),
        lax.all_gather(pieces[2].astype(jnp.bfloat16), "expert", axis=0, tiled=True).astype(
            jnp.float32
        ),
        lax.all_gather(pieces[3].astype(jnp.bfloat16), "expert", axis=0, tiled=True).astype(
            jnp.float32
        ),
        lax.all_gather(pieces[4].astype(jnp.bfloat16), "expert", axis=0, tiled=True).astype(
            jnp.float32
        ),
        lax.all_gather(pieces[5].astype(jnp.bfloat16), "expert", axis=0, tiled=True).astype(
            jnp.float32
        ),
        lax.all_gather(pieces[6].astype(jnp.bfloat16), "expert", axis=0, tiled=True).astype(
            jnp.float32
        ),
    )
    return (
        block_out,
        grad_tokens,
        summed[0],
        summed[1],
        summed[2],
        summed[3],
        summed[4],
        summed[5],
        summed[6],
        grad_gate_up_weight,
        grad_down_weight,
    )


def solution(mesh):
    return jax.shard_map(
        body,
        mesh=mesh,
        in_specs=(
            P(("expert", "shard"), None),
            P(("expert", "shard"), None),
            P(("expert", "shard"), None),
            P(("expert", "shard"), None),
            P(),
            P("shard"),
            P("shard"),
            P("shard"),
            P("shard"),
            P("shard", None),
            P("shard", None),
            P("shard", None),
            P("expert", None, None),
            P("expert", None, None),
        ),
        out_specs=(
            P(("expert", "shard"), None),
            P(("expert", "shard"), None),
            P("shard"),
            P("shard"),
            P("shard"),
            P("shard"),
            P("shard", None),
            P("shard", None),
            P("shard", None),
            P("expert", "shard", None),
            P("expert", None, "shard"),
        ),
        check_vma=False,
    )
```

profile of v0, /device:TPU:0, one launch (start us, length us, event | category | flops | bytes accessed | tf_op | source)
XLA Modules:
  0.0 2250.1 jit_solution(11328596843966210705)
XLA Ops:
  9.3 6.1 all-gather
  37.4 8.0 scatter_custom_fusion
  48.1 119.2 %all-gather.10.cloned.1.call-done = bf16[2048,6144]{1,0:T(8,128)(2,1)} async-done(((bf16[512,6144]{1,0:T(8,128)(2,1)}), bf16[2048,6144]{1,0:T(8,128)(2,1)}) %all-gather.10.cloned.1.call-update) | async-done | bytes 25165840 | tf_op jit(solution)/shard_map/all_gather | solution.py:95
  167.2 12.2 fusion.74
  196.6 30.6 %all-gather.12.cloned.1.call-done = bf16[2048,2048]{1,0:T(8,128)(2,1)} async-done(((bf16[512,2048]{1,0:T(8,128)(2,1)}), bf16[2048,2048]{1,0:T(8,128)(2,1)}) %all-gather.12.cloned.1.call-update) | async-done | bytes 8388624 | tf_op jit(solution)/shard_map/all_gather | solution.py:96
  234.7 10.9 gather_fusion
  245.5 8.4 copy.267
  261.4 12.5 gather_fusion.3
  281.3 11.8 gather_fusion.2
  293.1 9.0 fusion.2
  302.2 141.3 %all-to-all-done = bf16[2,8,128,2048]{3,2,0,1:T(8,128)(2,1)} async-done(((bf16[2,8,128,2048]{3,2,0,1:T(8,128)(2,1)}), bf16[2,8,128,2048]{3,2,0,1:T(8,128)(2,1)}, u32[]{:S(2)}, u32[]{:S(2)}) %all-to-all-start) | async-done | bytes 8388640 | tf_op jit(solution)/shard_map/all_to_all | solution.py:171
  448.4 8.4 copy.268
  456.9 24.5 %fusion.75 = f32[2,1024,2048]{2,1,0:T(8,128)} fusion(bf16[2,1024,2048]{2,1,0:T(8,128)(2,1)} %bitcast.151, bf16[2,2048,2048]{2,1,0:T(8,128)(2,1)} %param.26), kind=kOutput, calls=%fused_computation.185 | convolution fusion | flops 17179869184 | bytes 41943040 | tf_op jit(solution)/shard_map/erd,edf->erf/dot_general | solution.py:174
  481.4 149.7 %all-to-all-done.2 = bf16[2,8,128,2048]{3,2,0,1:T(8,128)(2,1)} async-done(((bf16[2,8,128,2048]{3,2,0,1:T(8,128)(2,1)}), bf16[2,8,128,2048]{3,2,0,1:T(8,128)(2,1)}, u32[]{:S(2)}, u32[]{:S(2)}) %all-to-all-start.2) | async-done | bytes 8388640 | tf_op jit(solution)/shard_map/all_to_all | solution.py:208
  631.1 8.3 copy.274
  639.4 24.8 %fusion.31 = (f32[2,1024,1024]{2,1,0:T(8,128)}, f32[2,1024,1024]{2,1,0:T(8,128)}, bf16[2,1024,1024]{2,1,0:T(8,128)(2,1)}) fusion(f32[2,1024,2048]{2,1,0:T(8,128)} %fusion.75, bf16[2,1024,2048]{2,1,0:T(8,128)(2,1)} %bitcast.153, bf16[2,1024,2048]{2,1,0:T(8,128)(2,1)} %param.27), kind=kOutput, calls=%fused_computation.85 | convolution fusion | flops 8623489024 | bytes 54525952 | tf_op jit(solution)/shard_map/erd,efd->erf/dot_general | solution.py:215
  664.3 15.2 convolution_convert_fusion.3
  679.5 8.4 copy.269
  692.8 25.0 %convolution_convert_fusion.2 = bf16[2,1024,2048]{2,1,0:T(8,128)(2,1)} fusion(bf16[2,2048,2048]{2,1,0:T(8,128)(2,1)} %param.26, f32[2,1024,1024]{2,1,0:T(8,128)} %get-tuple-element.40, f32[2,1024,1024]{2,1,0:T(8,128)} %get-tuple-element.39), kind=kOutput, calls=%fused_computation.20 | convolution fusion | flops 17192452096 | bytes 41943040 | tf_op jit(solution)/shard_map/erf,edf->erd/dot_general | solution.py:225
  717.9 8.3 copy.275
  726.2 148.6 %all-to-all-done.1 = bf16[2,8,128,2048]{3,2,0,1:T(8,128)(2,1)} async-done(((bf16[2,8,128,2048]{3,2,0,1:T(8,128)(2,1)}), bf16[2,8,128,2048]{3,2,0,1:T(8,128)(2,1)}, u32[]{:S(2)}, u32[]{:S(2)}) %all-to-all-start.1) | async-done | bytes 8388640 | tf_op jit(solution)/shard_map/all_to_all | solution.py:182
  883.0 8.4 copy.270
  891.4 8.5 concatenate.40
  899.9 20.8 gather_fusion.1
  920.7 9.5 fusion.1
  930.3 131.6 %all-to-all-done.3 = bf16[2,8,128,2048]{3,2,0,1:T(8,128)(2,1)} async-done(((bf16[2,8,128,2048]{3,2,0,1:T(8,128)(2,1)}), bf16[2,8,128,2048]{3,2,0,1:T(8,128)(2,1)}, u32[]{:S(2)}, u32[]{:S(2)}) %all-to-all-start.3) | async-done | bytes 8388640 | tf_op jit(solution)/shard_map/all_to_all | solution.py:236
  1061.9 8.3 copy.276
  1070.3 8.5 concatenate.43
  1078.7 21.2 gather_fusion.4
  1099.9 11.4 convert_reduce_fusion
  1117.6 8.1 fusion.40
  1128.7 7.1 convolution_convert_fusion.4
  1167.3 22.1 fusion.32
  1192.7 15.4 convolution_convert_fusion.1
  1208.2 27.3 %convolution_convert_fusion = bf16[2,2048,2048]{2,1,0:T(8,128)(2,1)} fusion(bf16[2,1024,2048]{2,1,0:T(8,128)(2,1)} %bitcast.152, f32[2,1024,1024]{2,1,0:T(8,128)} %get-tuple-element.40, f32[2,1024,1024]{2,1,0:T(8,128)} %get-tuple-element.39), kind=kOutput, calls=%fused_computation.14 | convolution fusion | flops 17196646400 | bytes 41943040 | tf_op jit(solution)/shard_map/erd,erf->edf/dot_general | solution.py:222
  1235.6 71.7 %reduce-scatter.10.cloned.1.call-done = f32[64,2048]{1,0:T(8,128)} async-done(((f32[2048,2048]{1,0:T(8,128)}), f32[64,2048]{1,0:T(8,128)}) %reduce-scatter.10.cloned.1.call-update) | async-done | bytes 524304 | tf_op jit(solution)/shard_map/reduce_scatter | solution.py:325
  1309.1 437.5 %reduce-scatter.8.cloned.1.call-done = f32[64,6144]{1,0:T(8,128)} async-done(((f32[2048,6144]{1,0:T(8,128)}), f32[64,6144]{1,0:T(8,128)}) %reduce-scatter.8.cloned.1.call-update) | async-done | bytes 1572880 | tf_op jit(solution)/shard_map/reduce_scatter | solution.py:324
  1750.4 14.2 fusion.8
  1765.2 39.5 %all-reduce.18 = (bf16[2048]{0:T(1024)(128)(2,1)S(1)}, bf16[2048]{0:T(1024)(128)(2,1)S(1)}, bf16[2048]{0:T(1024)(128)(2,1)S(1)}, bf16[2048]{0:T(1024)(128)(2,1)S(1)}) all-reduce(f32[2048]{0:T(1024)S(1)} %reshape.564, f32[2048]{0:T(1024)S(1)} %reshape.566, ...), channel_id=2, replica_groups=mesh['expert'=8,'shard'=4] {'expert','shard'}, use_global_device_ids=true, to_apply=%region_25.26.clone | all-reduce | flops 8192 | bytes 49152
  1805.9 21.1 all-reduce.19
  1832.8 49.8 %reduce-scatter.16.cloned.1.call-done = f32[64,16]{1,0:T(8,128)} async-done(((f32[2048,16]{1,0:T(8,128)}), f32[64,16]{1,0:T(8,128)}) %reduce-scatter.16.cloned.1.call-update) | async-done | bytes 4112
  1883.4 30.7 %all-gather.4 = bf16[8,64,16]{1,2,0:T(8,128)(2,1)S(1)} all-gather(bf16[1,64,16]{1,2,0:T(8,128)(2,1)S(1)} %bitcast.187), channel_id=1, replica_groups=mesh['expert'=8,'shard'=4] {'expert'}, dimensions={0}, use_global_device_ids=true | all-gather | bytes 18432 | tf_op jit(solution)/shard_map/all_gather | solution.py:347
  1914.9 38.7 %reduce-scatter.14.cloned.1.call-done = bf16[2,1024,512]{2,1,0:T(8,128)(2,1)} async-done(((bf16[2,1024,2048]{2,1,0:T(8,128)(2,1)}), bf16[2,1024,512]{2,1,0:T(8,128)(2,1)}) %reduce-scatter.14.cloned.1.call-update) | async-done | bytes 2097168 | tf_op jit(solution)/shard_map/reduce_scatter | solution.py:232
  1957.7 124.5 %reduce-scatter.12.cloned.1.call-done = bf16[2,512,2048]{2,1,0:T(8,128)(2,1)} async-done(((bf16[2,2048,2048]{2,1,0:T(8,128)(2,1)}), bf16[2,512,2048]{2,1,0:T(8,128)(2,1)}) %reduce-scatter.12.cloned.1.call-update) | async-done | bytes 4194320 | tf_op jit(solution)/shard_map/reduce_scatter | solution.py:229
  2082.2 6.7 convert_element_type.218
  2088.9 45.0 %all-gather.16.cloned.1.call-done = bf16[512,2048]{1,0:T(8,128)(2,1)} async-done(((bf16[64,2048]{1,0:T(8,128)(2,1)}), bf16[512,2048]{1,0:T(8,128)(2,1)}) %all-gather.16.cloned.1.call-update) | async-done | bytes 2097168 | tf_op jit(solution)/shard_map/all_gather | solution.py:344
  2138.0 95.8 %all-gather.14.cloned.1.call-done = bf16[512,6144]{1,0:T(8,128)(2,1)} async-done(((bf16[64,6144]{1,0:T(8,128)(2,1)}), bf16[512,6144]{1,0:T(8,128)(2,1)}) %all-gather.14.cloned.1.call-update) | async-done | bytes 6291472 | tf_op jit(solution)/shard_map/all_gather | solution.py:341
  2233.9 9.2 convert_element_type.211
  (317 shorter events, 149.9 us)
Async XLA Ops:
  7.2 13.6 copy-start.74
  7.2 18.8 copy-start.75
  7.2 29.4 %copy-start.76 = (s32[16]{0:T(128)S(1)}, s32[16]{0:T(128)}, u32[]{:S(2)}) copy-start(s32[16]{0:T(128)} %param.18) | copy-start | bytes 196
  7.2 39.5 %copy-start.11 = (bf16[256,2048]{1,0:T(8,128)(2,1)S(1)}, bf16[256,2048]{1,0:T(8,128)(2,1)}, u32[]{:S(2)}) copy-start(bf16[256,2048]{1,0:T(8,128)(2,1)} %param.14) | copy-start | bytes 3145732
  7.3 160.0 %all-gather.10.cloned.1.call-start = ((), (), s32[]{:S(2)}) async-start(), calls=%async_computation.9 | async-start | bytes 31457280 | tf_op jit(solution)/shard_map/all_gather | solution.py:95
  8.0 39.7 %copy-start.71 = (s32[1,256]{1,0:T(1,128)S(1)}, s32[1,256]{1,0:T(1,128)}, u32[]{:S(2)}) copy-start(s32[1,256]{1,0:T(1,128)} %param.16) | copy-start | bytes 3076
  8.0 219.1 %all-gather.12.cloned.1.call-start = ((), (), s32[]{:S(2)}) async-start(), calls=%async_computation.10 | async-start | bytes 10485760 | tf_op jit(solution)/shard_map/all_gather | solution.py:96
  15.4 164.0 %copy-start.39 = (f32[4,1,512]{2,1,0:T(1,128)}, f32[4,1,512]{2,1,0:T(1,128)S(1)}, u32[]{:S(2)}) copy-start(f32[4,1,512]{2,1,0:T(1,128)S(1)} %convert_element_type.223) | copy-start | bytes 24580
  20.9 159.0 %copy-start.35 = (f32[4,1,512]{2,1,0:T(1,128)}, f32[4,1,512]{2,1,0:T(1,128)S(1)}, u32[]{:S(2)}) copy-start(f32[4,1,512]{2,1,0:T(1,128)S(1)} %convert_element_type.224) | copy-start | bytes 24580
  26.1 153.8 %copy-start.37 = (f32[4,1,512]{2,1,0:T(1,128)}, f32[4,1,512]{2,1,0:T(1,128)S(1)}, u32[]{:S(2)}) copy-start(f32[4,1,512]{2,1,0:T(1,128)S(1)} %convert_element_type.225) | copy-start | bytes 24580
  31.3 202.3 %copy-start.33 = (f32[4,1,512]{2,1,0:T(1,128)}, f32[4,1,512]{2,1,0:T(1,128)S(1)}, u32[]{:S(2)}) copy-start(f32[4,1,512]{2,1,0:T(1,128)S(1)} %convert_element_type.226) | copy-start | bytes 24580
  47.6 131.8 %copy-start.60 = (f32[256]{0:T(256)}, f32[256]{0:T(256)S(1)}, u32[]{:S(2)}) copy-start(f32[256]{0:T(256)S(1)} %fusion.60) | copy-start | bytes 3076
  48.1 131.4 %copy-start.24 = (bf16[256,2048]{1,0:T(8,128)(2,1)}, bf16[256,2048]{1,0:T(8,128)(2,1)S(1)}, u32[]{:S(2)}) copy-start(bf16[256,2048]{1,0:T(8,128)(2,1)S(1)} %fusion.7) | copy-start | bytes 3145732
  196.6 36.4 %copy-start.21 = (bf16[16,128,256]{2,1,0:T(8,128)(2,1)}, bf16[16,128,256]{2,1,0:T(8,128)(2,1)S(1)}, u32[]{:S(2)}) copy-start(bf16[16,128,256]{2,1,0:T(8,128)(2,1)S(1)} %fusion.27) | copy-start | bytes 3145732
  233.0 12.5 copy-start.51
  234.5 44.7 %copy-start.13 = (bf16[256,2048]{1,0:T(8,128)(2,1)}, bf16[256,2048]{1,0:T(8,128)(2,1)S(1)}, u32[]{:S(2)}) copy-start(bf16[256,2048]{1,0:T(8,128)(2,1)S(1)} %multiply_convert_fusion.2) | copy-start | bytes 3145732
  254.0 189.5 %all-to-all-start = ((bf16[2,8,128,2048]{3,2,0,1:T(8,128)(2,1)}), bf16[2,8,128,2048]{3,2,0,1:T(8,128)(2,1)}, u32[]{:S(2)}, u32[]{:S(2)}) async-start(bf16[2,8,128,2048]{3,2,0,1:T(8,128)(2,1)} %copy.267), calls=%async_computation | async-start | bytes 16777216 | tf_op jit(solution)/shard_map/all_to_all | solution.py:171
  261.4 12.5 copy-start.53
  279.8 13.3 copy-start.49
  280.5 12.6 copy-start.41
  443.5 187.6 %all-to-all-start.2 = ((bf16[2,8,128,2048]{3,2,0,1:T(8,128)(2,1)}), bf16[2,8,128,2048]{3,2,0,1:T(8,128)(2,1)}, u32[]{:S(2)}, u32[]{:S(2)}) async-start(bf16[2,8,128,2048]{3,2,0,1:T(8,128)(2,1)} %fusion.2), calls=%async_computation.2 | async-start | bytes 16777216 | tf_op jit(solution)/shard_map/all_to_all | solution.py:208
  687.9 186.9 %all-to-all-start.1 = ((bf16[2,8,128,2048]{3,2,0,1:T(8,128)(2,1)}), bf16[2,8,128,2048]{3,2,0,1:T(8,128)(2,1)}, u32[]{:S(2)}, u32[]{:S(2)}) async-start(bf16[2,8,128,2048]{3,2,0,1:T(8,128)(2,1)} %copy.269), calls=%async_computation.1 | async-start | bytes 16777216 | tf_op jit(solution)/shard_map/all_to_all | solution.py:182
  726.2 153.8 %copy-start.15 = (bf16[256,2048]{1,0:T(8,128)(2,1)S(1)}, bf16[256,2048]{1,0:T(8,128)(2,1)}, u32[]{:S(2)}) copy-start(bf16[256,2048]{1,0:T(8,128)(2,1)} %param.15) | copy-start | bytes 3145732
  726.2 154.1 %copy-start.48 = (s32[2048,1]{0,1:T(1,128)S(1)}, s32[2048,1]{0,1:T(1,128)}, u32[]{:S(2)}) copy-start(s32[2048,1]{0,1:T(1,128)} %get-tuple-element.37) | copy-start | bytes 24580
  726.2 154.1 %copy-start.70 = (pred[2048]{0:T(1024)(128)(4,1)S(1)}, pred[2048]{0:T(1024)(128)(4,1)}, u32[]{:S(2)}) copy-start(pred[2048]{0:T(1024)(128)(4,1)} %get-tuple-element.36) | copy-start | bytes 6148
  726.2 154.3 %copy-start.42 = (f32[256,8]{0,1:T(8,128)S(1)}, f32[256,8]{0,1:T(8,128)}, u32[]{:S(2)}) copy-start(f32[256,8]{0,1:T(8,128)} %copy-done.41) | copy-start | bytes 24580
  874.8 187.1 %all-to-all-start.3 = ((bf16[2,8,128,2048]{3,2,0,1:T(8,128)(2,1)}), bf16[2,8,128,2048]{3,2,0,1:T(8,128)(2,1)}, u32[]{:S(2)}, u32[]{:S(2)}) async-start(bf16[2,8,128,2048]{3,2,0,1:T(8,128)(2,1)} %copy.275), calls=%async_computation.3 | async-start | bytes 16777216 | tf_op jit(solution)/shard_map/all_to_all | solution.py:236
  879.8 427.5 %reduce-scatter.10.cloned.1.call-start = ((), (), s32[]{:S(2)}) async-start(), calls=%async_computation.13 | async-start | bytes 17301504 | tf_op jit(solution)/shard_map/reduce_scatter | solution.py:325
  920.7 9.6 copy-start.50
  920.7 9.6 copy-start.55
  1099.9 11.5 copy-start.4
  1099.9 11.5 copy-start.26
  1099.9 11.5 copy-start.34
  1099.9 11.4 copy-start.52
  1125.8 620.8 %reduce-scatter.8.cloned.1.call-start = ((), (), s32[]{:S(2)}) async-start(), calls=%async_computation.11 | async-start | bytes 51904512 | tf_op jit(solution)/shard_map/reduce_scatter | solution.py:324
  1152.5 11.3 slice-start
  1189.4 693.2 %reduce-scatter.16.cloned.1.call-start = ((), (), s32[]{:S(2)}) async-start(), calls=%async_computation.17 | async-start | bytes 1081344
  1192.7 760.9 %reduce-scatter.14.cloned.1.call-start = ((), (), s32[]{:S(2)}) async-start(), calls=%async_computation.16 | async-start | bytes 10485760 | tf_op jit(solution)/shard_map/reduce_scatter | solution.py:232
  1208.1 874.1 %reduce-scatter.12.cloned.1.call-start = ((), (), s32[]{:S(2)}) async-start(), calls=%async_computation.15 | async-start | bytes 20971520 | tf_op jit(solution)/shard_map/reduce_scatter | solution.py:229
  1235.5 513.6 %copy-start.77 = (u32[32]{0:T(128)S(1)}, u32[32]{0:T(128)}, u32[]{:S(2)}) copy-start(u32[32]{0:T(128)} %constant.119) | copy-start | bytes 388
  1235.5 514.8 %copy-start.12 = (bf16[256,2048]{1,0:T(8,128)(2,1)S(1)}, bf16[256,2048]{1,0:T(8,128)(2,1)}, u32[]{:S(2)}) copy-start(bf16[256,2048]{1,0:T(8,128)(2,1)} %param.14) | copy-start | bytes 3145732
  1235.5 514.8 %copy-start.40 = (f32[4,1,512]{2,1,0:T(1,128)S(1)}, f32[4,1,512]{2,1,0:T(1,128)}, u32[]{:S(2)}) copy-start(f32[4,1,512]{2,1,0:T(1,128)} %copy-done.39) | copy-start | bytes 24580
  1235.5 514.8 %copy-start.61 = (f32[256]{0:T(256)S(1)}, f32[256]{0:T(256)}, u32[]{:S(2)}) copy-start(f32[256]{0:T(256)} %copy-done.60) | copy-start | bytes 3076
  1235.5 898.4 %all-gather.16.cloned.1.call-start = ((), (), s32[]{:S(2)}) async-start(), calls=%async_computation.14 | async-start | bytes 2359296 | tf_op jit(solution)/shard_map/all_gather | solution.py:344
  1309.0 924.8 %all-gather.14.cloned.1.call-start = ((), (), s32[]{:S(2)}) async-start(), calls=%async_computation.12 | async-start | bytes 7077888 | tf_op jit(solution)/shard_map/all_gather | solution.py:341
  1750.3 14.7 copy-start.47
  1750.3 79.0 %copy-start.63 = (f32[256]{0:T(256)S(1)}, f32[256]{0:T(256)}, u32[]{:S(2)}) copy-start(f32[256]{0:T(256)} %copy-done.62) | copy-start | bytes 3076
  1750.3 79.0 %copy-start.7 = (f32[256,2048]{1,0:T(8,128)S(1)}, f32[256,2048]{1,0:T(8,128)}, u32[]{:S(2)}) copy-start(f32[256,2048]{1,0:T(8,128)} %copy-done.5) | copy-start | bytes 6291460
  (45 other events, 150.7 us)
Sparse Core Ops, SparseCore 0:
  9.7 157.5 all-gather.9
  168.8 58.2 all-gather.11
  1125.9 181.3 reduce-scatter.9
  1313.5 433.0 reduce-scatter.7
  1748.7 133.8 reduce-scatter.15
  1885.8 67.6 reduce-scatter.13
  1956.1 126.0 reduce-scatter.11
  2084.6 49.2 all-gather.15
  2136.3 97.4 all-gather.13
where the time goes:
time: 2260 us; the launch traced here: 2250 us
  waiting for transfers between devices  1590 us (70%)
  matrix products  220 us (10%)
  local copies, waits for them, and re-layouts  198 us (9%)
  blocking collectives  118 us (5%)
  other arithmetic  90.1 us (4%)
    reduce_scatter x1, waiting for transfers between devices, body(): lax.psum_scatter(grad_qkv_full, ('expert', 'shard'), scatter_dimension=0,...  438 us
    all_to_all x1, waiting for transfers between devices, body(): lax.all_to_all(send_grads.reshape(local_experts, expert_group, capacity,...  150 us
    all_to_all x1, waiting for transfers between devices, body(): lax.all_to_all(expert_out.reshape(local_experts, expert_group, capacity,...  149 us
    all_to_all x1, waiting for transfers between devices, body(): lax.all_to_all(send_rows, 'expert', split_axis=1, concat_axis=1, tiled=True)  141 us
    all_to_all x1, waiting for transfers between devices, body(): lax.all_to_all(grad_rows_in.reshape(local_experts, expert_group, capacity...  132 us
    reduce_scatter x1, waiting for transfers between devices, body(): lax.psum_scatter(grad_gate_up_full.astype(jnp.bfloat16), 'shard', scatter...  124 us
    all_gather x1, waiting for transfers between devices, body(): lax.all_gather(qkv_weight, 'shard', axis=0, tiled=True)  119 us
    all_gather x1, waiting for transfers between devices, body(): lax.all_gather(pieces[4].astype(jnp.bfloat16), 'expert', axis=0, tiled=True)  95.8 us
  transfers between devices with their start and end apart: 13, of which 13 were waited for; matrix products, arithmetic and copies ran while one was open for 15% of the time, Pallas kernels for 0%

commit v1 on v0

v1 whole, which is shorter than its diff:
```python
import jax
import jax.numpy as jnp
from jax import lax
from jax.sharding import PartitionSpec as P

HEADS = 16
HEAD_DIM = 128
TOP = 8
TILE = 8


epsilon = 1e-05
rope_base = 10000.0


def rms_scale(values, scale_gain):
    return (
        values * lax.rsqrt(jnp.mean(values * values, axis=-1, keepdims=True) + epsilon) * scale_gain
    )


def rotary_tables(length):
    half_dim = HEAD_DIM // 2
    position = jnp.arange(length, dtype=jnp.float32)[:, None]
    frequency = rope_base ** (-jnp.arange(half_dim, dtype=jnp.float32) * 2.0 / HEAD_DIM)
    angles = position * frequency[None, :]
    angles = jnp.concatenate([angles, angles], axis=-1)
    return (jnp.cos(angles)[:, None, :], jnp.sin(angles)[:, None, :])


def rotate(vectors, cosine, sine_table):
    half_dim = vectors.shape[-1] // 2
    turned = jnp.concatenate([-vectors[..., half_dim:], vectors[..., :half_dim]], axis=-1)
    return vectors * cosine + turned * sine_table


def query_key(raw_query, raw_key, query_gain, key_gain, cosine, sine_table):
    length = raw_query.shape[0]
    queries = rms_scale(raw_query, query_gain).reshape(length, HEADS, HEAD_DIM)
    keys_rot = rms_scale(raw_key, key_gain).reshape(length, HEADS, HEAD_DIM)
    return (rotate(queries, cosine, sine_table), rotate(keys_rot, cosine, sine_table))


def swiglu(gate_up):
    half_dim = gate_up.shape[-1] // 2
    gate_part = gate_up[..., :half_dim]
    return gate_part / (1.0 + jnp.exp(-gate_part)) * gate_up[..., half_dim:]


def softmax_rows(logits):
    largest = jnp.max(logits, axis=-1, keepdims=True)
    raised = jnp.exp(logits - largest)
    return raised / jnp.sum(raised, axis=-1, keepdims=True)


def z_size(expert_group):
    return 4 if expert_group % 4 == 0 else 1


def shift(values, expert_group, dz, dx):
    z_all = z_size(expert_group)
    x_all = expert_group // z_all
    pairs = [
        (i, ((i // x_all + dz) % z_all) * x_all + (i % x_all + dx) % x_all)
        for i in range(expert_group)
    ]
    return lax.ppermute(values, "expert", pairs)


def gather_expert(block, expert_group):
    z_all = z_size(expert_group)
    x_all = expert_group // z_all
    rows = [block] + [shift(block, expert_group, dz, 0) for dz in range(1, z_all)]
    return [
        rows[dz] if dx == 0 else shift(rows[dz], expert_group, 0, dx)
        for dz in range(z_all)
        for dx in range(x_all)
    ]


def reduce_expert(parts, expert_group):
    z_all = z_size(expert_group)
    x_all = expert_group // z_all
    rows = []
    for dz in range(z_all):
        total = parts[dz * x_all].astype(jnp.float32)
        for dx in range(1, x_all):
            total = total + shift(parts[dz * x_all + dx], expert_group, 0, -dx).astype(jnp.float32)
        rows.append(total)
    total = rows[0]
    for dz in range(1, z_all):
        total = total + shift(
            rows[dz].astype(jnp.bfloat16), expert_group, -dz, 0
        ).astype(jnp.float32)
    return total


def relative_sources(expert_group):
    z_all = z_size(expert_group)
    x_all = expert_group // z_all
    me = lax.axis_index("expert")
    order = jnp.arange(expert_group, dtype=jnp.int32)
    return ((me // x_all - order // x_all) % z_all) * x_all + (me % x_all - order % x_all) % x_all


def body(
    tokens,
    cotangent,
    segments,
    routes,
    tile_counts,
    norm_one,
    norm_query,
    norm_key,
    norm_two,
    qkv_weight,
    out_weight,
    router_weight,
    gate_up_weight,
    down_weight,
):
    f32, bf16 = jnp.float32, jnp.bfloat16
    length, model_width = tokens.shape
    experts_all = tile_counts.shape[0]
    local_experts = gate_up_weight.shape[0]
    expert_group = lax.axis_size("expert")
    shard_group = lax.axis_size("shard")
    capacity = length * TOP // (experts_all * TILE) * TILE
    score_scale = HEAD_DIM ** (-0.5)
    own_expert = lax.axis_index("expert")
    own_shard = lax.axis_index("shard")
    sources = relative_sources(expert_group)

    def gather(values, axis):
        return lax.all_gather(values, axis, axis=0, tiled=True)

    qkv_full = gather(qkv_weight, "shard")
    out_full = gather(out_weight, "shard")
    router_full = gather(router_weight, "shard")
    gains = lax.all_gather(
        jnp.stack([norm_one, norm_query, norm_key, norm_two]), "shard", axis=1, tiled=True
    ).astype(f32)
    gain_one, gain_query, gain_key, gain_two = gains[0], gains[1], gains[2], gains[3]

    expert_ids = jnp.arange(experts_all, dtype=jnp.int32)
    chosen = jnp.any(routes[:, :, None] == expert_ids[None, None, :], axis=1)
    position = jnp.arange(length, dtype=jnp.int32)
    earlier = (position[:, None] > position[None, :]).astype(bf16)
    rank = jnp.dot(earlier, chosen.astype(bf16), preferred_element_type=f32)
    kept = chosen & (rank < (tile_counts * TILE).astype(f32)[None, :])
    place = jnp.where(kept, rank, -1.0)
    place_all = lax.all_gather(place, "expert", axis=0, tiled=False)[sources]
    place_own = lax.dynamic_slice_in_dim(
        place_all, own_expert * local_experts, local_experts, axis=2
    )
    place_own = place_own.transpose(0, 2, 1)
    slots = jnp.arange(capacity, dtype=jnp.int32).astype(f32)
    one_hot = place_own[:, :, None, :] == slots[None, None, :, None]
    one_hot_low = one_hot.astype(bf16)
    upstream_all = jnp.stack(gather_expert(cotangent, expert_group))

    inputs = tokens.astype(f32)
    scaled_one, first_pull = jax.vjp(rms_scale, inputs, gain_one)
    hidden_one = scaled_one.astype(bf16)
    hidden_one_columns = lax.all_to_all(
        hidden_one, "shard", split_axis=1, concat_axis=0, tiled=True
    )
    projected = jnp.dot(hidden_one, qkv_full, preferred_element_type=f32)
    cosine, sine_table = rotary_tables(length)

    def query_key_local(raw_query, raw_key, query_gain, key_gain):
        return query_key(raw_query, raw_key, query_gain, key_gain, cosine, sine_table)

    rotated, rotary_pull = jax.vjp(
        query_key_local,
        projected[:, :model_width],
        projected[:, model_width : 2 * model_width],
        gain_query,
        gain_key,
    )
    query_low = rotated[0].astype(bf16)
    key_low = rotated[1].astype(bf16)
    value_low = projected[:, 2 * model_width :].astype(bf16).reshape(length, HEADS, HEAD_DIM)
    allowed = (position[:, None] >= position[None, :]) & (
        segments[0][:, None] == segments[0][None, :]
    )
    masked = jnp.where(
        allowed[None],
        jnp.einsum("qhd,khd->hqk", query_low, key_low, preferred_element_type=f32) * score_scale,
        -1e30,
    )
    probs = softmax_rows(masked)
    probs_low = probs.astype(bf16)
    attended_low = (
        jnp.einsum("hqk,khd->qhd", probs_low, value_low, preferred_element_type=f32)
        .reshape(length, model_width)
        .astype(bf16)
    )
    attended_columns = lax.all_to_all(
        attended_low, "shard", split_axis=1, concat_axis=0, tiled=True
    )
    middle = inputs + jnp.dot(attended_low, out_full, preferred_element_type=f32)
    scaled_two, second_pull = jax.vjp(rms_scale, middle, gain_two)
    hidden_two = scaled_two.astype(bf16)
    hidden_all = jnp.stack(gather_expert(hidden_two, expert_group))
    router = softmax_rows(jnp.dot(hidden_two, router_full, preferred_element_type=f32))
    prob = jnp.where(kept, router, 0.0)
    prob_all = lax.all_gather(prob, "expert", axis=0, tiled=False)[sources]
    prob_own = lax.dynamic_slice_in_dim(
        prob_all, own_expert * local_experts, local_experts, axis=2
    ).transpose(0, 2, 1)

    expert_rows = jnp.einsum(
        "sect,std->escd", one_hot_low, hidden_all, preferred_element_type=f32
    ).astype(bf16)
    row_count = expert_group * capacity
    expert_rows = expert_rows.reshape(local_experts, row_count, model_width)
    gate_up = jnp.einsum("erd,edf->erf", expert_rows, gate_up_weight, preferred_element_type=f32)
    activated_full, swiglu_pull = jax.vjp(swiglu, gate_up)
    activated = activated_full.astype(bf16)
    expert_out = jnp.einsum(
        "erf,efd->erd", activated, down_weight, preferred_element_type=f32
    ).astype(bf16)
    weighted = jnp.where(one_hot, prob_own[:, :, None, :], 0.0)
    weighted_high = weighted.astype(bf16)
    weighted_low = (weighted - weighted_high.astype(f32)).astype(bf16)
    out_rows = expert_out.reshape(local_experts, expert_group, capacity, model_width)
    mixture_parts = (
        jnp.einsum("sect,escd->std", weighted_high, out_rows, preferred_element_type=f32)
        + jnp.einsum("sect,escd->std", weighted_low, out_rows, preferred_element_type=f32)
    ).astype(bf16)
    mixture = reduce_expert([mixture_parts[i] for i in range(expert_group)], expert_group)
    block_out = (middle + mixture).astype(bf16)

    prob_rows = jnp.sum(weighted, axis=3).transpose(1, 0, 2).reshape(local_experts, row_count)
    upstream_rows = jnp.einsum(
        "sect,std->escd", one_hot_low, upstream_all, preferred_element_type=f32
    ).reshape(local_experts, row_count, model_width)
    grad_expert = (prob_rows[:, :, None] * upstream_rows).astype(bf16)
    grad_prob_rows = jnp.sum(upstream_rows * expert_out.astype(f32), axis=-1).reshape(
        local_experts, expert_group, capacity
    )
    grad_router_parts = jnp.sum(
        jnp.where(one_hot, grad_prob_rows.transpose(1, 0, 2)[:, :, :, None], 0.0), axis=2
    )
    back = jnp.zeros((expert_group, local_experts, length), f32).at[sources].set(grad_router_parts)
    grad_router = lax.all_to_all(back, "expert", split_axis=0, concat_axis=0, tiled=True)
    grad_router = grad_router.reshape(experts_all, length).T
    grad_activated = jnp.einsum("erd,efd->erf", grad_expert, down_weight, preferred_element_type=f32)
    grad_gate_up_low = swiglu_pull(grad_activated)[0].astype(bf16)
    grad_row = jnp.einsum(
        "erf,edf->erd", grad_gate_up_low, gate_up_weight, preferred_element_type=f32
    ).astype(bf16)
    grad_hidden_parts = jnp.einsum(
        "sect,escd->std",
        one_hot_low,
        grad_row.reshape(local_experts, expert_group, capacity, model_width),
        preferred_element_type=f32,
    ).astype(bf16)
    grad_rows_sum = reduce_expert([grad_hidden_parts[i] for i in range(expert_group)], expert_group)
    grad_down_full = jnp.einsum("erf,erd->efd", activated, grad_expert, preferred_element_type=f32)
    grad_gate_up_full = jnp.einsum(
        "erd,erf->edf", expert_rows, grad_gate_up_low, preferred_element_type=f32
    )
    grad_gate_up_weight = lax.psum_scatter(
        grad_gate_up_full.astype(bf16), "shard", scatter_dimension=1, tiled=True
    ).astype(f32)
    grad_down_weight = lax.psum_scatter(
        grad_down_full.astype(bf16), "shard", scatter_dimension=2, tiled=True
    ).astype(f32)

    upstream = cotangent.astype(f32)
    grad_logits = (
        router * (grad_router - jnp.sum(router * grad_router, axis=-1, keepdims=True))
    ).astype(bf16)
    grad_hidden_two = grad_rows_sum + jnp.einsum(
        "te,de->td", grad_logits, router_full, preferred_element_type=f32
    )
    grad_middle_norm, grad_gain_two = second_pull(grad_hidden_two)
    grad_middle = upstream + grad_middle_norm
    grad_branch_low = grad_middle.astype(bf16)
    grad_attended_low = (
        jnp.einsum("te,de->td", grad_branch_low, out_full, preferred_element_type=f32)
        .astype(bf16)
        .reshape(length, HEADS, HEAD_DIM)
    )
    grad_probs = jnp.einsum(
        "qhd,khd->hqk", grad_attended_low, value_low, preferred_element_type=f32
    )
    grad_scores_low = (
        probs * (grad_probs - jnp.sum(probs * grad_probs, axis=-1, keepdims=True))
    ).astype(bf16)
    grad_queries = (
        jnp.einsum("hqk,khd->qhd", grad_scores_low, key_low, preferred_element_type=f32)
        * score_scale
    )
    grad_keys = (
        jnp.einsum("hqk,qhd->khd", grad_scores_low, query_low, preferred_element_type=f32)
        * score_scale
    )
    grad_values = jnp.einsum(
        "hqk,qhd->khd", probs_low, grad_attended_low, preferred_element_type=f32
    )
    grad_raw_query, grad_raw_key, grad_gain_query, grad_gain_key = rotary_pull(
        (grad_queries, grad_keys)
    )
    grad_projected_low = jnp.concatenate(
        [grad_raw_query, grad_raw_key, grad_values.reshape(length, model_width)], axis=-1
    ).astype(bf16)
    grad_hidden_one = jnp.einsum(
        "te,de->td", grad_projected_low, qkv_full, preferred_element_type=f32
    )
    grad_inputs_norm, grad_gain_one = first_pull(grad_hidden_one)
    grad_tokens = grad_middle + grad_inputs_norm

    def over_sequences(columns, grads):
        part = jnp.einsum("td,te->de", columns, gather(grads, "shard"), preferred_element_type=f32)
        return lax.psum(part.astype(bf16), "expert").astype(f32)

    grad_out_weight = over_sequences(attended_columns, grad_branch_low)
    grad_qkv_weight = over_sequences(hidden_one_columns, grad_projected_low)
    grad_router_part = jnp.einsum(
        "td,te->ed", hidden_two, grad_logits, preferred_element_type=f32
    )
    small = jnp.concatenate(
        [
            grad_router_part,
            jnp.stack([grad_gain_one, grad_gain_query, grad_gain_key, grad_gain_two]),
        ],
        axis=0,
    )
    small = lax.psum(small, ("expert", "shard"))
    width = norm_one.shape[0]
    small = lax.dynamic_slice_in_dim(small, own_shard * width, width, axis=1)
    return (
        block_out,
        grad_tokens,
        small[experts_all],
        small[experts_all + 1],
        small[experts_all + 2],
        small[experts_all + 3],
        grad_qkv_weight,
        grad_out_weight,
        small[:experts_all].T,
        grad_gate_up_weight,
        grad_down_weight,
    )


def solution(mesh):
    return jax.shard_map(
        body,
        mesh=mesh,
        in_specs=(
            P(("expert", "shard"), None),
            P(("expert", "shard"), None),
            P(("expert", "shard"), None),
            P(("expert", "shard"), None),
            P(),
            P("shard"),
            P("shard"),
            P("shard"),
            P("shard"),
            P("shard", None),
            P("shard", None),
            P("shard", None),
            P("expert", None, None),
            P("expert", None, None),
        ),
        out_specs=(
            P(("expert", "shard"), None),
            P(("expert", "shard"), None),
            P("shard"),
            P("shard"),
            P("shard"),
            P("shard"),
            P("shard", None),
            P("shard", None),
            P("shard", None),
            P("expert", "shard", None),
            P("expert", None, "shard"),
        ),
        check_vma=False,
    )
```

time: 2260 us -> 1530 us (0.68)
  waiting for transfers between devices: 1590 us -> 822 us
  local copies, waits for them, and re-layouts: 198 us -> 90.3 us
  blocking collectives: 118 us -> 215 us
  matrix products: 220 us -> 252 us
  starting transfers between devices: 21.5 us -> 47.3 us
    reduce_scatter x4 -> x2, waiting for transfers between devices: 672 us -> 115 us  [the longest x1 115 us: body(): lax.psum_scatter(grad_gate_up_full.astype(bf16), 'shard', scatter_dimensi...]
    all_to_all x4 -> x2, waiting for transfers between devices: 571 us -> 44.8 us  [the longest x1 24.9 us: body(): lax.all_to_all(attended_low, 'shard', split_axis=1, concat_axis=0, tiled=...]
    ppermute x0 -> x28, waiting for transfers between devices: none -> 315 us  [shift(): return lax.ppermute(values, 'expert', pairs)]
    psum x0 -> x2, waiting for transfers between devices: none -> 270 us  [the longest x1 270 us: over_sequences(): return lax.psum(part.astype(bf16), 'expert').astype(f32)]
    all_gather x4, waiting for transfers between devices: 291 us -> 74.8 us  [gather(): return lax.all_gather(values, axis, axis=0, tiled=True)]
    all_gather x6 -> x4, blocking collectives: 57.8 us -> 149 us  [the longest x1 108 us: body(): place_all = lax.all_gather(place, 'expert', axis=0, tiled=False)[sources]]
    gather x5 -> x2, local copies, waits for them, and re-layouts: 77.1 us -> 1.11 us  [the longest x1 0.56 us: body(): prob_all = lax.all_gather(prob, 'expert', axis=0, tiled=False)[sources]]
    all_to_all x0 -> x1, blocking collectives: none -> 65.4 us  [body(): lax.all_to_all(back, 'expert', split_axis=0, concat_axis=0, tiled=True)]
  transfers between devices with their start and end apart: 13 -> 38, of which waited for: 13 -> 22; matrix products, arithmetic and copies ran while one was open for 15% -> 17% of each run, Pallas kernels for 0% -> 0%
where the time goes in v1:
time: 1530 us; the launch traced here: 1520 us
  waiting for transfers between devices  822 us (54%)
  matrix products  252 us (16%)
  blocking collectives  215 us (14%)
  local copies, waits for them, and re-layouts  90.3 us (6%)
  other arithmetic  81.2 us (5%)
  starting transfers between devices  47.3 us (3%)
  between operations  15.5 us (1%)
    ppermute x28, waiting for transfers between devices, shift(): return lax.ppermute(values, 'expert', pairs)  315 us
    psum x1, waiting for transfers between devices, over_sequences(): return lax.psum(part.astype(bf16), 'expert').astype(f32)  270 us
    reduce_scatter x1, waiting for transfers between devices, body(): lax.psum_scatter(grad_gate_up_full.astype(bf16), 'shard', scatter_dimensi...  115 us
    all_gather x1, blocking collectives, body(): place_all = lax.all_gather(place, 'expert', axis=0, tiled=False)[sources]  108 us
    all_gather x4, waiting for transfers between devices, gather(): return lax.all_gather(values, axis, axis=0, tiled=True)  74.8 us
    all_to_all x1, blocking collectives, body(): lax.all_to_all(back, 'expert', split_axis=0, concat_axis=0, tiled=True)  65.4 us
    unnamed x171, local copies, waits for them, and re-layouts  41.2 us
    ppermute x28, starting transfers between devices, shift(): return lax.ppermute(values, 'expert', pairs)  40 us
  transfers between devices with their start and end apart: 38, of which 22 were waited for; matrix products, arithmetic and copies ran while one was open for 17% of the time, Pallas kernels for 0%

profile of v1, /device:TPU:0, one launch (start us, length us, event | category | flops | bytes accessed | tf_op | source)
XLA Modules:
  0.0 1522.5 jit_solution(4606797809171483096)
XLA Ops:
  26.5 11.6 collective-permute-done.15
  45.7 36.6 %collective-permute-done.17 = bf16[256,2048]{1,0:T(8,128)(2,1)} collective-permute-done((bf16[256,2048]{1,0:T(8,128)(2,1)S(1)}, bf16[256,2048]{1,0:T(8,128)(2,1)}, u32[]{:S(2)}, u32[]{:S(2)}) %collective-permute-start.17) | collective-permute-done | bytes 1048608 | tf_op jit(solution)/shard_map/ppermute | solution.py:67
  93.5 15.0 collective-permute-done.18
  111.9 18.1 %collective-permute-done.20 = bf16[256,2048]{1,0:T(8,128)(2,1)S(1)} collective-permute-done((bf16[256,2048]{1,0:T(8,128)(2,1)}, bf16[256,2048]{1,0:T(8,128)(2,1)S(1)}, u32[]{:S(2)}, u32[]{:S(2)}) %collective-permute-start.20) | collective-permute-done | bytes 1048608 | tf_op jit(solution)/shard_map/ppermute | solution.py:67
  131.0 36.6 %all-gather.7.cloned.1.call-done = bf16[2048,6144]{1,0:T(8,128)(2,1)} async-done(((bf16[512,6144]{1,0:T(8,128)(2,1)}), bf16[2048,6144]{1,0:T(8,128)(2,1)}) %all-gather.7.cloned.1.call-update) | async-done | bytes 25165840 | tf_op jit(solution)/shard_map/all_gather | solution.py:135
  167.6 11.9 fusion.133
  201.3 26.1 %all-gather.9.cloned.1.call-done = bf16[2048,2048]{1,0:T(8,128)(2,1)} async-done(((bf16[512,2048]{1,0:T(8,128)(2,1)}), bf16[2048,2048]{1,0:T(8,128)(2,1)}) %all-gather.9.cloned.1.call-update) | async-done | bytes 8388624 | tf_op jit(solution)/shard_map/all_gather | solution.py:135
  227.5 5.8 multiply_reduce_fusion.7
  243.3 107.6 %all-gather = f32[2048,16]{0,1:T(8,128)S(1)} all-gather(f32[256,16]{0,1:T(8,128)S(1)} %get-tuple-element.75), channel_id=2, replica_groups=mesh['expert'=8,'shard'=4] {'expert'}, dimensions={0}, use_global_device_ids=true | all-gather | bytes 147456 | tf_op jit(solution)/shard_map/all_gather | solution.py:152
  350.9 30.8 %all-gather.1 = f32[2048,16]{0,1:T(8,128)S(1)} all-gather(f32[256,16]{0,1:T(8,128)S(1)} %get-tuple-element.74), channel_id=3, replica_groups=mesh['expert'=8,'shard'=4] {'expert'}, dimensions={0}, use_global_device_ids=true | all-gather | bytes 147456 | tf_op jit(solution)/shard_map/all_gather | solution.py:208
  382.9 10.6 fusion.14
  394.2 11.7 copy.138
  412.6 7.3 collective-permute-done.2
  423.2 18.9 %collective-permute-done.4 = bf16[256,2048]{1,0:T(8,128)(2,1)S(1)} collective-permute-done((bf16[256,2048]{1,0:T(8,128)(2,1)}, bf16[256,2048]{1,0:T(8,128)(2,1)S(1)}, u32[]{:S(2)}, u32[]{:S(2)}) %collective-permute-start.4) | collective-permute-done | bytes 1048608 | tf_op jit(solution)/shard_map/ppermute | solution.py:67
  444.1 9.2 collective-permute-done.6
  454.3 8.4 convert_bitcast_fusion
  462.7 8.4 copy.134
  471.1 21.5 %fusion.134 = f32[2,1024,2048]{2,1,0:T(8,128)S(1)} fusion(bf16[2,1024,2048]{2,1,0:T(8,128)(2,1)} %bitcast.271, bf16[2,2048,2048]{2,1,0:T(8,128)(2,1)} %param.26), kind=kOutput, calls=%fused_computation.266 | convolution fusion | flops 17179869184 | bytes 41943040 | tf_op jit(solution)/shard_map/erd,edf->erf/dot_general | solution.py:218
  492.6 5.8 copy-done.8
  502.6 18.1 %fusion.2 = (f32[2,1024]{1,0:T(2,128)S(1)}, bf16[2,1024,2048]{2,1,0:T(8,128)(2,1)}) fusion(f32[2,8,128,2048]{3,2,1,0:T(8,128)} %copy.138, bf16[2,1024,1024]{2,1,0:T(8,128)(2,1)} %multiply_convert_fusion, bf16[2,1024,2048]{2,1,0:T(8,128)(2,1)} %param.27), kind=kOutput, calls=%fused_computation.8 | convolution fusion | flops 8606709760 | bytes 37756928 | tf_op jit(solution)/shard_map/erf,efd->erd/dot_general | solution.py:221
  522.6 9.0 fusion.1
  531.6 21.5 %fusion.68 = (f32[2,1024,1024]{2,1,0:T(8,128)}, f32[2,1024,1024]{2,1,0:T(8,128)}) fusion(f32[2,1024,2048]{2,1,0:T(8,128)} %copy-done.8, bf16[2,1024,2048]{2,1,0:T(8,128)(2,1)} %fusion.1, bf16[2,1024,2048]{2,1,0:T(8,128)(2,1)} %param.27), kind=kOutput, calls=%fused_computation.126 | convolution fusion | flops 8619294720 | bytes 50331648 | tf_op jit(solution)/shard_map/erd,efd->erf/dot_general | solution.py:249
  553.1 25.3 %convolution_convert_fusion.3 = bf16[2,1024,2048]{2,1,0:T(8,128)(2,1)} fusion(bf16[2,2048,2048]{2,1,0:T(8,128)(2,1)} %param.26, f32[2,1024,1024]{2,1,0:T(8,128)} %get-tuple-element.31, f32[2,1024,1024]{2,1,0:T(8,128)} %get-tuple-element.30), kind=kOutput, calls=%fused_computation.31 | convolution fusion | flops 17192452096 | bytes 41943040 | tf_op jit(solution)/shard_map/erf,edf->erd/dot_general | solution.py:251
  589.2 21.9 %collective-permute-done.22 = bf16[256,2048]{1,0:T(8,128)(2,1)S(1)} collective-permute-done((bf16[256,2048]{1,0:T(8,128)(2,1)S(1)}, bf16[256,2048]{1,0:T(8,128)(2,1)S(1)}, u32[]{:S(2)}, u32[]{:S(2)}) %collective-permute-start.22) | collective-permute-done | bytes 1048608 | tf_op jit(solution)/shard_map/ppermute | solution.py:67
  611.1 22.5 %collective-permute-done.24 = bf16[256,2048]{1,0:T(8,128)(2,1)S(1)} collective-permute-done((bf16[256,2048]{1,0:T(8,128)(2,1)S(1)}, bf16[256,2048]{1,0:T(8,128)(2,1)S(1)}, u32[]{:S(2)}, u32[]{:S(2)}) %collective-permute-start.24) | collective-permute-done | bytes 1048608 | tf_op jit(solution)/shard_map/ppermute | solution.py:67
  633.6 21.4 %collective-permute-done.26 = bf16[256,2048]{1,0:T(8,128)(2,1)S(1)} collective-permute-done((bf16[256,2048]{1,0:T(8,128)(2,1)S(1)}, bf16[256,2048]{1,0:T(8,128)(2,1)S(1)}, u32[]{:S(2)}, u32[]{:S(2)}) %collective-permute-start.26) | collective-permute-done | bytes 1048608 | tf_op jit(solution)/shard_map/ppermute | solution.py:67
  662.0 65.4 %all_to_all.40 = f32[8,2,256]{2,1,0:T(2,128)S(1)} all-to-all(f32[8,2,256]{2,1,0:T(2,128)S(1)} %scatter_fusion), channel_id=1, replica_groups=mesh['expert'=8,'shard'=4] {'expert'}, dimensions={0} | all-to-all | bytes 32768 | tf_op jit(solution)/shard_map/all_to_all | solution.py:247
  734.9 6.1 convolution_convert_fusion.6
  777.1 15.0 fusion.33
  793.5 15.6 %convolution_convert_fusion.2 = bf16[2,1024,2048]{2,1,0:T(8,128)(2,1)} fusion(bf16[2,1024,1024]{2,1,0:T(8,128)(2,1)} %multiply_convert_fusion, bf16[2,1024,2048]{2,1,0:T(8,128)(2,1)} %fusion.1), kind=kOutput, calls=%fused_computation.30 | convolution fusion | flops 8594128896 | bytes 20971520 | tf_op jit(solution)/shard_map/erf,erd->efd/dot_general | solution.py:261
  816.2 24.9 %all-to-all-done.2 = bf16[256,4,512]{2,0,1:T(8,128)(2,1)S(1)} async-done(((bf16[256,4,512]{2,0,1:T(8,128)(2,1)}), bf16[256,4,512]{2,0,1:T(8,128)(2,1)S(1)}, u32[]{:S(2)}, u32[]{:S(2)}) %all-to-all-start.2) | async-done | bytes 1048608 | tf_op jit(solution)/shard_map/all_to_all | solution.py:199
  844.7 6.0 convolution_convert_fusion.5
  850.7 19.9 %all-to-all-done.1 = bf16[256,4,512]{2,0,1:T(8,128)(2,1)S(1)} async-done(((bf16[256,4,512]{2,0,1:T(8,128)(2,1)}), bf16[256,4,512]{2,0,1:T(8,128)(2,1)S(1)}, u32[]{:S(2)}, u32[]{:S(2)}) %all-to-all-start.1) | async-done | bytes 1048608 | tf_op jit(solution)/shard_map/all_to_all | solution.py:165
  870.6 12.0 all-gather.11.cloned.1.call-done
  882.7 13.3 convolution_convert_fusion.1
  896.1 27.0 %convolution_convert_fusion = bf16[2,2048,2048]{2,1,0:T(8,128)(2,1)} fusion(bf16[2,1024,2048]{2,1,0:T(8,128)(2,1)} %bitcast.272, f32[2,1024,1024]{2,1,0:T(8,128)} %get-tuple-element.31, f32[2,1024,1024]{2,1,0:T(8,128)} %get-tuple-element.30), kind=kOutput, calls=%fused_computation.12 | convolution fusion | flops 17196646400 | bytes 41943040 | tf_op jit(solution)/shard_map/erd,erf->edf/dot_general | solution.py:262
  923.8 9.4 fusion.10
  933.2 11.7 fusion.3
  952.8 22.0 %collective-permute-done.10 = bf16[256,2048]{1,0:T(8,128)(2,1)S(1)} collective-permute-done((bf16[256,2048]{1,0:T(8,128)(2,1)S(1)}, bf16[256,2048]{1,0:T(8,128)(2,1)S(1)}, u32[]{:S(2)}, u32[]{:S(2)}) %collective-permute-start.10) | collective-permute-done | bytes 1048608 | tf_op jit(solution)/shard_map/ppermute | solution.py:67
  974.8 22.9 %collective-permute-done.12 = bf16[256,2048]{1,0:T(8,128)(2,1)S(1)} collective-permute-done((bf16[256,2048]{1,0:T(8,128)(2,1)S(1)}, bf16[256,2048]{1,0:T(8,128)(2,1)S(1)}, u32[]{:S(2)}, u32[]{:S(2)}) %collective-permute-start.12) | collective-permute-done | bytes 1048608 | tf_op jit(solution)/shard_map/ppermute | solution.py:67
  997.7 22.6 %collective-permute-done.8 = bf16[256,2048]{1,0:T(8,128)(2,1)S(1)} collective-permute-done((bf16[256,2048]{1,0:T(8,128)(2,1)S(1)}, bf16[256,2048]{1,0:T(8,128)(2,1)S(1)}, u32[]{:S(2)}, u32[]{:S(2)}) %collective-permute-start.8) | collective-permute-done | bytes 1048608 | tf_op jit(solution)/shard_map/ppermute | solution.py:67
  1031.0 11.2 collective-permute-done.7
  1042.2 54.4 %collective-permute-done.11 = bf16[256,2048]{1,0:T(8,128)(2,1)} collective-permute-done((bf16[256,2048]{1,0:T(8,128)(2,1)}, bf16[256,2048]{1,0:T(8,128)(2,1)}, u32[]{:S(2)}, u32[]{:S(2)}) %collective-permute-start.11) | collective-permute-done | bytes 1048608 | tf_op jit(solution)/shard_map/ppermute | solution.py:67
  1096.6 6.8 fusion.37
  1110.6 270.3 %all-reduce.12.cloned.1.call-done = (bf16[512,6144]{1,0:T(8,128)(2,1)}, bf16[512,2048]{1,0:T(8,128)(2,1)}) async-done(((bf16[512,6144]{1,0:T(8,128)(2,1)}, bf16[512,2048]{1,0:T(8,128)(2,1)}), (bf16[512,6144]{1,0:T(8,128)(2,1)}, bf16[512,2048]{1,0:T(8,128)(2,1)})) %all-reduce.12.cloned.1.call-update) | async-done | bytes 8388624 | tf_op jit(solution)/shard_map/psum | solution.py:318
  1380.9 10.2 convert_element_type.307
  1394.1 114.7 %reduce-scatter.3.cloned.1.call-done = bf16[2,512,2048]{2,1,0:T(8,128)(2,1)} async-done(((bf16[2,2048,2048]{2,1,0:T(8,128)(2,1)}), bf16[2,512,2048]{2,1,0:T(8,128)(2,1)}) %reduce-scatter.3.cloned.1.call-update) | async-done | bytes 4194320 | tf_op jit(solution)/shard_map/reduce_scatter | solution.py:265
  1508.8 6.7 convert_element_type.312
  (317 shorter events, 197.4 us)
Async XLA Ops:
  7.3 160.3 %all-gather.7.cloned.1.call-start = ((), (), s32[]{:S(2)}) async-start(), calls=%async_computation.5 | async-start | bytes 31457280 | tf_op jit(solution)/shard_map/all_gather | solution.py:135
  8.0 219.5 %all-gather.9.cloned.1.call-start = ((), (), s32[]{:S(2)}) async-start(), calls=%async_computation.6 | async-start | bytes 10485760 | tf_op jit(solution)/shard_map/all_gather | solution.py:135
  8.8 836.0 %all-gather.13.cloned.1.call-start = ((), (), s32[]{:S(2)}) async-start(), calls=%async_computation.9 | async-start | bytes 5242880 | tf_op jit(solution)/shard_map/all_gather | solution.py:135
  8.8 29.3 %collective-permute-start.15 = (bf16[256,2048]{1,0:T(8,128)(2,1)S(1)}, bf16[256,2048]{1,0:T(8,128)(2,1)}, u32[]{:S(2)}, u32[]{:S(2)}) collective-permute-start(bf16[256,2048]{1,0:T(8,128)(2,1)S(1)} %copy-done.13), channel_id=1, source_target_pairs={{0,8},{4,12},{8,16},{12,20},{16,24},{20,28},{24,0},{28,4},{1,9},{5... | collective-permute-start | bytes 3145736 | tf_op jit(solution)/shard_map/ppermute | solution.py:67
  11.9 71.9 %collective-permute-start.14 = (bf16[256,2048]{1,0:T(8,128)(2,1)S(1)}, bf16[256,2048]{1,0:T(8,128)(2,1)}, u32[]{:S(2)}, u32[]{:S(2)}) collective-permute-start(bf16[256,2048]{1,0:T(8,128)(2,1)S(1)} %copy-done.13), channel_id=1, source_target_pairs={{0,4},{4,0},{8,12},{12,8},{16,20},{20,16},{24,28},{28,24},{1,5},{5... | collective-permute-start | bytes 3145736 | tf_op jit(solution)/shard_map/ppermute | solution.py:67
  13.4 68.9 %collective-permute-start.17 = (bf16[256,2048]{1,0:T(8,128)(2,1)S(1)}, bf16[256,2048]{1,0:T(8,128)(2,1)}, u32[]{:S(2)}, u32[]{:S(2)}) collective-permute-start(bf16[256,2048]{1,0:T(8,128)(2,1)S(1)} %copy-done.13), channel_id=1, source_target_pairs={{0,16},{4,20},{8,24},{12,28},{16,0},{20,4},{24,8},{28,12},{1,17},{... | collective-permute-start | bytes 3145736 | tf_op jit(solution)/shard_map/ppermute | solution.py:67
  16.0 72.4 %collective-permute-start.19 = (bf16[256,2048]{1,0:T(8,128)(2,1)S(1)}, bf16[256,2048]{1,0:T(8,128)(2,1)}, u32[]{:S(2)}, u32[]{:S(2)}) collective-permute-start(bf16[256,2048]{1,0:T(8,128)(2,1)S(1)} %copy-done.13), channel_id=1, source_target_pairs={{0,24},{4,28},{8,0},{12,4},{16,8},{20,12},{24,16},{28,20},{1,25},{... | collective-permute-start | bytes 3145736 | tf_op jit(solution)/shard_map/ppermute | solution.py:67
  26.2 154.6 %copy-start.38 = (f32[1,2048]{1,0:T(1,128)}, f32[1,2048]{1,0:T(1,128)S(1)}, u32[]{:S(2)}) copy-start(f32[1,2048]{1,0:T(1,128)S(1)} %get-tuple-element.77) | copy-start | bytes 24580
  26.2 154.6 %copy-start.40 = (f32[1,2048]{1,0:T(1,128)}, f32[1,2048]{1,0:T(1,128)S(1)}, u32[]{:S(2)}) copy-start(f32[1,2048]{1,0:T(1,128)S(1)} %get-tuple-element.78) | copy-start | bytes 24580
  26.2 207.2 %copy-start.35 = (f32[1,2048]{1,0:T(1,128)}, f32[1,2048]{1,0:T(1,128)S(1)}, u32[]{:S(2)}) copy-start(f32[1,2048]{1,0:T(1,128)S(1)} %get-tuple-element.76) | copy-start | bytes 24580
  38.2 50.7 %collective-permute-start.16 = (bf16[256,2048]{1,0:T(8,128)(2,1)}, bf16[256,2048]{1,0:T(8,128)(2,1)}, u32[]{:S(2)}, u32[]{:S(2)}) collective-permute-start(bf16[256,2048]{1,0:T(8,128)(2,1)} %collective-permute-done.15), channel_id=1, source_target_pairs={{0,4},{4,0},{8,12},{12,8},{16,20},{20,16},{24,28},{28,24},{1,5},{5... | collective-permute-start | bytes 3145736 | tf_op jit(solution)/shard_map/ppermute | solution.py:67
  45.7 197.0 %copy-start.27 = (bf16[2048,16]{0,1:T(8,128)(2,1)}, bf16[2048,16]{0,1:T(8,128)(2,1)S(1)}, u32[]{:S(2)}) copy-start(bf16[2048,16]{0,1:T(8,128)(2,1)S(1)} %all_gather.35) | copy-start | bytes 196612
  82.3 26.2 %collective-permute-start.18 = (bf16[256,2048]{1,0:T(8,128)(2,1)}, bf16[256,2048]{1,0:T(8,128)(2,1)S(1)}, u32[]{:S(2)}, u32[]{:S(2)}) collective-permute-start(bf16[256,2048]{1,0:T(8,128)(2,1)} %collective-permute-done.17), channel_id=1, source_target_pairs={{0,4},{4,0},{8,12},{12,8},{16,20},{20,16},{24,28},{28,24},{1,5},{5... | collective-permute-start | bytes 3145736 | tf_op jit(solution)/shard_map/ppermute | solution.py:67
  88.4 41.6 %collective-permute-start.20 = (bf16[256,2048]{1,0:T(8,128)(2,1)}, bf16[256,2048]{1,0:T(8,128)(2,1)S(1)}, u32[]{:S(2)}, u32[]{:S(2)}) collective-permute-start(bf16[256,2048]{1,0:T(8,128)(2,1)} %collective-permute-done.19), channel_id=1, source_target_pairs={{0,4},{4,0},{8,12},{12,8},{16,20},{20,16},{24,28},{28,24},{1,5},{5... | collective-permute-start | bytes 3145736 | tf_op jit(solution)/shard_map/ppermute | solution.py:67
  233.3 148.9 %copy-start.44 = (f32[256]{0:T(256)}, f32[256]{0:T(256)S(1)}, u32[]{:S(2)}) copy-start(f32[256]{0:T(256)S(1)} %fusion.110) | copy-start | bytes 3076
  235.9 157.6 %copy-start.11 = (bf16[256,2048]{1,0:T(8,128)(2,1)}, bf16[256,2048]{1,0:T(8,128)(2,1)S(1)}, u32[]{:S(2)}) copy-start(bf16[256,2048]{1,0:T(8,128)(2,1)S(1)} %get-tuple-element.29) | copy-start | bytes 3145732
  235.9 171.4 %collective-permute-start = (bf16[256,2048]{1,0:T(8,128)(2,1)S(1)}, bf16[256,2048]{1,0:T(8,128)(2,1)}, u32[]{:S(2)}, u32[]{:S(2)}) collective-permute-start(bf16[256,2048]{1,0:T(8,128)(2,1)S(1)} %get-tuple-element.29), channel_id=1, source_target_pairs={{0,4},{4,0},{8,12},{12,8},{16,20},{20,16},{24,28},{28,24},{1,5},{5... | collective-permute-start | bytes 3145736 | tf_op jit(solution)/shard_map/ppermute | solution.py:67
  237.3 156.2 %collective-permute-start.1 = (bf16[256,2048]{1,0:T(8,128)(2,1)S(1)}, bf16[256,2048]{1,0:T(8,128)(2,1)}, u32[]{:S(2)}, u32[]{:S(2)}) collective-permute-start(bf16[256,2048]{1,0:T(8,128)(2,1)S(1)} %get-tuple-element.29), channel_id=1, source_target_pairs={{0,8},{4,12},{8,16},{12,20},{16,24},{20,28},{24,0},{28,4},{1,9},{5... | collective-permute-start | bytes 3145736 | tf_op jit(solution)/shard_map/ppermute | solution.py:67
  238.8 167.1 %collective-permute-start.3 = (bf16[256,2048]{1,0:T(8,128)(2,1)S(1)}, bf16[256,2048]{1,0:T(8,128)(2,1)}, u32[]{:S(2)}, u32[]{:S(2)}) collective-permute-start(bf16[256,2048]{1,0:T(8,128)(2,1)S(1)} %get-tuple-element.29), channel_id=1, source_target_pairs={{0,16},{4,20},{8,24},{12,28},{16,0},{20,4},{24,8},{28,12},{1,17},{... | collective-permute-start | bytes 3145736 | tf_op jit(solution)/shard_map/ppermute | solution.py:67
  241.2 170.7 %collective-permute-start.5 = (bf16[256,2048]{1,0:T(8,128)(2,1)S(1)}, bf16[256,2048]{1,0:T(8,128)(2,1)S(1)}, u32[]{:S(2)}, u32[]{:S(2)}) collective-permute-start(bf16[256,2048]{1,0:T(8,128)(2,1)S(1)} %get-tuple-element.29), channel_id=1, source_target_pairs={{0,24},{4,28},{8,0},{12,4},{16,8},{20,12},{24,16},{28,20},{1,25},{... | collective-permute-start | bytes 3145736 | tf_op jit(solution)/shard_map/ppermute | solution.py:67
  243.1 150.4 %copy-start.49 = (f32[256]{0:T(256)}, f32[256]{0:T(256)S(1)}, u32[]{:S(2)}) copy-start(f32[256]{0:T(256)S(1)} %get-tuple-element.84) | copy-start | bytes 3076
  243.1 150.4 %copy-start.64 = (f32[256]{0:T(256)}, f32[256]{0:T(256)S(1)}, u32[]{:S(2)}) copy-start(f32[256]{0:T(256)S(1)} %fusion.104) | copy-start | bytes 3076
  393.5 26.3 %collective-permute-start.2 = (bf16[256,2048]{1,0:T(8,128)(2,1)}, bf16[256,2048]{1,0:T(8,128)(2,1)S(1)}, u32[]{:S(2)}, u32[]{:S(2)}) collective-permute-start(bf16[256,2048]{1,0:T(8,128)(2,1)} %collective-permute-done.1), channel_id=1, source_target_pairs={{0,4},{4,0},{8,12},{12,8},{16,20},{20,16},{24,28},{28,24},{1,5},{5... | collective-permute-start | bytes 3145736 | tf_op jit(solution)/shard_map/ppermute | solution.py:67
  405.9 36.1 %collective-permute-start.4 = (bf16[256,2048]{1,0:T(8,128)(2,1)}, bf16[256,2048]{1,0:T(8,128)(2,1)S(1)}, u32[]{:S(2)}, u32[]{:S(2)}) collective-permute-start(bf16[256,2048]{1,0:T(8,128)(2,1)} %collective-permute-done.3), channel_id=1, source_target_pairs={{0,4},{4,0},{8,12},{12,8},{16,20},{20,16},{24,28},{28,24},{1,5},{5... | collective-permute-start | bytes 3145736 | tf_op jit(solution)/shard_map/ppermute | solution.py:67
  411.9 41.4 %collective-permute-start.6 = (bf16[256,2048]{1,0:T(8,128)(2,1)S(1)}, bf16[256,2048]{1,0:T(8,128)(2,1)S(1)}, u32[]{:S(2)}, u32[]{:S(2)}) collective-permute-start(bf16[256,2048]{1,0:T(8,128)(2,1)S(1)} %collective-permute-done.5), channel_id=1, source_target_pairs={{0,4},{4,0},{8,12},{12,8},{16,20},{20,16},{24,28},{28,24},{1,5},{5... | collective-permute-start | bytes 3145736 | tf_op jit(solution)/shard_map/ppermute | solution.py:67
  585.0 26.1 %collective-permute-start.22 = (bf16[256,2048]{1,0:T(8,128)(2,1)S(1)}, bf16[256,2048]{1,0:T(8,128)(2,1)S(1)}, u32[]{:S(2)}, u32[]{:S(2)}) collective-permute-start(bf16[256,2048]{1,0:T(8,128)(2,1)S(1)} %get-tuple-element.35), channel_id=1, source_target_pairs={{0,4},{4,0},{8,12},{12,8},{16,20},{20,16},{24,28},{28,24},{1,5},{5... | collective-permute-start | bytes 3145736 | tf_op jit(solution)/shard_map/ppermute | solution.py:67
  585.4 48.2 %collective-permute-start.24 = (bf16[256,2048]{1,0:T(8,128)(2,1)S(1)}, bf16[256,2048]{1,0:T(8,128)(2,1)S(1)}, u32[]{:S(2)}, u32[]{:S(2)}) collective-permute-start(bf16[256,2048]{1,0:T(8,128)(2,1)S(1)} %get-tuple-element.34), channel_id=1, source_target_pairs={{0,4},{4,0},{8,12},{12,8},{16,20},{20,16},{24,28},{28,24},{1,5},{5... | collective-permute-start | bytes 3145736 | tf_op jit(solution)/shard_map/ppermute | solution.py:67
  587.0 67.9 %collective-permute-start.26 = (bf16[256,2048]{1,0:T(8,128)(2,1)S(1)}, bf16[256,2048]{1,0:T(8,128)(2,1)S(1)}, u32[]{:S(2)}, u32[]{:S(2)}) collective-permute-start(bf16[256,2048]{1,0:T(8,128)(2,1)S(1)} %get-tuple-element.33), channel_id=1, source_target_pairs={{0,4},{4,0},{8,12},{12,8},{16,20},{20,16},{24,28},{28,24},{1,5},{5... | collective-permute-start | bytes 3145736 | tf_op jit(solution)/shard_map/ppermute | solution.py:67
  587.5 140.6 %collective-permute-start.21 = (bf16[256,2048]{1,0:T(8,128)(2,1)}, bf16[256,2048]{1,0:T(8,128)(2,1)S(1)}, u32[]{:S(2)}, u32[]{:S(2)}) collective-permute-start(bf16[256,2048]{1,0:T(8,128)(2,1)} %get-tuple-element.32), channel_id=1, source_target_pairs={{0,4},{4,0},{8,12},{12,8},{16,20},{20,16},{24,28},{28,24},{1,5},{5... | collective-permute-start | bytes 3145736 | tf_op jit(solution)/shard_map/ppermute | solution.py:67
  657.5 70.6 %collective-permute-start.23 = (bf16[256,2048]{1,0:T(8,128)(2,1)}, bf16[256,2048]{1,0:T(8,128)(2,1)}, u32[]{:S(2)}, u32[]{:S(2)}) collective-permute-start(bf16[256,2048]{1,0:T(8,128)(2,1)} %get-tuple-element.36), channel_id=1, source_target_pairs={{0,24},{4,28},{8,0},{12,4},{16,8},{20,12},{24,16},{28,20},{1,25},{... | collective-permute-start | bytes 3145736 | tf_op jit(solution)/shard_map/ppermute | solution.py:67
  660.7 67.4 %collective-permute-start.25 = (bf16[256,2048]{1,0:T(8,128)(2,1)}, bf16[256,2048]{1,0:T(8,128)(2,1)}, u32[]{:S(2)}, u32[]{:S(2)}) collective-permute-start(bf16[256,2048]{1,0:T(8,128)(2,1)} %get-tuple-element.38), channel_id=1, source_target_pairs={{0,16},{4,20},{8,24},{12,28},{16,0},{20,4},{24,8},{28,12},{1,17},{... | collective-permute-start | bytes 3145736 | tf_op jit(solution)/shard_map/ppermute | solution.py:67
  660.7 67.4 %collective-permute-start.27 = (bf16[256,2048]{1,0:T(8,128)(2,1)}, bf16[256,2048]{1,0:T(8,128)(2,1)}, u32[]{:S(2)}, u32[]{:S(2)}) collective-permute-start(bf16[256,2048]{1,0:T(8,128)(2,1)} %get-tuple-element.37), channel_id=1, source_target_pairs={{0,8},{4,12},{8,16},{12,20},{16,24},{20,28},{24,0},{28,4},{1,9},{5... | collective-permute-start | bytes 3145736 | tf_op jit(solution)/shard_map/ppermute | solution.py:67
  734.9 147.8 %all-gather.11.cloned.1.call-start = ((), (), s32[]{:S(2)}) async-start(), calls=%async_computation.8 | async-start | bytes 15728640 | tf_op jit(solution)/shard_map/all_gather | solution.py:135
  775.8 327.6 %all-reduce.10.cloned.1.call-start = ((), (), s32[]{:S(2)}) async-start(), calls=%async_computation.7 | async-start | bytes 393216 | tf_op jit(solution)/shard_map/psum | solution.py:332
  793.5 312.9 %reduce-scatter.5.cloned.1.call-start = ((), (), s32[]{:S(2)}) async-start(), calls=%async_computation.11 | async-start | bytes 10485760 | tf_op jit(solution)/shard_map/reduce_scatter | solution.py:268
  811.6 29.5 %all-to-all-start.2 = ((bf16[256,4,512]{2,0,1:T(8,128)(2,1)}), bf16[256,4,512]{2,0,1:T(8,128)(2,1)S(1)}, u32[]{:S(2)}, u32[]{:S(2)}) async-start(bf16[256,4,512]{2,0,1:T(8,128)(2,1)} %copy.150), calls=%async_computation.2 | async-start | bytes 2097152 | tf_op jit(solution)/shard_map/all_to_all | solution.py:199
  841.1 29.5 %all-to-all-start.1 = ((bf16[256,4,512]{2,0,1:T(8,128)(2,1)}), bf16[256,4,512]{2,0,1:T(8,128)(2,1)S(1)}, u32[]{:S(2)}, u32[]{:S(2)}) async-start(bf16[256,4,512]{2,0,1:T(8,128)(2,1)} %bitcast.257), calls=%async_computation.1 | async-start | bytes 2097152 | tf_op jit(solution)/shard_map/all_to_all | solution.py:165
  844.7 536.2 %all-reduce.12.cloned.1.call-start = ((), (), s32[]{:S(2)}) async-start(), calls=%async_computation.12 | async-start | bytes 16777216 | tf_op jit(solution)/shard_map/psum | solution.py:318
  896.0 612.8 %reduce-scatter.3.cloned.1.call-start = ((), (), s32[]{:S(2)}) async-start(), calls=%async_computation.10 | async-start | bytes 20971520 | tf_op jit(solution)/shard_map/reduce_scatter | solution.py:265
  948.7 26.1 %collective-permute-start.10 = (bf16[256,2048]{1,0:T(8,128)(2,1)S(1)}, bf16[256,2048]{1,0:T(8,128)(2,1)S(1)}, u32[]{:S(2)}, u32[]{:S(2)}) collective-permute-start(bf16[256,2048]{1,0:T(8,128)(2,1)S(1)} %get-tuple-element.41), channel_id=1, source_target_pairs={{0,4},{4,0},{8,12},{12,8},{16,20},{20,16},{24,28},{28,24},{1,5},{5... | collective-permute-start | bytes 3145736 | tf_op jit(solution)/shard_map/ppermute | solution.py:67
  950.1 47.6 %collective-permute-start.12 = (bf16[256,2048]{1,0:T(8,128)(2,1)S(1)}, bf16[256,2048]{1,0:T(8,128)(2,1)S(1)}, u32[]{:S(2)}, u32[]{:S(2)}) collective-permute-start(bf16[256,2048]{1,0:T(8,128)(2,1)S(1)} %get-tuple-element.40), channel_id=1, source_target_pairs={{0,4},{4,0},{8,12},{12,8},{16,20},{20,16},{24,28},{28,24},{1,5},{5... | collective-permute-start | bytes 3145736 | tf_op jit(solution)/shard_map/ppermute | solution.py:67
  950.7 69.6 %collective-permute-start.8 = (bf16[256,2048]{1,0:T(8,128)(2,1)S(1)}, bf16[256,2048]{1,0:T(8,128)(2,1)S(1)}, u32[]{:S(2)}, u32[]{:S(2)}) collective-permute-start(bf16[256,2048]{1,0:T(8,128)(2,1)S(1)} %get-tuple-element.42), channel_id=1, source_target_pairs={{0,4},{4,0},{8,12},{12,8},{16,20},{20,16},{24,28},{28,24},{1,5},{5... | collective-permute-start | bytes 3145736 | tf_op jit(solution)/shard_map/ppermute | solution.py:67
  952.1 144.4 %copy-start.46 = (f32[256]{0:T(256)S(1)}, f32[256]{0:T(256)}, u32[]{:S(2)}) copy-start(f32[256]{0:T(256)} %copy-done.44) | copy-start | bytes 3076
  952.2 144.4 %copy-start.57 = (f32[256]{0:T(256)S(1)}, f32[256]{0:T(256)}, u32[]{:S(2)}) copy-start(f32[256]{0:T(256)} %copy-done.56) | copy-start | bytes 3076
  952.2 90.0 %collective-permute-start.7 = (bf16[256,2048]{1,0:T(8,128)(2,1)}, bf16[256,2048]{1,0:T(8,128)(2,1)}, u32[]{:S(2)}, u32[]{:S(2)}) collective-permute-start(bf16[256,2048]{1,0:T(8,128)(2,1)} %get-tuple-element.39), channel_id=1, source_target_pairs={{0,4},{4,0},{8,12},{12,8},{16,20},{20,16},{24,28},{28,24},{1,5},{5... | collective-permute-start | bytes 3145736 | tf_op jit(solution)/shard_map/ppermute | solution.py:67
  1024.8 71.8 %collective-permute-start.11 = (bf16[256,2048]{1,0:T(8,128)(2,1)}, bf16[256,2048]{1,0:T(8,128)(2,1)}, u32[]{:S(2)}, u32[]{:S(2)}) collective-permute-start(bf16[256,2048]{1,0:T(8,128)(2,1)} %get-tuple-element.45), channel_id=1, source_target_pairs={{0,16},{4,20},{8,24},{12,28},{16,0},{20,4},{24,8},{28,12},{1,17},{... | collective-permute-start | bytes 3145736 | tf_op jit(solution)/shard_map/ppermute | solution.py:67
  1027.2 69.4 %collective-permute-start.13 = (bf16[256,2048]{1,0:T(8,128)(2,1)}, bf16[256,2048]{1,0:T(8,128)(2,1)}, u32[]{:S(2)}, u32[]{:S(2)}) collective-permute-start(bf16[256,2048]{1,0:T(8,128)(2,1)} %get-tuple-element.44), channel_id=1, source_target_pairs={{0,8},{4,12},{8,16},{12,20},{16,24},{20,28},{24,0},{28,4},{1,9},{5... | collective-permute-start | bytes 3145736 | tf_op jit(solution)/shard_map/ppermute | solution.py:67
  1028.6 68.0 %collective-permute-start.9 = (bf16[256,2048]{1,0:T(8,128)(2,1)}, bf16[256,2048]{1,0:T(8,128)(2,1)}, u32[]{:S(2)}, u32[]{:S(2)}) collective-permute-start(bf16[256,2048]{1,0:T(8,128)(2,1)} %get-tuple-element.43), channel_id=1, source_target_pairs={{0,24},{4,28},{8,0},{12,4},{16,8},{20,12},{24,16},{28,20},{1,25},{... | collective-permute-start | bytes 3145736 | tf_op jit(solution)/shard_map/ppermute | solution.py:67
  (69 other events, 2221.6 us)
Sparse Core Ops, SparseCore 0:
  9.7 157.8 all-gather.6
  169.1 58.2 all-gather.8
  735.0 36.5 all-gather.12
  775.9 106.6 all-gather.10
  888.1 123.1 all-reduce.9
  1013.7 72.6 reduce-scatter.4
  1091.5 289.2 all-reduce.11
  1383.6 125.1 reduce-scatter.2

commit v2 on v1

--- a/solution.py
+++ b/solution.py
@@ -1,6 +1,10 @@
+import functools
+
 import jax
 import jax.numpy as jnp
 from jax import lax
+from jax.experimental import pallas as pl
+from jax.experimental.pallas import tpu as pltpu
 from jax.sharding import PartitionSpec as P
 
 HEADS = 16
@@ -101,6 +105,238 @@
     me = lax.axis_index("expert")
     order = jnp.arange(expert_group, dtype=jnp.int32)
     return ((me // x_all - order // x_all) % z_all) * x_all + (me % x_all - order % x_all) % x_all
+
+
+def shard_shift(values, shard_group, dy, flip):
+    y_all = shard_group // 2
+    pairs = [(i, ((i // 2 + dy) % y_all) * 2 + (i % 2 + flip) % 2) for i in range(shard_group)]
+    return lax.ppermute(values, "shard", pairs)
+
+
+def gather_shard(block, shard_group):
+    found = []
+    for dy in range(shard_group // 2):
+        straight = block if dy == 0 else shard_shift(block, shard_group, dy, 0)
+        found += [straight, shard_shift(straight, shard_group, 0, 1)]
+    return found
+
+
+def own_columns(values, shard_group):
+    me = lax.axis_index("shard")
+    y_all = shard_group // 2
+    width = values.shape[1] // shard_group
+    found = []
+    for dy in range(y_all):
+        for flip in range(2):
+            there = ((me // 2 + dy) % y_all) * 2 + (me % 2 + flip) % 2
+            piece = lax.dynamic_slice_in_dim(values, there * width, width, axis=1)
+            found.append(piece if dy + flip == 0 else shard_shift(piece, shard_group, dy, flip))
+    return jnp.concatenate(found, axis=0)
+
+
+def tail_kernel(dims, grads_ref, columns_ref, out_ref, gall, xsend, xrecv, zsend, zrecv, acc, fin, *sems):
+    steps, width, x_all, z_all, y_all, lag = dims
+    (y_s, y_r, core_s, core_r, fwd_s, fwd_r, x_s, x_r, z_s, z_r, zb_s, zb_r, xb_s, xb_r) = sems
+    f32, bf16 = jnp.float32, jnp.bfloat16
+    length = grads_ref.shape[0]
+    rows = columns_ref.shape[0]
+    block = rows // (x_all * z_all)
+    half = z_all * block
+    e = lax.axis_index("expert")
+    s = lax.axis_index("shard")
+    z, x = e // x_all, lax.rem(e, x_all)
+    y, core = s // 2, lax.rem(s, 2)
+
+    def y_peer(d):
+        return {"shard": lax.rem(y + d, y_all) * 2 + core}
+
+    partner = {"shard": y * 2 + (1 - core)}
+
+    def x_peer(d):
+        return {"expert": z * x_all + lax.rem(x + d, x_all)}
+
+    def z_peer(d):
+        return {"expert": lax.rem(z + d, z_all) * x_all + x}
+
+    def copy(src, dst, send, recv, peer):
+        return pltpu.make_async_remote_copy(
+            src_ref=src, dst_ref=dst, send_sem=send, recv_sem=recv, device_id=peer,
+            device_id_type=pl.DeviceIdType.MESH,
+        )
+
+    def cols(c):
+        return pl.ds(pl.multiple_of(c * width, width), width)
+
+    def y_copy(d, c):
+        return copy(grads_ref.at[:, cols(c)], gall.at[2 * d - 1, c], y_s.at[d - 1], y_r.at[d - 1, c], y_peer(d))
+
+    def core_copy(c):
+        return copy(grads_ref.at[:, cols(c)], gall.at[0, c], core_s.at[0], core_r.at[c], partner)
+
+    def fwd_copy(d, c):
+        return copy(gall.at[2 * d - 1, c], gall.at[2 * d, c], fwd_s.at[d - 1], fwd_r.at[d - 1, c], partner)
+
+    def x_copy(d, c):
+        return copy(xsend.at[d - 1, c], xrecv.at[d - 1, c], x_s.at[d - 1], x_r.at[d - 1, c], x_peer(d))
+
+    def z_copy(d, c):
+        return copy(zsend.at[d - 1, c], zrecv.at[d - 1, c], z_s.at[d - 1], z_r.at[d - 1, c], z_peer(d))
+
+    def zb_copy(d, c):
+        here = fin.at[c, pl.ds(pl.multiple_of((x * z_all + z) * block, block), block)]
+        return copy(here, here, zb_s.at[d - 1], zb_r.at[d - 1, c], z_peer(d))
+
+    def xb_copy(d, c):
+        here = fin.at[c, pl.ds(pl.multiple_of(x * half, half), half)]
+        return copy(here, here, xb_s.at[d - 1], xb_r.at[d - 1, c], x_peer(d))
+
+    barrier = pltpu.get_barrier_semaphore()
+    peers = (
+        [y_peer(d) for d in range(1, y_all)]
+        + [partner]
+        + [x_peer(d) for d in range(1, x_all)]
+        + [z_peer(d) for d in range(1, z_all)]
+    )
+    for peer in peers:
+        pl.semaphore_signal(barrier, inc=1, device_id=peer, device_id_type=pl.DeviceIdType.MESH)
+    pl.semaphore_wait(barrier, len(peers))
+
+    def first(c, carry):
+        for d in range(1, y_all):
+            y_copy(d, c).start()
+        core_copy(c).start()
+        return carry
+
+    lax.fori_loop(0, steps, first, 0)
+    slots = acc.shape[0]
+
+    def step(t, carry):
+        def stage(k, body):
+            c = t - k * lag
+            pl.when((c >= 0) & (c < steps))(lambda: body(c))
+
+        @functools.partial(stage, 5)
+        def _(c):
+            for d in range(1, x_all):
+                xb_copy(d, c).wait_recv()
+            out_ref[:, cols(c)] = fin[c]
+
+        @functools.partial(stage, 4)
+        def _(c):
+            for d in range(1, z_all):
+                zb_copy(d, c).wait_recv()
+            for d in range(1, x_all):
+                xb_copy(d, c).start()
+
+        @functools.partial(stage, 3)
+        def _(c):
+            slot = lax.rem(c, slots)
+            total = acc[slot, pl.ds(pl.multiple_of(z * block, block), block), :]
+            for d in range(1, z_all):
+                z_copy(d, c).wait_recv()
+                total = total + zrecv[d - 1, c].astype(f32)
+            fin[c, pl.ds(pl.multiple_of((x * z_all + z) * block, block), block), :] = total.astype(bf16)
+            for d in range(1, z_all):
+                zb_copy(d, c).start()
+
+        @functools.partial(stage, 2)
+        def _(c):
+            slot = lax.rem(c, slots)
+            total = acc[slot]
+            for d in range(1, x_all):
+                x_copy(d, c).wait_recv()
+                total = total + xrecv[d - 1, c].astype(f32)
+            acc[slot] = total
+            for d in range(1, z_all):
+                there = lax.rem(z + d, z_all)
+                zsend[d - 1, c] = acc[slot, pl.ds(pl.multiple_of(there * block, block), block), :].astype(bf16)
+                z_copy(d, c).start()
+
+        @functools.partial(stage, 1)
+        def _(c):
+            core_copy(c).wait_recv()
+            for d in range(1, y_all):
+                fwd_copy(d, c).wait_recv()
+            others = gall[:, c].reshape((2 * y_all - 1) * length, width)
+            mine = grads_ref[:, cols(c)]
+
+            def product(there):
+                at = pl.ds(pl.multiple_of(there * half, half), half)
+                return jnp.dot(columns_ref[at, :length], mine, preferred_element_type=f32) + jnp.dot(
+                    columns_ref[at, length:], others, preferred_element_type=f32
+                )
+
+            for d in range(1, x_all):
+                xsend[d - 1, c] = product(lax.rem(x + d, x_all)).astype(bf16)
+                x_copy(d, c).start()
+            acc[lax.rem(c, slots)] = product(x)
+
+        @functools.partial(stage, 0)
+        def _(c):
+            for d in range(1, y_all):
+                y_copy(d, c).wait_recv()
+                fwd_copy(d, c).start()
+
+        return carry
+
+    lax.fori_loop(0, steps + 5 * lag, step, 0)
+
+    for d in range(1, y_all):
+        copy(grads_ref, grads_ref, y_s.at[d - 1], y_r.at[d - 1, 0], y_peer(d)).wait_send()
+        whole = gall.at[2 * d - 1]
+        copy(whole, whole, fwd_s.at[d - 1], fwd_r.at[d - 1, 0], partner).wait_send()
+    copy(grads_ref, grads_ref, core_s.at[0], core_r.at[0], partner).wait_send()
+    for d in range(1, x_all):
+        whole = xsend.at[d - 1]
+        copy(whole, whole, x_s.at[d - 1], x_r.at[d - 1, 0], x_peer(d)).wait_send()
+        copy(whole, whole, xb_s.at[d - 1], xb_r.at[d - 1, 0], x_peer(d)).wait_send()
+    for d in range(1, z_all):
+        whole = zsend.at[d - 1]
+        copy(whole, whole, z_s.at[d - 1], z_r.at[d - 1, 0], z_peer(d)).wait_send()
+        copy(whole, whole, zb_s.at[d - 1], zb_r.at[d - 1, 0], z_peer(d)).wait_send()
+
+
+def summed_rows(columns, grads, expert_group, shard_group, z_all, width, lag, name_id):
+    x_all, y_all = expert_group // z_all, shard_group // 2
+    length, total = grads.shape
+    rows = columns.shape[0]
+    steps = total // width
+    block = rows // expert_group
+    half = z_all * block
+    bf16 = jnp.bfloat16
+    dma = pltpu.SemaphoreType.DMA
+    n1 = max(y_all - 1, 1)
+    x1 = max(x_all - 1, 1)
+    z1 = max(z_all - 1, 1)
+    slots = min(steps, 2 * lag + 1)
+    return pl.pallas_call(
+        functools.partial(tail_kernel, (steps, width, x_all, z_all, y_all, lag)),
+        out_shape=jax.ShapeDtypeStruct((rows, total), bf16),
+        in_specs=[pl.BlockSpec(memory_space=pltpu.VMEM)] * 2,
+        out_specs=pl.BlockSpec(memory_space=pltpu.VMEM),
+        scratch_shapes=[
+            pltpu.VMEM((shard_group - 1, steps, length, width), bf16),
+            pltpu.VMEM((x1, steps, half, width), bf16),
+            pltpu.VMEM((x1, steps, half, width), bf16),
+            pltpu.VMEM((z1, steps, block, width), bf16),
+            pltpu.VMEM((z1, steps, block, width), bf16),
+            pltpu.VMEM((slots, half, width), jnp.float32),
+            pltpu.VMEM((steps, rows, width), bf16),
+            dma((n1,)), dma((n1, steps)),
+            dma((1,)), dma((steps,)),
+            dma((n1,)), dma((n1, steps)),
+            dma((x1,)), dma((x1, steps)),
+            dma((z1,)), dma((z1, steps)),
+            dma((z1,)), dma((z1, steps)),
+            dma((x1,)), dma((x1, steps)),
+        ],
+        compiler_params=pltpu.CompilerParams(
+            collective_id=name_id, has_side_effects=True, vmem_limit_bytes=60 * 1024 * 1024
+        ),
+        cost_estimate=pl.CostEstimate(
+            flops=2 * rows * length * shard_group * total, bytes_accessed=16 * 1024 * 1024, transcendentals=0
+        ),
+    )(grads, columns)
 
 
 def body(
@@ -162,9 +398,7 @@
     inputs = tokens.astype(f32)
     scaled_one, first_pull = jax.vjp(rms_scale, inputs, gain_one)
     hidden_one = scaled_one.astype(bf16)
-    hidden_one_columns = lax.all_to_all(
-        hidden_one, "shard", split_axis=1, concat_axis=0, tiled=True
-    )
+    hidden_one_columns = own_columns(hidden_one, shard_group).T
     projected = jnp.dot(hidden_one, qkv_full, preferred_element_type=f32)
     cosine, sine_table = rotary_tables(length)
 
@@ -196,18 +430,15 @@
         .reshape(length, model_width)
         .astype(bf16)
     )
-    attended_columns = lax.all_to_all(
-        attended_low, "shard", split_axis=1, concat_axis=0, tiled=True
-    )
+    attended_columns = own_columns(attended_low, shard_group)
     middle = inputs + jnp.dot(attended_low, out_full, preferred_element_type=f32)
     scaled_two, second_pull = jax.vjp(rms_scale, middle, gain_two)
     hidden_two = scaled_two.astype(bf16)
     hidden_all = jnp.stack(gather_expert(hidden_two, expert_group))
     router = softmax_rows(jnp.dot(hidden_two, router_full, preferred_element_type=f32))
-    prob = jnp.where(kept, router, 0.0)
-    prob_all = lax.all_gather(prob, "expert", axis=0, tiled=False)[sources]
+    router_all = softmax_rows(jnp.dot(hidden_all, router_full, preferred_element_type=f32))
     prob_own = lax.dynamic_slice_in_dim(
-        prob_all, own_expert * local_experts, local_experts, axis=2
+        router_all, own_expert * local_experts, local_experts, axis=2
     ).transpose(0, 2, 1)
 
     expert_rows = jnp.einsum(
@@ -243,9 +474,19 @@
     grad_router_parts = jnp.sum(
         jnp.where(one_hot, grad_prob_rows.transpose(1, 0, 2)[:, :, :, None], 0.0), axis=2
     )
-    back = jnp.zeros((expert_group, local_experts, length), f32).at[sources].set(grad_router_parts)
-    grad_router = lax.all_to_all(back, "expert", split_axis=0, concat_axis=0, tiled=True)
-    grad_router = grad_router.reshape(experts_all, length).T
+    z_all = z_size(expert_group)
+    x_all = expert_group // z_all
+    back = jnp.stack(
+        [
+            part if i == 0 else shift(part, expert_group, -(i // x_all), -(i % x_all))
+            for i, part in enumerate(grad_router_parts)
+        ]
+    )
+    owners = jnp.arange(expert_group, dtype=jnp.int32)
+    entry = ((owners // x_all - own_expert // x_all) % z_all) * x_all + (
+        owners % x_all - own_expert % x_all
+    ) % x_all
+    grad_router = back[entry].reshape(experts_all, length).T
     grad_activated = jnp.einsum("erd,efd->erf", grad_expert, down_weight, preferred_element_type=f32)
     grad_gate_up_low = swiglu_pull(grad_activated)[0].astype(bf16)
     grad_row = jnp.einsum(
@@ -313,12 +554,14 @@
     grad_inputs_norm, grad_gain_one = first_pull(grad_hidden_one)
     grad_tokens = grad_middle + grad_inputs_norm
 
-    def over_sequences(columns, grads):
-        part = jnp.einsum("td,te->de", columns, gather(grads, "shard"), preferred_element_type=f32)
-        return lax.psum(part.astype(bf16), "expert").astype(f32)
-
-    grad_out_weight = over_sequences(attended_columns, grad_branch_low)
-    grad_qkv_weight = over_sequences(hidden_one_columns, grad_projected_low)
+    branch_all = jnp.concatenate(gather_shard(grad_branch_low, shard_group), axis=0)
+    grad_out_part = jnp.einsum(
+        "td,te->de", attended_columns, branch_all, preferred_element_type=f32
+    )
+    grad_out_weight = lax.psum(grad_out_part.astype(bf16), "expert").astype(f32)
+    grad_qkv_weight = summed_rows(
+        hidden_one_columns, grad_projected_low, expert_group, shard_group, z_all, 256, 2, 1
+    ).astype(f32)
     grad_router_part = jnp.einsum(
         "td,te->ed", hidden_two, grad_logits, preferred_element_type=f32
     )

time: 1530 us -> 1310 us (0.86)
  waiting for transfers between devices: 822 us -> 401 us
  Pallas kernels: 0 us -> 266 us
  blocking collectives: 215 us -> 119 us
  starting transfers between devices: 47.3 us -> 88.4 us
    psum x1, waiting for transfers between devices: 270 us -> 0.01 us  [body(): grad_out_weight = lax.psum(grad_out_part.astype(bf16), 'expert').astype(f32)]
    pallas_call x0 -> x1, Pallas kernels: none -> 266 us  [summed_rows(): pl.pallas_call(functools.partial(tail_kernel, (steps, width, x_all, z_all...]
    reduce_scatter x1, waiting for transfers between devices: 115 us -> 38.6 us  [body(): lax.psum_scatter(grad_gate_up_full.astype(bf16), 'shard', scatter_dimensi...]
    all_gather x4 -> x2, waiting for transfers between devices: 74.8 us -> 0.02 us  [gather(): return lax.all_gather(values, axis, axis=0, tiled=True)]
    all_to_all x1 -> x0, blocking collectives: 65.4 us -> none  [body(): lax.all_to_all(back, 'expert', split_axis=0, concat_axis=0, tiled=True)]
    all_to_all x2 -> x0, waiting for transfers between devices: 44.8 us -> none  [the longest x1 24.9 us: body(): lax.all_to_all(attended_low, 'shard', split_axis=1, concat_axis=0, tiled=...]
    ppermute x28 -> x35, starting transfers between devices: 40 us -> 81.6 us  [shift(): return lax.ppermute(values, 'expert', pairs)]
    ppermute x28 -> x35, waiting for transfers between devices: 315 us -> 348 us  [shift(): return lax.ppermute(values, 'expert', pairs)]
  transfers between devices with their start and end apart: 38 -> 50, of which waited for: 22 -> 18; matrix products, arithmetic and copies ran while one was open for 17% -> 20% of each run, Pallas kernels for 0% -> 20%
where the time goes in v2:
time: 1310 us
  waiting for transfers between devices  401 us (31%)
  Pallas kernels  266 us (20%)
  matrix products  252 us (19%)
  blocking collectives  119 us (9%)
  starting transfers between devices  88.4 us (7%)
  local copies, waits for them, and re-layouts  84.1 us (6%)
  other arithmetic  81.3 us (6%)
  between operations  15.7 us (1%)
    ppermute x35, waiting for transfers between devices, shift(): return lax.ppermute(values, 'expert', pairs)  348 us
    pallas_call x1, Pallas kernels, summed_rows(): pl.pallas_call(functools.partial(tail_kernel, (steps, width, x_all, z_all...  266 us
    all_gather x1, blocking collectives, body(): place_all = lax.all_gather(place, 'expert', axis=0, tiled=False)[sources]  108 us
    ppermute x35, starting transfers between devices, shift(): return lax.ppermute(values, 'expert', pairs)  81.6 us
    reduce_scatter x1, waiting for transfers between devices, body(): lax.psum_scatter(grad_gate_up_full.astype(bf16), 'shard', scatter_dimensi...  38.6 us
    unnamed x185, local copies, waits for them, and re-layouts  36.9 us
    dot_general x1, matrix products, body(): jnp.einsum('erd,erf->edf', expert_rows, grad_gate_up_low, preferred_eleme...  27.2 us
  transfers between devices with their start and end apart: 50, of which 18 were waited for; matrix products, arithmetic and copies ran while one was open for 20% of the time, Pallas kernels for 20%

profile of v2, /device:TPU:0, one launch (start us, length us, event | category | flops | bytes accessed | tf_op | source)
XLA Modules:
  0.0 1307.2 jit_solution(18280248400723823013)
XLA Ops:
  16.7 108.2 %all-gather = f32[2048,16]{0,1:T(8,128)S(1)} all-gather(f32[256,16]{0,1:T(8,128)S(1)} %and_select_fusion), channel_id=2, replica_groups=mesh['expert'=8,'shard'=4] {'expert'}, dimensions={0}, use_global_device_ids=true | all-gather | bytes 147456 | tf_op jit(solution)/shard_map/all_gather | solution.py:388
  127.1 5.2 all_gather.18
  138.3 5.6 all_gather.23
  150.5 12.7 collective-permute-done.16
  167.8 39.5 %collective-permute-done.18 = bf16[256,2048]{1,0:T(8,128)(2,1)S(1)} collective-permute-done((bf16[256,2048]{1,0:T(8,128)(2,1)}, bf16[256,2048]{1,0:T(8,128)(2,1)S(1)}, u32[]{:S(2)}, u32[]{:S(2)}) %collective-permute-start.18) | collective-permute-done | bytes 1048608 | tf_op jit(solution)/shard_map/ppermute | solution.py:71
  211.7 12.5 fusion.158
  237.7 5.1 fusion.155
  246.2 6.8 multiply_reduce_fusion.7
  258.9 10.8 fusion.14
  269.7 12.7 copy.176
  283.8 41.1 %collective-permute-done.1 = bf16[256,2048]{0,1:T(8,128)(2,1)} collective-permute-done((bf16[256,2048]{0,1:T(8,128)(2,1)S(1)}, bf16[256,2048]{0,1:T(8,128)(2,1)}, u32[]{:S(2)}, u32[]{:S(2)}) %collective-permute-start.1) | collective-permute-done | bytes 1048608 | tf_op jit(solution)/shard_map/ppermute | solution.py:71
  328.0 18.1 %collective-permute-done.3 = bf16[256,2048]{0,1:T(8,128)(2,1)} collective-permute-done((bf16[256,2048]{0,1:T(8,128)(2,1)S(1)}, bf16[256,2048]{0,1:T(8,128)(2,1)}, u32[]{:S(2)}, u32[]{:S(2)}) %collective-permute-start.3) | collective-permute-done | bytes 1048608 | tf_op jit(solution)/shard_map/ppermute | solution.py:71
  352.6 41.7 %collective-permute-done.4 = bf16[256,2048]{0,1:T(8,128)(2,1)S(1)} collective-permute-done((bf16[256,2048]{0,1:T(8,128)(2,1)}, bf16[256,2048]{0,1:T(8,128)(2,1)S(1)}, u32[]{:S(2)}, u32[]{:S(2)}) %collective-permute-start.4) | collective-permute-done | bytes 1048608 | tf_op jit(solution)/shard_map/ppermute | solution.py:71
  399.2 11.3 convert_bitcast_fusion
  410.5 8.4 copy.169
  418.9 21.5 %fusion.159 = f32[2,1024,2048]{2,1,0:T(8,128)S(1)} fusion(bf16[2,1024,2048]{2,1,0:T(8,128)(2,1)} %bitcast.285, bf16[2,2048,2048]{2,1,0:T(8,128)(2,1)} %param.26), kind=kOutput, calls=%fused_computation.317 | convolution fusion | flops 17179869184 | bytes 41943040 | tf_op jit(solution)/shard_map/erd,edf->erf/dot_general | solution.py:449
  440.4 4.9 multiply_convert_fusion
  447.6 17.9 %fusion.2 = (f32[2,1024]{1,0:T(2,128)S(1)}, bf16[2,1024,2048]{2,1,0:T(8,128)(2,1)}) fusion(f32[2,8,128,2048]{3,2,1,0:T(8,128)} %copy.176, bf16[2,1024,1024]{2,1,0:T(8,128)(2,1)} %multiply_convert_fusion, bf16[2,1024,2048]{2,1,0:T(8,128)(2,1)} %param.27), kind=kOutput, calls=%fused_computation.7 | convolution fusion | flops 8606709760 | bytes 37756928 | tf_op jit(solution)/shard_map/erf,efd->erd/dot_general | solution.py:452
  467.3 9.1 fusion.1
  476.4 21.5 %fusion.79 = (f32[2,1024,1024]{2,1,0:T(8,128)}, f32[2,1024,1024]{2,1,0:T(8,128)}) fusion(f32[2,1024,2048]{2,1,0:T(8,128)} %copy-done.10, bf16[2,1024,2048]{2,1,0:T(8,128)(2,1)} %fusion.1, bf16[2,1024,2048]{2,1,0:T(8,128)(2,1)} %param.27), kind=kOutput, calls=%fused_computation.132 | convolution fusion | flops 8619294720 | bytes 50331648 | tf_op jit(solution)/shard_map/erd,efd->erf/dot_general | solution.py:490
  497.8 25.5 %convolution_convert_fusion.2 = bf16[2,1024,2048]{2,1,0:T(8,128)(2,1)} fusion(bf16[2,2048,2048]{2,1,0:T(8,128)(2,1)} %param.26, f32[2,1024,1024]{2,1,0:T(8,128)} %get-tuple-element.75, f32[2,1024,1024]{2,1,0:T(8,128)} %get-tuple-element.74), kind=kOutput, calls=%fused_computation.29 | convolution fusion | flops 17192452096 | bytes 41943040 | tf_op jit(solution)/shard_map/erf,edf->erd/dot_general | solution.py:492
  523.3 9.6 bitcast_convert_fusion
  538.6 22.6 %collective-permute-start.33 = (f32[2,256]{1,0:T(2,128)S(1)}, f32[2,256]{1,0:T(2,128)S(1)}, u32[]{:S(2)}, u32[]{:S(2)}) collective-permute-start(f32[2,256]{1,0:T(2,128)S(1)} %get-tuple-element.127), channel_id=1, source_target_pairs={{0,8},{4,12},{8,16},{12,20},{16,24},{20,28},{24,0},{28,4},{1,9},{5... | collective-permute-start | bytes 6152 | tf_op jit(solution)/shard_map/ppermute | solution.py:71
  561.1 41.6 %collective-permute-done.28 = f32[2,256]{1,0:T(2,128)S(1)} collective-permute-done((f32[2,256]{1,0:T(2,128)S(1)}, f32[2,256]{1,0:T(2,128)S(1)}, u32[]{:S(2)}, u32[]{:S(2)}) %collective-permute-start.28) | collective-permute-done | bytes 2080 | tf_op jit(solution)/shard_map/ppermute | solution.py:71
  602.8 24.2 %collective-permute-done.29 = f32[2,256]{1,0:T(2,128)S(1)} collective-permute-done((f32[2,256]{1,0:T(2,128)S(1)}, f32[2,256]{1,0:T(2,128)S(1)}, u32[]{:S(2)}, u32[]{:S(2)}) %collective-permute-start.29) | collective-permute-done | bytes 2080 | tf_op jit(solution)/shard_map/ppermute | solution.py:71
  646.9 13.9 %collective-permute-start.34 = (f32[2,256]{1,0:T(2,128)S(1)}, f32[2,256]{1,0:T(2,128)S(1)}, u32[]{:S(2)}, u32[]{:S(2)}) collective-permute-start(f32[2,256]{1,0:T(2,128)S(1)} %get-tuple-element.126), channel_id=1, source_target_pairs={{0,12},{4,8},{8,20},{12,16},{16,28},{20,24},{24,4},{28,0},{1,13},{... | collective-permute-start | bytes 6152 | tf_op jit(solution)/shard_map/ppermute | solution.py:71
  660.8 46.8 %collective-permute-done.34 = f32[2,256]{1,0:T(2,128)S(1)} collective-permute-done((f32[2,256]{1,0:T(2,128)S(1)}, f32[2,256]{1,0:T(2,128)S(1)}, u32[]{:S(2)}, u32[]{:S(2)}) %collective-permute-start.34) | collective-permute-done | bytes 2080 | tf_op jit(solution)/shard_map/ppermute | solution.py:71
  711.2 20.2 %collective-permute-done.25 = bf16[256,2048]{0,1:T(8,128)(2,1)} collective-permute-done((bf16[256,2048]{0,1:T(8,128)(2,1)}, bf16[256,2048]{0,1:T(8,128)(2,1)}, u32[]{:S(2)}, u32[]{:S(2)}) %collective-permute-start.25) | collective-permute-done | bytes 1048608 | tf_op jit(solution)/shard_map/ppermute | solution.py:71
  739.6 6.1 convolution_convert_fusion.4
  773.8 12.9 fusion.44
  788.2 5.8 fusion.38
  794.1 15.2 %convolution_convert_fusion.1 = bf16[2,1024,2048]{2,1,0:T(8,128)(2,1)} fusion(bf16[2,1024,1024]{2,1,0:T(8,128)(2,1)} %multiply_convert_fusion, bf16[2,1024,2048]{2,1,0:T(8,128)(2,1)} %fusion.1), kind=kOutput, calls=%fused_computation.28 | convolution fusion | flops 8594128896 | bytes 20971520 | tf_op jit(solution)/shard_map/erf,erd->efd/dot_general | solution.py:502
  809.4 27.2 %convolution_convert_fusion = bf16[2,2048,2048]{2,1,0:T(8,128)(2,1)} fusion(bf16[2,1024,2048]{2,1,0:T(8,128)(2,1)} %bitcast.286, f32[2,1024,1024]{2,1,0:T(8,128)} %get-tuple-element.75, f32[2,1024,1024]{2,1,0:T(8,128)} %get-tuple-element.74), kind=kOutput, calls=%fused_computation.11 | convolution fusion | flops 17196646400 | bytes 41943040 | tf_op jit(solution)/shard_map/erd,erf->edf/dot_general | solution.py:503
  837.4 10.1 fusion.10
  847.5 15.2 %fusion.3 = bf16[8,256,2048]{1,2,0:T(8,128)(2,1)} fusion(f32[8,256,2048,1]{1,2,3,0:T(8,128)} %fusion.10, bf16[2,8,128,2048]{3,2,1,0:T(8,128)(2,1)} %bitcast.276, f32[8,2,256]{2,1,0:T(2,128)S(1)} %copy-done.38, f32[128]{0:T(128)S(1)} %iota_convert_fusion, f32[8,2,256]{2,1,0:T(2,128)S(1)} %dynamic-slice_bitcast_fusion.1), kind=kOutput, calls=%fused_computation.9 | convolution fusion | flops 2156920832 | bytes 33587712 | tf_op jit(solution)/shard_map/sect,escd->std/dot_general | solution.py:460
  862.7 4.3 slice_bitcast_fusion.14
  871.6 7.5 collective-permute-done.37
  879.8 4.7 collective-permute-done.36
  888.4 5.0 collective-permute-done.12
  893.4 22.9 %collective-permute-done.10 = bf16[256,2048]{0,1:T(8,128)(2,1)S(1)} collective-permute-done((bf16[256,2048]{0,1:T(8,128)(2,1)}, bf16[256,2048]{0,1:T(8,128)(2,1)S(1)}, u32[]{:S(2)}, u32[]{:S(2)}) %collective-permute-start.10) | collective-permute-done | bytes 1048608 | tf_op jit(solution)/shard_map/ppermute | solution.py:71
  916.3 30.1 %collective-permute-done.8 = bf16[256,2048]{0,1:T(8,128)(2,1)} collective-permute-done((bf16[256,2048]{0,1:T(8,128)(2,1)}, bf16[256,2048]{0,1:T(8,128)(2,1)}, u32[]{:S(2)}, u32[]{:S(2)}) %collective-permute-start.8) | collective-permute-done | bytes 1048608 | tf_op jit(solution)/shard_map/ppermute | solution.py:71
  946.4 4.4 fusion.66
  958.9 266.1 %shard_map.221 = bf16[512,6144]{1,0:T(8,128)(2,1)} custom-call(bf16[256,6144]{1,0:T(8,128)(2,1)} %pad_maximum_fusion.grads_ref, bf16[512,1024]{1,0:T(8,128)(2,1)} %maximum_bitcast_fusion.columns_ref), custom_call_target="tpu_custom_call" | custom-call | flops 6442450944 | bytes 16777216 | tf_op jit(solution)/shard_map/pallas_call | solution.py:312
  1225.0 9.6 convert_element_type.298
  1236.1 4.4 fusion.48
  1250.7 4.2 convert_element_type.304
  1254.9 38.6 %reduce-scatter.3.cloned.1.call-done = bf16[2,512,2048]{2,1,0:T(8,128)(2,1)} async-done(((bf16[2,2048,2048]{2,1,0:T(8,128)(2,1)}), bf16[2,512,2048]{2,1,0:T(8,128)(2,1)}) %reduce-scatter.3.cloned.1.call-update) | async-done | bytes 4194320 | tf_op jit(solution)/shard_map/reduce_scatter | solution.py:506
  1293.6 6.7 convert_element_type.302
  (354 shorter events, 171.5 us)
Async XLA Ops:
  7.2 204.5 %all-gather.4.cloned.1.call-start = ((), (), s32[]{:S(2)}) async-start(), calls=%async_computation.2 | async-start | bytes 31457280 | tf_op jit(solution)/shard_map/all_gather | solution.py:371
  8.0 238.2 %all-gather.6.cloned.1.call-start = ((), (), s32[]{:S(2)}) async-start(), calls=%async_computation.3 | async-start | bytes 10485760 | tf_op jit(solution)/shard_map/all_gather | solution.py:371
  8.7 1234.9 %all-reduce.9.cloned.1.call-start = ((), (), s32[]{:S(2)}) async-start(), calls=%async_computation.4 | async-start | bytes 393216 | tf_op jit(solution)/shard_map/psum | solution.py:575
  8.8 128.0 %collective-permute-start.15 = (bf16[256,2048]{1,0:T(8,128)(2,1)S(1)}, bf16[256,2048]{1,0:T(8,128)(2,1)}, u32[]{:S(2)}, u32[]{:S(2)}) collective-permute-start(bf16[256,2048]{1,0:T(8,128)(2,1)S(1)} %copy-done.20), channel_id=1, source_target_pairs={{0,8},{4,12},{8,16},{12,20},{16,24},{20,28},{24,0},{28,4},{1,9},{5... | collective-permute-start | bytes 3145736 | tf_op jit(solution)/shard_map/ppermute | solution.py:71
  11.9 134.0 %collective-permute-start.14 = (bf16[256,2048]{1,0:T(8,128)(2,1)S(1)}, bf16[256,2048]{1,0:T(8,128)(2,1)}, u32[]{:S(2)}, u32[]{:S(2)}) collective-permute-start(bf16[256,2048]{1,0:T(8,128)(2,1)S(1)} %copy-done.20), channel_id=1, source_target_pairs={{0,4},{4,0},{8,12},{12,8},{16,20},{20,16},{24,28},{28,24},{1,5},{5... | collective-permute-start | bytes 3145736 | tf_op jit(solution)/shard_map/ppermute | solution.py:71
  13.4 130.5 %collective-permute-start.19 = (bf16[256,2048]{1,0:T(8,128)(2,1)S(1)}, bf16[256,2048]{1,0:T(8,128)(2,1)}, u32[]{:S(2)}, u32[]{:S(2)}) collective-permute-start(bf16[256,2048]{1,0:T(8,128)(2,1)S(1)} %copy-done.20), channel_id=1, source_target_pairs={{0,24},{4,28},{8,0},{12,4},{16,8},{20,12},{24,16},{28,20},{1,25},{... | collective-permute-start | bytes 3145736 | tf_op jit(solution)/shard_map/ppermute | solution.py:71
  15.6 130.1 %collective-permute-start.17 = (bf16[256,2048]{1,0:T(8,128)(2,1)S(1)}, bf16[256,2048]{1,0:T(8,128)(2,1)}, u32[]{:S(2)}, u32[]{:S(2)}) collective-permute-start(bf16[256,2048]{1,0:T(8,128)(2,1)S(1)} %copy-done.20), channel_id=1, source_target_pairs={{0,16},{4,20},{8,24},{12,28},{16,0},{20,4},{24,8},{28,12},{1,17},{... | collective-permute-start | bytes 3145736 | tf_op jit(solution)/shard_map/ppermute | solution.py:71
  136.8 26.4 %collective-permute-start.16 = (bf16[256,2048]{1,0:T(8,128)(2,1)}, bf16[256,2048]{1,0:T(8,128)(2,1)}, u32[]{:S(2)}, u32[]{:S(2)}) collective-permute-start(bf16[256,2048]{1,0:T(8,128)(2,1)} %collective-permute-done.15), channel_id=1, source_target_pairs={{0,4},{4,0},{8,12},{12,8},{16,20},{20,16},{24,28},{28,24},{1,5},{5... | collective-permute-start | bytes 3145736 | tf_op jit(solution)/shard_map/ppermute | solution.py:71
  143.8 66.9 %collective-permute-start.20 = (bf16[256,2048]{1,0:T(8,128)(2,1)}, bf16[256,2048]{1,0:T(8,128)(2,1)S(1)}, u32[]{:S(2)}, u32[]{:S(2)}) collective-permute-start(bf16[256,2048]{1,0:T(8,128)(2,1)} %collective-permute-done.19), channel_id=1, source_target_pairs={{0,4},{4,0},{8,12},{12,8},{16,20},{20,16},{24,28},{28,24},{1,5},{5... | collective-permute-start | bytes 3145736 | tf_op jit(solution)/shard_map/ppermute | solution.py:71
  145.7 61.6 %collective-permute-start.18 = (bf16[256,2048]{1,0:T(8,128)(2,1)}, bf16[256,2048]{1,0:T(8,128)(2,1)S(1)}, u32[]{:S(2)}, u32[]{:S(2)}) collective-permute-start(bf16[256,2048]{1,0:T(8,128)(2,1)} %collective-permute-done.17), channel_id=1, source_target_pairs={{0,4},{4,0},{8,12},{12,8},{16,20},{20,16},{24,28},{28,24},{1,5},{5... | collective-permute-start | bytes 3145736 | tf_op jit(solution)/shard_map/ppermute | solution.py:71
  255.6 71.7 %collective-permute-start.5 = (bf16[256,2048]{0,1:T(8,128)(2,1)S(1)}, bf16[256,2048]{0,1:T(8,128)(2,1)S(1)}, u32[]{:S(2)}, u32[]{:S(2)}) collective-permute-start(bf16[256,2048]{0,1:T(8,128)(2,1)S(1)} %get-tuple-element.73), channel_id=1, source_target_pairs={{0,24},{4,28},{8,0},{12,4},{16,8},{20,12},{24,16},{28,20},{1,25},{... | collective-permute-start | bytes 3145736 | tf_op jit(solution)/shard_map/ppermute | solution.py:71
  256.5 89.5 %collective-permute-start.3 = (bf16[256,2048]{0,1:T(8,128)(2,1)S(1)}, bf16[256,2048]{0,1:T(8,128)(2,1)}, u32[]{:S(2)}, u32[]{:S(2)}) collective-permute-start(bf16[256,2048]{0,1:T(8,128)(2,1)S(1)} %get-tuple-element.73), channel_id=1, source_target_pairs={{0,16},{4,20},{8,24},{12,28},{16,0},{20,4},{24,8},{28,12},{1,17},{... | collective-permute-start | bytes 3145736 | tf_op jit(solution)/shard_map/ppermute | solution.py:71
  256.5 68.4 %collective-permute-start.1 = (bf16[256,2048]{0,1:T(8,128)(2,1)S(1)}, bf16[256,2048]{0,1:T(8,128)(2,1)}, u32[]{:S(2)}, u32[]{:S(2)}) collective-permute-start(bf16[256,2048]{0,1:T(8,128)(2,1)S(1)} %get-tuple-element.73), channel_id=1, source_target_pairs={{0,8},{4,12},{8,16},{12,20},{16,24},{20,28},{24,0},{28,4},{1,9},{5... | collective-permute-start | bytes 3145736 | tf_op jit(solution)/shard_map/ppermute | solution.py:71
  257.7 89.6 %collective-permute-start = (bf16[256,2048]{0,1:T(8,128)(2,1)S(1)}, bf16[256,2048]{0,1:T(8,128)(2,1)}, u32[]{:S(2)}, u32[]{:S(2)}) collective-permute-start(bf16[256,2048]{0,1:T(8,128)(2,1)S(1)} %get-tuple-element.73), channel_id=1, source_target_pairs={{0,4},{4,0},{8,12},{12,8},{16,20},{20,16},{24,28},{28,24},{1,5},{5... | collective-permute-start | bytes 3145736 | tf_op jit(solution)/shard_map/ppermute | solution.py:71
  324.9 26.3 %collective-permute-start.2 = (bf16[256,2048]{0,1:T(8,128)(2,1)}, bf16[256,2048]{0,1:T(8,128)(2,1)S(1)}, u32[]{:S(2)}, u32[]{:S(2)}) collective-permute-start(bf16[256,2048]{0,1:T(8,128)(2,1)} %collective-permute-done.1), channel_id=1, source_target_pairs={{0,4},{4,0},{8,12},{12,8},{16,20},{20,16},{24,28},{28,24},{1,5},{5... | collective-permute-start | bytes 3145736 | tf_op jit(solution)/shard_map/ppermute | solution.py:71
  327.4 67.1 %collective-permute-start.6 = (bf16[256,2048]{0,1:T(8,128)(2,1)S(1)}, bf16[256,2048]{0,1:T(8,128)(2,1)S(1)}, u32[]{:S(2)}, u32[]{:S(2)}) collective-permute-start(bf16[256,2048]{0,1:T(8,128)(2,1)S(1)} %collective-permute-done.5), channel_id=1, source_target_pairs={{0,4},{4,0},{8,12},{12,8},{16,20},{20,16},{24,28},{28,24},{1,5},{5... | collective-permute-start | bytes 3145736 | tf_op jit(solution)/shard_map/ppermute | solution.py:71
  346.0 48.3 %collective-permute-start.4 = (bf16[256,2048]{0,1:T(8,128)(2,1)}, bf16[256,2048]{0,1:T(8,128)(2,1)S(1)}, u32[]{:S(2)}, u32[]{:S(2)}) collective-permute-start(bf16[256,2048]{0,1:T(8,128)(2,1)} %collective-permute-done.3), channel_id=1, source_target_pairs={{0,4},{4,0},{8,12},{12,8},{16,20},{20,16},{24,28},{28,24},{1,5},{5... | collective-permute-start | bytes 3145736 | tf_op jit(solution)/shard_map/ppermute | solution.py:71
  534.5 105.7 %collective-permute-start.26 = (bf16[256,2048]{0,1:T(8,128)(2,1)S(1)}, bf16[256,2048]{0,1:T(8,128)(2,1)S(1)}, u32[]{:S(2)}, u32[]{:S(2)}) collective-permute-start(bf16[256,2048]{0,1:T(8,128)(2,1)S(1)} %get-tuple-element.77), channel_id=1, source_target_pairs={{0,4},{4,0},{8,12},{12,8},{16,20},{20,16},{24,28},{28,24},{1,5},{5... | collective-permute-start | bytes 3145736 | tf_op jit(solution)/shard_map/ppermute | solution.py:71
  535.7 106.0 %collective-permute-start.24 = (bf16[256,2048]{0,1:T(8,128)(2,1)S(1)}, bf16[256,2048]{0,1:T(8,128)(2,1)S(1)}, u32[]{:S(2)}, u32[]{:S(2)}) collective-permute-start(bf16[256,2048]{0,1:T(8,128)(2,1)S(1)} %get-tuple-element.78), channel_id=1, source_target_pairs={{0,4},{4,0},{8,12},{12,8},{16,20},{20,16},{24,28},{28,24},{1,5},{5... | collective-permute-start | bytes 3145736 | tf_op jit(solution)/shard_map/ppermute | solution.py:71
  536.5 105.1 %collective-permute-start.22 = (bf16[256,2048]{0,1:T(8,128)(2,1)S(1)}, bf16[256,2048]{0,1:T(8,128)(2,1)S(1)}, u32[]{:S(2)}, u32[]{:S(2)}) collective-permute-start(bf16[256,2048]{0,1:T(8,128)(2,1)S(1)} %get-tuple-element.79), channel_id=1, source_target_pairs={{0,4},{4,0},{8,12},{12,8},{16,20},{20,16},{24,28},{28,24},{1,5},{5... | collective-permute-start | bytes 3145736 | tf_op jit(solution)/shard_map/ppermute | solution.py:71
  537.7 65.1 %collective-permute-start.28 = (f32[2,256]{1,0:T(2,128)S(1)}, f32[2,256]{1,0:T(2,128)S(1)}, u32[]{:S(2)}, u32[]{:S(2)}) collective-permute-start(f32[2,256]{1,0:T(2,128)S(1)} %get-tuple-element.132), channel_id=1, source_target_pairs={{0,4},{4,0},{8,12},{12,8},{16,20},{20,16},{24,28},{28,24},{1,5},{5... | collective-permute-start | bytes 6152 | tf_op jit(solution)/shard_map/ppermute | solution.py:71
  538.6 108.3 %collective-permute-start.33 = (f32[2,256]{1,0:T(2,128)S(1)}, f32[2,256]{1,0:T(2,128)S(1)}, u32[]{:S(2)}, u32[]{:S(2)}) collective-permute-start(f32[2,256]{1,0:T(2,128)S(1)} %get-tuple-element.127), channel_id=1, source_target_pairs={{0,8},{4,12},{8,16},{12,20},{16,24},{20,28},{24,0},{28,4},{1,9},{5... | collective-permute-start | bytes 6152 | tf_op jit(solution)/shard_map/ppermute | solution.py:71
  602.8 24.2 %collective-permute-start.29 = (f32[2,256]{1,0:T(2,128)S(1)}, f32[2,256]{1,0:T(2,128)S(1)}, u32[]{:S(2)}, u32[]{:S(2)}) collective-permute-start(f32[2,256]{1,0:T(2,128)S(1)} %get-tuple-element.131), channel_id=1, source_target_pairs={{0,24},{4,28},{8,0},{12,4},{16,8},{20,12},{24,16},{28,20},{1,25},{... | collective-permute-start | bytes 6152 | tf_op jit(solution)/shard_map/ppermute | solution.py:71
  631.7 5.4 collective-permute-start.31
  637.1 8.8 collective-permute-start.32
  640.2 68.6 %collective-permute-start.21 = (bf16[256,2048]{0,1:T(8,128)(2,1)}, bf16[256,2048]{0,1:T(8,128)(2,1)}, u32[]{:S(2)}, u32[]{:S(2)}) collective-permute-start(bf16[256,2048]{0,1:T(8,128)(2,1)} %get-tuple-element.76), channel_id=1, source_target_pairs={{0,4},{4,0},{8,12},{12,8},{16,20},{20,16},{24,28},{28,24},{1,5},{5... | collective-permute-start | bytes 3145736 | tf_op jit(solution)/shard_map/ppermute | solution.py:71
  643.9 67.2 %collective-permute-start.23 = (bf16[256,2048]{0,1:T(8,128)(2,1)}, bf16[256,2048]{0,1:T(8,128)(2,1)}, u32[]{:S(2)}, u32[]{:S(2)}) collective-permute-start(bf16[256,2048]{0,1:T(8,128)(2,1)} %get-tuple-element.80), channel_id=1, source_target_pairs={{0,24},{4,28},{8,0},{12,4},{16,8},{20,12},{24,16},{28,20},{1,25},{... | collective-permute-start | bytes 3145736 | tf_op jit(solution)/shard_map/ppermute | solution.py:71
  644.8 66.4 %collective-permute-start.27 = (bf16[256,2048]{0,1:T(8,128)(2,1)}, bf16[256,2048]{0,1:T(8,128)(2,1)}, u32[]{:S(2)}, u32[]{:S(2)}) collective-permute-start(bf16[256,2048]{0,1:T(8,128)(2,1)} %get-tuple-element.81), channel_id=1, source_target_pairs={{0,8},{4,12},{8,16},{12,20},{16,24},{20,28},{24,0},{28,4},{1,9},{5... | collective-permute-start | bytes 3145736 | tf_op jit(solution)/shard_map/ppermute | solution.py:71
  645.9 85.6 %collective-permute-start.25 = (bf16[256,2048]{0,1:T(8,128)(2,1)}, bf16[256,2048]{0,1:T(8,128)(2,1)}, u32[]{:S(2)}, u32[]{:S(2)}) collective-permute-start(bf16[256,2048]{0,1:T(8,128)(2,1)} %get-tuple-element.82), channel_id=1, source_target_pairs={{0,16},{4,20},{8,24},{12,28},{16,0},{20,4},{24,8},{28,12},{1,17},{... | collective-permute-start | bytes 3145736 | tf_op jit(solution)/shard_map/ppermute | solution.py:71
  646.9 60.8 %collective-permute-start.34 = (f32[2,256]{1,0:T(2,128)S(1)}, f32[2,256]{1,0:T(2,128)S(1)}, u32[]{:S(2)}, u32[]{:S(2)}) collective-permute-start(f32[2,256]{1,0:T(2,128)S(1)} %get-tuple-element.126), channel_id=1, source_target_pairs={{0,12},{4,8},{8,20},{12,16},{16,28},{20,24},{24,4},{28,0},{1,13},{... | collective-permute-start | bytes 6152 | tf_op jit(solution)/shard_map/ppermute | solution.py:71
  707.6 80.5 %collective-permute-start.40 = (bf16[256,512]{0,1:T(8,128)(2,1)}, bf16[256,512]{0,1:T(8,128)(2,1)}, u32[]{:S(2)}, u32[]{:S(2)}) collective-permute-start(bf16[256,512]{0,1:T(8,128)(2,1)} %get-tuple-element.105), channel_id=1, source_target_pairs={{0,3},{1,2},{2,1},{3,0},{4,7},{5,6},{6,5},{7,4},{8,11},{9,10},{10,... | collective-permute-start | bytes 786440 | tf_op jit(solution)/shard_map/ppermute | solution.py:113
  708.8 79.4 %collective-permute-start.39 = (bf16[256,512]{0,1:T(8,128)(2,1)}, bf16[256,512]{0,1:T(8,128)(2,1)}, u32[]{:S(2)}, u32[]{:S(2)}) collective-permute-start(bf16[256,512]{0,1:T(8,128)(2,1)} %get-tuple-element.106), channel_id=1, source_target_pairs={{0,2},{1,3},{2,0},{3,1},{4,6},{5,7},{6,4},{7,5},{8,10},{9,11},{10,... | collective-permute-start | bytes 786440 | tf_op jit(solution)/shard_map/ppermute | solution.py:113
  711.0 77.2 %collective-permute-start.38 = (bf16[256,512]{0,1:T(8,128)(2,1)}, bf16[256,512]{0,1:T(8,128)(2,1)}, u32[]{:S(2)}, u32[]{:S(2)}) collective-permute-start(bf16[256,512]{0,1:T(8,128)(2,1)} %get-tuple-element.107), channel_id=1, source_target_pairs={{0,1},{1,0},{2,3},{3,2},{4,5},{5,4},{6,7},{7,6},{8,9},{9,8},{10,11... | collective-permute-start | bytes 786440 | tf_op jit(solution)/shard_map/ppermute | solution.py:113
  737.3 35.9 %collective-permute-start.42 = (bf16[256,2048]{0,1:T(8,128)(2,1)}, bf16[256,2048]{0,1:T(8,128)(2,1)}, u32[]{:S(2)}, u32[]{:S(2)}) collective-permute-start(bf16[256,2048]{0,1:T(8,128)(2,1)} %fusion.147), channel_id=1, source_target_pairs={{0,2},{1,3},{2,0},{3,1},{4,6},{5,7},{6,4},{7,5},{8,10},{9,11},{10,... | collective-permute-start | bytes 3145736 | tf_op jit(solution)/shard_map/ppermute | solution.py:113
  739.6 48.6 %collective-permute-start.41 = (bf16[256,2048]{0,1:T(8,128)(2,1)}, bf16[256,2048]{0,1:T(8,128)(2,1)}, u32[]{:S(2)}, u32[]{:S(2)}) collective-permute-start(bf16[256,2048]{0,1:T(8,128)(2,1)} %fusion.147), channel_id=1, source_target_pairs={{0,1},{1,0},{2,3},{3,2},{4,5},{5,4},{6,7},{7,6},{8,9},{9,8},{10,11... | collective-permute-start | bytes 3145736 | tf_op jit(solution)/shard_map/ppermute | solution.py:113
  773.2 15.0 %collective-permute-start.43 = (bf16[256,2048]{0,1:T(8,128)(2,1)}, bf16[256,2048]{0,1:T(8,128)(2,1)S(1)}, u32[]{:S(2)}, u32[]{:S(2)}) collective-permute-start(bf16[256,2048]{0,1:T(8,128)(2,1)} %collective-permute-done.42), channel_id=1, source_target_pairs={{0,1},{1,0},{2,3},{3,2},{4,5},{5,4},{6,7},{7,6},{8,9},{9,8},{10,11... | collective-permute-start | bytes 3145736 | tf_op jit(solution)/shard_map/ppermute | solution.py:113
  788.1 458.5 %all-reduce.11.cloned.1.call-start = ((), (), s32[]{:S(2)}) async-start(), calls=%async_computation.5 | async-start | bytes 4194304 | tf_op jit(solution)/shard_map/psum | solution.py:561
  794.0 456.7 %reduce-scatter.5.cloned.1.call-start = ((), (), s32[]{:S(2)}) async-start(), calls=%async_computation.7 | async-start | bytes 10485760 | tf_op jit(solution)/shard_map/reduce_scatter | solution.py:509
  809.4 484.2 %reduce-scatter.3.cloned.1.call-start = ((), (), s32[]{:S(2)}) async-start(), calls=%async_computation.6 | async-start | bytes 20971520 | tf_op jit(solution)/shard_map/reduce_scatter | solution.py:506
  867.0 26.4 %collective-permute-start.12 = (bf16[256,2048]{0,1:T(8,128)(2,1)}, bf16[256,2048]{0,1:T(8,128)(2,1)S(1)}, u32[]{:S(2)}, u32[]{:S(2)}) collective-permute-start(bf16[256,2048]{0,1:T(8,128)(2,1)} %get-tuple-element.84), channel_id=1, source_target_pairs={{0,4},{4,0},{8,12},{12,8},{16,20},{20,16},{24,28},{28,24},{1,5},{5... | collective-permute-start | bytes 3145736 | tf_op jit(solution)/shard_map/ppermute | solution.py:71
  867.4 48.9 %collective-permute-start.10 = (bf16[256,2048]{0,1:T(8,128)(2,1)}, bf16[256,2048]{0,1:T(8,128)(2,1)S(1)}, u32[]{:S(2)}, u32[]{:S(2)}) collective-permute-start(bf16[256,2048]{0,1:T(8,128)(2,1)} %get-tuple-element.85), channel_id=1, source_target_pairs={{0,4},{4,0},{8,12},{12,8},{16,20},{20,16},{24,28},{28,24},{1,5},{5... | collective-permute-start | bytes 3145736 | tf_op jit(solution)/shard_map/ppermute | solution.py:71
  869.1 77.4 %collective-permute-start.8 = (bf16[256,2048]{0,1:T(8,128)(2,1)}, bf16[256,2048]{0,1:T(8,128)(2,1)}, u32[]{:S(2)}, u32[]{:S(2)}) collective-permute-start(bf16[256,2048]{0,1:T(8,128)(2,1)} %get-tuple-element.86), channel_id=1, source_target_pairs={{0,4},{4,0},{8,12},{12,8},{16,20},{20,16},{24,28},{28,24},{1,5},{5... | collective-permute-start | bytes 3145736 | tf_op jit(solution)/shard_map/ppermute | solution.py:71
  870.3 8.8 collective-permute-start.37
  870.3 14.2 %collective-permute-start.36 = (bf16[256,512]{0,1:T(8,128)(2,1)}, bf16[256,512]{0,1:T(8,128)(2,1)}, u32[]{:S(2)}, u32[]{:S(2)}) collective-permute-start(bf16[256,512]{0,1:T(8,128)(2,1)} %get-tuple-element.110), channel_id=1, source_target_pairs={{0,2},{1,3},{2,0},{3,1},{4,6},{5,7},{6,4},{7,5},{8,10},{9,11},{10,... | collective-permute-start | bytes 786440 | tf_op jit(solution)/shard_map/ppermute | solution.py:113
  886.8 347.9 %collective-permute-start.7 = (bf16[256,2048]{0,1:T(8,128)(2,1)}, bf16[256,2048]{0,1:T(8,128)(2,1)}, u32[]{:S(2)}, u32[]{:S(2)}) collective-permute-start(bf16[256,2048]{0,1:T(8,128)(2,1)} %get-tuple-element.83), channel_id=1, source_target_pairs={{0,4},{4,0},{8,12},{12,8},{16,20},{20,16},{24,28},{28,24},{1,5},{5... | collective-permute-start | bytes 3145736 | tf_op jit(solution)/shard_map/ppermute | solution.py:71
  950.8 283.9 %collective-permute-start.9 = (bf16[256,2048]{0,1:T(8,128)(2,1)}, bf16[256,2048]{0,1:T(8,128)(2,1)S(1)}, u32[]{:S(2)}, u32[]{:S(2)}) collective-permute-start(bf16[256,2048]{0,1:T(8,128)(2,1)} %get-tuple-element.87), channel_id=1, source_target_pairs={{0,24},{4,28},{8,0},{12,4},{16,8},{20,12},{24,16},{28,20},{1,25},{... | collective-permute-start | bytes 3145736 | tf_op jit(solution)/shard_map/ppermute | solution.py:71
  952.6 282.1 %collective-permute-start.13 = (bf16[256,2048]{0,1:T(8,128)(2,1)}, bf16[256,2048]{0,1:T(8,128)(2,1)S(1)}, u32[]{:S(2)}, u32[]{:S(2)}) collective-permute-start(bf16[256,2048]{0,1:T(8,128)(2,1)} %get-tuple-element.88), channel_id=1, source_target_pairs={{0,8},{4,12},{8,16},{12,20},{16,24},{20,28},{24,0},{28,4},{1,9},{5... | collective-permute-start | bytes 3145736 | tf_op jit(solution)/shard_map/ppermute | solution.py:71
  952.9 281.8 %collective-permute-start.11 = (bf16[256,2048]{0,1:T(8,128)(2,1)}, bf16[256,2048]{0,1:T(8,128)(2,1)}, u32[]{:S(2)}, u32[]{:S(2)}) collective-permute-start(bf16[256,2048]{0,1:T(8,128)(2,1)} %get-tuple-element.89), channel_id=1, source_target_pairs={{0,16},{4,20},{8,24},{12,28},{16,0},{20,4},{24,8},{28,12},{1,17},{... | collective-permute-start | bytes 3145736 | tf_op jit(solution)/shard_map/ppermute | solution.py:71
  (83 other events, 2159.5 us)
Sparse Core Ops, SparseCore 0:
  9.7 157.9 all-gather.3
  169.2 58.2 all-gather.5
  788.3 123.9 all-reduce.8
  915.7 168.7 all-reduce.10
  1086.9 77.6 reduce-scatter.4
  1167.2 126.2 reduce-scatter.2

commit v3 on v2

--- a/solution.py
+++ b/solution.py
@@ -84,13 +84,9 @@
 
 def reduce_expert(parts, expert_group):
     z_all = z_size(expert_group)
-    x_all = expert_group // z_all
-    rows = []
-    for dz in range(z_all):
-        total = parts[dz * x_all].astype(jnp.float32)
-        for dx in range(1, x_all):
-            total = total + shift(parts[dz * x_all + dx], expert_group, 0, -dx).astype(jnp.float32)
-        rows.append(total)
+    rows = parts[0].astype(jnp.float32)
+    for dx in range(1, len(parts)):
+        rows = rows + shift(parts[dx], expert_group, 0, -dx).astype(jnp.float32)
     total = rows[0]
     for dz in range(1, z_all):
         total = total + shift(
@@ -339,6 +335,463 @@
     )(grads, columns)
 
 
+MOE_CHUNKS = 4
+
+
+def moe_kernel(
+    dims, hidden_hbm, upstream_hbm, place_ref, place_t_ref, router_ref, router_t_ref, gate_up_hbm, down_hbm,
+    rows_hbm, activated_hbm, grad_out_hbm, grad_gate_up_hbm, grad_ref, grad_router_ref, found_hbm, summed_hbm,
+    *rest,
+):
+    x_all, capacity = dims
+    mixture_hbm = rest[:x_all]
+    (
+    gate_up_w, down_w, hid, ups, prob, prob_t, rows, gate_up, activated, out_rows, grad_expert, grad_gate_up, grad_rows,
+    mix_stage, part_stage, own_part, z_landed, router_stage,
+    w_sem, own_sem, load_sem, store_sem, zs, zr, xs, xr, fs, fr, ps, pr, qs, qr, rs, rr, lsem, mix_sem,
+    ) = rest[x_all:]
+    z_all = 4
+    f32, bf16 = jnp.float32, jnp.bfloat16
+    length, width = hidden_hbm.shape
+    local_experts, _, twice = gate_up_w.shape
+    half = twice // 2
+    tile = min(512, half)
+    narrow = min(256, half)
+    chunk = length // MOE_CHUNKS
+    e = lax.axis_index("expert")
+    z, x = e // x_all, lax.rem(e, x_all)
+
+    def peer(dz, dx):
+        return {"expert": lax.rem(z + dz + 4 * z_all, z_all) * x_all + lax.rem(x + dx + 4 * x_all, x_all)}
+
+    def copy(src, dst, send, recv, to):
+        return pltpu.make_async_remote_copy(
+            src_ref=src, dst_ref=dst, send_sem=send, recv_sem=recv, device_id=to,
+            device_id_type=pl.DeviceIdType.MESH,
+        )
+
+    def at(c):
+        return pl.ds(pl.multiple_of(c * chunk, chunk), chunk)
+
+    def z_copy(d, c):
+        return copy(hidden_hbm.at[at(c)], found_hbm.at[d, 0, at(c)], zs.at[d - 1, c], zr.at[d - 1, c], peer(d, 0))
+
+    def x_copy(d, c):
+        return copy(hidden_hbm.at[at(c)], found_hbm.at[0, d, at(c)], xs.at[d - 1, c], xr.at[d - 1, c], peer(0, d))
+
+    def f_copy(dz, dx, c):
+        return copy(
+            found_hbm.at[dz, 0, at(c)], found_hbm.at[dz, dx, at(c)],
+            fs.at[dz - 1, dx - 1, c], fr.at[dz - 1, dx - 1, c], peer(0, dx),
+        )
+
+    def p_copy(dz, dx):
+        return copy(part_stage.at[dx - 1], summed_hbm.at[dz, dx - 1], ps.at[dx - 1], pr.at[dz, dx - 1], peer(0, -dx))
+
+    def q_copy(dz):
+        return copy(own_part.at[dz], z_landed.at[dz - 1], qs.at[dz - 1], qr.at[dz - 1], peer(-dz, 0))
+
+    def r_copy(dz, dx):
+        return copy(
+            router_stage.at[dz, dx], grad_router_ref.at[e], rs.at[dz, dx], rr.at[dz, dx], peer(-dz, -dx)
+        )
+
+    def cols(n, w):
+        return pl.ds(pl.multiple_of(n * w, w), w)
+
+    barrier = pltpu.get_barrier_semaphore()
+    others = [(dz, dx) for dz in range(z_all) for dx in range(x_all) if dz + dx > 0]
+    for dz, dx in others:
+        pl.semaphore_signal(barrier, inc=1, device_id=peer(dz, dx), device_id_type=pl.DeviceIdType.MESH)
+    pl.semaphore_wait(barrier, len(others))
+
+    own = pltpu.make_async_copy(hidden_hbm, found_hbm.at[0, 0], own_sem)
+    own.start()
+    weights = [
+        pltpu.make_async_copy(gate_up_hbm, gate_up_w, w_sem.at[0]),
+        pltpu.make_async_copy(down_hbm, down_w, w_sem.at[1]),
+    ]
+    for w in weights:
+        w.start()
+
+    def send_own(c, carry):
+        for d in range(1, x_all):
+            x_copy(d, c).start()
+        return carry
+
+    lax.fori_loop(0, MOE_CHUNKS, send_own, 0)
+    for d in (2, 1, 3):
+
+        def send_z(c, carry):
+            z_copy(d, c).start()
+            return carry
+
+        lax.fori_loop(0, MOE_CHUNKS, send_z, 0)
+
+    def events(first):
+        def one(k, carry):
+            @pl.when(k < 3 * MOE_CHUNKS)
+            def _():
+                j = k // MOE_CHUNKS
+                c = lax.rem(k, MOE_CHUNKS)
+                d = 2 - j + 3 * (j // 2)
+                z_copy(d, c).wait_recv()
+                for dx in range(1, x_all):
+                    f_copy(d, dx, c).start()
+
+            return carry
+
+        lax.fori_loop(first, first + 2, one, 0)
+
+    def finish(g):
+        dz = g // 2 + 2 * lax.rem(g, 2)
+        for dx in range(1, x_all):
+            p_copy(dz, dx).wait_recv()
+            load = pltpu.make_async_copy(summed_hbm.at[dz, dx - 1], hid.at[0], lsem)
+            load.start()
+            load.wait()
+
+            def add(n, carry):
+                c = cols(n, tile)
+                own_part[dz, :, c] = (own_part[dz, :, c].astype(f32) + hid[0, :, c].astype(f32)).astype(bf16)
+                return carry
+
+            lax.fori_loop(0, width // tile, add, 0)
+
+        @pl.when(dz > 0)
+        def _():
+            q_copy(dz).start()
+
+    mix_slots = mix_stage.shape[0]
+
+    def mix_copy(dz, dx):
+        slot = dx % mix_slots
+        return pltpu.make_async_copy(mix_stage.at[slot], mixture_hbm[dx].at[dz], mix_sem.at[slot])
+
+    slot_row = lax.broadcasted_iota(jnp.int32, (capacity, length), 0).astype(f32)
+    slot_col = lax.broadcasted_iota(jnp.int32, (length, capacity), 1).astype(f32)
+    own.wait()
+    events(0)
+
+    def group(g, carry):
+        dz = g // 2 + 2 * lax.rem(g, 2)
+
+        def arrive(c, inner):
+            for dx in range(1, x_all):
+
+                @pl.when(dz == 0)
+                def _():
+                    x_copy(dx, c).wait_recv()
+
+                @pl.when(dz > 0)
+                def _():
+                    f_copy(dz, dx, c).wait_recv()
+
+            return inner
+
+        lax.fori_loop(0, MOE_CHUNKS, arrive, 0)
+        loads = []
+        for dx in range(x_all):
+            loads.append(pltpu.make_async_copy(found_hbm.at[dz, dx], hid.at[dx], load_sem.at[0, dx]))
+            loads.append(pltpu.make_async_copy(upstream_hbm.at[dz, dx], ups.at[dx], load_sem.at[1, dx]))
+        for load in loads:
+            load.start()
+        for load in loads:
+            load.wait()
+        pl.when(g == 0)(lambda: [w.wait() for w in weights] and None)
+
+        for dx in range(x_all):
+            logits = jnp.dot(hid[dx], router_ref[...], preferred_element_type=f32)
+            raised = jnp.exp(logits - jnp.max(logits, axis=1, keepdims=True))
+            prob[dx] = raised / jnp.sum(raised, axis=1, keepdims=True)
+            logits = lax.dot_general(
+                router_t_ref[...], hid[dx], (((1,), (1,)), ((), ())), preferred_element_type=f32
+            )
+            raised = jnp.exp(logits - jnp.max(logits, axis=0, keepdims=True))
+            prob_t[dx] = raised / jnp.sum(raised, axis=0, keepdims=True)
+            router_stage[dz, dx] = jnp.zeros(router_stage.shape[2:], f32)
+
+        def store(kind, buffer, hbm, le):
+            return pltpu.make_async_copy(buffer, hbm.at[le, dz], store_sem.at[kind])
+
+        def expert(le, inner):
+            @pl.when(g + le > 0)
+            def _():
+                store(0, rows, rows_hbm, le).wait()
+                store(1, activated, activated_hbm, le).wait()
+                store(2, grad_expert, grad_out_hbm, le).wait()
+                store(3, grad_gate_up, grad_gate_up_hbm, le).wait()
+
+            chosen = [place_ref[dz, dx, pl.ds(le, 1), :] == slot_row for dx in range(x_all)]
+            chosen_low = [c.astype(f32).astype(bf16) for c in chosen]
+
+            def dispatch(n, c0):
+                c = cols(n, tile)
+                for dx in range(x_all):
+                    rows[dx * capacity : (dx + 1) * capacity, c] = jnp.dot(
+                        chosen_low[dx], hid[dx, :, c], preferred_element_type=f32
+                    ).astype(bf16)
+                return c0
+
+            lax.fori_loop(0, width // tile, dispatch, 0)
+            store(0, rows, rows_hbm, le).start()
+
+            def up_step(n, c0):
+                c = cols(n, tile)
+                gate_up[:, c] = jnp.dot(rows[...], gate_up_w[le, :, c], preferred_element_type=f32)
+                return c0
+
+            lax.fori_loop(0, twice // tile, up_step, 0)
+
+            def act_step(n, c0):
+                gate = gate_up[:, cols(n, narrow)]
+                up = gate_up[:, pl.ds(pl.multiple_of(half + n * narrow, narrow), narrow)]
+                activated[:, cols(n, narrow)] = (gate / (1.0 + jnp.exp(-gate)) * up).astype(bf16)
+                return c0
+
+            lax.fori_loop(0, half // narrow, act_step, 0)
+            store(1, activated, activated_hbm, le).start()
+
+            def down_step(n, c0):
+                c = cols(n, tile)
+                out_rows[le, :, c] = jnp.dot(
+                    activated[...], down_w[le, :, c], preferred_element_type=f32
+                ).astype(bf16)
+                return c0
+
+            lax.fori_loop(0, width // tile, down_step, 0)
+
+            mine = e * local_experts + le
+            weight_rows = [
+                jnp.sum(jnp.where(chosen[dx], prob_t[dx, pl.ds(mine, 1), :], 0.0), axis=1, keepdims=True)
+                for dx in range(x_all)
+            ]
+
+            def grad_step(n, totals):
+                c = cols(n, tile)
+                new = []
+                for dx in range(x_all):
+                    r = slice(dx * capacity, (dx + 1) * capacity)
+                    up_rows = jnp.dot(chosen_low[dx], ups[dx, :, c], preferred_element_type=f32)
+                    grad_expert[r, c] = (weight_rows[dx] * up_rows).astype(bf16)
+                    new.append(
+                        totals[dx]
+                        + jnp.sum(up_rows * out_rows[le, r, c].astype(f32), axis=1, keepdims=True)
+                    )
+                return tuple(new)
+
+            totals = lax.fori_loop(
+                0, width // tile, grad_step, tuple(jnp.zeros((capacity, 1), f32) for _ in range(x_all))
+            )
+            store(2, grad_expert, grad_out_hbm, le).start()
+            for dx in range(x_all):
+                router_stage[dz, dx, pl.ds(le, 1), :] = jnp.sum(
+                    jnp.where(chosen[dx], totals[dx], 0.0), axis=0, keepdims=True
+                )
+
+            def back_step(n, c0):
+                ga = lax.dot_general(
+                    grad_expert[...], down_w[le, cols(n, narrow), :], (((1,), (1,)), ((), ())),
+                    preferred_element_type=f32,
+                )
+                gate = gate_up[:, cols(n, narrow)]
+                c_up = pl.ds(pl.multiple_of(half + n * narrow, narrow), narrow)
+                up = gate_up[:, c_up]
+                sg = 1.0 / (1.0 + jnp.exp(-gate))
+                grad_gate_up[:, cols(n, narrow)] = (ga * up * sg * (1.0 + gate * (1.0 - sg))).astype(bf16)
+                grad_gate_up[:, c_up] = (ga * (gate * sg)).astype(bf16)
+                return c0
+
+            lax.fori_loop(0, half // narrow, back_step, 0)
+            store(3, grad_gate_up, grad_gate_up_hbm, le).start()
+
+            def row_step(n, c0):
+                grad_rows[le, :, cols(n, narrow)] = lax.dot_general(
+                    grad_gate_up[...], gate_up_w[le, cols(n, narrow), :], (((1,), (1,)), ((), ())),
+                    preferred_element_type=f32,
+                ).astype(bf16)
+                return c0
+
+            lax.fori_loop(0, width // narrow, row_step, 0)
+            events(4 * g + 2 + 2 * le)
+            return inner
+
+        assert local_experts == 2
+        lax.fori_loop(0, local_experts, expert, 0)
+
+        def stages():
+            for dx in range(1, x_all):
+                p_copy(dz, dx).wait_send()
+
+        pl.when(g > 0)(stages)
+        for dx in range(x_all):
+            r = slice(dx * capacity, (dx + 1) * capacity)
+            low, high, remainder = [], [], []
+            for le in range(local_experts):
+                mask = place_t_ref[dz, dx, :, le : le + 1] == slot_col
+                lane = lax.broadcasted_iota(jnp.int32, prob.shape[1:], 1)
+                p = jnp.sum(jnp.where(lane == e * local_experts + le, prob[dx], 0.0), axis=1, keepdims=True)
+                weight = jnp.where(mask, p, 0.0)
+                top = weight.astype(bf16)
+                low.append(mask.astype(f32).astype(bf16))
+                high.append(top)
+                remainder.append((weight - top.astype(f32)).astype(bf16))
+
+            if dx < mix_slots:
+                pl.when(g > 0)(mix_copy(0, dx).wait)
+            else:
+                mix_copy(0, dx).wait()
+
+            def combine(n, c0):
+                c = cols(n, tile)
+                mix = jnp.zeros((length, tile), f32)
+                grad = jnp.zeros((length, tile), f32)
+                for le in range(local_experts):
+                    mix = mix + jnp.dot(high[le], out_rows[le, r, c], preferred_element_type=f32)
+                    mix = mix + jnp.dot(remainder[le], out_rows[le, r, c], preferred_element_type=f32)
+                    grad = grad + jnp.dot(low[le], grad_rows[le, r, c], preferred_element_type=f32)
+                mix_stage[dx % mix_slots, :, c] = mix.astype(bf16)
+                if dx == 0:
+                    own_part[dz, :, c] = grad.astype(bf16)
+                else:
+                    part_stage[dx - 1, :, c] = grad.astype(bf16)
+                return c0
+
+            lax.fori_loop(0, width // tile, combine, 0)
+            mix_copy(dz, dx).start()
+            if dx > 0:
+                p_copy(dz, dx).start()
+                r_copy(dz, dx).start()
+            else:
+
+                @pl.when(dz > 0)
+                def _():
+                    r_copy(dz, 0).start()
+
+                @pl.when(dz == 0)
+                def _():
+                    grad_router_ref[e] = router_stage[0, 0]
+
+        pl.when(g > 0)(lambda: finish(g - 1))
+        return carry
+
+    lax.fori_loop(0, z_all, group, 0)
+    finish(jnp.int32(z_all - 1))
+
+    def total(n, carry):
+        c = cols(n, tile)
+        grad_ref[:, c] = own_part[0, :, c].astype(f32)
+        return carry
+
+    lax.fori_loop(0, width // tile, total, 0)
+    for d in (2, 1, 3):
+        q_copy(d).wait_recv()
+
+        def more(n, carry):
+            c = cols(n, tile)
+            grad_ref[:, c] = grad_ref[:, c] + z_landed[d - 1, :, c].astype(f32)
+            return carry
+
+        lax.fori_loop(0, width // tile, more, 0)
+
+    for kind, buffer, hbm in (
+        (0, rows, rows_hbm), (1, activated, activated_hbm), (2, grad_expert, grad_out_hbm),
+        (3, grad_gate_up, grad_gate_up_hbm),
+    ):
+        pltpu.make_async_copy(buffer, hbm.at[0, 0], store_sem.at[kind]).wait()
+    for dx in range(mix_slots):
+        mix_copy(0, dx).wait()
+    for dx in range(1, x_all):
+        p_copy(0, dx).wait_send()
+    for d in range(1, z_all):
+        q_copy(d).wait_send()
+    for dz, dx in others:
+        r_copy(dz, dx).wait_send()
+        r_copy(dz, dx).wait_recv()
+
+    def sent(c, carry):
+        for d in range(1, z_all):
+            z_copy(d, c).wait_send()
+            for dx in range(1, x_all):
+                f_copy(d, dx, c).wait_send()
+        for d in range(1, x_all):
+            x_copy(d, c).wait_send()
+        return carry
+
+    lax.fori_loop(0, MOE_CHUNKS, sent, 0)
+
+
+def moe_layer(hidden, upstream_all, place, router_weight, gate_up_weight, down_weight, expert_group, capacity, name_id):
+    f32, bf16 = jnp.float32, jnp.bfloat16
+    length, width = hidden.shape
+    local_experts, _, twice = gate_up_weight.shape
+    half = twice // 2
+    experts_all = router_weight.shape[1]
+    x_all = expert_group // 4
+    count = x_all * capacity
+    dma = pltpu.SemaphoreType.DMA
+    x1 = max(x_all - 1, 1)
+    place_t = place.transpose(0, 1, 3, 2)
+    spare = (-local_experts) % 8
+    place = jnp.pad(place, ((0, 0), (0, 0), (0, spare), (0, 0)), constant_values=-1.0)
+    any_spec = pl.BlockSpec(memory_space=pl.ANY)
+    vmem_spec = pl.BlockSpec(memory_space=pltpu.VMEM)
+    out = pl.pallas_call(
+        functools.partial(moe_kernel, (x_all, capacity)),
+        out_shape=[
+            jax.ShapeDtypeStruct((local_experts, 4, count, width), bf16),
+            jax.ShapeDtypeStruct((local_experts, 4, count, half), bf16),
+            jax.ShapeDtypeStruct((local_experts, 4, count, width), bf16),
+            jax.ShapeDtypeStruct((local_experts, 4, count, twice), bf16),
+            jax.ShapeDtypeStruct((length, width), f32),
+            jax.ShapeDtypeStruct((expert_group, 8, length), f32),
+            jax.ShapeDtypeStruct((4, x_all, length, width), bf16),
+            jax.ShapeDtypeStruct((4, x1, length, width), bf16),
+        ]
+        + [jax.ShapeDtypeStruct((4, length, width), bf16)] * x_all,
+        in_specs=[any_spec, any_spec, vmem_spec, vmem_spec, vmem_spec, vmem_spec, any_spec, any_spec],
+        out_specs=[any_spec] * 4 + [vmem_spec, vmem_spec] + [any_spec] * (2 + x_all),
+        scratch_shapes=[
+            pltpu.VMEM(gate_up_weight.shape, bf16),
+            pltpu.VMEM(down_weight.shape, bf16),
+            pltpu.VMEM((x_all, length, width), bf16),
+            pltpu.VMEM((x_all, length, width), bf16),
+            pltpu.VMEM((x_all, length, experts_all), f32),
+            pltpu.VMEM((x_all, experts_all, length), f32),
+            pltpu.VMEM((count, width), bf16),
+            pltpu.VMEM((count, twice), f32),
+            pltpu.VMEM((count, half), bf16),
+            pltpu.VMEM((local_experts, count, width), bf16),
+            pltpu.VMEM((count, width), bf16),
+            pltpu.VMEM((count, twice), bf16),
+            pltpu.VMEM((local_experts, count, width), bf16),
+            pltpu.VMEM((min(2, x_all), length, width), bf16),
+            pltpu.VMEM((x1, length, width), bf16),
+            pltpu.VMEM((4, length, width), bf16),
+            pltpu.VMEM((3, length, width), bf16),
+            pltpu.VMEM((4, x_all, 8, length), f32),
+            dma((2,)), dma, dma((2, x_all)), dma((4,)),
+            dma((3, MOE_CHUNKS)), dma((3, MOE_CHUNKS)),
+            dma((x1, MOE_CHUNKS)), dma((x1, MOE_CHUNKS)),
+            dma((3, x1, MOE_CHUNKS)), dma((3, x1, MOE_CHUNKS)),
+            dma((x1,)), dma((4, x1)),
+            dma((3,)), dma((3,)),
+            dma((4, x_all)), dma((4, x_all)),
+            dma, dma((min(2, x_all),)),
+        ],
+        compiler_params=pltpu.CompilerParams(
+            collective_id=name_id, has_side_effects=True, vmem_limit_bytes=62 * 1024 * 1024
+        ),
+        cost_estimate=pl.CostEstimate(
+            flops=12 * 4 * local_experts * count * width * twice, bytes_accessed=64 * 1024 * 1024,
+            transcendentals=0,
+        ),
+    )(
+        hidden, upstream_all, place, place_t, router_weight, router_weight.T, gate_up_weight, down_weight
+    )
+    return out[:6], out[8:]
+
+
 def body(
     tokens,
     cotangent,
@@ -389,11 +842,11 @@
     place_own = lax.dynamic_slice_in_dim(
         place_all, own_expert * local_experts, local_experts, axis=2
     )
-    place_own = place_own.transpose(0, 2, 1)
-    slots = jnp.arange(capacity, dtype=jnp.int32).astype(f32)
-    one_hot = place_own[:, :, None, :] == slots[None, None, :, None]
-    one_hot_low = one_hot.astype(bf16)
+    z_all = z_size(expert_group)
+    x_all = expert_group // z_all
+    place_own = place_own.transpose(0, 2, 1).reshape(z_all, x_all, local_experts, length)
     upstream_all = jnp.stack(gather_expert(cotangent, expert_group))
+    upstream_all = upstream_all.reshape(z_all, x_all, length, model_width)
 
     inputs = tokens.astype(f32)
     scaled_one, first_pull = jax.vjp(rms_scale, inputs, gain_one)
@@ -434,71 +887,26 @@
     middle = inputs + jnp.dot(attended_low, out_full, preferred_element_type=f32)
     scaled_two, second_pull = jax.vjp(rms_scale, middle, gain_two)
     hidden_two = scaled_two.astype(bf16)
-    hidden_all = jnp.stack(gather_expert(hidden_two, expert_group))
     router = softmax_rows(jnp.dot(hidden_two, router_full, preferred_element_type=f32))
-    router_all = softmax_rows(jnp.dot(hidden_all, router_full, preferred_element_type=f32))
-    prob_own = lax.dynamic_slice_in_dim(
-        router_all, own_expert * local_experts, local_experts, axis=2
-    ).transpose(0, 2, 1)
-
-    expert_rows = jnp.einsum(
-        "sect,std->escd", one_hot_low, hidden_all, preferred_element_type=f32
-    ).astype(bf16)
     row_count = expert_group * capacity
-    expert_rows = expert_rows.reshape(local_experts, row_count, model_width)
-    gate_up = jnp.einsum("erd,edf->erf", expert_rows, gate_up_weight, preferred_element_type=f32)
-    activated_full, swiglu_pull = jax.vjp(swiglu, gate_up)
-    activated = activated_full.astype(bf16)
-    expert_out = jnp.einsum(
-        "erf,efd->erd", activated, down_weight, preferred_element_type=f32
-    ).astype(bf16)
-    weighted = jnp.where(one_hot, prob_own[:, :, None, :], 0.0)
-    weighted_high = weighted.astype(bf16)
-    weighted_low = (weighted - weighted_high.astype(f32)).astype(bf16)
-    out_rows = expert_out.reshape(local_experts, expert_group, capacity, model_width)
-    mixture_parts = (
-        jnp.einsum("sect,escd->std", weighted_high, out_rows, preferred_element_type=f32)
-        + jnp.einsum("sect,escd->std", weighted_low, out_rows, preferred_element_type=f32)
-    ).astype(bf16)
-    mixture = reduce_expert([mixture_parts[i] for i in range(expert_group)], expert_group)
+    done, mixture_parts = moe_layer(
+        hidden_two,
+        upstream_all,
+        place_own,
+        router_full,
+        gate_up_weight,
+        down_weight,
+        expert_group,
+        capacity,
+        2,
+    )
+    expert_rows, activated, grad_expert, grad_gate_up_low = (
+        a.reshape(local_experts, row_count, a.shape[-1]) for a in done[:4]
+    )
+    grad_rows_sum = done[4]
+    grad_router = done[5][:, :local_experts].reshape(experts_all, length).T
+    mixture = reduce_expert(mixture_parts, expert_group)
     block_out = (middle + mixture).astype(bf16)
-
-    prob_rows = jnp.sum(weighted, axis=3).transpose(1, 0, 2).reshape(local_experts, row_count)
-    upstream_rows = jnp.einsum(
-        "sect,std->escd", one_hot_low, upstream_all, preferred_element_type=f32
-    ).reshape(local_experts, row_count, model_width)
-    grad_expert = (prob_rows[:, :, None] * upstream_rows).astype(bf16)
-    grad_prob_rows = jnp.sum(upstream_rows * expert_out.astype(f32), axis=-1).reshape(
-        local_experts, expert_group, capacity
-    )
-    grad_router_parts = jnp.sum(
-        jnp.where(one_hot, grad_prob_rows.transpose(1, 0, 2)[:, :, :, None], 0.0), axis=2
-    )
-    z_all = z_size(expert_group)
-    x_all = expert_group // z_all
-    back = jnp.stack(
-        [
-            part if i == 0 else shift(part, expert_group, -(i // x_all), -(i % x_all))
-            for i, part in enumerate(grad_router_parts)
-        ]
-    )
-    owners = jnp.arange(expert_group, dtype=jnp.int32)
-    entry = ((owners // x_all - own_expert // x_all) % z_all) * x_all + (
-        owners % x_all - own_expert % x_all
-    ) % x_all
-    grad_router = back[entry].reshape(experts_all, length).T
-    grad_activated = jnp.einsum("erd,efd->erf", grad_expert, down_weight, preferred_element_type=f32)
-    grad_gate_up_low = swiglu_pull(grad_activated)[0].astype(bf16)
-    grad_row = jnp.einsum(
-        "erf,edf->erd", grad_gate_up_low, gate_up_weight, preferred_element_type=f32
-    ).astype(bf16)
-    grad_hidden_parts = jnp.einsum(
-        "sect,escd->std",
-        one_hot_low,
-        grad_row.reshape(local_experts, expert_group, capacity, model_width),
-        preferred_element_type=f32,
-    ).astype(bf16)
-    grad_rows_sum = reduce_expert([grad_hidden_parts[i] for i in range(expert_group)], expert_group)
     grad_down_full = jnp.einsum("erf,erd->efd", activated, grad_expert, preferred_element_type=f32)
     grad_gate_up_full = jnp.einsum(
         "erd,erf->edf", expert_rows, grad_gate_up_low, preferred_element_type=f32

time: 1310 us -> 1110 us (0.85)
  Pallas kernels: 266 us -> 539 us
  waiting for transfers between devices: 401 us -> 166 us
  matrix products: 252 us -> 104 us
  starting transfers between devices: 88.4 us -> 23.3 us
  other arithmetic: 81.3 us -> 62.3 us
    pallas_call x0 -> x1, Pallas kernels: none -> 265 us  [moe_layer(): pl.pallas_call(functools.partial(moe_kernel, (x_all, capacity)), out_shap...]
    ppermute x35 -> x11, waiting for transfers between devices: 348 us -> 121 us  [shift(): return lax.ppermute(values, 'expert', pairs)]
    dot_general x10 -> x0, matrix products: 145 us -> none  [the longest x1 25.5 us: body(): jnp.einsum('erf,edf->erd', grad_gate_up_low, gate_up_weight, preferred_el...]
    ppermute x35 -> x11, starting transfers between devices: 81.6 us -> 16.7 us  [shift(): return lax.ppermute(values, 'expert', pairs)]
    convert_element_type x5 -> x1, other arithmetic: 20.6 us -> 0.34 us  [body(): hidden_two = scaled_two.astype(bf16)]
    pallas_call x0 -> x3, local copies, waits for them, and re-layouts: none -> 15.7 us  [moe_layer(): pl.pallas_call(functools.partial(moe_kernel, (x_all, capacity)), out_shap...]
    unnamed x185 -> x142, local copies, waits for them, and re-layouts: 36.9 us -> 29.6 us
  transfers between devices with their start and end apart: 50 -> 26, of which waited for: 18 -> 7; matrix products, arithmetic and copies ran while one was open for 20% -> 19% of each run, Pallas kernels for 20% -> 25%
where the time goes in v3:
time: 1110 us; the launch traced here: 1100 us
  Pallas kernels  539 us (49%)
  waiting for transfers between devices  166 us (15%)
  blocking collectives  117 us (11%)
  matrix products  104 us (9%)
  local copies, waits for them, and re-layouts  72.3 us (7%)
  other arithmetic  62.3 us (6%)
  starting transfers between devices  23.3 us (2%)
  between operations  15.6 us (1%)
    pallas_call x1, Pallas kernels, summed_rows(): pl.pallas_call(functools.partial(tail_kernel, (steps, width, x_all, z_all...  274 us
    pallas_call x1, Pallas kernels, moe_layer(): pl.pallas_call(functools.partial(moe_kernel, (x_all, capacity)), out_shap...  265 us
    ppermute x11, waiting for transfers between devices, shift(): return lax.ppermute(values, 'expert', pairs)  121 us
    all_gather x1, blocking collectives, body(): place_all = lax.all_gather(place, 'expert', axis=0, tiled=False)[sources]  107 us
    reduce_scatter x1, waiting for transfers between devices, body(): lax.psum_scatter(grad_gate_up_full.astype(bf16), 'shard', scatter_dimensi...  31.3 us
    unnamed x142, local copies, waits for them, and re-layouts  29.6 us
    dot_general x1, matrix products, body(): jnp.einsum('erd,erf->edf', expert_rows, grad_gate_up_low, preferred_eleme...  25.7 us
  transfers between devices with their start and end apart: 26, of which 7 were waited for; matrix products, arithmetic and copies ran while one was open for 19% of the time, Pallas kernels for 25%

profile of v3, /device:TPU:0, one launch (start us, length us, event | category | flops | bytes accessed | tf_op | source)
XLA Modules:
  0.0 1099.6 jit_solution(4810298568290600863)
XLA Ops:
  9.1 3.0 collective-permute-start.1
  13.7 2.6 collective-permute-start.3
  18.5 106.7 %all-gather = f32[2048,16]{0,1:T(8,128)S(1)} all-gather(f32[256,16]{0,1:T(8,128)S(1)} %and_select_fusion), channel_id=2, replica_groups=mesh['expert'=8,'shard'=4] {'expert'}, dimensions={0}, use_global_device_ids=true | all-gather | bytes 147456 | tf_op jit(solution)/shard_map/all_gather | solution.py:841
  125.8 5.2 all_gather.18
  139.3 5.6 all_gather.23
  148.5 2.3 bitcast_dynamic-update-slice_fusion.6
  150.8 2.3 bitcast_dynamic-update-slice_fusion.5
  153.2 8.0 collective-permute-done.2
  161.2 2.3 bitcast_dynamic-update-slice_fusion.4
  163.5 2.3 bitcast_dynamic-update-slice_fusion.3
  165.8 17.8 %collective-permute-done.4 = bf16[256,2048]{1,0:T(8,128)(2,1)S(1)} collective-permute-done((bf16[256,2048]{1,0:T(8,128)(2,1)}, bf16[256,2048]{1,0:T(8,128)(2,1)S(1)}, u32[]{:S(2)}, u32[]{:S(2)}) %collective-permute-start.4) | collective-permute-done | bytes 1048608 | tf_op jit(solution)/shard_map/ppermute | solution.py:71
  186.9 18.5 %collective-permute-done.6 = bf16[256,2048]{1,0:T(8,128)(2,1)S(1)} collective-permute-done((bf16[256,2048]{1,0:T(8,128)(2,1)}, bf16[256,2048]{1,0:T(8,128)(2,1)S(1)}, u32[]{:S(2)}, u32[]{:S(2)}) %collective-permute-start.6) | collective-permute-done | bytes 1048608 | tf_op jit(solution)/shard_map/ppermute | solution.py:71
  206.5 12.2 %fusion.89 = f32[256,6144]{1,0:T(8,128)S(1)} fusion(bf16[256,2048]{0,1:T(8,128)(2,1)S(1)} %fusion.15, bf16[2048,6144]{1,0:T(8,128)(2,1)} %all-gather.4.cloned.1.call-done), kind=kOutput, calls=%fused_computation.191 | convolution fusion | flops 6442450944 | bytes 32505856 | tf_op jit(solution)/shard_map/dot_general | solution.py:855
  221.4 2.4 multiply_multiply_fusion
  225.8 2.9 copy.150
  231.2 2.3 fusion.31
  233.6 5.1 fusion.87
  238.6 3.4 convolution_convert_fusion.4
  242.1 7.1 multiply_reduce_fusion.7
  253.0 264.9 %shard_map.221 = (bf16[2,4,256,2048]{3,2,1,0:T(8,128)(2,1)}, bf16[2,4,256,1024]{3,2,1,0:T(8,128)(2,1)}, bf16[2,4,256,2048]{3,2,1,0:T(8,128)(2,1)}, bf16[2,4,256,...) custom-call(bf16[256,2048]{1,0:T(8,128)(2,1)} %copy.113.hidden_hbm, ...), custom_call_target="tpu_custom_call" | custom-call | flops 103079215104 | bytes 67108864 | tf_op jit(solution)/shard_map/pallas_call | solution.py:739
  518.9 3.0 copy.119
  521.9 2.7 multiply_reduce_fusion.1
  527.8 6.1 convolution_convert_fusion.2
  534.7 3.7 multiply_reduce_fusion
  547.6 2.8 fusion.35
  552.4 2.9 copy.148
  555.3 3.9 multiply_reduce_fusion.2
  561.6 3.8 fusion.18
  566.3 12.8 %fusion.16 = (f32[2048]{0:T(1024)S(1)}, f32[256]{0:T(256)S(1)}, f32[256,2048]{0,1:T(8,128)}) fusion(bf16[256,2048]{0,1:T(8,128)(2,1)S(1)} %copy.99, f32[256]{0:T(256)S(1)} %copy-done.51, f32[2048]{0:T(1024)S(1)} %bitcast.171, bf16[2048,6144]{1,0:T(8,128)(2,1)} %all-gather.4.cloned.1.call-done, bf16[256,2048]{1,0:T(8,128)(2,1)S(1)} %copy-done.20, ...), kind=kOutput, calls=%fused_computation.34 | convolution fusion | flops 6455556096 | bytes 31475712 | tf_op jit(solution)/shard_map/te,de->td/dot_general | solution.py:959
  581.2 5.8 fusion.10
  587.0 15.3 %convolution_convert_fusion.1 = bf16[2,1024,2048]{2,1,0:T(8,128)(2,1)} fusion(bf16[2,1024,1024]{2,1,0:T(8,128)(2,1)} %bitcast.185, bf16[2,1024,2048]{2,1,0:T(8,128)(2,1)} %bitcast.184), kind=kOutput, calls=%fused_computation.4 | convolution fusion | flops 8594128896 | bytes 20971520 | tf_op jit(solution)/shard_map/erf,erd->efd/dot_general | solution.py:910
  602.4 25.7 %convolution_convert_fusion = bf16[2,2048,2048]{2,1,0:T(8,128)(2,1)} fusion(bf16[2,1024,2048]{2,1,0:T(8,128)(2,1)} %bitcast.182, bf16[2,1024,2048]{2,1,0:T(8,128)(2,1)} %bitcast.183), kind=kOutput, calls=%fused_computation.2 | convolution fusion | flops 17188257792 | bytes 33554432 | tf_op jit(solution)/shard_map/erd,erf->edf/dot_general | solution.py:911
  628.2 6.3 copy.117
  637.1 7.6 collective-permute-done.12
  644.7 4.1 collective-permute-done.13
  650.0 6.3 copy.116
  656.3 3.0 pad_maximum_fusion.grads_ref
  659.3 76.8 %collective-permute-done.7 = bf16[4,256,2048]{1,2,0:T(8,128)(2,1)} collective-permute-done((bf16[4,256,2048]{1,2,0:T(8,128)(2,1)}, bf16[4,256,2048]{1,2,0:T(8,128)(2,1)}, u32[]{:S(2)}, u32[]{:S(2)}) %collective-permute-start.7) | collective-permute-done | bytes 4194336 | tf_op jit(solution)/shard_map/ppermute | solution.py:71
  736.1 6.6 fusion.80
  744.5 2.8 collective-permute-start.10
  749.9 273.9 %shard_map.222 = bf16[512,6144]{1,0:T(8,128)(2,1)} custom-call(bf16[256,6144]{1,0:T(8,128)(2,1)} %pad_maximum_fusion.grads_ref, bf16[512,1024]{1,0:T(8,128)(2,1)} %maximum_bitcast_fusion.columns_ref), custom_call_target="tpu_custom_call" | custom-call | flops 6442450944 | bytes 16777216 | tf_op jit(solution)/shard_map/pallas_call | solution.py:308
  1023.8 9.3 convert_element_type.128
  1036.1 4.3 convert_element_type.130
  1040.5 5.1 fusion.20
  1045.6 3.1 copy.135
  1050.2 4.2 convert_element_type.134
  1054.4 31.3 %reduce-scatter.3.cloned.1.call-done = bf16[2,512,2048]{2,1,0:T(8,128)(2,1)} async-done(((bf16[2,2048,2048]{2,1,0:T(8,128)(2,1)}), bf16[2,512,2048]{2,1,0:T(8,128)(2,1)}) %reduce-scatter.3.cloned.1.call-update) | async-done | bytes 4194320 | tf_op jit(solution)/shard_map/reduce_scatter | solution.py:914
  1085.7 6.7 convert_element_type.132
  (246 shorter events, 67.0 us)
Async XLA Ops:
  7.2 199.3 %all-gather.4.cloned.1.call-start = ((), (), s32[]{:S(2)}) async-start(), calls=%async_computation.2 | async-start | bytes 31457280 | tf_op jit(solution)/shard_map/all_gather | solution.py:824
  7.9 9.7 copy-start.28
  7.9 10.2 copy-start.60
  7.9 10.2 copy-start.61
  8.0 10.2 copy-start.62
  8.0 10.2 copy-start.63
  8.0 10.3 copy-start.58
  8.0 10.3 copy-start.64
  8.0 234.1 %all-gather.6.cloned.1.call-start = ((), (), s32[]{:S(2)}) async-start(), calls=%async_computation.3 | async-start | bytes 10485760 | tf_op jit(solution)/shard_map/all_gather | solution.py:824
  8.7 1024.4 %all-reduce.8.cloned.1.call-start = ((), (), s32[]{:S(2)}) async-start(), calls=%async_computation.4 | async-start | bytes 393216 | tf_op jit(solution)/shard_map/psum | solution.py:983
  9.1 125.7 %collective-permute-start.1 = (bf16[256,2048]{1,0:T(8,128)(2,1)S(1)}, bf16[256,2048]{1,0:T(8,128)(2,1)}, u32[]{:S(2)}, u32[]{:S(2)}) collective-permute-start(bf16[256,2048]{1,0:T(8,128)(2,1)S(1)} %copy-done.15), channel_id=1, source_target_pairs={{0,8},{4,12},{8,16},{12,20},{16,24},{20,28},{24,0},{28,4},{1,9},{5... | collective-permute-start | bytes 3145736 | tf_op jit(solution)/shard_map/ppermute | solution.py:71
  12.2 136.3 %collective-permute-start = (bf16[256,2048]{1,0:T(8,128)(2,1)S(1)}, bf16[256,2048]{1,0:T(8,128)(2,1)}, u32[]{:S(2)}, u32[]{:S(2)}) collective-permute-start(bf16[256,2048]{1,0:T(8,128)(2,1)S(1)} %copy-done.15), channel_id=1, source_target_pairs={{0,4},{4,0},{8,12},{12,8},{16,20},{20,16},{24,28},{28,24},{1,5},{5... | collective-permute-start | bytes 3145736 | tf_op jit(solution)/shard_map/ppermute | solution.py:71
  13.7 132.8 %collective-permute-start.3 = (bf16[256,2048]{1,0:T(8,128)(2,1)S(1)}, bf16[256,2048]{1,0:T(8,128)(2,1)}, u32[]{:S(2)}, u32[]{:S(2)}) collective-permute-start(bf16[256,2048]{1,0:T(8,128)(2,1)S(1)} %copy-done.15), channel_id=1, source_target_pairs={{0,16},{4,20},{8,24},{12,28},{16,0},{20,4},{24,8},{28,12},{1,17},{... | collective-permute-start | bytes 3145736 | tf_op jit(solution)/shard_map/ppermute | solution.py:71
  16.2 136.9 %collective-permute-start.5 = (bf16[256,2048]{1,0:T(8,128)(2,1)S(1)}, bf16[256,2048]{1,0:T(8,128)(2,1)}, u32[]{:S(2)}, u32[]{:S(2)}) collective-permute-start(bf16[256,2048]{1,0:T(8,128)(2,1)S(1)} %copy-done.15), channel_id=1, source_target_pairs={{0,24},{4,28},{8,0},{12,4},{16,8},{20,12},{24,16},{28,20},{1,25},{... | collective-permute-start | bytes 3145736 | tf_op jit(solution)/shard_map/ppermute | solution.py:71
  18.1 113.3 %copy-start.59 = (s32[1,256]{1,0:T(1,128)S(1)}, s32[1,256]{1,0:T(1,128)}, u32[]{:S(2)}) copy-start(s32[1,256]{1,0:T(1,128)} %param.16) | copy-start | bytes 3076
  134.4 86.9 %copy-start.34 = (f32[1,2048]{1,0:T(1,128)}, f32[1,2048]{1,0:T(1,128)S(1)}, u32[]{:S(2)}) copy-start(f32[1,2048]{1,0:T(1,128)S(1)} %get-tuple-element.114) | copy-start | bytes 24580
  134.5 86.9 %copy-start.36 = (f32[1,2048]{1,0:T(1,128)}, f32[1,2048]{1,0:T(1,128)S(1)}, u32[]{:S(2)}) copy-start(f32[1,2048]{1,0:T(1,128)S(1)} %get-tuple-element.115) | copy-start | bytes 24580
  134.5 390.2 %copy-start.32 = (f32[1,2048]{1,0:T(1,128)}, f32[1,2048]{1,0:T(1,128)S(1)}, u32[]{:S(2)}) copy-start(f32[1,2048]{1,0:T(1,128)S(1)} %get-tuple-element.113) | copy-start | bytes 24580
  134.8 71.6 %copy-start.10 = (bf16[256,2048]{0,1:T(8,128)(2,1)}, bf16[256,2048]{0,1:T(8,128)(2,1)S(1)}, u32[]{:S(2)}) copy-start(bf16[256,2048]{0,1:T(8,128)(2,1)S(1)} %fusion.15) | copy-start | bytes 3145732
  134.9 26.4 %collective-permute-start.2 = (bf16[256,2048]{1,0:T(8,128)(2,1)}, bf16[256,2048]{1,0:T(8,128)(2,1)}, u32[]{:S(2)}, u32[]{:S(2)}) collective-permute-start(bf16[256,2048]{1,0:T(8,128)(2,1)} %collective-permute-done.1), channel_id=1, source_target_pairs={{0,4},{4,0},{8,12},{12,8},{16,20},{20,16},{24,28},{28,24},{1,5},{5... | collective-permute-start | bytes 3145736 | tf_op jit(solution)/shard_map/ppermute | solution.py:71
  144.8 107.8 %copy-start.24 = (bf16[2048,16]{0,1:T(8,128)(2,1)}, bf16[2048,16]{0,1:T(8,128)(2,1)S(1)}, u32[]{:S(2)}) copy-start(bf16[2048,16]{0,1:T(8,128)(2,1)S(1)} %all_gather.23) | copy-start | bytes 196612
  146.5 37.1 %collective-permute-start.4 = (bf16[256,2048]{1,0:T(8,128)(2,1)}, bf16[256,2048]{1,0:T(8,128)(2,1)S(1)}, u32[]{:S(2)}, u32[]{:S(2)}) collective-permute-start(bf16[256,2048]{1,0:T(8,128)(2,1)} %collective-permute-done.3), channel_id=1, source_target_pairs={{0,4},{4,0},{8,12},{12,8},{16,20},{20,16},{24,28},{28,24},{1,5},{5... | collective-permute-start | bytes 3145736 | tf_op jit(solution)/shard_map/ppermute | solution.py:71
  153.1 52.4 %collective-permute-start.6 = (bf16[256,2048]{1,0:T(8,128)(2,1)}, bf16[256,2048]{1,0:T(8,128)(2,1)S(1)}, u32[]{:S(2)}, u32[]{:S(2)}) collective-permute-start(bf16[256,2048]{1,0:T(8,128)(2,1)} %collective-permute-done.5), channel_id=1, source_target_pairs={{0,4},{4,0},{8,12},{12,8},{16,20},{20,16},{24,28},{28,24},{1,5},{5... | collective-permute-start | bytes 3145736 | tf_op jit(solution)/shard_map/ppermute | solution.py:71
  242.0 7.2 copy-start.26
  249.2 275.5 %copy-start.41 = (f32[256]{0:T(256)}, f32[256]{0:T(256)S(1)}, u32[]{:S(2)}) copy-start(f32[256]{0:T(256)S(1)} %fusion.69) | copy-start | bytes 3076
  526.4 39.1 %collective-permute-start.18 = (bf16[256,2048]{0,1:T(8,128)(2,1)}, bf16[256,2048]{0,1:T(8,128)(2,1)}, u32[]{:S(2)}, u32[]{:S(2)}) collective-permute-start(bf16[256,2048]{0,1:T(8,128)(2,1)} %fusion.81), channel_id=1, source_target_pairs={{0,2},{1,3},{2,0},{3,1},{4,6},{5,7},{6,4},{7,5},{8,10},{9,11},{10,... | collective-permute-start | bytes 3145736 | tf_op jit(solution)/shard_map/ppermute | solution.py:109
  527.8 53.3 %collective-permute-start.17 = (bf16[256,2048]{0,1:T(8,128)(2,1)}, bf16[256,2048]{0,1:T(8,128)(2,1)}, u32[]{:S(2)}, u32[]{:S(2)}) collective-permute-start(bf16[256,2048]{0,1:T(8,128)(2,1)} %fusion.81), channel_id=1, source_target_pairs={{0,1},{1,0},{2,3},{3,2},{4,5},{5,4},{6,7},{7,6},{8,9},{9,8},{10,11... | collective-permute-start | bytes 3145736 | tf_op jit(solution)/shard_map/ppermute | solution.py:109
  541.4 39.7 %collective-permute-start.14 = (bf16[256,512]{0,1:T(8,128)(2,1)}, bf16[256,512]{0,1:T(8,128)(2,1)}, u32[]{:S(2)}, u32[]{:S(2)}) collective-permute-start(bf16[256,512]{0,1:T(8,128)(2,1)} %get-tuple-element.94), channel_id=1, source_target_pairs={{0,1},{1,0},{2,3},{3,2},{4,5},{5,4},{6,7},{7,6},{8,9},{9,8},{10,11... | collective-permute-start | bytes 786440 | tf_op jit(solution)/shard_map/ppermute | solution.py:109
  542.0 39.2 %collective-permute-start.15 = (bf16[256,512]{0,1:T(8,128)(2,1)}, bf16[256,512]{0,1:T(8,128)(2,1)}, u32[]{:S(2)}, u32[]{:S(2)}) collective-permute-start(bf16[256,512]{0,1:T(8,128)(2,1)} %get-tuple-element.93), channel_id=1, source_target_pairs={{0,2},{1,3},{2,0},{3,1},{4,6},{5,7},{6,4},{7,5},{8,10},{9,11},{10,... | collective-permute-start | bytes 786440 | tf_op jit(solution)/shard_map/ppermute | solution.py:109
  542.5 38.6 %collective-permute-start.16 = (bf16[256,512]{0,1:T(8,128)(2,1)}, bf16[256,512]{0,1:T(8,128)(2,1)}, u32[]{:S(2)}, u32[]{:S(2)}) collective-permute-start(bf16[256,512]{0,1:T(8,128)(2,1)} %get-tuple-element.92), channel_id=1, source_target_pairs={{0,3},{1,2},{2,1},{3,0},{4,7},{5,6},{6,5},{7,4},{8,11},{9,10},{10,... | collective-permute-start | bytes 786440 | tf_op jit(solution)/shard_map/ppermute | solution.py:109
  565.4 13.7 %copy-start.16 = (bf16[256,2048]{1,0:T(8,128)(2,1)}, bf16[256,2048]{1,0:T(8,128)(2,1)S(1)}, u32[]{:S(2)}) copy-start(bf16[256,2048]{1,0:T(8,128)(2,1)S(1)} %get-tuple-element.74) | copy-start | bytes 3145732
  565.4 13.7 %copy-start.18 = (bf16[256,2048]{1,0:T(8,128)(2,1)}, bf16[256,2048]{1,0:T(8,128)(2,1)S(1)}, u32[]{:S(2)}) copy-start(bf16[256,2048]{1,0:T(8,128)(2,1)S(1)} %get-tuple-element.75) | copy-start | bytes 3145732
  565.4 15.7 %collective-permute-start.19 = (bf16[256,2048]{0,1:T(8,128)(2,1)}, bf16[256,2048]{0,1:T(8,128)(2,1)S(1)}, u32[]{:S(2)}, u32[]{:S(2)}) collective-permute-start(bf16[256,2048]{0,1:T(8,128)(2,1)} %collective-permute-done.18), channel_id=1, source_target_pairs={{0,1},{1,0},{2,3},{3,2},{4,5},{5,4},{6,7},{7,6},{8,9},{9,8},{10,11... | collective-permute-start | bytes 3145736 | tf_op jit(solution)/shard_map/ppermute | solution.py:109
  566.3 12.8 %copy-start.9 = (bf16[256,2048]{0,1:T(8,128)(2,1)S(1)}, bf16[256,2048]{0,1:T(8,128)(2,1)}, u32[]{:S(2)}) copy-start(bf16[256,2048]{0,1:T(8,128)(2,1)} %copy-done.8) | copy-start | bytes 3145732
  580.8 455.2 %all-reduce.10.cloned.1.call-start = ((), (), s32[]{:S(2)}) async-start(), calls=%async_computation.5 | async-start | bytes 4194304 | tf_op jit(solution)/shard_map/psum | solution.py:969
  587.0 463.2 %reduce-scatter.5.cloned.1.call-start = ((), (), s32[]{:S(2)}) async-start(), calls=%async_computation.7 | async-start | bytes 10485760 | tf_op jit(solution)/shard_map/reduce_scatter | solution.py:917
  602.3 483.3 %reduce-scatter.3.cloned.1.call-start = ((), (), s32[]{:S(2)}) async-start(), calls=%async_computation.6 | async-start | bytes 20971520 | tf_op jit(solution)/shard_map/reduce_scatter | solution.py:914
  628.1 7.0 copy-start.11
  634.4 101.7 %collective-permute-start.7 = (bf16[4,256,2048]{1,2,0:T(8,128)(2,1)}, bf16[4,256,2048]{1,2,0:T(8,128)(2,1)}, u32[]{:S(2)}, u32[]{:S(2)}) collective-permute-start(bf16[4,256,2048]{1,2,0:T(8,128)(2,1)} %copy.117), channel_id=1, source_target_pairs={{0,4},{4,0},{8,12},{12,8},{16,20},{20,16},{24,28},{28,24},{1,5},{5... | collective-permute-start | bytes 12582920 | tf_op jit(solution)/shard_map/ppermute | solution.py:71
  635.2 1.9 collective-permute-start.11
  635.6 9.1 collective-permute-start.12
  636.0 12.9 %collective-permute-start.13 = (bf16[256,512]{0,1:T(8,128)(2,1)S(1)}, bf16[256,512]{0,1:T(8,128)(2,1)S(1)}, u32[]{:S(2)}, u32[]{:S(2)}) collective-permute-start(bf16[256,512]{0,1:T(8,128)(2,1)S(1)} %get-tuple-element.96), channel_id=1, source_target_pairs={{0,3},{1,2},{2,1},{3,0},{4,7},{5,6},{6,5},{7,4},{8,11},{9,10},{10,... | collective-permute-start | bytes 786440 | tf_op jit(solution)/shard_map/ppermute | solution.py:109
  650.0 6.3 copy-start.19
  656.3 79.8 %copy-start.7 = (bf16[4,256,2048]{1,2,0:T(8,128)(2,1)S(1)}, bf16[4,256,2048]{1,2,0:T(8,128)(2,1)}, u32[]{:S(2)}) copy-start(bf16[4,256,2048]{1,2,0:T(8,128)(2,1)} %copy.116) | copy-start | bytes 12582916
  744.5 295.9 %collective-permute-start.10 = (bf16[256,2048]{0,1:T(8,128)(2,1)}, bf16[256,2048]{0,1:T(8,128)(2,1)}, u32[]{:S(2)}, u32[]{:S(2)}) collective-permute-start(bf16[256,2048]{0,1:T(8,128)(2,1)} %get-tuple-element.79), channel_id=1, source_target_pairs={{0,8},{4,12},{8,16},{12,20},{16,24},{20,28},{24,0},{28,4},{1,9},{5... | collective-permute-start | bytes 3145736 | tf_op jit(solution)/shard_map/ppermute | solution.py:71
  747.2 293.2 %collective-permute-start.8 = (bf16[256,2048]{0,1:T(8,128)(2,1)}, bf16[256,2048]{0,1:T(8,128)(2,1)}, u32[]{:S(2)}, u32[]{:S(2)}) collective-permute-start(bf16[256,2048]{0,1:T(8,128)(2,1)} %get-tuple-element.78), channel_id=1, source_target_pairs={{0,24},{4,28},{8,0},{12,4},{16,8},{20,12},{24,16},{28,20},{1,25},{... | collective-permute-start | bytes 3145736 | tf_op jit(solution)/shard_map/ppermute | solution.py:71
  749.2 291.2 %collective-permute-start.9 = (bf16[256,2048]{0,1:T(8,128)(2,1)}, bf16[256,2048]{0,1:T(8,128)(2,1)}, u32[]{:S(2)}, u32[]{:S(2)}) collective-permute-start(bf16[256,2048]{0,1:T(8,128)(2,1)} %get-tuple-element.80), channel_id=1, source_target_pairs={{0,16},{4,20},{8,24},{12,28},{16,0},{20,4},{24,8},{28,12},{1,17},{... | collective-permute-start | bytes 3145736 | tf_op jit(solution)/shard_map/ppermute | solution.py:71
  1023.8 9.3 copy-start.53
  (43 other events, 127.9 us)
Sparse Core Ops, SparseCore 0:
  9.6 157.9 all-gather.3
  169.1 58.2 all-gather.5
  581.0 123.7 all-reduce.7
  708.3 171.6 all-reduce.9
  882.4 74.3 reduce-scatter.4
  959.3 126.2 reduce-scatter.2

commit v4 on v3

--- a/solution.py
+++ b/solution.py
@@ -84,15 +84,17 @@
 
 def reduce_expert(parts, expert_group):
     z_all = z_size(expert_group)
-    rows = parts[0].astype(jnp.float32)
-    for dx in range(1, len(parts)):
-        rows = rows + shift(parts[dx], expert_group, 0, -dx).astype(jnp.float32)
-    total = rows[0]
-    for dz in range(1, z_all):
-        total = total + shift(
-            rows[dz].astype(jnp.bfloat16), expert_group, -dz, 0
-        ).astype(jnp.float32)
-    return total
+    x_all = expert_group // z_all
+    rows = {}
+    for dz in sorted(range(z_all), key=lambda d: -min(d, z_all - d)):
+        rows[dz] = parts[dz * x_all].astype(jnp.float32)
+        for dx in range(1, x_all):
+            rows[dz] = rows[dz] + shift(parts[dz * x_all + dx], expert_group, 0, -dx).astype(
+                jnp.float32
+            )
+        if dz:
+            rows[dz] = shift(rows[dz].astype(jnp.bfloat16), expert_group, -dz, 0).astype(jnp.float32)
+    return sum(rows[dz] for dz in range(z_all))
 
 
 def relative_sources(expert_group):
@@ -107,14 +109,6 @@
     y_all = shard_group // 2
     pairs = [(i, ((i // 2 + dy) % y_all) * 2 + (i % 2 + flip) % 2) for i in range(shard_group)]
     return lax.ppermute(values, "shard", pairs)
-
-
-def gather_shard(block, shard_group):
-    found = []
-    for dy in range(shard_group // 2):
-        straight = block if dy == 0 else shard_shift(block, shard_group, dy, 0)
-        found += [straight, shard_shift(straight, shard_group, 0, 1)]
-    return found
 
 
 def own_columns(values, shard_group):
@@ -130,12 +124,16 @@
     return jnp.concatenate(found, axis=0)
 
 
-def tail_kernel(dims, grads_ref, columns_ref, out_ref, gall, xsend, xrecv, zsend, zrecv, acc, fin, *sems):
-    steps, width, x_all, z_all, y_all, lag = dims
-    (y_s, y_r, core_s, core_r, fwd_s, fwd_r, x_s, x_r, z_s, z_r, zb_s, zb_r, xb_s, xb_r) = sems
+def tail_kernel(
+    dims, grads_ref, columns_ref, small_ref, out_ref, small_out_ref,
+    gall, xsend, xrecv, zsend, zrecv, acc, fin, group_small, own_small, all_small, *sems
+):
+    steps, width, x_all, z_all, y_all, lag, first_steps = dims
+    (gs_s, gs_r, es_s, es_r) = sems[14:]
+    (y_s, y_r, core_s, core_r, fwd_s, fwd_r, x_s, x_r, z_s, z_r, zb_s, zb_r, xb_s, xb_r) = sems[:14]
     f32, bf16 = jnp.float32, jnp.bfloat16
     length = grads_ref.shape[0]
-    rows = columns_ref.shape[0]
+    rows = columns_ref.shape[1]
     block = rows // (x_all * z_all)
     half = z_all * block
     e = lax.axis_index("expert")
@@ -186,16 +184,31 @@
         here = fin.at[c, pl.ds(pl.multiple_of(x * half, half), half)]
         return copy(here, here, xb_s.at[d - 1], xb_r.at[d - 1, c], x_peer(d))
 
+    near = [(d, flip) for d in range(y_all) for flip in range(2) if d + flip > 0]
+    far = [(dz, dx) for dz in range(z_all) for dx in range(x_all) if dz + dx > 0]
+
+    def near_peer(d, flip):
+        return {"shard": lax.rem(y + d, y_all) * 2 + lax.rem(core + flip, 2)}
+
+    def far_peer(dz, dx):
+        return {"expert": lax.rem(z + dz, z_all) * x_all + lax.rem(x + dx, x_all)}
+
+    def near_small(d, flip):
+        j = 2 * d + flip
+        return copy(small_ref.at[j], group_small.at[j - 1], gs_s.at[j - 1], gs_r.at[j - 1], near_peer(d, flip))
+
+    def far_small(dz, dx):
+        i = dz * x_all + dx
+        return copy(own_small, all_small.at[i - 1], es_s.at[i - 1], es_r.at[i - 1], far_peer(dz, dx))
+
     barrier = pltpu.get_barrier_semaphore()
-    peers = (
-        [y_peer(d) for d in range(1, y_all)]
-        + [partner]
-        + [x_peer(d) for d in range(1, x_all)]
-        + [z_peer(d) for d in range(1, z_all)]
-    )
+    peers = [near_peer(*p) for p in near] + [far_peer(*p) for p in far]
     for peer in peers:
         pl.semaphore_signal(barrier, inc=1, device_id=peer, device_id_type=pl.DeviceIdType.MESH)
     pl.semaphore_wait(barrier, len(peers))
+
+    for p in near:
+        near_small(*p).start()
 
     def first(c, carry):
         for d in range(1, y_all):
@@ -253,13 +266,14 @@
             core_copy(c).wait_recv()
             for d in range(1, y_all):
                 fwd_copy(d, c).wait_recv()
+            kind = (c >= first_steps).astype(jnp.int32)
             others = gall[:, c].reshape((2 * y_all - 1) * length, width)
             mine = grads_ref[:, cols(c)]
 
             def product(there):
                 at = pl.ds(pl.multiple_of(there * half, half), half)
-                return jnp.dot(columns_ref[at, :length], mine, preferred_element_type=f32) + jnp.dot(
-                    columns_ref[at, length:], others, preferred_element_type=f32
+                return jnp.dot(columns_ref[kind, at, :length], mine, preferred_element_type=f32) + jnp.dot(
+                    columns_ref[kind, at, length:], others, preferred_element_type=f32
                 )
 
             for d in range(1, x_all):
@@ -273,9 +287,28 @@
                 y_copy(d, c).wait_recv()
                 fwd_copy(d, c).start()
 
+        @pl.when(t == 2)
+        def _():
+            total = small_ref[0]
+            for j, p in enumerate(near):
+                near_small(*p).wait_recv()
+                total = total + group_small[j]
+            own_small[...] = total
+            for p in far:
+                far_small(*p).start()
+
         return carry
 
     lax.fori_loop(0, steps + 5 * lag, step, 0)
+    total = own_small[...]
+    for i, p in enumerate(far):
+        far_small(*p).wait_recv()
+        total = total + all_small[i]
+    small_out_ref[...] = total
+    for p in near:
+        near_small(*p).wait_send()
+    for p in far:
+        far_small(*p).wait_send()
 
     for d in range(1, y_all):
         copy(grads_ref, grads_ref, y_s.at[d - 1], y_r.at[d - 1, 0], y_peer(d)).wait_send()
@@ -292,10 +325,10 @@
         copy(whole, whole, zb_s.at[d - 1], zb_r.at[d - 1, 0], z_peer(d)).wait_send()
 
 
-def summed_rows(columns, grads, expert_group, shard_group, z_all, width, lag, name_id):
+def summed_rows(columns, grads, first_total, small, expert_group, shard_group, z_all, width, lag, name_id):
     x_all, y_all = expert_group // z_all, shard_group // 2
     length, total = grads.shape
-    rows = columns.shape[0]
+    rows = columns.shape[1]
     steps = total // width
     block = rows // expert_group
     half = z_all * block
@@ -306,10 +339,13 @@
     z1 = max(z_all - 1, 1)
     slots = min(steps, 2 * lag + 1)
     return pl.pallas_call(
-        functools.partial(tail_kernel, (steps, width, x_all, z_all, y_all, lag)),
-        out_shape=jax.ShapeDtypeStruct((rows, total), bf16),
-        in_specs=[pl.BlockSpec(memory_space=pltpu.VMEM)] * 2,
-        out_specs=pl.BlockSpec(memory_space=pltpu.VMEM),
+        functools.partial(tail_kernel, (steps, width, x_all, z_all, y_all, lag, first_total // width)),
+        out_shape=[
+            jax.ShapeDtypeStruct((rows, total), bf16),
+            jax.ShapeDtypeStruct(small.shape[1:], jnp.float32),
+        ],
+        in_specs=[pl.BlockSpec(memory_space=pltpu.VMEM)] * 3,
+        out_specs=[pl.BlockSpec(memory_space=pltpu.VMEM)] * 2,
         scratch_shapes=[
             pltpu.VMEM((shard_group - 1, steps, length, width), bf16),
             pltpu.VMEM((x1, steps, half, width), bf16),
@@ -318,6 +354,9 @@
             pltpu.VMEM((z1, steps, block, width), bf16),
             pltpu.VMEM((slots, half, width), jnp.float32),
             pltpu.VMEM((steps, rows, width), bf16),
+            pltpu.VMEM((shard_group - 1, *small.shape[1:]), jnp.float32),
+            pltpu.VMEM(small.shape[1:], jnp.float32),
+            pltpu.VMEM((expert_group - 1, *small.shape[1:]), jnp.float32),
             dma((n1,)), dma((n1, steps)),
             dma((1,)), dma((steps,)),
             dma((n1,)), dma((n1, steps)),
@@ -325,6 +364,8 @@
             dma((z1,)), dma((z1, steps)),
             dma((z1,)), dma((z1, steps)),
             dma((x1,)), dma((x1, steps)),
+            dma((shard_group - 1,)), dma((shard_group - 1,)),
+            dma((expert_group - 1,)), dma((expert_group - 1,)),
         ],
         compiler_params=pltpu.CompilerParams(
             collective_id=name_id, has_side_effects=True, vmem_limit_bytes=60 * 1024 * 1024
@@ -332,7 +373,7 @@
         cost_estimate=pl.CostEstimate(
             flops=2 * rows * length * shard_group * total, bytes_accessed=16 * 1024 * 1024, transcendentals=0
         ),
-    )(grads, columns)
+    )(grads, columns, small)
 
 
 MOE_CHUNKS = 4
@@ -344,12 +385,12 @@
     *rest,
 ):
     x_all, capacity = dims
-    mixture_hbm = rest[:x_all]
+    mixture_hbm = rest[: 4 * x_all]
     (
     gate_up_w, down_w, hid, ups, prob, prob_t, rows, gate_up, activated, out_rows, grad_expert, grad_gate_up, grad_rows,
     mix_stage, part_stage, own_part, z_landed, router_stage,
     w_sem, own_sem, load_sem, store_sem, zs, zr, xs, xr, fs, fr, ps, pr, qs, qr, rs, rr, lsem, mix_sem,
-    ) = rest[x_all:]
+    ) = rest[4 * x_all :]
     z_all = 4
     f32, bf16 = jnp.float32, jnp.bfloat16
     length, width = hidden_hbm.shape
@@ -443,6 +484,9 @@
 
         lax.fori_loop(first, first + 2, one, 0)
 
+    def own_slots(le):
+        return pl.ds(pl.multiple_of(le * capacity, capacity), capacity)
+
     def finish(g):
         dz = g // 2 + 2 * lax.rem(g, 2)
         for dx in range(1, x_all):
@@ -466,10 +510,10 @@
 
     def mix_copy(dz, dx):
         slot = dx % mix_slots
-        return pltpu.make_async_copy(mix_stage.at[slot], mixture_hbm[dx].at[dz], mix_sem.at[slot])
+        return pltpu.make_async_copy(mix_stage.at[slot], mixture_hbm[dz * x_all + dx], mix_sem.at[slot])
 
     slot_row = lax.broadcasted_iota(jnp.int32, (capacity, length), 0).astype(f32)
-    slot_col = lax.broadcasted_iota(jnp.int32, (length, capacity), 1).astype(f32)
+    slot_col = lax.broadcasted_iota(jnp.int32, (length, local_experts * capacity), 1).astype(f32)
     own.wait()
     events(0)
 
@@ -554,9 +598,10 @@
 
             def down_step(n, c0):
                 c = cols(n, tile)
-                out_rows[le, :, c] = jnp.dot(
-                    activated[...], down_w[le, :, c], preferred_element_type=f32
-                ).astype(bf16)
+                result = jnp.dot(activated[...], down_w[le, :, c], preferred_element_type=f32)
+                for dx in range(x_all):
+                    r = slice(dx * capacity, (dx + 1) * capacity)
+                    out_rows[dx, own_slots(le), c] = result[r].astype(bf16)
                 return c0
 
             lax.fori_loop(0, width // tile, down_step, 0)
@@ -576,7 +621,7 @@
                     grad_expert[r, c] = (weight_rows[dx] * up_rows).astype(bf16)
                     new.append(
                         totals[dx]
-                        + jnp.sum(up_rows * out_rows[le, r, c].astype(f32), axis=1, keepdims=True)
+                        + jnp.sum(up_rows * out_rows[dx, own_slots(le), c].astype(f32), axis=1, keepdims=True)
                     )
                 return tuple(new)
 
@@ -606,10 +651,13 @@
             store(3, grad_gate_up, grad_gate_up_hbm, le).start()
 
             def row_step(n, c0):
-                grad_rows[le, :, cols(n, narrow)] = lax.dot_general(
+                result = lax.dot_general(
                     grad_gate_up[...], gate_up_w[le, cols(n, narrow), :], (((1,), (1,)), ((), ())),
                     preferred_element_type=f32,
-                ).astype(bf16)
+                )
+                for dx in range(x_all):
+                    r = slice(dx * capacity, (dx + 1) * capacity)
+                    grad_rows[dx, own_slots(le), cols(n, narrow)] = result[r].astype(bf16)
                 return c0
 
             lax.fori_loop(0, width // narrow, row_step, 0)
@@ -625,17 +673,18 @@
 
         pl.when(g > 0)(stages)
         for dx in range(x_all):
-            r = slice(dx * capacity, (dx + 1) * capacity)
-            low, high, remainder = [], [], []
+            weight = jnp.zeros(slot_col.shape, f32)
+            mask = jnp.zeros(slot_col.shape, f32)
+            lane = lax.broadcasted_iota(jnp.int32, prob.shape[1:], 1)
             for le in range(local_experts):
-                mask = place_t_ref[dz, dx, :, le : le + 1] == slot_col
-                lane = lax.broadcasted_iota(jnp.int32, prob.shape[1:], 1)
+                spot = place_t_ref[dz, dx, :, le : le + 1]
+                here = jnp.where(spot < 0.0, -1.0, spot + le * capacity) == slot_col
                 p = jnp.sum(jnp.where(lane == e * local_experts + le, prob[dx], 0.0), axis=1, keepdims=True)
-                weight = jnp.where(mask, p, 0.0)
-                top = weight.astype(bf16)
-                low.append(mask.astype(f32).astype(bf16))
-                high.append(top)
-                remainder.append((weight - top.astype(f32)).astype(bf16))
+                weight = jnp.where(here, p, weight)
+                mask = jnp.where(here, 1.0, mask)
+            low = mask.astype(bf16)
+            high = weight.astype(bf16)
+            remainder = (weight - high.astype(f32)).astype(bf16)
 
             if dx < mix_slots:
                 pl.when(g > 0)(mix_copy(0, dx).wait)
@@ -644,12 +693,10 @@
 
             def combine(n, c0):
                 c = cols(n, tile)
-                mix = jnp.zeros((length, tile), f32)
-                grad = jnp.zeros((length, tile), f32)
-                for le in range(local_experts):
-                    mix = mix + jnp.dot(high[le], out_rows[le, r, c], preferred_element_type=f32)
-                    mix = mix + jnp.dot(remainder[le], out_rows[le, r, c], preferred_element_type=f32)
-                    grad = grad + jnp.dot(low[le], grad_rows[le, r, c], preferred_element_type=f32)
+                mix = jnp.dot(high, out_rows[dx, :, c], preferred_element_type=f32) + jnp.dot(
+                    remainder, out_rows[dx, :, c], preferred_element_type=f32
+                )
+                grad = jnp.dot(low, grad_rows[dx, :, c], preferred_element_type=f32)
                 mix_stage[dx % mix_slots, :, c] = mix.astype(bf16)
                 if dx == 0:
                     own_part[dz, :, c] = grad.astype(bf16)
@@ -658,7 +705,8 @@
                 return c0
 
             lax.fori_loop(0, width // tile, combine, 0)
-            mix_copy(dz, dx).start()
+            for k in range(z_all):
+                pl.when(dz == k)(mix_copy(k, dx).start)
             if dx > 0:
                 p_copy(dz, dx).start()
                 r_copy(dz, dx).start()
@@ -748,9 +796,9 @@
             jax.ShapeDtypeStruct((4, x_all, length, width), bf16),
             jax.ShapeDtypeStruct((4, x1, length, width), bf16),
         ]
-        + [jax.ShapeDtypeStruct((4, length, width), bf16)] * x_all,
+        + [jax.ShapeDtypeStruct((length, width), bf16)] * (4 * x_all),
         in_specs=[any_spec, any_spec, vmem_spec, vmem_spec, vmem_spec, vmem_spec, any_spec, any_spec],
-        out_specs=[any_spec] * 4 + [vmem_spec, vmem_spec] + [any_spec] * (2 + x_all),
+        out_specs=[any_spec] * 4 + [vmem_spec, vmem_spec] + [any_spec] * (2 + 4 * x_all),
         scratch_shapes=[
             pltpu.VMEM(gate_up_weight.shape, bf16),
             pltpu.VMEM(down_weight.shape, bf16),
@@ -761,10 +809,10 @@
             pltpu.VMEM((count, width), bf16),
             pltpu.VMEM((count, twice), f32),
             pltpu.VMEM((count, half), bf16),
-            pltpu.VMEM((local_experts, count, width), bf16),
+            pltpu.VMEM((x_all, local_experts * capacity, width), bf16),
             pltpu.VMEM((count, width), bf16),
             pltpu.VMEM((count, twice), bf16),
-            pltpu.VMEM((local_experts, count, width), bf16),
+            pltpu.VMEM((x_all, local_experts * capacity, width), bf16),
             pltpu.VMEM((min(2, x_all), length, width), bf16),
             pltpu.VMEM((x1, length, width), bf16),
             pltpu.VMEM((4, length, width), bf16),
@@ -851,7 +899,7 @@
     inputs = tokens.astype(f32)
     scaled_one, first_pull = jax.vjp(rms_scale, inputs, gain_one)
     hidden_one = scaled_one.astype(bf16)
-    hidden_one_columns = own_columns(hidden_one, shard_group).T
+    hidden_one_columns = own_columns(hidden_one, shard_group)
     projected = jnp.dot(hidden_one, qkv_full, preferred_element_type=f32)
     cosine, sine_table = rotary_tables(length)
 
@@ -906,18 +954,6 @@
     grad_rows_sum = done[4]
     grad_router = done[5][:, :local_experts].reshape(experts_all, length).T
     mixture = reduce_expert(mixture_parts, expert_group)
-    block_out = (middle + mixture).astype(bf16)
-    grad_down_full = jnp.einsum("erf,erd->efd", activated, grad_expert, preferred_element_type=f32)
-    grad_gate_up_full = jnp.einsum(
-        "erd,erf->edf", expert_rows, grad_gate_up_low, preferred_element_type=f32
-    )
-    grad_gate_up_weight = lax.psum_scatter(
-        grad_gate_up_full.astype(bf16), "shard", scatter_dimension=1, tiled=True
-    ).astype(f32)
-    grad_down_weight = lax.psum_scatter(
-        grad_down_full.astype(bf16), "shard", scatter_dimension=2, tiled=True
-    ).astype(f32)
-
     upstream = cotangent.astype(f32)
     grad_logits = (
         router * (grad_router - jnp.sum(router * grad_router, axis=-1, keepdims=True))
@@ -933,6 +969,25 @@
         .astype(bf16)
         .reshape(length, HEADS, HEAD_DIM)
     )
+    grad_attended_low, expert_rows, activated, grad_expert, grad_gate_up_low = (
+        lax.optimization_barrier(
+            (grad_attended_low, expert_rows, activated, grad_expert, grad_gate_up_low)
+        )
+    )
+    grad_down_full = jnp.einsum("erf,erd->efd", activated, grad_expert, preferred_element_type=f32)
+    grad_gate_up_full = jnp.einsum(
+        "erd,erf->edf", expert_rows, grad_gate_up_low, preferred_element_type=f32
+    )
+    grad_gate_up_full, grad_down_full, grad_attended_low = lax.optimization_barrier(
+        (grad_gate_up_full.astype(bf16), grad_down_full.astype(bf16), grad_attended_low)
+    )
+    grad_gate_up_weight = lax.psum_scatter(
+        grad_gate_up_full, "shard", scatter_dimension=1, tiled=True
+    ).astype(f32)
+    grad_down_weight = lax.psum_scatter(
+        grad_down_full, "shard", scatter_dimension=2, tiled=True
+    ).astype(f32)
+
     grad_probs = jnp.einsum(
         "qhd,khd->hqk", grad_attended_low, value_low, preferred_element_type=f32
     )
@@ -962,27 +1017,38 @@
     grad_inputs_norm, grad_gain_one = first_pull(grad_hidden_one)
     grad_tokens = grad_middle + grad_inputs_norm
 
-    branch_all = jnp.concatenate(gather_shard(grad_branch_low, shard_group), axis=0)
-    grad_out_part = jnp.einsum(
-        "td,te->de", attended_columns, branch_all, preferred_element_type=f32
-    )
-    grad_out_weight = lax.psum(grad_out_part.astype(bf16), "expert").astype(f32)
-    grad_qkv_weight = summed_rows(
-        hidden_one_columns, grad_projected_low, expert_group, shard_group, z_all, 256, 2, 1
-    ).astype(f32)
-    grad_router_part = jnp.einsum(
-        "td,te->ed", hidden_two, grad_logits, preferred_element_type=f32
-    )
+    grad_router_part = jnp.einsum("td,te->ed", hidden_two, grad_logits, preferred_element_type=f32)
     small = jnp.concatenate(
         [
             grad_router_part,
             jnp.stack([grad_gain_one, grad_gain_query, grad_gain_key, grad_gain_two]),
+            jnp.zeros((-(experts_all + 4) % 8, model_width), f32),
         ],
         axis=0,
     )
-    small = lax.psum(small, ("expert", "shard"))
-    width = norm_one.shape[0]
-    small = lax.dynamic_slice_in_dim(small, own_shard * width, width, axis=1)
+    keep = norm_one.shape[0]
+    small = jnp.stack(
+        [
+            lax.dynamic_slice_in_dim(
+                small,
+                (((own_shard // 2 + dy) % (shard_group // 2)) * 2 + (own_shard % 2 + flip) % 2) * keep,
+                keep,
+                axis=1,
+            )
+            for dy in range(shard_group // 2)
+            for flip in range(2)
+        ]
+    )
+
+    grads_low = jnp.concatenate([grad_branch_low, grad_projected_low], axis=1)
+    grads_low, mixture = lax.optimization_barrier((grads_low, mixture))
+    block_out = (middle + mixture).astype(bf16)
+    columns = jnp.stack([attended_columns.T, hidden_one_columns.T])
+    grad_rows_kept, small = summed_rows(
+        columns, grads_low, model_width, small, expert_group, shard_group, z_all, 256, 2, 1
+    )
+    grad_out_weight = grad_rows_kept[:, :model_width].astype(f32)
+    grad_qkv_weight = grad_rows_kept[:, model_width:].astype(f32)
     return (
         block_out,
         grad_tokens,

time: 1110 us -> 1030 us (0.928)
  Pallas kernels: 539 us -> 497 us
  waiting for transfers between devices: 166 us -> 126 us
    pallas_call x1, Pallas kernels: 274 us -> 233 us  [summed_rows(): pl.pallas_call(functools.partial(tail_kernel, (steps, width, x_all, z_all...]
    reduce_scatter x2, waiting for transfers between devices: 31.3 us -> 0.01 us  [the longest x1 0.01 us: body(): lax.psum_scatter(grad_down_full, 'shard', scatter_dimension=2, tiled=True)]
    ppermute x11 -> x14, waiting for transfers between devices: 121 us -> 101 us  [shift(): return lax.ppermute(values, 'expert', pairs)]
    ppermute x9 -> x6, waiting for transfers between devices: 11.7 us -> 24.4 us  [shard_shift(): return lax.ppermute(values, 'shard', pairs)]
    reshape x6 -> x0, local copies, waits for them, and re-layouts: 12.7 us -> none  [the longest x2 4.86 us: query_key(): queries = rms_scale(raw_query, query_gain).reshape(length, HEADS, HEAD_DIM)]
    unnamed x142 -> x175, local copies, waits for them, and re-layouts: 29.6 us -> 37.8 us
    convert_element_type x4 -> x7, other arithmetic: 24.4 us -> 32.4 us  [the longest x1 9.21 us: body(): grad_qkv_weight = grad_rows_kept[:, model_width:].astype(f32)]
  transfers between devices with their start and end apart: 26 -> 24, of which waited for: 7 -> 9; matrix products, arithmetic and copies ran while one was open for 19% -> 16% of each run, Pallas kernels for 25% -> 23%
where the time goes in v4:
time: 1030 us; the launch traced here: 1020 us
  Pallas kernels  497 us (48%)
  waiting for transfers between devices  126 us (12%)
  blocking collectives  118 us (11%)
  matrix products  95.1 us (9%)
  local copies, waits for them, and re-layouts  82 us (8%)
  other arithmetic  65.7 us (6%)
  starting transfers between devices  25.4 us (2%)
  between operations  15.4 us (1%)
    pallas_call x1, Pallas kernels, moe_layer(): pl.pallas_call(functools.partial(moe_kernel, (x_all, capacity)), out_shap...  264 us
    pallas_call x1, Pallas kernels, summed_rows(): pl.pallas_call(functools.partial(tail_kernel, (steps, width, x_all, z_all...  233 us
    all_gather x1, blocking collectives, body(): place_all = lax.all_gather(place, 'expert', axis=0, tiled=False)[sources]  107 us
    ppermute x14, waiting for transfers between devices, shift(): return lax.ppermute(values, 'expert', pairs)  101 us
    unnamed x175, local copies, waits for them, and re-layouts  37.8 us
    dot_general x1, matrix products, body(): jnp.einsum('erd,erf->edf', expert_rows, grad_gate_up_low, preferred_eleme...  25.8 us
    ppermute x6, waiting for transfers between devices, shard_shift(): return lax.ppermute(values, 'shard', pairs)  24.4 us
    ppermute x14, starting transfers between devices, shift(): return lax.ppermute(values, 'expert', pairs)  21.8 us
  transfers between devices with their start and end apart: 24, of which 9 were waited for; matrix products, arithmetic and copies ran while one was open for 16% of the time, Pallas kernels for 23%

profile of v4, /device:TPU:0, one launch (start us, length us, event | category | flops | bytes accessed | tf_op | source)
XLA Modules:
  0.0 1024.9 jit_solution(12049326220386174249)
XLA Ops:
  8.0 3.1 collective-permute-start.1
  12.6 2.6 collective-permute-start.3
  17.5 106.8 %all-gather = f32[2048,16]{0,1:T(8,128)S(1)} all-gather(f32[256,16]{0,1:T(8,128)S(1)} %and_select_fusion), channel_id=2, replica_groups=mesh['expert'=8,'shard'=4] {'expert'}, dimensions={0}, use_global_device_ids=true | all-gather | bytes 147456 | tf_op jit(solution)/shard_map/all_gather | solution.py:889
  124.9 5.2 all_gather.18
  135.4 2.5 copy.107
  138.6 5.6 all_gather.23
  147.6 2.3 bitcast_dynamic-update-slice_fusion.6
  149.9 2.3 bitcast_dynamic-update-slice_fusion.5
  152.6 9.0 collective-permute-done.2
  161.6 2.3 bitcast_dynamic-update-slice_fusion.4
  166.2 17.8 %collective-permute-done.4 = bf16[256,2048]{1,0:T(8,128)(2,1)S(1)} collective-permute-done((bf16[256,2048]{1,0:T(8,128)(2,1)}, bf16[256,2048]{1,0:T(8,128)(2,1)S(1)}, u32[]{:S(2)}, u32[]{:S(2)}) %collective-permute-start.4) | collective-permute-done | bytes 1048608 | tf_op jit(solution)/shard_map/ppermute | solution.py:71
  187.3 18.7 %collective-permute-done.6 = bf16[256,2048]{1,0:T(8,128)(2,1)S(1)} collective-permute-done((bf16[256,2048]{1,0:T(8,128)(2,1)}, bf16[256,2048]{1,0:T(8,128)(2,1)S(1)}, u32[]{:S(2)}, u32[]{:S(2)}) %collective-permute-start.6) | collective-permute-done | bytes 1048608 | tf_op jit(solution)/shard_map/ppermute | solution.py:71
  207.0 12.0 %fusion.74 = f32[256,6144]{1,0:T(8,128)S(1)} fusion(bf16[256,2048]{0,1:T(8,128)(2,1)S(1)} %fusion.10, bf16[2048,6144]{1,0:T(8,128)(2,1)} %all-gather.4.cloned.1.call-done), kind=kOutput, calls=%fused_computation.189 | convolution fusion | flops 6442450944 | bytes 32505856 | tf_op jit(solution)/shard_map/dot_general | solution.py:903
  219.0 2.7 copy-done.6
  227.3 2.7 multiply_reduce_fusion.7
  233.0 3.5 fusion.72
  236.6 3.4 convolution_convert_fusion.4
  240.0 7.1 multiply_reduce_fusion.5
  250.6 264.4 %shard_map.221 = (bf16[2,4,256,2048]{3,2,1,0:T(8,128)(2,1)}, bf16[2,4,256,1024]{3,2,1,0:T(8,128)(2,1)}, bf16[2,4,256,2048]{3,2,1,0:T(8,128)(2,1)}, bf16[2,4,256,...) custom-call(bf16[256,2048]{1,0:T(8,128)(2,1)} %copy.110.hidden_hbm, ...), custom_call_target="tpu_custom_call" | custom-call | flops 103079215104 | bytes 67108864 | tf_op jit(solution)/shard_map/pallas_call | solution.py:787
  515.9 3.0 copy.113
  519.0 4.5 multiply_reduce_fusion.1
  523.5 2.3 fusion.66
  525.9 6.2 fusion.31
  533.4 11.5 %convolution_convert_fusion.1 = bf16[2,1024,2048]{2,1,0:T(8,128)(2,1)} fusion(bf16[2,1024,1024]{2,1,0:T(8,128)(2,1)S(1)} %bitcast.199, bf16[2,1024,2048]{2,1,0:T(8,128)(2,1)S(1)} %bitcast.198), kind=kOutput, calls=%fused_computation.4 | convolution fusion | flops 8594128896 | bytes 20971520 | tf_op jit(solution)/shard_map/erf,erd->efd/dot_general | solution.py:977
  544.8 25.8 %convolution_convert_fusion = bf16[2,2048,2048]{2,1,0:T(8,128)(2,1)} fusion(bf16[2,1024,2048]{2,1,0:T(8,128)(2,1)} %bitcast.194, bf16[2,1024,2048]{2,1,0:T(8,128)(2,1)} %bitcast.195), kind=kOutput, calls=%fused_computation.2 | convolution fusion | flops 17188257792 | bytes 33554432 | tf_op jit(solution)/shard_map/erd,erf->edf/dot_general | solution.py:978
  574.0 7.3 collective-permute-done.18
  581.3 4.7 collective-permute-done.19
  593.3 2.4 copy.128
  602.7 4.3 multiply_reduce_fusion
  619.9 13.6 %fusion.11 = (f32[2048]{0:T(1024)}, f32[256]{0:T(256)}, f32[256,2048]{0,1:T(8,128)}) fusion(bf16[256,2048]{0,1:T(8,128)(2,1)S(1)} %copy-done.10, f32[256]{0:T(256)S(1)} %copy-done.63, f32[2048]{0:T(1024)S(1)} %bitcast.183, bf16[2048,6144]{1,0:T(8,128)(2,1)} %all-gather.4.cloned.1.call-done, bf16[256,2048]{0,1:T(8,128)(2,1)S(1)} %bitcast.168, ...), kind=kOutput, calls=%fused_computation.31 | convolution fusion | flops 6455556096 | bytes 31475712 | tf_op jit(solution)/shard_map/te,de->td/dot_general | solution.py:1014
  638.1 2.5 copy.129
  640.6 2.9 add_convert_fusion.3
  643.5 4.5 collective-permute-start.9
  647.9 2.6 add_convert_fusion.2
  650.5 13.4 %collective-permute-done.12 = bf16[256,2048]{0,1:T(8,128)(2,1)} collective-permute-done((bf16[256,2048]{0,1:T(8,128)(2,1)}, bf16[256,2048]{0,1:T(8,128)(2,1)}, u32[]{:S(2)}, u32[]{:S(2)}) %collective-permute-start.12) | collective-permute-done | bytes 1048608 | tf_op jit(solution)/shard_map/ppermute | solution.py:71
  664.0 2.8 add_convert_fusion.1
  666.7 2.7 collective-permute-start.13
  682.6 10.4 %collective-permute-done.16 = bf16[256,512]{0,1:T(8,128)(2,1)} collective-permute-done((bf16[256,512]{0,1:T(8,128)(2,1)}, bf16[256,512]{0,1:T(8,128)(2,1)}, u32[]{:S(2)}, u32[]{:S(2)}) %collective-permute-start.16) | collective-permute-done | bytes 262176 | tf_op jit(solution)/shard_map/ppermute | solution.py:111
  695.9 41.7 %collective-permute-done.11 = bf16[256,2048]{0,1:T(8,128)(2,1)} collective-permute-done((bf16[256,2048]{0,1:T(8,128)(2,1)}, bf16[256,2048]{0,1:T(8,128)(2,1)}, u32[]{:S(2)}, u32[]{:S(2)}) %collective-permute-start.11) | collective-permute-done | bytes 1048608 | tf_op jit(solution)/shard_map/ppermute | solution.py:71
  737.5 4.3 convert_add_fusion.1
  741.9 6.4 copy.133.grads_ref
  748.3 5.1 fusion.15
  753.4 3.0 copy.135
  757.8 233.1 %shard_map.222 = (bf16[512,8192]{1,0:T(8,128)(2,1)}, f32[24,512]{1,0:T(8,128)}) custom-call(bf16[256,8192]{1,0:T(8,128)(2,1)} %copy.133.grads_ref, bf16[2,512,1024]{2,1,0:T(8,128)(2,1)} %pad_maximum_fusion.1.columns_ref, f32[4,24,512]{2,1,0:T(8,128)} %pad_maximum_fusion.2.small_ref), custom_call_target="tpu_custom_call" | custom-call | flops 8589934592 | bytes 16777216 | tf_op jit(solution)/shard_map/pallas_call | solution.py:341
  993.8 4.1 slice_convert_fusion.2
  997.9 9.2 slice_convert_fusion
  1007.1 4.2 convert_element_type.151
  1011.3 6.7 convert_element_type.150
  (287 shorter events, 90.5 us)
Async XLA Ops:
  7.2 199.8 %all-gather.4.cloned.1.call-start = ((), (), s32[]{:S(2)}) async-start(), calls=%async_computation.2 | async-start | bytes 31457280 | tf_op jit(solution)/shard_map/all_gather | solution.py:872
  7.9 9.2 copy-start.72
  7.9 9.3 copy-start.73
  7.9 9.3 copy-start.74
  8.0 9.3 copy-start.75
  8.0 9.3 copy-start.70
  8.0 9.4 copy-start.76
  8.0 232.0 %all-gather.6.cloned.1.call-start = ((), (), s32[]{:S(2)}) async-start(), calls=%async_computation.3 | async-start | bytes 10485760 | tf_op jit(solution)/shard_map/all_gather | solution.py:872
  8.0 127.2 %collective-permute-start.1 = (bf16[256,2048]{1,0:T(8,128)(2,1)}, bf16[256,2048]{1,0:T(8,128)(2,1)}, u32[]{:S(2)}, u32[]{:S(2)}) collective-permute-start(bf16[256,2048]{1,0:T(8,128)(2,1)} %param.15), channel_id=1, source_target_pairs={{0,8},{4,12},{8,16},{12,20},{16,24},{20,28},{24,0},{28,4},{1,9},{5... | collective-permute-start | bytes 3145736 | tf_op jit(solution)/shard_map/ppermute | solution.py:71
  11.1 136.5 %collective-permute-start = (bf16[256,2048]{1,0:T(8,128)(2,1)}, bf16[256,2048]{1,0:T(8,128)(2,1)}, u32[]{:S(2)}, u32[]{:S(2)}) collective-permute-start(bf16[256,2048]{1,0:T(8,128)(2,1)} %param.15), channel_id=1, source_target_pairs={{0,4},{4,0},{8,12},{12,8},{16,20},{20,16},{24,28},{28,24},{1,5},{5... | collective-permute-start | bytes 3145736 | tf_op jit(solution)/shard_map/ppermute | solution.py:71
  12.6 133.2 %collective-permute-start.3 = (bf16[256,2048]{1,0:T(8,128)(2,1)}, bf16[256,2048]{1,0:T(8,128)(2,1)}, u32[]{:S(2)}, u32[]{:S(2)}) collective-permute-start(bf16[256,2048]{1,0:T(8,128)(2,1)} %param.15), channel_id=1, source_target_pairs={{0,16},{4,20},{8,24},{12,28},{16,0},{20,4},{24,8},{28,12},{1,17},{... | collective-permute-start | bytes 3145736 | tf_op jit(solution)/shard_map/ppermute | solution.py:71
  15.2 137.0 %collective-permute-start.5 = (bf16[256,2048]{1,0:T(8,128)(2,1)}, bf16[256,2048]{1,0:T(8,128)(2,1)}, u32[]{:S(2)}, u32[]{:S(2)}) collective-permute-start(bf16[256,2048]{1,0:T(8,128)(2,1)} %param.15), channel_id=1, source_target_pairs={{0,24},{4,28},{8,0},{12,4},{16,8},{20,12},{24,16},{28,20},{1,25},{... | collective-permute-start | bytes 3145736 | tf_op jit(solution)/shard_map/ppermute | solution.py:71
  16.6 990.5 %reduce-scatter.5.cloned.1.call-start = ((), (), s32[]{:S(2)}) async-start(), calls=%async_computation.5 | async-start | bytes 10485760 | tf_op jit(solution)/shard_map/reduce_scatter | solution.py:987
  17.2 222.9 %copy-start.9 = (bf16[256,2048]{0,1:T(8,128)(2,1)}, bf16[256,2048]{0,1:T(8,128)(2,1)S(1)}, u32[]{:S(2)}) copy-start(bf16[256,2048]{0,1:T(8,128)(2,1)S(1)} %copy.99) | copy-start | bytes 3145732
  17.2 113.4 %copy-start.71 = (s32[1,256]{1,0:T(1,128)S(1)}, s32[1,256]{1,0:T(1,128)}, u32[]{:S(2)}) copy-start(s32[1,256]{1,0:T(1,128)} %param.16) | copy-start | bytes 3076
  134.9 95.7 %copy-start.45 = (f32[1,2048]{1,0:T(1,128)}, f32[1,2048]{1,0:T(1,128)S(1)}, u32[]{:S(2)}) copy-start(f32[1,2048]{1,0:T(1,128)S(1)} %get-tuple-element.144) | copy-start | bytes 24580
  134.9 96.2 %copy-start.43 = (f32[1,2048]{1,0:T(1,128)}, f32[1,2048]{1,0:T(1,128)S(1)}, u32[]{:S(2)}) copy-start(f32[1,2048]{1,0:T(1,128)S(1)} %get-tuple-element.143) | copy-start | bytes 24580
  135.2 71.8 %copy-start.11 = (bf16[256,2048]{0,1:T(8,128)(2,1)}, bf16[256,2048]{0,1:T(8,128)(2,1)S(1)}, u32[]{:S(2)}) copy-start(bf16[256,2048]{0,1:T(8,128)(2,1)S(1)} %fusion.10) | copy-start | bytes 3145732
  135.2 26.3 %collective-permute-start.2 = (bf16[256,2048]{1,0:T(8,128)(2,1)}, bf16[256,2048]{1,0:T(8,128)(2,1)}, u32[]{:S(2)}, u32[]{:S(2)}) collective-permute-start(bf16[256,2048]{1,0:T(8,128)(2,1)} %collective-permute-done.1), channel_id=1, source_target_pairs={{0,4},{4,0},{8,12},{12,8},{16,20},{20,16},{24,28},{28,24},{1,5},{5... | collective-permute-start | bytes 3145736 | tf_op jit(solution)/shard_map/ppermute | solution.py:71
  138.3 13.9 %copy-start.20 = (f32[8,2,256]{1,2,0:T(8,128)}, f32[8,2,256]{1,2,0:T(8,128)S(1)}, u32[]{:S(2)}) copy-start(f32[8,2,256]{1,2,0:T(8,128)S(1)} %copy.109) | copy-start | bytes 49156
  144.2 106.1 %copy-start.32 = (bf16[2048,16]{0,1:T(8,128)(2,1)}, bf16[2048,16]{0,1:T(8,128)(2,1)S(1)}, u32[]{:S(2)}) copy-start(bf16[2048,16]{0,1:T(8,128)(2,1)S(1)} %all_gather.23) | copy-start | bytes 196612
  145.8 38.1 %collective-permute-start.4 = (bf16[256,2048]{1,0:T(8,128)(2,1)}, bf16[256,2048]{1,0:T(8,128)(2,1)S(1)}, u32[]{:S(2)}, u32[]{:S(2)}) collective-permute-start(bf16[256,2048]{1,0:T(8,128)(2,1)} %collective-permute-done.3), channel_id=1, source_target_pairs={{0,4},{4,0},{8,12},{12,8},{16,20},{20,16},{24,28},{28,24},{1,5},{5... | collective-permute-start | bytes 3145736 | tf_op jit(solution)/shard_map/ppermute | solution.py:71
  152.2 53.8 %collective-permute-start.6 = (bf16[256,2048]{1,0:T(8,128)(2,1)}, bf16[256,2048]{1,0:T(8,128)(2,1)S(1)}, u32[]{:S(2)}, u32[]{:S(2)}) collective-permute-start(bf16[256,2048]{1,0:T(8,128)(2,1)} %collective-permute-done.5), channel_id=1, source_target_pairs={{0,4},{4,0},{8,12},{12,8},{16,20},{20,16},{24,28},{28,24},{1,5},{5... | collective-permute-start | bytes 3145736 | tf_op jit(solution)/shard_map/ppermute | solution.py:71
  247.2 276.3 %copy-start.51 = (f32[256]{0:T(256)}, f32[256]{0:T(256)S(1)}, u32[]{:S(2)}) copy-start(f32[256]{0:T(256)S(1)} %fusion.55) | copy-start | bytes 3076
  523.5 9.8 slice-start
  570.7 440.6 %reduce-scatter.3.cloned.1.call-start = ((), (), s32[]{:S(2)}) async-start(), calls=%async_computation.4 | async-start | bytes 20971520 | tf_op jit(solution)/shard_map/reduce_scatter | solution.py:984
  572.0 15.2 %copy-start.19 = (bf16[32,8,16,128]{3,2,1,0:T(8,128)(2,1)S(1)}, bf16[32,8,16,128]{3,2,1,0:T(8,128)(2,1)}, u32[]{:S(2)}) copy-start(bf16[32,8,16,128]{3,2,1,0:T(8,128)(2,1)} %copy.152) | copy-start | bytes 3145732
  572.0 1.9 collective-permute-start.17
  572.1 9.2 collective-permute-start.18
  573.4 12.6 %collective-permute-start.19 = (bf16[256,512]{0,1:T(8,128)(2,1)S(1)}, bf16[256,512]{0,1:T(8,128)(2,1)S(1)}, u32[]{:S(2)}, u32[]{:S(2)}) collective-permute-start(bf16[256,512]{0,1:T(8,128)(2,1)S(1)} %get-tuple-element.121), channel_id=1, source_target_pairs={{0,3},{1,2},{2,1},{3,0},{4,7},{5,6},{6,5},{7,4},{8,11},{9,10},{10,... | collective-permute-start | bytes 786440 | tf_op jit(solution)/shard_map/ppermute | solution.py:111
  591.1 80.5 %collective-permute-start.14 = (bf16[256,512]{0,1:T(8,128)(2,1)}, bf16[256,512]{0,1:T(8,128)(2,1)}, u32[]{:S(2)}, u32[]{:S(2)}) collective-permute-start(bf16[256,512]{0,1:T(8,128)(2,1)} %get-tuple-element.119), channel_id=1, source_target_pairs={{0,1},{1,0},{2,3},{3,2},{4,5},{5,4},{6,7},{7,6},{8,9},{9,8},{10,11... | collective-permute-start | bytes 786440 | tf_op jit(solution)/shard_map/ppermute | solution.py:111
  592.7 47.9 %collective-permute-start.8 = (bf16[256,2048]{0,1:T(8,128)(2,1)}, bf16[256,2048]{0,1:T(8,128)(2,1)}, u32[]{:S(2)}, u32[]{:S(2)}) collective-permute-start(bf16[256,2048]{0,1:T(8,128)(2,1)} %copy.126), channel_id=1, source_target_pairs={{0,4},{4,0},{8,12},{12,8},{16,20},{20,16},{24,28},{28,24},{1,5},{5... | collective-permute-start | bytes 3145736 | tf_op jit(solution)/shard_map/ppermute | solution.py:71
  595.7 52.2 %collective-permute-start.10 = (bf16[256,2048]{0,1:T(8,128)(2,1)}, bf16[256,2048]{0,1:T(8,128)(2,1)}, u32[]{:S(2)}, u32[]{:S(2)}) collective-permute-start(bf16[256,2048]{0,1:T(8,128)(2,1)} %copy.128), channel_id=1, source_target_pairs={{0,4},{4,0},{8,12},{12,8},{16,20},{20,16},{24,28},{28,24},{1,5},{5... | collective-permute-start | bytes 3145736 | tf_op jit(solution)/shard_map/ppermute | solution.py:71
  599.4 64.6 %collective-permute-start.12 = (bf16[256,2048]{0,1:T(8,128)(2,1)}, bf16[256,2048]{0,1:T(8,128)(2,1)}, u32[]{:S(2)}, u32[]{:S(2)}) collective-permute-start(bf16[256,2048]{0,1:T(8,128)(2,1)} %copy.130), channel_id=1, source_target_pairs={{0,4},{4,0},{8,12},{12,8},{16,20},{20,16},{24,28},{28,24},{1,5},{5... | collective-permute-start | bytes 3145736 | tf_op jit(solution)/shard_map/ppermute | solution.py:71
  601.3 94.5 %collective-permute-start.7 = (bf16[256,2048]{0,1:T(8,128)(2,1)}, bf16[256,2048]{0,1:T(8,128)(2,1)}, u32[]{:S(2)}, u32[]{:S(2)}) collective-permute-start(bf16[256,2048]{0,1:T(8,128)(2,1)} %copy.124), channel_id=1, source_target_pairs={{0,4},{4,0},{8,12},{12,8},{16,20},{20,16},{24,28},{28,24},{1,5},{5... | collective-permute-start | bytes 3145736 | tf_op jit(solution)/shard_map/ppermute | solution.py:71
  619.2 14.4 %copy-start.39 = (bf16[16,128,256]{2,1,0:T(8,128)(2,1)}, bf16[16,128,256]{2,1,0:T(8,128)(2,1)S(1)}, u32[]{:S(2)}) copy-start(bf16[16,128,256]{2,1,0:T(8,128)(2,1)S(1)} %convolution_convert_fusion.3) | copy-start | bytes 3145732
  643.5 20.5 %copy-start.15 = (bf16[256,2048]{0,1:T(8,128)(2,1)S(1)}, bf16[256,2048]{0,1:T(8,128)(2,1)}, u32[]{:S(2)}) copy-start(bf16[256,2048]{0,1:T(8,128)(2,1)} %copy.129) | copy-start | bytes 3145732
  643.5 52.4 %collective-permute-start.9 = (bf16[256,2048]{0,1:T(8,128)(2,1)}, bf16[256,2048]{0,1:T(8,128)(2,1)}, u32[]{:S(2)}, u32[]{:S(2)}) collective-permute-start(bf16[256,2048]{0,1:T(8,128)(2,1)} %add_convert_fusion.3), channel_id=1, source_target_pairs={{0,24},{4,28},{8,0},{12,4},{16,8},{20,12},{24,16},{28,20},{1,25},{... | collective-permute-start | bytes 3145736 | tf_op jit(solution)/shard_map/ppermute | solution.py:71
  647.9 21.5 %copy-start.40 = (bf16[16,128,256]{2,1,0:T(8,128)(2,1)S(1)}, bf16[16,128,256]{2,1,0:T(8,128)(2,1)}, u32[]{:S(2)}) copy-start(bf16[16,128,256]{2,1,0:T(8,128)(2,1)} %copy-done.39) | copy-start | bytes 3145732
  650.5 18.9 %copy-start.27 = (bf16[256,2048]{0,1:T(8,128)(2,1)S(1)}, bf16[256,2048]{0,1:T(8,128)(2,1)}, u32[]{:S(2)}) copy-start(bf16[256,2048]{0,1:T(8,128)(2,1)} %copy-done.26) | copy-start | bytes 3145732
  650.5 18.9 %copy-start.29 = (bf16[256,2048]{0,1:T(8,128)(2,1)S(1)}, bf16[256,2048]{0,1:T(8,128)(2,1)}, u32[]{:S(2)}) copy-start(bf16[256,2048]{0,1:T(8,128)(2,1)} %copy-done.28) | copy-start | bytes 3145732
  650.5 18.9 %copy-start.31 = (bf16[256,2048]{0,1:T(8,128)(2,1)S(1)}, bf16[256,2048]{0,1:T(8,128)(2,1)}, u32[]{:S(2)}) copy-start(bf16[256,2048]{0,1:T(8,128)(2,1)} %copy-done.30) | copy-start | bytes 3145732
  650.5 87.0 %collective-permute-start.11 = (bf16[256,2048]{0,1:T(8,128)(2,1)}, bf16[256,2048]{0,1:T(8,128)(2,1)}, u32[]{:S(2)}, u32[]{:S(2)}) collective-permute-start(bf16[256,2048]{0,1:T(8,128)(2,1)} %add_convert_fusion.2), channel_id=1, source_target_pairs={{0,16},{4,20},{8,24},{12,28},{16,0},{20,4},{24,8},{28,12},{1,17},{... | collective-permute-start | bytes 3145736 | tf_op jit(solution)/shard_map/ppermute | solution.py:71
  666.7 70.8 %collective-permute-start.13 = (bf16[256,2048]{0,1:T(8,128)(2,1)}, bf16[256,2048]{0,1:T(8,128)(2,1)}, u32[]{:S(2)}, u32[]{:S(2)}) collective-permute-start(bf16[256,2048]{0,1:T(8,128)(2,1)} %add_convert_fusion.1), channel_id=1, source_target_pairs={{0,8},{4,12},{8,16},{12,20},{16,24},{20,28},{24,0},{28,4},{1,9},{5... | collective-permute-start | bytes 3145736 | tf_op jit(solution)/shard_map/ppermute | solution.py:71
  671.6 7.3 collective-permute-start.15
  678.8 14.2 %collective-permute-start.16 = (bf16[256,512]{0,1:T(8,128)(2,1)}, bf16[256,512]{0,1:T(8,128)(2,1)}, u32[]{:S(2)}, u32[]{:S(2)}) collective-permute-start(bf16[256,512]{0,1:T(8,128)(2,1)} %get-tuple-element.117), channel_id=1, source_target_pairs={{0,3},{1,2},{2,1},{3,0},{4,7},{5,6},{6,5},{7,4},{8,11},{9,10},{10,... | collective-permute-start | bytes 786440 | tf_op jit(solution)/shard_map/ppermute | solution.py:111
  681.8 12.5 %copy-start.21 = (bf16[1,512,1024]{2,1,0:T(8,128)(2,1)S(1)}, bf16[1,512,1024]{2,1,0:T(8,128)(2,1)}, u32[]{:S(2)}) copy-start(bf16[1,512,1024]{2,1,0:T(8,128)(2,1)} %maximum_bitcast_fusion.1) | copy-start | bytes 3145732
  694.4 43.2 %copy-start.14 = (bf16[256,2048]{0,1:T(8,128)(2,1)S(1)}, bf16[256,2048]{0,1:T(8,128)(2,1)}, u32[]{:S(2)}) copy-start(bf16[256,2048]{0,1:T(8,128)(2,1)} %copy.123) | copy-start | bytes 3145732
  (56 other events, 180.1 us)
Sparse Core Ops, SparseCore 0:
  9.6 157.9 all-gather.3
  169.1 58.2 all-gather.5
  570.8 72.6 reduce-scatter.4
  646.2 142.4 reduce-scatter.2

commit v5 on v4

--- a/solution.py
+++ b/solution.py
@@ -82,27 +82,18 @@
     ]
 
 
-def reduce_expert(parts, expert_group):
-    z_all = z_size(expert_group)
-    x_all = expert_group // z_all
-    rows = {}
-    for dz in sorted(range(z_all), key=lambda d: -min(d, z_all - d)):
-        rows[dz] = parts[dz * x_all].astype(jnp.float32)
-        for dx in range(1, x_all):
-            rows[dz] = rows[dz] + shift(parts[dz * x_all + dx], expert_group, 0, -dx).astype(
-                jnp.float32
-            )
-        if dz:
-            rows[dz] = shift(rows[dz].astype(jnp.bfloat16), expert_group, -dz, 0).astype(jnp.float32)
-    return sum(rows[dz] for dz in range(z_all))
-
-
-def relative_sources(expert_group):
-    z_all = z_size(expert_group)
-    x_all = expert_group // z_all
-    me = lax.axis_index("expert")
-    order = jnp.arange(expert_group, dtype=jnp.int32)
-    return ((me // x_all - order // x_all) % z_all) * x_all + (me % x_all - order % x_all) % x_all
+def sum_over_x(parts, dz, expert_group):
+    x_all = expert_group // z_size(expert_group)
+    total = parts[dz * x_all].astype(jnp.float32)
+    for dx in range(1, x_all):
+        total = total + shift(parts[dz * x_all + dx], expert_group, 0, -dx).astype(jnp.float32)
+    return total
+
+
+def back_along_z(total, dz, expert_group):
+    if dz == 0:
+        return total
+    return shift(total.astype(jnp.bfloat16), expert_group, -dz, 0).astype(jnp.float32)
 
 
 def shard_shift(values, shard_group, dy, flip):
@@ -426,11 +417,20 @@
             fs.at[dz - 1, dx - 1, c], fr.at[dz - 1, dx - 1, c], peer(0, dx),
         )
 
-    def p_copy(dz, dx):
-        return copy(part_stage.at[dx - 1], summed_hbm.at[dz, dx - 1], ps.at[dx - 1], pr.at[dz, dx - 1], peer(0, -dx))
-
-    def q_copy(dz):
-        return copy(own_part.at[dz], z_landed.at[dz - 1], qs.at[dz - 1], qr.at[dz - 1], peer(-dz, 0))
+    def p_copy(dz, dx, c):
+        return copy(
+            part_stage.at[dx - 1, at(c)], summed_hbm.at[dz, dx - 1, at(c)],
+            ps.at[dx - 1], pr.at[dz, dx - 1, c], peer(0, -dx),
+        )
+
+    def p_sent(dx):
+        whole = part_stage.at[dx - 1]
+        copy(whole, whole, ps.at[dx - 1], pr.at[0, dx - 1, 0], peer(0, -dx)).wait_send()
+
+    def q_copy(dz, c):
+        return copy(
+            own_part.at[dz, at(c)], z_landed.at[dz - 1, at(c)], qs.at[dz - 1], qr.at[dz - 1, c], peer(-dz, 0)
+        )
 
     def r_copy(dz, dx):
         return copy(
@@ -461,7 +461,7 @@
         return carry
 
     lax.fori_loop(0, MOE_CHUNKS, send_own, 0)
-    for d in (2, 1, 3):
+    for d in (1, 3, 2):
 
         def send_z(c, carry):
             z_copy(d, c).start()
@@ -469,42 +469,51 @@
 
         lax.fori_loop(0, MOE_CHUNKS, send_z, 0)
 
-    def events(first):
+    def events(first, last):
         def one(k, carry):
-            @pl.when(k < 3 * MOE_CHUNKS)
+            @pl.when(k < last)
             def _():
                 j = k // MOE_CHUNKS
                 c = lax.rem(k, MOE_CHUNKS)
-                d = 2 - j + 3 * (j // 2)
+                d = 1 + 2 * j - 3 * (j // 2)
                 z_copy(d, c).wait_recv()
                 for dx in range(1, x_all):
                     f_copy(d, dx, c).start()
 
             return carry
 
-        lax.fori_loop(first, first + 2, one, 0)
+        lax.fori_loop(first, first + MOE_CHUNKS, one, 0)
 
     def own_slots(le):
         return pl.ds(pl.multiple_of(le * capacity, capacity), capacity)
 
-    def finish(g):
-        dz = g // 2 + 2 * lax.rem(g, 2)
+    def finish(dz, last):
+        def load(c):
+            return pltpu.make_async_copy(summed_hbm.at[dz, dx - 1, at(c)], hid.at[0, at(c)], lsem.at[c])
+
+        def add(c):
+            load(c).wait()
+            own_part[dz, at(c), :] = (
+                own_part[dz, at(c), :].astype(f32) + hid[0, at(c), :].astype(f32)
+            ).astype(bf16)
+            if dx == x_all - 1:
+                pl.when(dz > 0)(lambda: q_copy(dz, c).start())
+
+        def arrive(c, carry):
+            p_copy(dz, dx, c).wait_recv()
+            load(c).start()
+            if last:
+                add(c)
+            return carry
+
+        def rest(c, carry):
+            add(c)
+            return carry
+
         for dx in range(1, x_all):
-            p_copy(dz, dx).wait_recv()
-            load = pltpu.make_async_copy(summed_hbm.at[dz, dx - 1], hid.at[0], lsem)
-            load.start()
-            load.wait()
-
-            def add(n, carry):
-                c = cols(n, tile)
-                own_part[dz, :, c] = (own_part[dz, :, c].astype(f32) + hid[0, :, c].astype(f32)).astype(bf16)
-                return carry
-
-            lax.fori_loop(0, width // tile, add, 0)
-
-        @pl.when(dz > 0)
-        def _():
-            q_copy(dz).start()
+            lax.fori_loop(0, MOE_CHUNKS, arrive, 0)
+            if not last:
+                lax.fori_loop(0, MOE_CHUNKS, rest, 0)
 
     mix_slots = mix_stage.shape[0]
 
@@ -515,10 +524,16 @@
     slot_row = lax.broadcasted_iota(jnp.int32, (capacity, length), 0).astype(f32)
     slot_col = lax.broadcasted_iota(jnp.int32, (length, local_experts * capacity), 1).astype(f32)
     own.wait()
-    events(0)
-
-    def group(g, carry):
-        dz = g // 2 + 2 * lax.rem(g, 2)
+    events(0, 4)
+
+    def load_upstream(dz):
+        return [pltpu.make_async_copy(upstream_hbm.at[dz, dx], ups.at[dx], load_sem.at[1, dx]) for dx in range(x_all)]
+
+    for load in load_upstream(0):
+        load.start()
+
+    def group(dz, carry):
+        g = dz
 
         def arrive(c, inner):
             for dx in range(1, x_all):
@@ -537,10 +552,9 @@
         loads = []
         for dx in range(x_all):
             loads.append(pltpu.make_async_copy(found_hbm.at[dz, dx], hid.at[dx], load_sem.at[0, dx]))
-            loads.append(pltpu.make_async_copy(upstream_hbm.at[dz, dx], ups.at[dx], load_sem.at[1, dx]))
         for load in loads:
             load.start()
-        for load in loads:
+        for load in loads + load_upstream(dz):
             load.wait()
         pl.when(g == 0)(lambda: [w.wait() for w in weights] and None)
 
@@ -577,7 +591,7 @@
                     ).astype(bf16)
                 return c0
 
-            lax.fori_loop(0, width // tile, dispatch, 0)
+            lax.fori_loop(0, width // tile, dispatch, 0, unroll=True)
             store(0, rows, rows_hbm, le).start()
 
             def up_step(n, c0):
@@ -585,7 +599,7 @@
                 gate_up[:, c] = jnp.dot(rows[...], gate_up_w[le, :, c], preferred_element_type=f32)
                 return c0
 
-            lax.fori_loop(0, twice // tile, up_step, 0)
+            lax.fori_loop(0, twice // tile, up_step, 0, unroll=True)
 
             def act_step(n, c0):
                 gate = gate_up[:, cols(n, narrow)]
@@ -593,7 +607,7 @@
                 activated[:, cols(n, narrow)] = (gate / (1.0 + jnp.exp(-gate)) * up).astype(bf16)
                 return c0
 
-            lax.fori_loop(0, half // narrow, act_step, 0)
+            lax.fori_loop(0, half // narrow, act_step, 0, unroll=True)
             store(1, activated, activated_hbm, le).start()
 
             def down_step(n, c0):
@@ -604,7 +618,7 @@
                     out_rows[dx, own_slots(le), c] = result[r].astype(bf16)
                 return c0
 
-            lax.fori_loop(0, width // tile, down_step, 0)
+            lax.fori_loop(0, width // tile, down_step, 0, unroll=True)
 
             mine = e * local_experts + le
             weight_rows = [
@@ -626,7 +640,8 @@
                 return tuple(new)
 
             totals = lax.fori_loop(
-                0, width // tile, grad_step, tuple(jnp.zeros((capacity, 1), f32) for _ in range(x_all))
+                0, width // tile, grad_step, tuple(jnp.zeros((capacity, 1), f32) for _ in range(x_all)),
+                unroll=True,
             )
             store(2, grad_expert, grad_out_hbm, le).start()
             for dx in range(x_all):
@@ -647,7 +662,7 @@
                 grad_gate_up[:, c_up] = (ga * (gate * sg)).astype(bf16)
                 return c0
 
-            lax.fori_loop(0, half // narrow, back_step, 0)
+            lax.fori_loop(0, half // narrow, back_step, 0, unroll=True)
             store(3, grad_gate_up, grad_gate_up_hbm, le).start()
 
             def row_step(n, c0):
@@ -660,16 +675,25 @@
                     grad_rows[dx, own_slots(le), cols(n, narrow)] = result[r].astype(bf16)
                 return c0
 
-            lax.fori_loop(0, width // narrow, row_step, 0)
-            events(4 * g + 2 + 2 * le)
+            lax.fori_loop(0, width // narrow, row_step, 0, unroll=True)
+            k = 2 * g + le
+            events(
+                jnp.where(k == 0, 4, jnp.where(k == 1, 7, jnp.where(k == 2, 9, 11))),
+                jnp.where(k == 0, 7, jnp.where(k == 1, 9, jnp.where(k == 2, 11, jnp.where(k == 3, 12, 0)))),
+            )
             return inner
 
         assert local_experts == 2
         lax.fori_loop(0, local_experts, expert, 0)
 
+        @pl.when(g < z_all - 1)
+        def _():
+            for load in load_upstream(dz + 1):
+                load.start()
+
         def stages():
             for dx in range(1, x_all):
-                p_copy(dz, dx).wait_send()
+                p_sent(dx)
 
         pl.when(g > 0)(stages)
         for dx in range(x_all):
@@ -704,11 +728,12 @@
                     part_stage[dx - 1, :, c] = grad.astype(bf16)
                 return c0
 
-            lax.fori_loop(0, width // tile, combine, 0)
+            lax.fori_loop(0, width // tile, combine, 0, unroll=True)
             for k in range(z_all):
                 pl.when(dz == k)(mix_copy(k, dx).start)
             if dx > 0:
-                p_copy(dz, dx).start()
+                for c in range(MOE_CHUNKS):
+                    p_copy(dz, dx, c).start()
                 r_copy(dz, dx).start()
             else:
 
@@ -720,27 +745,20 @@
                 def _():
                     grad_router_ref[e] = router_stage[0, 0]
 
-        pl.when(g > 0)(lambda: finish(g - 1))
+        pl.when(g > 0)(lambda: finish(dz - 1, False))
         return carry
 
     lax.fori_loop(0, z_all, group, 0)
-    finish(jnp.int32(z_all - 1))
-
-    def total(n, carry):
-        c = cols(n, tile)
-        grad_ref[:, c] = own_part[0, :, c].astype(f32)
+    finish(z_all - 1, True)
+
+    def total(c, carry):
+        grad_ref[at(c), :] = own_part[0, at(c), :].astype(f32)
+        for d in (1, 2, 3):
+            q_copy(d, c).wait_recv()
+            grad_ref[at(c), :] = grad_ref[at(c), :] + z_landed[d - 1, at(c), :].astype(f32)
         return carry
 
-    lax.fori_loop(0, width // tile, total, 0)
-    for d in (2, 1, 3):
-        q_copy(d).wait_recv()
-
-        def more(n, carry):
-            c = cols(n, tile)
-            grad_ref[:, c] = grad_ref[:, c] + z_landed[d - 1, :, c].astype(f32)
-            return carry
-
-        lax.fori_loop(0, width // tile, more, 0)
+    lax.fori_loop(0, MOE_CHUNKS, total, 0)
 
     for kind, buffer, hbm in (
         (0, rows, rows_hbm), (1, activated, activated_hbm), (2, grad_expert, grad_out_hbm),
@@ -750,9 +768,10 @@
     for dx in range(mix_slots):
         mix_copy(0, dx).wait()
     for dx in range(1, x_all):
-        p_copy(0, dx).wait_send()
+        p_sent(dx)
     for d in range(1, z_all):
-        q_copy(d).wait_send()
+        whole = own_part.at[d]
+        copy(whole, whole, qs.at[d - 1], qr.at[d - 1, 0], peer(-d, 0)).wait_send()
     for dz, dx in others:
         r_copy(dz, dx).wait_send()
         r_copy(dz, dx).wait_recv()
@@ -822,10 +841,10 @@
             dma((3, MOE_CHUNKS)), dma((3, MOE_CHUNKS)),
             dma((x1, MOE_CHUNKS)), dma((x1, MOE_CHUNKS)),
             dma((3, x1, MOE_CHUNKS)), dma((3, x1, MOE_CHUNKS)),
-            dma((x1,)), dma((4, x1)),
-            dma((3,)), dma((3,)),
+            dma((x1,)), dma((4, x1, MOE_CHUNKS)),
+            dma((3,)), dma((3, MOE_CHUNKS)),
             dma((4, x_all)), dma((4, x_all)),
-            dma, dma((min(2, x_all),)),
+            dma((MOE_CHUNKS,)), dma((min(2, x_all),)),
         ],
         compiler_params=pltpu.CompilerParams(
             collective_id=name_id, has_side_effects=True, vmem_limit_bytes=62 * 1024 * 1024
@@ -838,6 +857,245 @@
         hidden, upstream_all, place, place_t, router_weight, router_weight.T, gate_up_weight, down_weight
     )
     return out[:6], out[8:]
+
+
+def start_kernel(
+    dims, weight_hbm, upstream_hbm, router_hbm, gains_ref, tokens_ref, routes_ref, tiles_ref,
+    full_hbm, ups_hbm, router_full_hbm, gains_full_ref, place_all_ref, hidden_ref, *sems,
+):
+    x_all, y_all = dims
+    z_all, parts = 4, 4
+    (own_sem, ys, yr, rs, rr, cs, cr, fs, fr, gs, gr, zs, zr, xs, xr, us, ur, ns, nr, ps, pr, ms, mr) = sems
+    f32, bf16 = jnp.float32, jnp.bfloat16
+    rows = weight_hbm.shape[0]
+    length = tokens_ref.shape[0]
+    piece = rows // 8
+    chunk = length // parts
+    e = lax.axis_index("expert")
+    s = lax.axis_index("shard")
+    z, x = e // x_all, lax.rem(e, x_all)
+    y, core = s // 2, lax.rem(s, 2)
+    parity = lax.rem(z, 2)
+
+    def expert_peer(dz, dx):
+        return {"expert": lax.rem(z + dz, z_all) * x_all + lax.rem(x + dx, x_all)}
+
+    def shard_peer(dy, flip):
+        return {"shard": lax.rem(y + dy, y_all) * 2 + lax.rem(core + flip, 2)}
+
+    beside = {"expert": (z + 1 - 2 * parity) * x_all + x}
+    partner = shard_peer(0, 1)
+    far = [(dz, dx) for dz in range(z_all) for dx in range(x_all) if dz + dx > 0]
+    near = [(dy, flip) for dy in range(y_all) for flip in range(2) if dy + flip > 0]
+
+    def copy(src, dst, send, recv, to):
+        return pltpu.make_async_remote_copy(
+            src_ref=src, dst_ref=dst, send_sem=send, recv_sem=recv, device_id=to,
+            device_id_type=pl.DeviceIdType.MESH,
+        )
+
+    def piece_of(i, who):
+        return jnp.where(i < 2, 4 + 2 * who + i, i - 2)
+
+    def span(owner, k):
+        return pl.ds(pl.multiple_of(owner * rows + k * piece, piece), piece)
+
+    def y_copy(dy, i):
+        k = piece_of(i, parity)
+        src = weight_hbm.at[pl.ds(pl.multiple_of(k * piece, piece), piece)]
+        return copy(src, full_hbm.at[span(s, k)], ys.at[dy - 1, i], yr.at[dy - 1, i], shard_peer(dy, 0))
+
+    def owner(dy):
+        return lax.rem(y - dy + y_all, y_all) * 2 + core
+
+    def relay(dy, i):
+        here = full_hbm.at[span(owner(dy), 4 + 2 * parity + i)]
+        return copy(here, here, rs.at[dy - 1, i], rr.at[dy - 1, i], beside)
+
+    def core_y(dy, i):
+        here = full_hbm.at[span(owner(dy), piece_of(i, parity))]
+        return copy(here, here, cs.at[dy - 1, i], cr.at[dy - 1, i], partner)
+
+    def core_r(dy, i):
+        here = full_hbm.at[span(owner(dy), 4 + 2 * (1 - parity) + i)]
+        return copy(here, here, fs.at[dy - 1, i], fr.at[dy - 1, i], partner)
+
+    whole = pl.ds(pl.multiple_of(s * rows, rows), rows)
+    core_own = copy(weight_hbm, full_hbm.at[whole], gs, gr, partner)
+
+    def at(c):
+        return pl.ds(pl.multiple_of(c * chunk, chunk), chunk)
+
+    def z_copy(d, c):
+        return copy(upstream_hbm.at[at(c)], ups_hbm.at[d, 0, at(c)], zs.at[d - 1, c], zr.at[d - 1, c], expert_peer(d, 0))
+
+    def x_copy(d):
+        return copy(upstream_hbm, ups_hbm.at[0, d], xs.at[d - 1], xr.at[d - 1], expert_peer(0, d))
+
+    def u_copy(dz, dx, c):
+        return copy(
+            ups_hbm.at[dz, 0, at(c)], ups_hbm.at[dz, dx, at(c)],
+            us.at[dz - 1, dx - 1, c], ur.at[dz - 1, dx - 1, c], expert_peer(0, dx),
+        )
+
+    def router_copy(n, p):
+        return copy(router_hbm, router_full_hbm.at[whole], ns.at[n], nr.at[n], shard_peer(*p))
+
+    def gains_copy(n, p):
+        return copy(gains_ref, gains_full_ref.at[s], ms.at[n], mr.at[n], shard_peer(*p))
+
+    def place_copy(n, p):
+        return copy(place_all_ref.at[0, 0], place_all_ref.at[p[0], p[1]], ps.at[n], pr.at[n], expert_peer(*p))
+
+    barrier = pltpu.get_barrier_semaphore()
+    peers = [expert_peer(*p) for p in far] + [shard_peer(*p) for p in near]
+    for peer in peers:
+        pl.semaphore_signal(barrier, inc=1, device_id=peer, device_id_type=pl.DeviceIdType.MESH)
+    pl.semaphore_wait(barrier, len(peers))
+
+    own = [
+        pltpu.make_async_copy(weight_hbm, full_hbm.at[whole], own_sem.at[0]),
+        pltpu.make_async_copy(upstream_hbm, ups_hbm.at[0, 0], own_sem.at[1]),
+        pltpu.make_async_copy(router_hbm, router_full_hbm.at[whole], own_sem.at[2]),
+    ]
+    for n, p in enumerate(near):
+        gains_copy(n, p).start()
+        router_copy(n, p).start()
+    for i in range(2):
+        for dy in range(1, y_all):
+            y_copy(dy, i).start()
+    for d in range(1, x_all):
+        x_copy(d).start()
+    for d in (1, 3, 2):
+        for c in range(parts):
+            z_copy(d, c).start()
+    core_own.start()
+    for o in own:
+        o.start()
+
+    count = place_all_ref.shape[2]
+    ids = lax.broadcasted_iota(jnp.int32, (count, length), 0)
+    chosen = jnp.zeros((count, length), f32)
+    for k in range(TOP):
+        chosen = jnp.where(routes_ref[k : k + 1, :] == ids, 1.0, chosen)
+    before = lax.broadcasted_iota(jnp.int32, (length, length), 0)
+    after = lax.broadcasted_iota(jnp.int32, (length, length), 1)
+    earlier = jnp.where(before < after, 1.0, 0.0).astype(bf16)
+    rank = jnp.dot(chosen.astype(bf16), earlier, preferred_element_type=f32)
+    limit = (tiles_ref[...] * TILE).astype(f32)
+    place_all_ref[0, 0] = jnp.where((chosen > 0.5) & (rank < limit), rank, -1.0)
+    for n, p in enumerate(far):
+        place_copy(n, p).start()
+
+    gains_full_ref[s] = gains_ref[...]
+    for n, p in enumerate(near):
+        gains_copy(n, p).wait_recv()
+    keep = gains_ref.shape[1]
+    tall = 64
+
+    def norm(t, carry):
+        r = pl.ds(pl.multiple_of(t * tall, tall), tall)
+        values = tokens_ref[r, :].astype(f32)
+        scale = lax.rsqrt(jnp.mean(values * values, axis=1, keepdims=True) + epsilon)
+        for j in range(2 * y_all):
+            c = slice(j * keep, (j + 1) * keep)
+            gain = gains_full_ref[j, 0:1, :].astype(f32)
+            hidden_ref[r, c] = (values[:, c] * scale * gain).astype(bf16)
+        return carry
+
+    lax.fori_loop(0, length // tall, norm, 0)
+
+    def forward(events):
+        for d, c in events:
+            z_copy(d, c).wait_recv()
+            for dx in range(1, x_all):
+                u_copy(d, dx, c).start()
+
+    order = {
+        0: [(1, 0)], 1: [(1, 1), (1, 2)], 2: [(1, 3), (3, 0), (3, 1)], 3: [(3, 2), (3, 3), (2, 0)],
+        4: [(2, 1), (2, 2), (2, 3)], 5: [],
+    }
+    for i in range(6):
+        for dy in range(1, y_all):
+            y_copy(dy, i).wait_recv()
+            if i < 2:
+                relay(dy, i).start()
+            core_y(dy, i).start()
+            if i < 4:
+                y_copy(dy, i + 2).start()
+        forward(order[i])
+        if i in (3, 4):
+            for dy in range(1, y_all):
+                here = full_hbm.at[span(owner(dy), 4 + 2 * (1 - parity) + i - 3)]
+                copy(here, here, rs.at[dy - 1, i - 3], rr.at[dy - 1, i - 3], beside).wait_recv()
+                core_r(dy, i - 3).start()
+
+    for o in own:
+        o.wait()
+    core_own.wait()
+    for n, p in enumerate(near):
+        gains_copy(n, p).wait_send()
+        router_copy(n, p).wait()
+    for n, p in enumerate(far):
+        place_copy(n, p).wait()
+    for d in range(1, x_all):
+        x_copy(d).wait()
+    for dy in range(1, y_all):
+        for i in range(6):
+            y_copy(dy, i).wait_send()
+            core_y(dy, i).wait()
+        for i in range(2):
+            relay(dy, i).wait_send()
+            core_r(dy, i).wait()
+    for d in range(1, z_all):
+        for c in range(parts):
+            z_copy(d, c).wait_send()
+            for dx in range(1, x_all):
+                u_copy(d, dx, c).wait()
+
+
+def start_layer(weight, upstream, router, gains, tokens, routes, tile_counts, expert_group, shard_group, name_id):
+    f32, bf16 = jnp.float32, jnp.bfloat16
+    length, width = tokens.shape
+    x_all, y_all = expert_group // 4, shard_group // 2
+    experts_all = tile_counts.shape[0]
+    dma = pltpu.SemaphoreType.DMA
+    y1, x1 = max(y_all - 1, 1), max(x_all - 1, 1)
+    any_spec = pl.BlockSpec(memory_space=pl.ANY)
+    vmem_spec = pl.BlockSpec(memory_space=pltpu.VMEM)
+    return pl.pallas_call(
+        functools.partial(start_kernel, (x_all, y_all)),
+        out_shape=[
+            jax.ShapeDtypeStruct((weight.shape[0] * shard_group, weight.shape[1]), bf16),
+            jax.ShapeDtypeStruct((4, x_all, length, width), bf16),
+            jax.ShapeDtypeStruct((router.shape[0] * shard_group, router.shape[1]), bf16),
+            jax.ShapeDtypeStruct((shard_group, *gains.shape), bf16),
+            jax.ShapeDtypeStruct((4, x_all, experts_all, length), f32),
+            jax.ShapeDtypeStruct((length, width), bf16),
+        ],
+        in_specs=[any_spec] * 3 + [vmem_spec] * 4,
+        out_specs=[any_spec] * 3 + [vmem_spec] * 3,
+        scratch_shapes=[
+            dma((3,)),
+            dma((y1, 6)), dma((y1, 6)),
+            dma((y1, 2)), dma((y1, 2)),
+            dma((y1, 6)), dma((y1, 6)),
+            dma((y1, 2)), dma((y1, 2)),
+            dma, dma,
+            dma((3, 4)), dma((3, 4)),
+            dma((x1,)), dma((x1,)),
+            dma((3, x1, 4)), dma((3, x1, 4)),
+            dma((shard_group - 1,)), dma((shard_group - 1,)),
+            dma((expert_group - 1,)), dma((expert_group - 1,)),
+            dma((shard_group - 1,)), dma((shard_group - 1,)),
+        ],
+        compiler_params=pltpu.CompilerParams(
+            collective_id=name_id, has_side_effects=True, vmem_limit_bytes=32 * 1024 * 1024
+        ),
+        cost_estimate=pl.CostEstimate(
+            flops=16 * length * width, bytes_accessed=64 * 1024 * 1024, transcendentals=0
+        ),
+    )(weight, upstream, router, gains, tokens, routes.T, tile_counts[:, None])
 
 
 def body(
@@ -866,39 +1124,34 @@
     score_scale = HEAD_DIM ** (-0.5)
     own_expert = lax.axis_index("expert")
     own_shard = lax.axis_index("shard")
-    sources = relative_sources(expert_group)
-
-    def gather(values, axis):
-        return lax.all_gather(values, axis, axis=0, tiled=True)
-
-    qkv_full = gather(qkv_weight, "shard")
-    out_full = gather(out_weight, "shard")
-    router_full = gather(router_weight, "shard")
-    gains = lax.all_gather(
-        jnp.stack([norm_one, norm_query, norm_key, norm_two]), "shard", axis=1, tiled=True
-    ).astype(f32)
+    z_all = z_size(expert_group)
+    x_all = expert_group // z_all
+
+    gain_rows = jnp.stack([norm_one, norm_query, norm_key, norm_two])
+    gain_rows = jnp.pad(gain_rows, ((0, 12), (0, 0)))
+    qkv_full, upstream_all, router_full, gains, place_all, hidden_one = start_layer(
+        qkv_weight,
+        cotangent,
+        router_weight,
+        gain_rows,
+        tokens,
+        routes,
+        tile_counts,
+        expert_group,
+        shard_group,
+        3,
+    )
+    out_own, gains = lax.optimization_barrier((out_weight, gains))
+    out_full = lax.all_gather(out_own, "shard", axis=0, tiled=True)
+    gains = gains.transpose(1, 0, 2).reshape(gains.shape[1], model_width).astype(f32)
     gain_one, gain_query, gain_key, gain_two = gains[0], gains[1], gains[2], gains[3]
-
-    expert_ids = jnp.arange(experts_all, dtype=jnp.int32)
-    chosen = jnp.any(routes[:, :, None] == expert_ids[None, None, :], axis=1)
-    position = jnp.arange(length, dtype=jnp.int32)
-    earlier = (position[:, None] > position[None, :]).astype(bf16)
-    rank = jnp.dot(earlier, chosen.astype(bf16), preferred_element_type=f32)
-    kept = chosen & (rank < (tile_counts * TILE).astype(f32)[None, :])
-    place = jnp.where(kept, rank, -1.0)
-    place_all = lax.all_gather(place, "expert", axis=0, tiled=False)[sources]
     place_own = lax.dynamic_slice_in_dim(
         place_all, own_expert * local_experts, local_experts, axis=2
     )
-    z_all = z_size(expert_group)
-    x_all = expert_group // z_all
-    place_own = place_own.transpose(0, 2, 1).reshape(z_all, x_all, local_experts, length)
-    upstream_all = jnp.stack(gather_expert(cotangent, expert_group))
-    upstream_all = upstream_all.reshape(z_all, x_all, length, model_width)
+    position = jnp.arange(length, dtype=jnp.int32)
 
     inputs = tokens.astype(f32)
-    scaled_one, first_pull = jax.vjp(rms_scale, inputs, gain_one)
-    hidden_one = scaled_one.astype(bf16)
+    _, first_pull = jax.vjp(rms_scale, inputs, gain_one)
     hidden_one_columns = own_columns(hidden_one, shard_group)
     projected = jnp.dot(hidden_one, qkv_full, preferred_element_type=f32)
     cosine, sine_table = rotary_tables(length)
@@ -953,7 +1206,6 @@
     )
     grad_rows_sum = done[4]
     grad_router = done[5][:, :local_experts].reshape(experts_all, length).T
-    mixture = reduce_expert(mixture_parts, expert_group)
     upstream = cotangent.astype(f32)
     grad_logits = (
         router * (grad_router - jnp.sum(router * grad_router, axis=-1, keepdims=True))
@@ -969,18 +1221,46 @@
         .astype(bf16)
         .reshape(length, HEADS, HEAD_DIM)
     )
-    grad_attended_low, expert_rows, activated, grad_expert, grad_gate_up_low = (
+    mixture_two = sum_over_x(mixture_parts, 2, expert_group)
+    grad_attended_low, expert_rows, activated, grad_expert, grad_gate_up_low, mixture_two = (
         lax.optimization_barrier(
-            (grad_attended_low, expert_rows, activated, grad_expert, grad_gate_up_low)
+            (
+                grad_attended_low,
+                expert_rows,
+                activated,
+                grad_expert,
+                grad_gate_up_low,
+                mixture_two,
+            )
         )
     )
+    mixture_two = back_along_z(mixture_two, 2, expert_group)
+    mixture_one = sum_over_x(mixture_parts, 1, expert_group)
+    mixture_three = sum_over_x(mixture_parts, 3, expert_group)
     grad_down_full = jnp.einsum("erf,erd->efd", activated, grad_expert, preferred_element_type=f32)
     grad_gate_up_full = jnp.einsum(
         "erd,erf->edf", expert_rows, grad_gate_up_low, preferred_element_type=f32
     )
-    grad_gate_up_full, grad_down_full, grad_attended_low = lax.optimization_barrier(
-        (grad_gate_up_full.astype(bf16), grad_down_full.astype(bf16), grad_attended_low)
-    )
+    (
+        grad_gate_up_full,
+        grad_down_full,
+        grad_attended_low,
+        mixture_one,
+        mixture_two,
+        mixture_three,
+    ) = lax.optimization_barrier(
+        (
+            grad_gate_up_full.astype(bf16),
+            grad_down_full.astype(bf16),
+            grad_attended_low,
+            mixture_one,
+            mixture_two,
+            mixture_three,
+        )
+    )
+    mixture_one = back_along_z(mixture_one, 1, expert_group)
+    mixture_three = back_along_z(mixture_three, 3, expert_group)
+    mixture_own = sum_over_x(mixture_parts, 0, expert_group)
     grad_gate_up_weight = lax.psum_scatter(
         grad_gate_up_full, "shard", scatter_dimension=1, tiled=True
     ).astype(f32)
@@ -994,6 +1274,9 @@
     grad_scores_low = (
         probs * (grad_probs - jnp.sum(probs * grad_probs, axis=-1, keepdims=True))
     ).astype(bf16)
+    grad_scores_low, mixture_own, mixture_one = lax.optimization_barrier(
+        (grad_scores_low, mixture_own, mixture_one)
+    )
     grad_queries = (
         jnp.einsum("hqk,khd->qhd", grad_scores_low, key_low, preferred_element_type=f32)
         * score_scale
@@ -1041,7 +1324,8 @@
     )
 
     grads_low = jnp.concatenate([grad_branch_low, grad_projected_low], axis=1)
-    grads_low, mixture = lax.optimization_barrier((grads_low, mixture))
+    grads_low, mixture_three = lax.optimization_barrier((grads_low, mixture_three))
+    mixture = mixture_own + mixture_one + mixture_two + mixture_three
     block_out = (middle + mixture).astype(bf16)
     columns = jnp.stack([attended_columns.T, hidden_one_columns.T])
     grad_rows_kept, small = summed_rows(

time: 1030 us -> 976 us (0.948)
  blocking collectives: 118 us -> 0 us
  Pallas kernels: 497 us -> 601 us
  local copies, waits for them, and re-layouts: 82 us -> 56.9 us
  starting transfers between devices: 25.4 us -> 8.28 us
  waiting for transfers between devices: 126 us -> 113 us
    pallas_call x0 -> x1, Pallas kernels: none -> 119 us  [start_layer(): pl.pallas_call(functools.partial(start_kernel, (x_all, y_all)), out_shape...]
    all_gather x3 -> x0, blocking collectives: 118 us -> none  [the longest x1 107 us: body(): place_all = lax.all_gather(place, 'expert', axis=0, tiled=False)[sources]]
    ppermute x14 -> x7, waiting for transfers between devices: 101 us -> 77.6 us  [shift(): return lax.ppermute(values, 'expert', pairs)]
    ppermute x14 -> x7, starting transfers between devices: 21.8 us -> 5.28 us  [shift(): return lax.ppermute(values, 'expert', pairs)]
    pallas_call x9 -> x3, local copies, waits for them, and re-layouts: 19.6 us -> 3.48 us  [start_layer(): pl.pallas_call(functools.partial(start_kernel, (x_all, y_all)), out_shape...]
    unnamed x175 -> x121, local copies, waits for them, and re-layouts: 37.8 us -> 22.1 us
    pallas_call x1, Pallas kernels: 264 us -> 251 us  [moe_layer(): pl.pallas_call(functools.partial(moe_kernel, (x_all, capacity)), out_shap...]
    reshape x0 -> x5, local copies, waits for them, and re-layouts: none -> 13 us  [the longest x2 5.94 us: query_key(): queries = rms_scale(raw_query, query_gain).reshape(length, HEADS, HEAD_DIM)]
  transfers between devices with their start and end apart: 24 -> 16, of which waited for: 9 -> 8; matrix products, arithmetic and copies ran while one was open for 16% -> 20% of each run, Pallas kernels for 23% -> 24%
where the time goes in v5:
time: 976 us; the launch traced here: 965 us
  Pallas kernels  601 us (62%)
  waiting for transfers between devices  113 us (12%)
  matrix products  100 us (10%)
  other arithmetic  70 us (7%)
  local copies, waits for them, and re-layouts  56.9 us (6%)
  between operations  14.7 us (2%)
    pallas_call x1, Pallas kernels, moe_layer(): pl.pallas_call(functools.partial(moe_kernel, (x_all, capacity)), out_shap...  251 us
    pallas_call x1, Pallas kernels, summed_rows(): pl.pallas_call(functools.partial(tail_kernel, (steps, width, x_all, z_all...  231 us
    pallas_call x1, Pallas kernels, start_layer(): pl.pallas_call(functools.partial(start_kernel, (x_all, y_all)), out_shape...  119 us
    ppermute x7, waiting for transfers between devices, shift(): return lax.ppermute(values, 'expert', pairs)  77.6 us
    dot_general x1, matrix products, body(): jnp.einsum('erd,erf->edf', expert_rows, grad_gate_up_low, preferred_eleme...  25.7 us
    unnamed x121, local copies, waits for them, and re-layouts  22.1 us
    ppermute x6, waiting for transfers between devices, shard_shift(): return lax.ppermute(values, 'shard', pairs)  21.6 us
  transfers between devices with their start and end apart: 16, of which 8 were waited for; matrix products, arithmetic and copies ran while one was open for 20% of the time, Pallas kernels for 24%

profile of v5, /device:TPU:0, one launch (start us, length us, event | category | flops | bytes accessed | tf_op | source)
XLA Modules:
  0.0 964.6 jit_solution(8800906549638985763)
XLA Ops:
  14.0 2.8 copy-done.5
  17.5 118.8 %shard_map.221 = (bf16[2048,6144]{1,0:T(8,128)(2,1)}, bf16[4,2,256,2048]{3,2,1,0:T(8,128)(2,1)S(1)}, bf16[2048,16]{1,0:T(8,128)(2,1)S(1)}, bf16[4,16,512]{2,1,0:...) custom-call(bf16[512,6144]{1,0:T(8,128)(2,1)S(1)} %copy-done.5, ...), custom_call_target="tpu_custom_call" | custom-call | flops 8388608 | bytes 67108864 | tf_op jit(solution)/shard_map/pallas_call | solution.py:1066
  136.3 3.4 copy-done.11
  139.8 13.0 %fusion.71 = f32[256,6144]{1,0:T(8,128)S(1)} fusion(bf16[256,2048]{1,0:T(8,128)(2,1)S(1)} %get-tuple-element.52, bf16[2048,6144]{1,0:T(8,128)(2,1)} %get-tuple-element.53), kind=kOutput, calls=%fused_computation.156 | convolution fusion | flops 6442450944 | bytes 32505856 | tf_op jit(solution)/shard_map/dot_general | solution.py:1156
  155.1 2.4 multiply_multiply_fusion
  157.6 1.9 copy.67
  159.5 2.9 copy.66
  163.7 2.5 constant_dynamic-slice_fusion.8
  170.6 2.5 fusion.101.place_t_ref
  175.0 2.3 fusion.23
  177.3 5.1 fusion.69
  182.4 3.5 convolution_convert_fusion.4
  185.9 13.0 %all-gather.2.cloned.1.call-done = bf16[2048,2048]{1,0:T(8,128)(2,1)} async-done(((bf16[512,2048]{1,0:T(8,128)(2,1)}), bf16[2048,2048]{1,0:T(8,128)(2,1)}) %all-gather.2.cloned.1.call-update) | async-done | bytes 8388624 | tf_op jit(solution)/shard_map/all_gather | solution.py:1145
  198.9 5.8 multiply_reduce_fusion.7
  206.5 251.1 %shard_map.222 = (bf16[2,4,256,2048]{3,2,1,0:T(8,128)(2,1)}, bf16[2,4,256,1024]{3,2,1,0:T(8,128)(2,1)}, bf16[2,4,256,2048]{3,2,1,0:T(8,128)(2,1)}, bf16[2,4,256,...) custom-call(bf16[256,2048]{1,0:T(8,128)(2,1)} %copy-done.21, ...), custom_call_target="tpu_custom_call" | custom-call | flops 103079215104 | bytes 67108864 | tf_op jit(solution)/shard_map/pallas_call | solution.py:806
  461.1 3.2 multiply_reduce_fusion.1
  466.3 6.1 fusion.31
  473.7 54.2 %collective-permute-done = bf16[256,2048]{1,0:T(8,128)(2,1)S(1)} collective-permute-done((bf16[256,2048]{1,0:T(8,128)(2,1)}, bf16[256,2048]{1,0:T(8,128)(2,1)S(1)}, u32[]{:S(2)}, u32[]{:S(2)}) %collective-permute-start) | collective-permute-done | bytes 1048608 | tf_op jit(solution)/shard_map/ppermute | solution.py:71
  529.9 25.7 %convolution_convert_fusion = bf16[2,2048,2048]{2,1,0:T(8,128)(2,1)} fusion(bf16[2,1024,2048]{2,1,0:T(8,128)(2,1)} %bitcast.155, bf16[2,1024,2048]{2,1,0:T(8,128)(2,1)} %bitcast.156), kind=kOutput, calls=%fused_computation.2 | convolution fusion | flops 17188257792 | bytes 33554432 | tf_op jit(solution)/shard_map/erd,erf->edf/dot_general | solution.py:1241
  555.7 15.6 %convolution_convert_fusion.1 = bf16[2,1024,2048]{2,1,0:T(8,128)(2,1)} fusion(bf16[2,1024,1024]{2,1,0:T(8,128)(2,1)} %bitcast.157, bf16[2,1024,2048]{2,1,0:T(8,128)(2,1)} %bitcast.154), kind=kOutput, calls=%fused_computation.4 | convolution fusion | flops 8594128896 | bytes 20971520 | tf_op jit(solution)/shard_map/erf,erd->efd/dot_general | solution.py:1240
  571.3 2.7 convert_add_fusion.2
  573.9 2.6 convert_add_fusion.3
  576.5 2.8 convert_element_type.134
  587.9 3.1 collective-permute-done.8
  590.9 4.8 collective-permute-done.9
  597.0 5.0 collective-permute-done.11
  602.1 8.7 collective-permute-done.12
  613.2 1.7 convert_add_fusion.1
  616.6 4.0 convolution_convert_fusion.3
  620.7 2.3 copy.65
  622.9 2.0 collective-permute-start.6
  625.0 2.4 fusion.34
  628.5 14.1 %collective-permute-done.5 = bf16[256,2048]{1,0:T(8,128)(2,1)} collective-permute-done((bf16[256,2048]{1,0:T(8,128)(2,1)}, bf16[256,2048]{1,0:T(8,128)(2,1)}, u32[]{:S(2)}, u32[]{:S(2)}) %collective-permute-start.5) | collective-permute-done | bytes 1048608 | tf_op jit(solution)/shard_map/ppermute | solution.py:71
  642.6 2.8 convert_element_type.141
  648.5 2.8 fusion.27
  651.3 3.1 copy.63
  654.3 2.9 copy.64
  657.2 9.4 collective-permute-done.6
  666.6 3.3 convert_element_type.143
  669.9 6.0 multiply_reduce_fusion.2
  678.9 2.2 pad_maximum_fusion.grads_ref
  681.1 13.8 %fusion.19 = (f32[2048]{0:T(1024)S(1)}, f32[256]{0:T(256)S(1)}, f32[256,2048]{1,0:T(8,128)}) fusion(bf16[256,2048]{1,0:T(8,128)(2,1)S(1)} %copy-done.2, f32[256]{0:T(256)S(1)} %fusion.60, f32[2048]{0:T(1024)S(1)} %bitcast.143, bf16[2048,6144]{1,0:T(8,128)(2,1)} %get-tuple-element.53, bf16[256,2048]{1,0:T(8,128)(2,1)S(1)} %copy-done.28, ...), kind=kOutput, calls=%fused_computation.36 | convolution fusion | flops 6455556096 | bytes 31475712 | tf_op jit(solution)/shard_map/te,de->td/dot_general | solution.py:1297
  695.7 231.4 %shard_map.223 = (bf16[512,8192]{1,0:T(8,128)(2,1)}, f32[24,512]{1,0:T(8,128)}) custom-call(bf16[256,8192]{1,0:T(8,128)(2,1)} %pad_maximum_fusion.grads_ref, bf16[2,512,1024]{2,1,0:T(8,128)(2,1)} %pad_maximum_fusion.1.columns_ref, f32[4,24,512]{2,1,0:T(8,128)} %pad_maximum_fusion.2.small_ref), custom_call_target="tpu_custom_call" | custom-call | flops 8589934592 | bytes 16777216 | tf_op jit(solution)/shard_map/pallas_call | solution.py:332
  930.0 4.4 slice_convert_fusion.2
  934.4 6.1 fusion.15
  940.6 6.4 slice_convert_fusion
  947.1 4.2 convert_element_type.148
  951.3 6.7 convert_element_type.147
  (202 shorter events, 52.5 us)
Async XLA Ops:
  7.2 191.7 %all-gather.2.cloned.1.call-start = ((), (), s32[]{:S(2)}) async-start(), calls=%async_computation.2 | async-start | bytes 10485760 | tf_op jit(solution)/shard_map/all_gather | solution.py:1145
  139.7 13.1 %copy-start.8 = (bf16[256,2048]{1,0:T(8,128)(2,1)}, bf16[256,2048]{1,0:T(8,128)(2,1)S(1)}, u32[]{:S(2)}) copy-start(bf16[256,2048]{1,0:T(8,128)(2,1)S(1)} %get-tuple-element.52) | copy-start | bytes 3145732
  139.7 65.3 %copy-start.6 = (bf16[2048,16]{1,0:T(8,128)(2,1)}, bf16[2048,16]{1,0:T(8,128)(2,1)S(1)}, u32[]{:S(2)}) copy-start(bf16[2048,16]{1,0:T(8,128)(2,1)S(1)} %get-tuple-element.59.router_ref) | copy-start | bytes 196612
  139.7 807.4 %reduce-scatter.5.cloned.1.call-start = ((), (), s32[]{:S(2)}) async-start(), calls=%async_computation.4 | async-start | bytes 10485760 | tf_op jit(solution)/shard_map/reduce_scatter | solution.py:1267
  152.7 4.8 copy-start.12
  153.1 4.4 copy-start.42
  153.9 3.6 copy-start.44
  166.2 6.9 copy-start.50
  182.4 16.5 %copy-start.1 = (bf16[256,2048]{1,0:T(8,128)(2,1)S(1)}, bf16[256,2048]{1,0:T(8,128)(2,1)}, u32[]{:S(2)}) copy-start(bf16[256,2048]{1,0:T(8,128)(2,1)} %tokens_ref.1) | copy-start | bytes 3145732
  185.9 18.8 %copy-start.24 = (bf16[16,128,256]{2,1,0:T(8,128)(2,1)}, bf16[16,128,256]{2,1,0:T(8,128)(2,1)S(1)}, u32[]{:S(2)}) copy-start(bf16[16,128,256]{2,1,0:T(8,128)(2,1)S(1)} %convolution_convert_fusion.4) | copy-start | bytes 3145732
  206.5 254.6 %copy-start.7 = (bf16[2048,16]{1,0:T(8,128)(2,1)S(1)}, bf16[2048,16]{1,0:T(8,128)(2,1)}, u32[]{:S(2)}) copy-start(bf16[2048,16]{1,0:T(8,128)(2,1)} %copy-done.6) | copy-start | bytes 196612
  457.6 113.7 %collective-permute-start.3 = (bf16[256,2048]{1,0:T(8,128)(2,1)}, bf16[256,2048]{1,0:T(8,128)(2,1)}, u32[]{:S(2)}, u32[]{:S(2)}) collective-permute-start(bf16[256,2048]{1,0:T(8,128)(2,1)} %get-tuple-element.77), channel_id=1, source_target_pairs={{0,4},{4,0},{8,12},{12,8},{16,20},{20,16},{24,28},{28,24},{1,5},{5... | collective-permute-start | bytes 3145736 | tf_op jit(solution)/shard_map/ppermute | solution.py:71
  458.1 115.9 %collective-permute-start.1 = (bf16[256,2048]{1,0:T(8,128)(2,1)}, bf16[256,2048]{1,0:T(8,128)(2,1)}, u32[]{:S(2)}, u32[]{:S(2)}) collective-permute-start(bf16[256,2048]{1,0:T(8,128)(2,1)} %get-tuple-element.74), channel_id=1, source_target_pairs={{0,4},{4,0},{8,12},{12,8},{16,20},{20,16},{24,28},{28,24},{1,5},{5... | collective-permute-start | bytes 3145736 | tf_op jit(solution)/shard_map/ppermute | solution.py:71
  459.7 68.2 %collective-permute-start = (bf16[256,2048]{1,0:T(8,128)(2,1)}, bf16[256,2048]{1,0:T(8,128)(2,1)S(1)}, u32[]{:S(2)}, u32[]{:S(2)}) collective-permute-start(bf16[256,2048]{1,0:T(8,128)(2,1)} %get-tuple-element.67), channel_id=1, source_target_pairs={{0,4},{4,0},{8,12},{12,8},{16,20},{20,16},{24,28},{28,24},{1,5},{5... | collective-permute-start | bytes 3145736 | tf_op jit(solution)/shard_map/ppermute | solution.py:71
  461.0 4.6 copy-start.4
  461.1 4.6 copy-start.14
  466.3 6.1 copy-start.29
  472.5 55.4 %copy-start.33 = (bf16[256,2048]{1,0:T(8,128)(2,1)S(1)}, bf16[256,2048]{1,0:T(8,128)(2,1)}, u32[]{:S(2)}) copy-start(bf16[256,2048]{1,0:T(8,128)(2,1)} %get-tuple-element.66) | copy-start | bytes 3145732
  529.3 47.3 %collective-permute-start.2 = (bf16[256,2048]{1,0:T(8,128)(2,1)}, bf16[256,2048]{1,0:T(8,128)(2,1)}, u32[]{:S(2)}, u32[]{:S(2)}) collective-permute-start(bf16[256,2048]{1,0:T(8,128)(2,1)} %convert_add_fusion.4), channel_id=1, source_target_pairs={{0,16},{4,20},{8,24},{12,28},{16,0},{20,4},{24,8},{28,12},{1,17},{... | collective-permute-start | bytes 3145736 | tf_op jit(solution)/shard_map/ppermute | solution.py:71
  555.7 15.6 %copy-start.32 = (bf16[256,2048]{1,0:T(8,128)(2,1)S(1)}, bf16[256,2048]{1,0:T(8,128)(2,1)}, u32[]{:S(2)}) copy-start(bf16[256,2048]{1,0:T(8,128)(2,1)} %get-tuple-element.76) | copy-start | bytes 3145732
  579.4 371.9 %reduce-scatter.3.cloned.1.call-start = ((), (), s32[]{:S(2)}) async-start(), calls=%async_computation.3 | async-start | bytes 20971520 | tf_op jit(solution)/shard_map/reduce_scatter | solution.py:1264
  581.5 5.7 collective-permute-start.7
  581.5 9.4 collective-permute-start.8
  582.1 4.8 copy-start.2
  582.1 13.7 %collective-permute-start.9 = (bf16[256,512]{0,1:T(8,128)(2,1)}, bf16[256,512]{0,1:T(8,128)(2,1)}, u32[]{:S(2)}, u32[]{:S(2)}) collective-permute-start(bf16[256,512]{0,1:T(8,128)(2,1)} %get-tuple-element.120), channel_id=1, source_target_pairs={{0,3},{1,2},{2,1},{3,0},{4,7},{5,6},{6,5},{7,4},{8,11},{9,10},{10,... | collective-permute-start | bytes 786440 | tf_op jit(solution)/shard_map/ppermute | solution.py:102
  586.4 10.7 %collective-permute-start.10 = (bf16[256,512]{0,1:T(8,128)(2,1)S(1)}, bf16[256,512]{0,1:T(8,128)(2,1)S(1)}, u32[]{:S(2)}, u32[]{:S(2)}) collective-permute-start(bf16[256,512]{0,1:T(8,128)(2,1)S(1)} %get-tuple-element.126), channel_id=1, source_target_pairs={{0,1},{1,0},{2,3},{3,2},{4,5},{5,4},{6,7},{7,6},{8,9},{9,8},{10,11... | collective-permute-start | bytes 786440 | tf_op jit(solution)/shard_map/ppermute | solution.py:102
  586.9 25.9 %collective-permute-start.4 = (bf16[256,2048]{1,0:T(8,128)(2,1)S(1)}, bf16[256,2048]{1,0:T(8,128)(2,1)S(1)}, u32[]{:S(2)}, u32[]{:S(2)}) collective-permute-start(bf16[256,2048]{1,0:T(8,128)(2,1)S(1)} %copy-done.51), channel_id=1, source_target_pairs={{0,4},{4,0},{8,12},{12,8},{16,20},{20,16},{24,28},{28,24},{1,5},{5... | collective-permute-start | bytes 3145736 | tf_op jit(solution)/shard_map/ppermute | solution.py:71
  587.2 14.9 %collective-permute-start.11 = (bf16[256,512]{0,1:T(8,128)(2,1)S(1)}, bf16[256,512]{0,1:T(8,128)(2,1)S(1)}, u32[]{:S(2)}, u32[]{:S(2)}) collective-permute-start(bf16[256,512]{0,1:T(8,128)(2,1)S(1)} %get-tuple-element.125), channel_id=1, source_target_pairs={{0,2},{1,3},{2,0},{3,1},{4,6},{5,7},{6,4},{7,5},{8,10},{9,11},{10,... | collective-permute-start | bytes 786440 | tf_op jit(solution)/shard_map/ppermute | solution.py:102
  590.9 19.8 %collective-permute-start.12 = (bf16[256,512]{0,1:T(8,128)(2,1)S(1)}, bf16[256,512]{0,1:T(8,128)(2,1)S(1)}, u32[]{:S(2)}, u32[]{:S(2)}) collective-permute-start(bf16[256,512]{0,1:T(8,128)(2,1)S(1)} %get-tuple-element.124), channel_id=1, source_target_pairs={{0,3},{1,2},{2,1},{3,0},{4,7},{5,6},{6,5},{7,4},{8,11},{9,10},{10,... | collective-permute-start | bytes 786440 | tf_op jit(solution)/shard_map/ppermute | solution.py:102
  616.5 26.0 %collective-permute-start.5 = (bf16[256,2048]{1,0:T(8,128)(2,1)}, bf16[256,2048]{1,0:T(8,128)(2,1)}, u32[]{:S(2)}, u32[]{:S(2)}) collective-permute-start(bf16[256,2048]{1,0:T(8,128)(2,1)} %convert_add_fusion.3), channel_id=1, source_target_pairs={{0,24},{4,28},{8,0},{12,4},{16,8},{20,12},{24,16},{28,20},{1,25},{... | collective-permute-start | bytes 3145736 | tf_op jit(solution)/shard_map/ppermute | solution.py:71
  622.9 4.5 copy-start.52
  622.9 43.7 %collective-permute-start.6 = (bf16[256,2048]{1,0:T(8,128)(2,1)}, bf16[256,2048]{1,0:T(8,128)(2,1)}, u32[]{:S(2)}, u32[]{:S(2)}) collective-permute-start(bf16[256,2048]{1,0:T(8,128)(2,1)} %convert_add_fusion.2), channel_id=1, source_target_pairs={{0,8},{4,12},{8,16},{12,20},{16,24},{20,28},{24,0},{28,4},{1,9},{5... | collective-permute-start | bytes 3145736 | tf_op jit(solution)/shard_map/ppermute | solution.py:71
  628.5 16.9 %copy-start.27 = (bf16[256,16,128]{0,2,1:T(8,128)(2,1)S(1)}, bf16[256,16,128]{0,2,1:T(8,128)(2,1)}, u32[]{:S(2)}) copy-start(bf16[256,16,128]{0,2,1:T(8,128)(2,1)} %get-tuple-element.128) | copy-start | bytes 3145732
  657.2 12.6 %copy-start.18 = (f32[256,2048]{1,0:T(8,128)S(1)}, f32[256,2048]{1,0:T(8,128)}, u32[]{:S(2)}) copy-start(f32[256,2048]{1,0:T(8,128)} %copy.63) | copy-start | bytes 6291460
  657.2 12.6 %copy-start.38 = (f32[1,4,512]{2,0,1:T(1,128)S(1)}, f32[1,4,512]{2,0,1:T(1,128)}, u32[]{:S(2)}) copy-start(f32[1,4,512]{2,0,1:T(1,128)} %copy-done.37) | copy-start | bytes 24580
  657.2 12.6 %copy-start.40 = (f32[1,4,512]{2,0,1:T(1,128)S(1)}, f32[1,4,512]{2,0,1:T(1,128)}, u32[]{:S(2)}) copy-start(f32[1,4,512]{2,0,1:T(1,128)} %copy-done.39) | copy-start | bytes 24580
  657.2 12.6 %copy-start.43 = (f32[256]{0:T(256)S(1)}, f32[256]{0:T(256)}, u32[]{:S(2)}) copy-start(f32[256]{0:T(256)} %copy-done.42) | copy-start | bytes 3076
  657.2 12.7 %copy-start.45 = (f32[256]{0:T(256)S(1)}, f32[256]{0:T(256)}, u32[]{:S(2)}) copy-start(f32[256]{0:T(256)} %copy-done.44) | copy-start | bytes 3076
  666.6 9.3 slice-start
  669.9 6.0 copy-start.47
  669.9 6.0 copy-start.49
  669.9 6.0 slice-start.1
  669.9 7.0 copy-start.19
  930.0 4.4 copy-start.15
  930.0 4.4 copy-start.17
  930.0 4.4 copy-start.23
  930.0 10.6 %slice-start.2 = ((s8[8388608]{0:T(1024)(128)(4,1)}), s8[4194304]{0:T(1024)(128)(4,1)S(1)}, s32[]{:S(2)}) async-start(s8[8388608]{0:T(1024)(128)(4,1)} %bitcast.125), calls=%async_computation.7 | async-start | bytes 8388608
  934.4 6.2 slice-start.3
  (27 other events, 49.0 us)
Sparse Core Ops, SparseCore 0:
  139.8 59.0 all-gather.1
  579.5 74.1 reduce-scatter.4
  656.4 201.5 reduce-scatter.2

commit v6 on v5

--- a/solution.py
+++ b/solution.py
@@ -94,25 +94,6 @@
     if dz == 0:
         return total
     return shift(total.astype(jnp.bfloat16), expert_group, -dz, 0).astype(jnp.float32)
-
-
-def shard_shift(values, shard_group, dy, flip):
-    y_all = shard_group // 2
-    pairs = [(i, ((i // 2 + dy) % y_all) * 2 + (i % 2 + flip) % 2) for i in range(shard_group)]
-    return lax.ppermute(values, "shard", pairs)
-
-
-def own_columns(values, shard_group):
-    me = lax.axis_index("shard")
-    y_all = shard_group // 2
-    width = values.shape[1] // shard_group
-    found = []
-    for dy in range(y_all):
-        for flip in range(2):
-            there = ((me // 2 + dy) % y_all) * 2 + (me % 2 + flip) % 2
-            piece = lax.dynamic_slice_in_dim(values, there * width, width, axis=1)
-            found.append(piece if dy + flip == 0 else shard_shift(piece, shard_group, dy, flip))
-    return jnp.concatenate(found, axis=0)
 
 
 def tail_kernel(
@@ -372,15 +353,15 @@
 
 def moe_kernel(
     dims, hidden_hbm, upstream_hbm, place_ref, place_t_ref, router_ref, router_t_ref, gate_up_hbm, down_hbm,
-    rows_hbm, activated_hbm, grad_out_hbm, grad_gate_up_hbm, grad_ref, grad_router_ref, found_hbm, summed_hbm,
+    first_hbm, second_hbm, rows_hbm, activated_hbm, grad_out_hbm, grad_gate_up_hbm, grad_ref, grad_router_ref, columns_hbm, found_hbm, summed_hbm,
     *rest,
 ):
-    x_all, capacity = dims
+    x_all, capacity, y_all = dims
     mixture_hbm = rest[: 4 * x_all]
     (
     gate_up_w, down_w, hid, ups, prob, prob_t, rows, gate_up, activated, out_rows, grad_expert, grad_gate_up, grad_rows,
     mix_stage, part_stage, own_part, z_landed, router_stage,
-    w_sem, own_sem, load_sem, store_sem, zs, zr, xs, xr, fs, fr, ps, pr, qs, qr, rs, rr, lsem, mix_sem,
+    w_sem, own_sem, load_sem, store_sem, zs, zr, xs, xr, fs, fr, ps, pr, qs, qr, rs, rr, lsem, mix_sem, cs, cr, own_c,
     ) = rest[4 * x_all :]
     z_all = 4
     f32, bf16 = jnp.float32, jnp.bfloat16
@@ -442,9 +423,37 @@
 
     barrier = pltpu.get_barrier_semaphore()
     others = [(dz, dx) for dz in range(z_all) for dx in range(x_all) if dz + dx > 0]
+    near = [(dy, flip) for dy in range(y_all) for flip in range(2) if dy + flip > 0]
+    shard = lax.axis_index("shard")
+
+    def near_at(dy, flip):
+        return lax.rem(shard // 2 + dy, y_all) * 2 + lax.rem(lax.rem(shard, 2) + flip, 2)
+
     for dz, dx in others:
         pl.semaphore_signal(barrier, inc=1, device_id=peer(dz, dx), device_id_type=pl.DeviceIdType.MESH)
-    pl.semaphore_wait(barrier, len(others))
+    for dy, flip in near:
+        pl.semaphore_signal(
+            barrier, inc=1, device_id={"shard": near_at(dy, flip)}, device_id_type=pl.DeviceIdType.MESH
+        )
+    pl.semaphore_wait(barrier, len(others) + len(near))
+
+    keep = columns_hbm.shape[3]
+
+    def column_copy(kind, source, dy, flip):
+        j = 2 * dy + flip
+        there = near_at(dy, flip)
+        src = source.at[:, pl.ds(pl.multiple_of(there * keep, keep), keep)]
+        if j == 0:
+            return pltpu.make_async_copy(src, columns_hbm.at[kind, 0], own_c.at[kind])
+        return copy(src, columns_hbm.at[kind, j], cs.at[kind, j - 1], cr.at[kind, j - 1], {"shard": there})
+
+    column_copies = [
+        column_copy(kind, source, dy, flip)
+        for kind, source in enumerate((first_hbm, second_hbm))
+        for dy, flip in [(0, 0)] + near
+    ]
+    for c in column_copies:
+        c.start()
 
     own = pltpu.make_async_copy(hidden_hbm, found_hbm.at[0, 0], own_sem)
     own.start()
@@ -760,6 +769,8 @@
 
     lax.fori_loop(0, MOE_CHUNKS, total, 0)
 
+    for c in column_copies:
+        c.wait()
     for kind, buffer, hbm in (
         (0, rows, rows_hbm), (1, activated, activated_hbm), (2, grad_expert, grad_out_hbm),
         (3, grad_gate_up, grad_gate_up_hbm),
@@ -788,7 +799,10 @@
     lax.fori_loop(0, MOE_CHUNKS, sent, 0)
 
 
-def moe_layer(hidden, upstream_all, place, router_weight, gate_up_weight, down_weight, expert_group, capacity, name_id):
+def moe_layer(
+    hidden, upstream_all, place, router_weight, gate_up_weight, down_weight, first, second, expert_group, shard_group,
+    capacity, name_id,
+):
     f32, bf16 = jnp.float32, jnp.bfloat16
     length, width = hidden.shape
     local_experts, _, twice = gate_up_weight.shape
@@ -804,7 +818,7 @@
     any_spec = pl.BlockSpec(memory_space=pl.ANY)
     vmem_spec = pl.BlockSpec(memory_space=pltpu.VMEM)
     out = pl.pallas_call(
-        functools.partial(moe_kernel, (x_all, capacity)),
+        functools.partial(moe_kernel, (x_all, capacity, shard_group // 2)),
         out_shape=[
             jax.ShapeDtypeStruct((local_experts, 4, count, width), bf16),
             jax.ShapeDtypeStruct((local_experts, 4, count, half), bf16),
@@ -812,12 +826,13 @@
             jax.ShapeDtypeStruct((local_experts, 4, count, twice), bf16),
             jax.ShapeDtypeStruct((length, width), f32),
             jax.ShapeDtypeStruct((expert_group, 8, length), f32),
+            jax.ShapeDtypeStruct((2, shard_group, length, width // shard_group), bf16),
             jax.ShapeDtypeStruct((4, x_all, length, width), bf16),
             jax.ShapeDtypeStruct((4, x1, length, width), bf16),
         ]
         + [jax.ShapeDtypeStruct((length, width), bf16)] * (4 * x_all),
-        in_specs=[any_spec, any_spec, vmem_spec, vmem_spec, vmem_spec, vmem_spec, any_spec, any_spec],
-        out_specs=[any_spec] * 4 + [vmem_spec, vmem_spec] + [any_spec] * (2 + 4 * x_all),
+        in_specs=[any_spec, any_spec, vmem_spec, vmem_spec, vmem_spec, vmem_spec, any_spec, any_spec, any_spec, any_spec],
+        out_specs=[any_spec] * 4 + [vmem_spec, vmem_spec] + [any_spec] * (3 + 4 * x_all),
         scratch_shapes=[
             pltpu.VMEM(gate_up_weight.shape, bf16),
             pltpu.VMEM(down_weight.shape, bf16),
@@ -845,6 +860,7 @@
             dma((3,)), dma((3, MOE_CHUNKS)),
             dma((4, x_all)), dma((4, x_all)),
             dma((MOE_CHUNKS,)), dma((min(2, x_all),)),
+            dma((2, shard_group - 1)), dma((2, shard_group - 1)), dma((2,)),
         ],
         compiler_params=pltpu.CompilerParams(
             collective_id=name_id, has_side_effects=True, vmem_limit_bytes=62 * 1024 * 1024
@@ -854,9 +870,10 @@
             transcendentals=0,
         ),
     )(
-        hidden, upstream_all, place, place_t, router_weight, router_weight.T, gate_up_weight, down_weight
-    )
-    return out[:6], out[8:]
+        hidden, upstream_all, place, place_t, router_weight, router_weight.T, gate_up_weight, down_weight,
+        first, second,
+    )
+    return out[:7], out[9:]
 
 
 def start_kernel(
@@ -1152,7 +1169,6 @@
 
     inputs = tokens.astype(f32)
     _, first_pull = jax.vjp(rms_scale, inputs, gain_one)
-    hidden_one_columns = own_columns(hidden_one, shard_group)
     projected = jnp.dot(hidden_one, qkv_full, preferred_element_type=f32)
     cosine, sine_table = rotary_tables(length)
 
@@ -1184,7 +1200,6 @@
         .reshape(length, model_width)
         .astype(bf16)
     )
-    attended_columns = own_columns(attended_low, shard_group)
     middle = inputs + jnp.dot(attended_low, out_full, preferred_element_type=f32)
     scaled_two, second_pull = jax.vjp(rms_scale, middle, gain_two)
     hidden_two = scaled_two.astype(bf16)
@@ -1197,15 +1212,52 @@
         router_full,
         gate_up_weight,
         down_weight,
+        attended_low,
+        hidden_one,
         expert_group,
+        shard_group,
         capacity,
         2,
     )
+    columns = done[6].reshape(2, shard_group * length, -1).swapaxes(1, 2)
     expert_rows, activated, grad_expert, grad_gate_up_low = (
         a.reshape(local_experts, row_count, a.shape[-1]) for a in done[:4]
     )
     grad_rows_sum = done[4]
     grad_router = done[5][:, :local_experts].reshape(experts_all, length).T
+    parts = dict(enumerate(mixture_parts))
+
+    def hold(values, *names):
+        held = lax.optimization_barrier((values, [parts[n] for n in names]))
+        parts.update(zip(names, held[1], strict=True))
+        return held[0]
+
+    def group(dz):
+        return [dz * x_all + dx for dx in range(x_all)]
+
+    two = sum_over_x(parts, 2, expert_group)
+    grad_gate_up_full = jnp.einsum(
+        "erd,erf->edf", expert_rows, grad_gate_up_low, preferred_element_type=f32
+    ).astype(bf16)
+    grad_gate_up_full, activated, two = hold(
+        (grad_gate_up_full, activated, two), *group(1)
+    )
+    two = back_along_z(two, 2, expert_group)
+    one = sum_over_x(parts, 1, expert_group)
+    grad_down_full = jnp.einsum(
+        "erf,erd->efd", activated, grad_expert, preferred_element_type=f32
+    ).astype(bf16)
+    grad_down_full, grad_rows_sum, one = hold(
+        (grad_down_full, grad_rows_sum, one), *group(3), *group(0)
+    )
+    one = back_along_z(one, 1, expert_group)
+    grad_gate_up_weight = lax.psum_scatter(
+        grad_gate_up_full, "shard", scatter_dimension=1, tiled=True
+    ).astype(f32)
+    grad_down_weight = lax.psum_scatter(
+        grad_down_full, "shard", scatter_dimension=2, tiled=True
+    ).astype(f32)
+
     upstream = cotangent.astype(f32)
     grad_logits = (
         router * (grad_router - jnp.sum(router * grad_router, axis=-1, keepdims=True))
@@ -1221,62 +1273,18 @@
         .astype(bf16)
         .reshape(length, HEADS, HEAD_DIM)
     )
-    mixture_two = sum_over_x(mixture_parts, 2, expert_group)
-    grad_attended_low, expert_rows, activated, grad_expert, grad_gate_up_low, mixture_two = (
-        lax.optimization_barrier(
-            (
-                grad_attended_low,
-                expert_rows,
-                activated,
-                grad_expert,
-                grad_gate_up_low,
-                mixture_two,
-            )
-        )
-    )
-    mixture_two = back_along_z(mixture_two, 2, expert_group)
-    mixture_one = sum_over_x(mixture_parts, 1, expert_group)
-    mixture_three = sum_over_x(mixture_parts, 3, expert_group)
-    grad_down_full = jnp.einsum("erf,erd->efd", activated, grad_expert, preferred_element_type=f32)
-    grad_gate_up_full = jnp.einsum(
-        "erd,erf->edf", expert_rows, grad_gate_up_low, preferred_element_type=f32
-    )
-    (
-        grad_gate_up_full,
-        grad_down_full,
-        grad_attended_low,
-        mixture_one,
-        mixture_two,
-        mixture_three,
-    ) = lax.optimization_barrier(
-        (
-            grad_gate_up_full.astype(bf16),
-            grad_down_full.astype(bf16),
-            grad_attended_low,
-            mixture_one,
-            mixture_two,
-            mixture_three,
-        )
-    )
-    mixture_one = back_along_z(mixture_one, 1, expert_group)
-    mixture_three = back_along_z(mixture_three, 3, expert_group)
-    mixture_own = sum_over_x(mixture_parts, 0, expert_group)
-    grad_gate_up_weight = lax.psum_scatter(
-        grad_gate_up_full, "shard", scatter_dimension=1, tiled=True
-    ).astype(f32)
-    grad_down_weight = lax.psum_scatter(
-        grad_down_full, "shard", scatter_dimension=2, tiled=True
-    ).astype(f32)
-
     grad_probs = jnp.einsum(
         "qhd,khd->hqk", grad_attended_low, value_low, preferred_element_type=f32
     )
     grad_scores_low = (
         probs * (grad_probs - jnp.sum(probs * grad_probs, axis=-1, keepdims=True))
     ).astype(bf16)
-    grad_scores_low, mixture_own, mixture_one = lax.optimization_barrier(
-        (grad_scores_low, mixture_own, mixture_one)
-    )
+    three = sum_over_x(parts, 3, expert_group)
+    here = sum_over_x(parts, 0, expert_group)
+    grad_scores_low, two, three, here = lax.optimization_barrier(
+        (grad_scores_low, two, three, here)
+    )
+    three = back_along_z(three, 3, expert_group)
     grad_queries = (
         jnp.einsum("hqk,khd->qhd", grad_scores_low, key_low, preferred_element_type=f32)
         * score_scale
@@ -1324,10 +1332,9 @@
     )
 
     grads_low = jnp.concatenate([grad_branch_low, grad_projected_low], axis=1)
-    grads_low, mixture_three = lax.optimization_barrier((grads_low, mixture_three))
-    mixture = mixture_own + mixture_one + mixture_two + mixture_three
+    grads_low, one, three = lax.optimization_barrier((grads_low, one, three))
+    mixture = here + one + two + three
     block_out = (middle + mixture).astype(bf16)
-    columns = jnp.stack([attended_columns.T, hidden_one_columns.T])
     grad_rows_kept, small = summed_rows(
         columns, grads_low, model_width, small, expert_group, shard_group, z_all, 256, 2, 1
     )

time: 976 us -> 938 us (0.961)
  waiting for transfers between devices: 113 us -> 50.8 us
  Pallas kernels: 601 us -> 620 us
  starting transfers between devices: 8.28 us -> 18.1 us
    ppermute x7, waiting for transfers between devices: 77.6 us -> 37.7 us  [shift(): return lax.ppermute(values, 'expert', pairs)]
    ppermute x6 -> x0, waiting for transfers between devices: 21.6 us -> none  [shard_shift(): return lax.ppermute(values, 'shard', pairs)]
    pallas_call x1, Pallas kernels: 251 us -> 267 us  [moe_layer(): pl.pallas_call(functools.partial(moe_kernel, (x_all, capacity, shard_grou...]
    ppermute x7, starting transfers between devices: 5.28 us -> 18 us  [shift(): return lax.ppermute(values, 'expert', pairs)]
    unnamed x121 -> x144, local copies, waits for them, and re-layouts: 22.1 us -> 20.2 us
  transfers between devices with their start and end apart: 16 -> 10, of which waited for: 8 -> 4; matrix products, arithmetic and copies ran while one was open for 20% -> 20% of each run, Pallas kernels for 24% -> 25%
where the time goes in v6:
time: 938 us; the launch traced here: 927 us
  Pallas kernels  620 us (66%)
  matrix products  96.3 us (10%)
  other arithmetic  71.7 us (8%)
  local copies, waits for them, and re-layouts  54.7 us (6%)
  waiting for transfers between devices  50.8 us (5%)
  starting transfers between devices  18.1 us (2%)
  between operations  14.7 us (2%)
    pallas_call x1, Pallas kernels, moe_layer(): pl.pallas_call(functools.partial(moe_kernel, (x_all, capacity, shard_grou...  267 us
    pallas_call x1, Pallas kernels, summed_rows(): pl.pallas_call(functools.partial(tail_kernel, (steps, width, x_all, z_all...  235 us
    pallas_call x1, Pallas kernels, start_layer(): pl.pallas_call(functools.partial(start_kernel, (x_all, y_all)), out_shape...  119 us
    ppermute x7, waiting for transfers between devices, shift(): return lax.ppermute(values, 'expert', pairs)  37.7 us
    dot_general x1, matrix products, body(): jnp.einsum('erd,erf->edf', expert_rows, grad_gate_up_low, preferred_eleme...  25.9 us
    unnamed x144, local copies, waits for them, and re-layouts  20.2 us
  transfers between devices with their start and end apart: 10, of which 4 were waited for; matrix products, arithmetic and copies ran while one was open for 20% of the time, Pallas kernels for 25%

profile of v6, /device:TPU:0, one launch (start us, length us, event | category | flops | bytes accessed | tf_op | source)
XLA Modules:
  0.0 926.7 jit_solution(18221480030108481611)
XLA Ops:
  12.8 2.8 copy-done.3
  17.5 118.8 %shard_map.221 = (bf16[2048,6144]{1,0:T(8,128)(2,1)}, bf16[4,2,256,2048]{3,2,1,0:T(8,128)(2,1)S(1)}, bf16[2048,16]{1,0:T(8,128)(2,1)S(1)}, bf16[4,16,512]{2,1,0:...) custom-call(bf16[512,6144]{1,0:T(8,128)(2,1)S(1)} %copy-done.3, ...), custom_call_target="tpu_custom_call" | custom-call | flops 8388608 | bytes 67108864 | tf_op jit(solution)/shard_map/pallas_call | solution.py:1083
  136.3 3.4 copy-done.9
  139.8 13.0 %fusion.71 = f32[256,6144]{1,0:T(8,128)S(1)} fusion(bf16[256,2048]{1,0:T(8,128)(2,1)S(1)} %get-tuple-element.55.second_hbm, bf16[2048,6144]{1,0:T(8,128)(2,1)} %get-tuple-element.56), kind=kOutput, calls=%fused_computation.143 | convolution fusion | flops 6442450944 | bytes 32505856 | tf_op jit(solution)/shard_map/dot_general | solution.py:1172
  155.1 2.4 multiply_multiply_fusion
  157.6 1.9 copy.67
  159.5 2.9 copy.66
  163.7 2.6 constant_dynamic-slice_fusion
  171.9 2.0 fusion.23
  173.8 5.1 fusion.69
  179.6 3.5 convolution_convert_fusion.4
  186.5 12.4 %all-gather.2.cloned.1.call-done = bf16[2048,2048]{1,0:T(8,128)(2,1)} async-done(((bf16[512,2048]{1,0:T(8,128)(2,1)}), bf16[2048,2048]{1,0:T(8,128)(2,1)}) %all-gather.2.cloned.1.call-update) | async-done | bytes 8388624 | tf_op jit(solution)/shard_map/all_gather | solution.py:1162
  198.9 5.8 multiply_reduce_fusion.7
  207.3 266.9 %shard_map.222 = (bf16[2,4,256,2048]{3,2,1,0:T(8,128)(2,1)}, bf16[2,4,256,1024]{3,2,1,0:T(8,128)(2,1)}, bf16[2,4,256,2048]{3,2,1,0:T(8,128)(2,1)}, bf16[2,4,256,...) custom-call(bf16[256,2048]{1,0:T(8,128)(2,1)} %multiply_convert_fusi, ...), custom_call_target="tpu_custom_call" | custom-call | flops 103079215104 | bytes 67108864 | tf_op jit(solution)/shard_map/pallas_call | solution.py:820
  474.6 25.9 %convolution_convert_fusion = bf16[2,2048,2048]{2,1,0:T(8,128)(2,1)} fusion(bf16[2,1024,2048]{2,1,0:T(8,128)(2,1)} %bitcast.151, bf16[2,1024,2048]{2,1,0:T(8,128)(2,1)} %bitcast.152), kind=kOutput, calls=%fused_computation.2 | convolution fusion | flops 17188257792 | bytes 33554432 | tf_op jit(solution)/shard_map/erd,erf->edf/dot_general | solution.py:1239
  501.9 1.6 collective-permute-start.1
  503.6 15.3 %convolution_convert_fusion.1 = bf16[2,1024,2048]{2,1,0:T(8,128)(2,1)} fusion(bf16[2,1024,1024]{2,1,0:T(8,128)(2,1)} %bitcast.153, bf16[2,1024,2048]{2,1,0:T(8,128)(2,1)} %bitcast.150), kind=kOutput, calls=%fused_computation.4 | convolution fusion | flops 8594128896 | bytes 20971520 | tf_op jit(solution)/shard_map/erf,erd->efd/dot_general | solution.py:1247
  518.9 7.8 collective-permute-done.1
  530.6 4.9 copy.65
  537.6 3.7 multiply_reduce_fusion.1
  541.4 2.1 fusion.63
  544.6 2.4 convolution_convert_fusion.2
  547.5 2.0 collective-permute-start.3
  549.5 2.5 fusion.33
  555.1 1.8 convolution_convert_fusion.3
  556.9 2.3 copy.64
  559.2 21.6 %collective-permute-done.2 = bf16[256,2048]{1,0:T(8,128)(2,1)} collective-permute-done((bf16[256,2048]{1,0:T(8,128)(2,1)}, bf16[256,2048]{1,0:T(8,128)(2,1)}, u32[]{:S(2)}, u32[]{:S(2)}) %collective-permute-start.2) | collective-permute-done | bytes 1048608 | tf_op jit(solution)/shard_map/ppermute | solution.py:71
  580.8 2.8 convert_element_type.133
  583.6 2.7 convert_add_fusion.2
  586.3 8.3 collective-permute-done.4
  594.6 2.9 convert_add_fusion.1
  600.6 2.0 fusion.27
  602.6 1.8 copy.62
  604.5 3.5 copy.63
  608.0 12.2 %collective-permute-start.6 = (bf16[256,2048]{1,0:T(8,128)(2,1)}, bf16[256,2048]{1,0:T(8,128)(2,1)}, u32[]{:S(2)}, u32[]{:S(2)}) collective-permute-start(bf16[256,2048]{1,0:T(8,128)(2,1)} %convert_add_fusion.2), channel_id=1, source_target_pairs={{0,8},{4,12},{8,16},{12,20},{16,24},{20,28},{24,0},{28,4},{1,9},{5... | collective-permute-start | bytes 3145736 | tf_op jit(solution)/shard_map/ppermute | solution.py:71
  620.2 6.2 multiply_reduce_fusion.2
  626.5 2.2 fusion.13
  628.8 15.1 %fusion.19 = (f32[2048]{0:T(1024)S(1)}, f32[256]{0:T(256)}, f32[256,2048]{1,0:T(8,128)}) fusion(bf16[256,2048]{1,0:T(8,128)(2,1)S(1)} %copy-done.2, f32[256]{0:T(256)S(1)} %fusion.59, f32[2048]{0:T(1024)S(1)} %bitcast.139, bf16[2048,6144]{1,0:T(8,128)(2,1)} %get-tuple-element.56, bf16[256,2048]{1,0:T(8,128)(2,1)} %copy.64, ...), kind=kOutput, calls=%fused_computation.35 | convolution fusion | flops 6455556096 | bytes 31475712 | tf_op jit(solution)/shard_map/te,de->td/dot_general | solution.py:1305
  644.7 3.5 fusion.15
  649.0 3.1 convert_element_type.139
  652.1 2.2 pad_maximum_fusion.grads_ref
  654.3 2.8 convert_element_type.141
  657.1 234.7 %shard_map.223 = (bf16[512,8192]{1,0:T(8,128)(2,1)}, f32[24,512]{1,0:T(8,128)}) custom-call(bf16[256,8192]{1,0:T(8,128)(2,1)} %pad_maximum_fusion.grads_ref, bf16[2,512,1024]{2,1,0:T(8,128)(2,1)} %bitcast.126, f32[4,24,512]{2,1,0:T(8,128)} %pad_maximum_fusion.1.small_ref), custom_call_target="tpu_custom_call" | custom-call | flops 8589934592 | bytes 16777216 | tf_op jit(solution)/shard_map/pallas_call | solution.py:313
  894.8 4.3 slice_convert_fusion.2
  899.1 3.6 add_convert_fusion
  902.7 6.4 slice_convert_fusion
  909.2 4.2 convert_element_type.146
  913.4 6.7 convert_element_type.145
  (211 shorter events, 43.2 us)
Async XLA Ops:
  7.2 191.7 %all-gather.2.cloned.1.call-start = ((), (), s32[]{:S(2)}) async-start(), calls=%async_computation.2 | async-start | bytes 10485760 | tf_op jit(solution)/shard_map/all_gather | solution.py:1162
  139.7 13.1 %copy-start.10 = (bf16[256,2048]{1,0:T(8,128)(2,1)}, bf16[256,2048]{1,0:T(8,128)(2,1)S(1)}, u32[]{:S(2)}) copy-start(bf16[256,2048]{1,0:T(8,128)(2,1)S(1)} %get-tuple-element.55.second_hbm) | copy-start | bytes 3145732
  139.7 28.2 %copy-start.4 = (bf16[2048,16]{1,0:T(8,128)(2,1)}, bf16[2048,16]{1,0:T(8,128)(2,1)S(1)}, u32[]{:S(2)}) copy-start(bf16[2048,16]{1,0:T(8,128)(2,1)S(1)} %get-tuple-element.62.router_ref) | copy-start | bytes 196612
  139.7 769.5 %reduce-scatter.5.cloned.1.call-start = ((), (), s32[]{:S(2)}) async-start(), calls=%async_computation.4 | async-start | bytes 10485760 | tf_op jit(solution)/shard_map/reduce_scatter | solution.py:1257
  152.7 4.8 copy-start.11
  153.1 4.4 copy-start.50
  155.1 49.6 %copy-start.41 = (f32[1,4,512]{2,0,1:T(1,128)}, f32[1,4,512]{2,0,1:T(1,128)S(1)}, u32[]{:S(2)}) copy-start(f32[1,4,512]{2,0,1:T(1,128)S(1)} %get-tuple-element.132) | copy-start | bytes 24580
  163.7 6.2 copy-start.60
  173.8 5.1 copy-start.27
  183.1 15.8 %copy-start.1 = (bf16[256,2048]{1,0:T(8,128)(2,1)S(1)}, bf16[256,2048]{1,0:T(8,128)(2,1)}, u32[]{:S(2)}) copy-start(bf16[256,2048]{1,0:T(8,128)(2,1)} %tokens_ref.1) | copy-start | bytes 3145732
  204.7 269.4 %copy-start.48 = (f32[256]{0:T(256)}, f32[256]{0:T(256)S(1)}, u32[]{:S(2)}) copy-start(f32[256]{0:T(256)S(1)} %fusion.58) | copy-start | bytes 3076
  474.2 26.4 %collective-permute-start = (bf16[256,2048]{1,0:T(8,128)(2,1)}, bf16[256,2048]{1,0:T(8,128)(2,1)S(1)}, u32[]{:S(2)}, u32[]{:S(2)}) collective-permute-start(bf16[256,2048]{1,0:T(8,128)(2,1)} %get-tuple-element.67), channel_id=1, source_target_pairs={{0,4},{4,0},{8,12},{12,8},{16,20},{20,16},{24,28},{28,24},{1,5},{5... | collective-permute-start | bytes 3145736 | tf_op jit(solution)/shard_map/ppermute | solution.py:71
  474.6 25.9 %copy-start.37 = (bf16[256,2048]{1,0:T(8,128)(2,1)S(1)}, bf16[256,2048]{1,0:T(8,128)(2,1)}, u32[]{:S(2)}) copy-start(bf16[256,2048]{1,0:T(8,128)(2,1)} %get-tuple-element.66) | copy-start | bytes 3145732
  501.9 24.8 %collective-permute-start.1 = (bf16[256,2048]{1,0:T(8,128)(2,1)S(1)}, bf16[256,2048]{1,0:T(8,128)(2,1)S(1)}, u32[]{:S(2)}, u32[]{:S(2)}) collective-permute-start(bf16[256,2048]{1,0:T(8,128)(2,1)S(1)} %copy-done.61), channel_id=1, source_target_pairs={{0,4},{4,0},{8,12},{12,8},{16,20},{20,16},{24,28},{28,24},{1,5},{5... | collective-permute-start | bytes 3145736 | tf_op jit(solution)/shard_map/ppermute | solution.py:71
  503.6 23.1 %copy-start.36 = (bf16[256,2048]{1,0:T(8,128)(2,1)S(1)}, bf16[256,2048]{1,0:T(8,128)(2,1)}, u32[]{:S(2)}) copy-start(bf16[256,2048]{1,0:T(8,128)(2,1)} %get-tuple-element.73) | copy-start | bytes 3145732
  528.2 385.2 %reduce-scatter.3.cloned.1.call-start = ((), (), s32[]{:S(2)}) async-start(), calls=%async_computation.3 | async-start | bytes 20971520 | tf_op jit(solution)/shard_map/reduce_scatter | solution.py:1254
  530.5 5.0 copy-start.5
  530.6 5.0 copy-start.19
  536.3 5.0 copy-start.55
  536.3 5.1 copy-start.7
  536.3 5.1 copy-start.20
  536.3 44.5 %collective-permute-start.2 = (bf16[256,2048]{1,0:T(8,128)(2,1)}, bf16[256,2048]{1,0:T(8,128)(2,1)}, u32[]{:S(2)}, u32[]{:S(2)}) collective-permute-start(bf16[256,2048]{1,0:T(8,128)(2,1)} %convert_add_fusion.4), channel_id=1, source_target_pairs={{0,16},{4,20},{8,24},{12,28},{16,0},{20,4},{24,8},{28,12},{1,17},{... | collective-permute-start | bytes 3145736 | tf_op jit(solution)/shard_map/ppermute | solution.py:71
  537.6 6.9 slice-start.2
  547.5 36.1 %collective-permute-start.3 = (bf16[256,2048]{1,0:T(8,128)(2,1)}, bf16[256,2048]{1,0:T(8,128)(2,1)}, u32[]{:S(2)}, u32[]{:S(2)}) collective-permute-start(bf16[256,2048]{1,0:T(8,128)(2,1)} %get-tuple-element.83), channel_id=1, source_target_pairs={{0,4},{4,0},{8,12},{12,8},{16,20},{20,16},{24,28},{28,24},{1,5},{5... | collective-permute-start | bytes 3145736 | tf_op jit(solution)/shard_map/ppermute | solution.py:71
  553.7 40.9 %collective-permute-start.4 = (bf16[256,2048]{1,0:T(8,128)(2,1)}, bf16[256,2048]{1,0:T(8,128)(2,1)}, u32[]{:S(2)}, u32[]{:S(2)}) collective-permute-start(bf16[256,2048]{1,0:T(8,128)(2,1)} %get-tuple-element.85), channel_id=1, source_target_pairs={{0,4},{4,0},{8,12},{12,8},{16,20},{20,16},{24,28},{28,24},{1,5},{5... | collective-permute-start | bytes 3145736 | tf_op jit(solution)/shard_map/ppermute | solution.py:71
  559.2 24.4 %copy-start.35 = (bf16[256,2048]{1,0:T(8,128)(2,1)S(1)}, bf16[256,2048]{1,0:T(8,128)(2,1)}, u32[]{:S(2)}) copy-start(bf16[256,2048]{1,0:T(8,128)(2,1)} %get-tuple-element.82) | copy-start | bytes 3145732
  559.2 89.8 %collective-permute-start.5 = (bf16[256,2048]{1,0:T(8,128)(2,1)}, bf16[256,2048]{1,0:T(8,128)(2,1)}, u32[]{:S(2)}, u32[]{:S(2)}) collective-permute-start(bf16[256,2048]{1,0:T(8,128)(2,1)} %convert_add_fusion.3), channel_id=1, source_target_pairs={{0,24},{4,28},{8,0},{12,4},{16,8},{20,12},{24,16},{28,20},{1,25},{... | collective-permute-start | bytes 3145736 | tf_op jit(solution)/shard_map/ppermute | solution.py:71
  583.6 11.0 %copy-start.38 = (bf16[256,2048]{1,0:T(8,128)(2,1)S(1)}, bf16[256,2048]{1,0:T(8,128)(2,1)}, u32[]{:S(2)}) copy-start(bf16[256,2048]{1,0:T(8,128)(2,1)} %get-tuple-element.84) | copy-start | bytes 3145732
  586.3 11.2 %copy-start.29 = (bf16[256,16,128]{0,2,1:T(8,128)(2,1)S(1)}, bf16[256,16,128]{0,2,1:T(8,128)(2,1)}, u32[]{:S(2)}) copy-start(bf16[256,16,128]{0,2,1:T(8,128)(2,1)} %get-tuple-element.126) | copy-start | bytes 3145732
  604.4 15.8 %copy-start.44 = (f32[1,4,512]{2,0,1:T(1,128)S(1)}, f32[1,4,512]{2,0,1:T(1,128)}, u32[]{:S(2)}) copy-start(f32[1,4,512]{2,0,1:T(1,128)} %copy-done.43) | copy-start | bytes 24580
  604.4 15.8 %copy-start.46 = (f32[1,4,512]{2,0,1:T(1,128)S(1)}, f32[1,4,512]{2,0,1:T(1,128)}, u32[]{:S(2)}) copy-start(f32[1,4,512]{2,0,1:T(1,128)} %copy-done.45) | copy-start | bytes 24580
  604.4 15.8 %copy-start.51 = (f32[256]{0:T(256)S(1)}, f32[256]{0:T(256)}, u32[]{:S(2)}) copy-start(f32[256]{0:T(256)} %copy-done.50) | copy-start | bytes 3076
  604.4 15.8 %copy-start.53 = (f32[256]{0:T(256)S(1)}, f32[256]{0:T(256)}, u32[]{:S(2)}) copy-start(f32[256]{0:T(256)} %copy-done.52) | copy-start | bytes 3076
  604.4 22.0 %slice-start = ((s8[6291456]{0:T(1024)(128)(4,1)}), s8[2097152]{0:T(1024)(128)(4,1)S(1)}, s32[]{:S(2)}) async-start(s8[6291456]{0:T(1024)(128)(4,1)} %bitcast.109), calls=%async_computation.5 | async-start | bytes 4194304
  608.0 18.5 %copy-start.57 = (f32[256]{0:T(256)S(1)}, f32[256]{0:T(256)}, u32[]{:S(2)}) copy-start(f32[256]{0:T(256)} %copy-done.56) | copy-start | bytes 3076
  608.0 18.5 %copy-start.59 = (f32[256]{0:T(256)S(1)}, f32[256]{0:T(256)}, u32[]{:S(2)}) copy-start(f32[256]{0:T(256)} %copy-done.58) | copy-start | bytes 3076
  608.0 18.5 %slice-start.1 = ((s8[6291456]{0:T(1024)(128)(4,1)}), s8[4194304]{0:T(1024)(128)(4,1)S(1)}, s32[]{:S(2)}) async-start(s8[6291456]{0:T(1024)(128)(4,1)} %bitcast.109), calls=%async_computation.6 | async-start | bytes 8388608
  608.0 18.5 %copy-start.15 = (f32[256,2048]{1,0:T(8,128)S(1)}, f32[256,2048]{1,0:T(8,128)}, u32[]{:S(2)}) copy-start(f32[256,2048]{1,0:T(8,128)} %copy.62) | copy-start | bytes 6291460
  608.0 18.5 %copy-start.16 = (f32[256,2048]{1,0:T(8,128)S(1)}, f32[256,2048]{1,0:T(8,128)}, u32[]{:S(2)}) copy-start(f32[256,2048]{1,0:T(8,128)} %copy.63) | copy-start | bytes 6291460
  608.0 46.3 %collective-permute-start.6 = (bf16[256,2048]{1,0:T(8,128)(2,1)}, bf16[256,2048]{1,0:T(8,128)(2,1)}, u32[]{:S(2)}, u32[]{:S(2)}) collective-permute-start(bf16[256,2048]{1,0:T(8,128)(2,1)} %convert_add_fusion.2), channel_id=1, source_target_pairs={{0,8},{4,12},{8,16},{12,20},{16,24},{20,28},{24,0},{28,4},{1,9},{5... | collective-permute-start | bytes 3145736 | tf_op jit(solution)/shard_map/ppermute | solution.py:71
  628.7 16.0 %copy-start.21 = (f32[256,2048]{1,0:T(8,128)S(1)}, f32[256,2048]{1,0:T(8,128)}, u32[]{:S(2)}) copy-start(f32[256,2048]{1,0:T(8,128)} %get-tuple-element.112) | copy-start | bytes 6291460
  644.7 7.4 copy-start.34
  648.3 3.8 copy-start.33
  657.1 242.0 %copy-start.22 = (f32[256,2048]{1,0:T(8,128)S(1)}, f32[256,2048]{1,0:T(8,128)}, u32[]{:S(2)}) copy-start(f32[256,2048]{1,0:T(8,128)} %convert_element_type.133) | copy-start | bytes 6291460
  893.3 5.8 copy-start.23
  893.3 5.8 copy-start.24
  894.8 4.3 copy-start.14
  894.8 7.9 slice-start.4
  (33 other events, 68.0 us)
Sparse Core Ops, SparseCore 0:
  139.8 59.0 all-gather.1
  528.3 69.2 reduce-scatter.4
  600.3 184.7 reduce-scatter.2

commit v7 on v6

--- a/solution.py
+++ b/solution.py
@@ -91,9 +91,7 @@
 
 
 def back_along_z(total, dz, expert_group):
-    if dz == 0:
-        return total
-    return shift(total.astype(jnp.bfloat16), expert_group, -dz, 0).astype(jnp.float32)
+    return shift(total, expert_group, -dz, 0)
 
 
 def tail_kernel(
@@ -452,9 +450,6 @@
         for kind, source in enumerate((first_hbm, second_hbm))
         for dy, flip in [(0, 0)] + near
     ]
-    for c in column_copies:
-        c.start()
-
     own = pltpu.make_async_copy(hidden_hbm, found_hbm.at[0, 0], own_sem)
     own.start()
     weights = [
@@ -469,14 +464,16 @@
             x_copy(d, c).start()
         return carry
 
-    lax.fori_loop(0, MOE_CHUNKS, send_own, 0)
-    for d in (1, 3, 2):
+    for d in (1, 2, 3):
 
         def send_z(c, carry):
             z_copy(d, c).start()
             return carry
 
         lax.fori_loop(0, MOE_CHUNKS, send_z, 0)
+
+    for c in column_copies:
+        c.start()
 
     def events(first, last):
         def one(k, carry):
@@ -484,7 +481,7 @@
             def _():
                 j = k // MOE_CHUNKS
                 c = lax.rem(k, MOE_CHUNKS)
-                d = 1 + 2 * j - 3 * (j // 2)
+                d = 1 + j
                 z_copy(d, c).wait_recv()
                 for dx in range(1, x_all):
                     f_copy(d, dx, c).start()
@@ -498,15 +495,16 @@
 
     def finish(dz, last):
         def load(c):
-            return pltpu.make_async_copy(summed_hbm.at[dz, dx - 1, at(c)], hid.at[0, at(c)], lsem.at[c])
+            return pltpu.make_async_copy(summed_hbm.at[dz, dx - 1, at(c)], mix_stage.at[0, at(c)], lsem.at[c])
 
         def add(c):
             load(c).wait()
             own_part[dz, at(c), :] = (
-                own_part[dz, at(c), :].astype(f32) + hid[0, at(c), :].astype(f32)
+                own_part[dz, at(c), :].astype(f32) + mix_stage[0, at(c), :].astype(f32)
             ).astype(bf16)
             if dx == x_all - 1:
-                pl.when(dz > 0)(lambda: q_copy(dz, c).start())
+                if not last:
+                    q_copy(dz, c).start()
 
         def arrive(c, carry):
             p_copy(dz, dx, c).wait_recv()
@@ -530,19 +528,26 @@
         slot = dx % mix_slots
         return pltpu.make_async_copy(mix_stage.at[slot], mixture_hbm[dz * x_all + dx], mix_sem.at[slot])
 
+    def pieces(p):
+        return 4 + sum(n * (p >= k).astype(jnp.int32) for k, n in enumerate((1, 1, 1, 1, 1, 2, 1, 0)))
+
+    def group_at(g):
+        return lax.rem(g + 1, z_all)
+
     slot_row = lax.broadcasted_iota(jnp.int32, (capacity, length), 0).astype(f32)
     slot_col = lax.broadcasted_iota(jnp.int32, (length, local_experts * capacity), 1).astype(f32)
     own.wait()
     events(0, 4)
+    lax.fori_loop(0, MOE_CHUNKS, send_own, 0)
 
     def load_upstream(dz):
         return [pltpu.make_async_copy(upstream_hbm.at[dz, dx], ups.at[dx], load_sem.at[1, dx]) for dx in range(x_all)]
 
-    for load in load_upstream(0):
+    for load in load_upstream(1):
         load.start()
 
-    def group(dz, carry):
-        g = dz
+    def group(g, carry):
+        dz = group_at(g)
 
         def arrive(c, inner):
             for dx in range(1, x_all):
@@ -628,6 +633,8 @@
                 return c0
 
             lax.fori_loop(0, width // tile, down_step, 0, unroll=True)
+
+            events(pieces(4 * g + 2 * le - 1), pieces(4 * g + 2 * le))
 
             mine = e * local_experts + le
             weight_rows = [
@@ -685,11 +692,14 @@
                 return c0
 
             lax.fori_loop(0, width // narrow, row_step, 0, unroll=True)
-            k = 2 * g + le
-            events(
-                jnp.where(k == 0, 4, jnp.where(k == 1, 7, jnp.where(k == 2, 9, 11))),
-                jnp.where(k == 0, 7, jnp.where(k == 1, 9, jnp.where(k == 2, 11, jnp.where(k == 3, 12, 0)))),
-            )
+            events(pieces(4 * g + 2 * le), pieces(4 * g + 2 * le + 1))
+
+            @pl.when((le == 0) & (g > 0))
+            def _():
+                for dx in range(mix_slots):
+                    mix_copy(0, dx).wait()
+                finish(group_at(g - 1), False)
+
             return inner
 
         assert local_experts == 2
@@ -697,7 +707,7 @@
 
         @pl.when(g < z_all - 1)
         def _():
-            for load in load_upstream(dz + 1):
+            for load in load_upstream(group_at(g + 1)):
                 load.start()
 
         def stages():
@@ -719,9 +729,7 @@
             high = weight.astype(bf16)
             remainder = (weight - high.astype(f32)).astype(bf16)
 
-            if dx < mix_slots:
-                pl.when(g > 0)(mix_copy(0, dx).wait)
-            else:
+            if dx >= mix_slots:
                 mix_copy(0, dx).wait()
 
             def combine(n, c0):
@@ -754,11 +762,12 @@
                 def _():
                     grad_router_ref[e] = router_stage[0, 0]
 
-        pl.when(g > 0)(lambda: finish(dz - 1, False))
         return carry
 
     lax.fori_loop(0, z_all, group, 0)
-    finish(z_all - 1, True)
+    for dx in range(mix_slots):
+        mix_copy(0, dx).wait()
+    finish(0, True)
 
     def total(c, carry):
         grad_ref[at(c), :] = own_part[0, at(c), :].astype(f32)
@@ -776,8 +785,6 @@
         (3, grad_gate_up, grad_gate_up_hbm),
     ):
         pltpu.make_async_copy(buffer, hbm.at[0, 0], store_sem.at[kind]).wait()
-    for dx in range(mix_slots):
-        mix_copy(0, dx).wait()
     for dx in range(1, x_all):
         p_sent(dx)
     for d in range(1, z_all):
@@ -1227,36 +1234,13 @@
     grad_router = done[5][:, :local_experts].reshape(experts_all, length).T
     parts = dict(enumerate(mixture_parts))
 
-    def hold(values, *names):
+    def slot(values, *names):
         held = lax.optimization_barrier((values, [parts[n] for n in names]))
         parts.update(zip(names, held[1], strict=True))
         return held[0]
 
     def group(dz):
         return [dz * x_all + dx for dx in range(x_all)]
-
-    two = sum_over_x(parts, 2, expert_group)
-    grad_gate_up_full = jnp.einsum(
-        "erd,erf->edf", expert_rows, grad_gate_up_low, preferred_element_type=f32
-    ).astype(bf16)
-    grad_gate_up_full, activated, two = hold(
-        (grad_gate_up_full, activated, two), *group(1)
-    )
-    two = back_along_z(two, 2, expert_group)
-    one = sum_over_x(parts, 1, expert_group)
-    grad_down_full = jnp.einsum(
-        "erf,erd->efd", activated, grad_expert, preferred_element_type=f32
-    ).astype(bf16)
-    grad_down_full, grad_rows_sum, one = hold(
-        (grad_down_full, grad_rows_sum, one), *group(3), *group(0)
-    )
-    one = back_along_z(one, 1, expert_group)
-    grad_gate_up_weight = lax.psum_scatter(
-        grad_gate_up_full, "shard", scatter_dimension=1, tiled=True
-    ).astype(f32)
-    grad_down_weight = lax.psum_scatter(
-        grad_down_full, "shard", scatter_dimension=2, tiled=True
-    ).astype(f32)
 
     upstream = cotangent.astype(f32)
     grad_logits = (
@@ -1267,6 +1251,33 @@
     )
     grad_middle_norm, grad_gain_two = second_pull(grad_hidden_two)
     grad_middle = upstream + grad_middle_norm
+    two = sum_over_x(parts, 2, expert_group).astype(bf16)
+    grad_middle, expert_rows, two = slot((grad_middle, expert_rows, two), *group(1))
+    halves = [two[: length // 2], two[length // 2 :]]
+    halves[0] = back_along_z(halves[0], 2, expert_group)
+    one = sum_over_x(parts, 1, expert_group).astype(bf16)
+    grad_gate_up_full = jnp.einsum(
+        "erd,erf->edf", expert_rows, grad_gate_up_low, preferred_element_type=f32
+    ).astype(bf16)
+    grad_middle, grad_gate_up_full, activated, halves, one = slot(
+        (grad_middle, grad_gate_up_full, activated, halves, one), *group(3)
+    )
+    grad_gate_up_weight = lax.psum_scatter(
+        grad_gate_up_full, "shard", scatter_dimension=1, tiled=True
+    ).astype(f32)
+    halves[1] = back_along_z(halves[1], 2, expert_group)
+    three = sum_over_x(parts, 3, expert_group).astype(bf16)
+    grad_down_full = jnp.einsum(
+        "erf,erd->efd", activated, grad_expert, preferred_element_type=f32
+    ).astype(bf16)
+    grad_middle, grad_down_full, halves, one, three = slot(
+        (grad_middle, grad_down_full, halves, one, three), *group(0)
+    )
+    grad_down_weight = lax.psum_scatter(
+        grad_down_full, "shard", scatter_dimension=2, tiled=True
+    ).astype(f32)
+    one = back_along_z(one, 1, expert_group)
+    here = sum_over_x(parts, 0, expert_group)
     grad_branch_low = grad_middle.astype(bf16)
     grad_attended_low = (
         jnp.einsum("te,de->td", grad_branch_low, out_full, preferred_element_type=f32)
@@ -1279,11 +1290,7 @@
     grad_scores_low = (
         probs * (grad_probs - jnp.sum(probs * grad_probs, axis=-1, keepdims=True))
     ).astype(bf16)
-    three = sum_over_x(parts, 3, expert_group)
-    here = sum_over_x(parts, 0, expert_group)
-    grad_scores_low, two, three, here = lax.optimization_barrier(
-        (grad_scores_low, two, three, here)
-    )
+    grad_scores_low, one, here, three = slot((grad_scores_low, one, here, three))
     three = back_along_z(three, 3, expert_group)
     grad_queries = (
         jnp.einsum("hqk,khd->qhd", grad_scores_low, key_low, preferred_element_type=f32)
@@ -1332,8 +1339,8 @@
     )
 
     grads_low = jnp.concatenate([grad_branch_low, grad_projected_low], axis=1)
-    grads_low, one, three = lax.optimization_barrier((grads_low, one, three))
-    mixture = here + one + two + three
+    grads_low, three = slot((grads_low, three))
+    mixture = sum((a.astype(f32) for a in (one, jnp.concatenate(halves), three)), here)
     block_out = (middle + mixture).astype(bf16)
     grad_rows_kept, small = summed_rows(
         columns, grads_low, model_width, small, expert_group, shard_group, z_all, 256, 2, 1

time: 938 us -> 905 us (0.965)
  Pallas kernels: 620 us -> 597 us
    pallas_call x1, Pallas kernels: 267 us -> 251 us  [moe_layer(): pl.pallas_call(functools.partial(moe_kernel, (x_all, capacity, shard_grou...]
    ppermute x7 -> x8, waiting for transfers between devices: 37.7 us -> 35.2 us  [shift(): return lax.ppermute(values, 'expert', pairs)]
    unnamed x144 -> x114, local copies, waits for them, and re-layouts: 20.2 us -> 19.4 us
  transfers between devices with their start and end apart: 10 -> 11, of which waited for: 4 -> 4; matrix products, arithmetic and copies ran while one was open for 20% -> 21% of each run, Pallas kernels for 25% -> 25%
where the time goes in v7:
time: 905 us; the launch traced here: 894 us
  Pallas kernels  597 us (66%)
  matrix products  103 us (11%)
  other arithmetic  64.4 us (7%)
  local copies, waits for them, and re-layouts  54.3 us (6%)
  waiting for transfers between devices  50.7 us (6%)
  between operations  14.9 us (2%)
  starting transfers between devices  9.17 us (1%)
    pallas_call x1, Pallas kernels, moe_layer(): pl.pallas_call(functools.partial(moe_kernel, (x_all, capacity, shard_grou...  251 us
    pallas_call x1, Pallas kernels, summed_rows(): pl.pallas_call(functools.partial(tail_kernel, (steps, width, x_all, z_all...  227 us
    pallas_call x1, Pallas kernels, start_layer(): pl.pallas_call(functools.partial(start_kernel, (x_all, y_all)), out_shape...  119 us
    ppermute x8, waiting for transfers between devices, shift(): return lax.ppermute(values, 'expert', pairs)  35.2 us
    dot_general x1, matrix products, body(): jnp.einsum('erd,erf->edf', expert_rows, grad_gate_up_low, preferred_eleme...  25.8 us
    unnamed x114, local copies, waits for them, and re-layouts  19.4 us
  transfers between devices with their start and end apart: 11, of which 4 were waited for; matrix products, arithmetic and copies ran while one was open for 21% of the time, Pallas kernels for 25%

profile of v7, /device:TPU:0, one launch (start us, length us, event | category | flops | bytes accessed | tf_op | source)
XLA Modules:
  0.0 893.6 jit_solution(9790213579682157820)
XLA Ops:
  12.8 2.8 copy-done.3
  17.5 118.8 %shard_map.221 = (bf16[2048,6144]{1,0:T(8,128)(2,1)}, bf16[4,2,256,2048]{3,2,1,0:T(8,128)(2,1)S(1)}, bf16[2048,16]{1,0:T(8,128)(2,1)S(1)}, bf16[4,16,512]{2,1,0:...) custom-call(bf16[512,6144]{1,0:T(8,128)(2,1)S(1)} %copy-done.3, ...), custom_call_target="tpu_custom_call" | custom-call | flops 8388608 | bytes 67108864 | tf_op jit(solution)/shard_map/pallas_call | solution.py:1090
  136.3 3.4 copy-done.9
  139.8 13.0 %fusion.70 = f32[256,6144]{1,0:T(8,128)S(1)} fusion(bf16[256,2048]{1,0:T(8,128)(2,1)S(1)} %get-tuple-element.63.second_hbm, bf16[2048,6144]{1,0:T(8,128)(2,1)} %get-tuple-element.64), kind=kOutput, calls=%fused_computation.144 | convolution fusion | flops 6442450944 | bytes 32505856 | tf_op jit(solution)/shard_map/dot_general | solution.py:1179
  155.1 2.4 multiply_multiply_fusion
  157.6 1.9 copy.67
  159.5 2.9 copy.66
  164.0 1.5 copy-done.17
  165.7 2.3 fusion.23
  168.0 5.1 fusion.68
  173.1 3.4 convolution_convert_fusion.4
  179.7 1.6 copy.68
  184.1 14.8 %all-gather.2.cloned.1.call-done = bf16[2048,2048]{1,0:T(8,128)(2,1)} async-done(((bf16[512,2048]{1,0:T(8,128)(2,1)}), bf16[2048,2048]{1,0:T(8,128)(2,1)}) %all-gather.2.cloned.1.call-update) | async-done | bytes 8388624 | tf_op jit(solution)/shard_map/all_gather | solution.py:1169
  198.9 6.2 multiply_reduce_fusion.7
  206.7 250.9 %shard_map.222 = (bf16[2,4,256,2048]{3,2,1,0:T(8,128)(2,1)}, bf16[2,4,256,1024]{3,2,1,0:T(8,128)(2,1)}, bf16[2,4,256,2048]{3,2,1,0:T(8,128)(2,1)}, bf16[2,4,256,...) custom-call(bf16[256,2048]{1,0:T(8,128)(2,1)} %copy-done.18, ...), custom_call_target="tpu_custom_call" | custom-call | flops 103079215104 | bytes 67108864 | tf_op jit(solution)/shard_map/pallas_call | solution.py:827
  460.1 3.2 multiply_reduce_fusion.1
  463.9 17.1 %collective-permute-done = bf16[256,2048]{1,0:T(8,128)(2,1)S(1)} collective-permute-done((bf16[256,2048]{1,0:T(8,128)(2,1)}, bf16[256,2048]{1,0:T(8,128)(2,1)S(1)}, u32[]{:S(2)}, u32[]{:S(2)}) %collective-permute-start) | collective-permute-done | bytes 1048608 | tf_op jit(solution)/shard_map/ppermute | solution.py:71
  484.6 25.8 %convolution_convert_fusion = bf16[2,2048,2048]{2,1,0:T(8,128)(2,1)} fusion(bf16[2,1024,2048]{2,1,0:T(8,128)(2,1)} %bitcast.145, bf16[2,1024,2048]{2,1,0:T(8,128)(2,1)} %bitcast.146), kind=kOutput, calls=%fused_computation.2 | convolution fusion | flops 17188257792 | bytes 33554432 | tf_op jit(solution)/shard_map/erd,erf->edf/dot_general | solution.py:1259
  510.3 2.6 add_convert_fusion.2
  513.5 2.4 collective-permute-start.3
  515.9 15.4 %convolution_convert_fusion.1 = bf16[2,1024,2048]{2,1,0:T(8,128)(2,1)} fusion(bf16[2,1024,1024]{2,1,0:T(8,128)(2,1)} %bitcast.147, bf16[2,1024,2048]{2,1,0:T(8,128)(2,1)} %bitcast.144), kind=kOutput, calls=%fused_computation.4 | convolution fusion | flops 8594128896 | bytes 20971520 | tf_op jit(solution)/shard_map/erf,erd->efd/dot_general | solution.py:1270
  531.4 3.7 collective-permute-done.4
  535.1 2.6 add_convert_fusion.1
  539.2 4.0 copy.65
  543.2 1.7 fusion.72
  546.4 8.4 convolution_convert_fusion.2
  554.8 2.3 copy.69
  557.1 2.7 fusion.33
  560.8 2.4 multiply_convert_fusion
  563.2 2.2 collective-permute-start.5
  565.4 1.8 convolution_convert_fusion.3
  567.2 2.5 copy.64
  569.7 3.4 convert_add_fusion.1
  573.1 14.4 %collective-permute-done.5 = bf16[256,2048]{1,0:T(8,128)(2,1)} collective-permute-done((bf16[256,2048]{1,0:T(8,128)(2,1)}, bf16[256,2048]{1,0:T(8,128)(2,1)}, u32[]{:S(2)}, u32[]{:S(2)}) %collective-permute-start.5) | collective-permute-done | bytes 1048608 | tf_op jit(solution)/shard_map/ppermute | solution.py:71
  590.2 2.8 fusion.27
  593.0 2.9 copy.62
  595.9 3.0 copy.63
  599.0 4.7 multiply_reduce_fusion.2
  603.8 3.2 fusion.13
  607.1 14.9 %fusion.19 = (f32[2048]{0:T(1024)S(1)}, f32[256]{0:T(256)}, f32[256,2048]{1,0:T(8,128)}) fusion(bf16[256,2048]{1,0:T(8,128)(2,1)S(1)} %copy-done.2, f32[256]{0:T(256)S(1)} %fusion.59, f32[2048]{0:T(1024)S(1)} %bitcast.133, bf16[2048,6144]{1,0:T(8,128)(2,1)} %get-tuple-element.64, bf16[256,2048]{1,0:T(8,128)(2,1)S(1)} %copy-done.32, ...), kind=kOutput, calls=%fused_computation.36 | convolution fusion | flops 6455556096 | bytes 31475712 | tf_op jit(solution)/shard_map/te,de->td/dot_general | solution.py:1312
  622.8 4.1 fusion.15
  627.8 2.8 pad_maximum_fusion.grads_ref
  630.5 227.0 %shard_map.223 = (bf16[512,8192]{1,0:T(8,128)(2,1)}, f32[24,512]{1,0:T(8,128)}) custom-call(bf16[256,8192]{1,0:T(8,128)(2,1)} %pad_maximum_fusion.grads_ref, bf16[2,512,1024]{2,1,0:T(8,128)(2,1)} %bitcast.120, f32[4,24,512]{2,1,0:T(8,128)} %pad_maximum_fusion.1.small_ref), custom_call_target="tpu_custom_call" | custom-call | flops 8589934592 | bytes 16777216 | tf_op jit(solution)/shard_map/pallas_call | solution.py:311
  860.4 4.3 slice_convert_fusion.2
  864.7 3.8 add_convert_fusion
  869.4 6.4 slice_convert_fusion
  875.9 4.2 convert_element_type.146
  880.1 6.7 convert_element_type.145
  (179 shorter events, 38.4 us)
Async XLA Ops:
  7.2 191.7 %all-gather.2.cloned.1.call-start = ((), (), s32[]{:S(2)}) async-start(), calls=%async_computation.2 | async-start | bytes 10485760 | tf_op jit(solution)/shard_map/all_gather | solution.py:1169
  136.3 3.4 copy-start.9
  139.7 13.1 %copy-start.10 = (bf16[256,2048]{1,0:T(8,128)(2,1)}, bf16[256,2048]{1,0:T(8,128)(2,1)S(1)}, u32[]{:S(2)}) copy-start(bf16[256,2048]{1,0:T(8,128)(2,1)S(1)} %get-tuple-element.63.second_hbm) | copy-start | bytes 3145732
  139.7 65.6 %copy-start.4 = (bf16[2048,16]{1,0:T(8,128)(2,1)}, bf16[2048,16]{1,0:T(8,128)(2,1)S(1)}, u32[]{:S(2)}) copy-start(bf16[2048,16]{1,0:T(8,128)(2,1)S(1)} %get-tuple-element.70.router_ref) | copy-start | bytes 196612
  139.7 736.2 %reduce-scatter.5.cloned.1.call-start = ((), (), s32[]{:S(2)}) async-start(), calls=%async_computation.4 | async-start | bytes 10485760 | tf_op jit(solution)/shard_map/reduce_scatter | solution.py:1276
  152.7 4.8 copy-start.11
  153.1 4.4 copy-start.44
  153.9 3.6 copy-start.46
  159.5 4.2 copy-start.52
  173.1 3.4 copy-start.54
  179.7 19.2 %copy-start.1 = (bf16[256,2048]{1,0:T(8,128)(2,1)S(1)}, bf16[256,2048]{1,0:T(8,128)(2,1)}, u32[]{:S(2)}) copy-start(bf16[256,2048]{1,0:T(8,128)(2,1)} %tokens_ref.1) | copy-start | bytes 3145732
  206.7 253.3 %copy-start.5 = (bf16[2048,16]{1,0:T(8,128)(2,1)S(1)}, bf16[2048,16]{1,0:T(8,128)(2,1)}, u32[]{:S(2)}) copy-start(bf16[2048,16]{1,0:T(8,128)(2,1)} %copy-done.4) | copy-start | bytes 196612
  457.6 23.5 %collective-permute-start = (bf16[256,2048]{1,0:T(8,128)(2,1)}, bf16[256,2048]{1,0:T(8,128)(2,1)S(1)}, u32[]{:S(2)}, u32[]{:S(2)}) collective-permute-start(bf16[256,2048]{1,0:T(8,128)(2,1)} %get-tuple-element.75), channel_id=1, source_target_pairs={{0,4},{4,0},{8,12},{12,8},{16,20},{20,16},{24,28},{28,24},{1,5},{5... | collective-permute-start | bytes 3145736 | tf_op jit(solution)/shard_map/ppermute | solution.py:71
  460.1 3.2 copy-start.7
  460.1 3.2 copy-start.13
  463.3 17.7 %copy-start.36 = (bf16[256,2048]{1,0:T(8,128)(2,1)S(1)}, bf16[256,2048]{1,0:T(8,128)(2,1)}, u32[]{:S(2)}) copy-start(bf16[256,2048]{1,0:T(8,128)(2,1)} %get-tuple-element.74) | copy-start | bytes 3145732
  481.5 28.9 %collective-permute-start.2 = (bf16[256,2048]{1,0:T(8,128)(2,1)}, bf16[256,2048]{1,0:T(8,128)(2,1)}, u32[]{:S(2)}, u32[]{:S(2)}) collective-permute-start(bf16[256,2048]{1,0:T(8,128)(2,1)} %get-tuple-element.84), channel_id=1, source_target_pairs={{0,4},{4,0},{8,12},{12,8},{16,20},{20,16},{24,28},{28,24},{1,5},{5... | collective-permute-start | bytes 3145736 | tf_op jit(solution)/shard_map/ppermute | solution.py:71
  484.0 29.0 %collective-permute-start.1 = (bf16[128,2048]{1,0:T(8,128)(2,1)}, bf16[128,2048]{1,0:T(8,128)(2,1)}, u32[]{:S(2)}, u32[]{:S(2)}) collective-permute-start(bf16[128,2048]{1,0:T(8,128)(2,1)} %get-tuple-element.140), channel_id=1, source_target_pairs={{0,16},{4,20},{8,24},{12,28},{16,0},{20,4},{24,8},{28,12},{1,17},{... | collective-permute-start | bytes 1572872 | tf_op jit(solution)/shard_map/ppermute | solution.py:71
  484.6 25.8 %copy-start.35 = (bf16[256,2048]{1,0:T(8,128)(2,1)S(1)}, bf16[256,2048]{1,0:T(8,128)(2,1)}, u32[]{:S(2)}) copy-start(bf16[256,2048]{1,0:T(8,128)(2,1)} %get-tuple-element.83) | copy-start | bytes 3145732
  513.0 22.1 %collective-permute-start.4 = (bf16[256,2048]{1,0:T(8,128)(2,1)}, bf16[256,2048]{1,0:T(8,128)(2,1)}, u32[]{:S(2)}, u32[]{:S(2)}) collective-permute-start(bf16[256,2048]{1,0:T(8,128)(2,1)} %get-tuple-element.94), channel_id=1, source_target_pairs={{0,4},{4,0},{8,12},{12,8},{16,20},{20,16},{24,28},{28,24},{1,5},{5... | collective-permute-start | bytes 3145736 | tf_op jit(solution)/shard_map/ppermute | solution.py:71
  513.5 24.1 %collective-permute-start.3 = (bf16[128,2048]{1,0:T(8,128)(2,1)}, bf16[128,2048]{1,0:T(8,128)(2,1)}, u32[]{:S(2)}, u32[]{:S(2)}) collective-permute-start(bf16[128,2048]{1,0:T(8,128)(2,1)} %get-tuple-element.91), channel_id=1, source_target_pairs={{0,16},{4,20},{8,24},{12,28},{16,0},{20,4},{24,8},{28,12},{1,17},{... | collective-permute-start | bytes 1572872 | tf_op jit(solution)/shard_map/ppermute | solution.py:71
  515.9 19.1 %copy-start.34 = (bf16[256,2048]{1,0:T(8,128)(2,1)S(1)}, bf16[256,2048]{1,0:T(8,128)(2,1)}, u32[]{:S(2)}) copy-start(bf16[256,2048]{1,0:T(8,128)(2,1)} %get-tuple-element.93) | copy-start | bytes 3145732
  537.7 342.4 %reduce-scatter.3.cloned.1.call-start = ((), (), s32[]{:S(2)}) async-start(), calls=%async_computation.3 | async-start | bytes 20971520 | tf_op jit(solution)/shard_map/reduce_scatter | solution.py:1265
  545.0 24.7 %collective-permute-start.6 = (bf16[256,2048]{1,0:T(8,128)(2,1)}, bf16[256,2048]{1,0:T(8,128)(2,1)}, u32[]{:S(2)}, u32[]{:S(2)}) collective-permute-start(bf16[256,2048]{1,0:T(8,128)(2,1)} %get-tuple-element.100), channel_id=1, source_target_pairs={{0,4},{4,0},{8,12},{12,8},{16,20},{20,16},{24,28},{28,24},{1,5},{5... | collective-permute-start | bytes 3145736 | tf_op jit(solution)/shard_map/ppermute | solution.py:71
  557.1 3.7 copy-start.53
  557.1 3.7 copy-start.55
  560.8 4.6 copy-start.23
  563.2 24.4 %collective-permute-start.5 = (bf16[256,2048]{1,0:T(8,128)(2,1)}, bf16[256,2048]{1,0:T(8,128)(2,1)}, u32[]{:S(2)}, u32[]{:S(2)}) collective-permute-start(bf16[256,2048]{1,0:T(8,128)(2,1)} %add_convert_fusion.2), channel_id=1, source_target_pairs={{0,24},{4,28},{8,0},{12,4},{16,8},{20,12},{24,16},{28,20},{1,25},{... | collective-permute-start | bytes 3145736 | tf_op jit(solution)/shard_map/ppermute | solution.py:71
  569.7 17.9 %copy-start.21 = (bf16[16,256,256]{1,2,0:T(8,128)(2,1)S(1)}, bf16[16,256,256]{1,2,0:T(8,128)(2,1)}, u32[]{:S(2)}) copy-start(bf16[16,256,256]{1,2,0:T(8,128)(2,1)} %multiply_convert_fusion) | copy-start | bytes 6291460
  569.7 17.9 %copy-start.25 = (bf16[256,16,128]{0,2,1:T(8,128)(2,1)S(1)}, bf16[256,16,128]{0,2,1:T(8,128)(2,1)}, u32[]{:S(2)}) copy-start(bf16[256,16,128]{0,2,1:T(8,128)(2,1)} %get-tuple-element.142) | copy-start | bytes 3145732
  573.1 15.3 %copy-start.24 = (bf16[256,16,128]{0,2,1:T(8,128)(2,1)S(1)}, bf16[256,16,128]{0,2,1:T(8,128)(2,1)}, u32[]{:S(2)}) copy-start(bf16[256,16,128]{0,2,1:T(8,128)(2,1)} %get-tuple-element.141) | copy-start | bytes 3145732
  573.1 15.3 %copy-start.38 = (f32[256,128]{0,1:T(8,128)S(1)}, f32[256,128]{0,1:T(8,128)}, u32[]{:S(2)}) copy-start(f32[256,128]{0,1:T(8,128)} %get-tuple-element.156) | copy-start | bytes 393220
  598.9 4.8 copy-start.49
  598.9 4.8 copy-start.51
  598.9 4.9 copy-start.15
  598.9 4.9 copy-start.16
  598.9 31.6 %collective-permute-start.7 = (bf16[256,2048]{1,0:T(8,128)(2,1)}, bf16[256,2048]{1,0:T(8,128)(2,1)}, u32[]{:S(2)}, u32[]{:S(2)}) collective-permute-start(bf16[256,2048]{1,0:T(8,128)(2,1)} %add_convert_fusion.1), channel_id=1, source_target_pairs={{0,8},{4,12},{8,16},{12,20},{16,24},{20,28},{24,0},{28,4},{1,9},{5... | collective-permute-start | bytes 3145736 | tf_op jit(solution)/shard_map/ppermute | solution.py:71
  603.8 3.3 copy-start.32
  603.8 3.3 copy-start.43
  607.0 14.9 %copy-start.28 = (bf16[256,2048]{1,0:T(8,128)(2,1)}, bf16[256,2048]{1,0:T(8,128)(2,1)S(1)}, u32[]{:S(2)}) copy-start(bf16[256,2048]{1,0:T(8,128)(2,1)S(1)} %get-tuple-element.127) | copy-start | bytes 3145732
  607.0 14.9 %copy-start.30 = (bf16[256,2048]{1,0:T(8,128)(2,1)}, bf16[256,2048]{1,0:T(8,128)(2,1)S(1)}, u32[]{:S(2)}) copy-start(bf16[256,2048]{1,0:T(8,128)(2,1)S(1)} %get-tuple-element.128) | copy-start | bytes 3145732
  622.8 4.9 copy-start.27
  622.8 4.9 copy-start.29
  622.8 4.8 copy-start.31
  622.8 5.0 copy-start.33
  860.4 4.3 copy-start.14
  860.4 4.3 copy-start.20
  864.7 4.7 copy-start.19
  (19 other events, 33.9 us)
Sparse Core Ops, SparseCore 0:
  139.8 59.0 all-gather.1
  537.8 70.1 reduce-scatter.4
  610.7 210.3 reduce-scatter.2

commit v8 on v7

--- a/solution.py
+++ b/solution.py
@@ -351,7 +351,8 @@
 
 def moe_kernel(
     dims, hidden_hbm, upstream_hbm, place_ref, place_t_ref, router_ref, router_t_ref, gate_up_hbm, down_hbm,
-    first_hbm, second_hbm, rows_hbm, activated_hbm, grad_out_hbm, grad_gate_up_hbm, grad_ref, grad_router_ref, columns_hbm, found_hbm, summed_hbm,
+    first_hbm, second_hbm, rows_hbm, activated_hbm, grad_out_hbm, grad_gate_up_hbm, grad_ref, grad_router_ref, columns_hbm, grad_up_w_hbm, grad_down_w_hbm,
+    came_hbm, found_hbm, summed_hbm,
     *rest,
 ):
     x_all, capacity, y_all = dims
@@ -359,7 +360,7 @@
     (
     gate_up_w, down_w, hid, ups, prob, prob_t, rows, gate_up, activated, out_rows, grad_expert, grad_gate_up, grad_rows,
     mix_stage, part_stage, own_part, z_landed, router_stage,
-    w_sem, own_sem, load_sem, store_sem, zs, zr, xs, xr, fs, fr, ps, pr, qs, qr, rs, rr, lsem, mix_sem, cs, cr, own_c,
+    w_sem, own_sem, load_sem, store_sem, zs, zr, xs, xr, fs, fr, ps, pr, qs, qr, rs, rr, lsem, mix_sem, cs, cr, own_c, back_sem, out_sem, ms, mr,
     ) = rest[4 * x_all :]
     z_all = 4
     f32, bf16 = jnp.float32, jnp.bfloat16
@@ -369,6 +370,7 @@
     tile = min(512, half)
     narrow = min(256, half)
     chunk = length // MOE_CHUNKS
+    count = x_all * capacity
     e = lax.axis_index("expert")
     z, x = e // x_all, lax.rem(e, x_all)
 
@@ -405,6 +407,12 @@
     def p_sent(dx):
         whole = part_stage.at[dx - 1]
         copy(whole, whole, ps.at[dx - 1], pr.at[0, dx - 1, 0], peer(0, -dx)).wait_send()
+
+    def m_copy(dz, dx):
+        return copy(
+            mixture_hbm[dz * x_all + dx], came_hbm.at[dz - 1, dx - 1],
+            ms.at[dz - 1, dx - 1], mr.at[dz - 1, dx - 1], peer(0, -dx),
+        )
 
     def q_copy(dz, c):
         return copy(
@@ -509,8 +517,6 @@
         def arrive(c, carry):
             p_copy(dz, dx, c).wait_recv()
             load(c).start()
-            if last:
-                add(c)
             return carry
 
         def rest(c, carry):
@@ -519,8 +525,7 @@
 
         for dx in range(1, x_all):
             lax.fori_loop(0, MOE_CHUNKS, arrive, 0)
-            if not last:
-                lax.fori_loop(0, MOE_CHUNKS, rest, 0)
+            lax.fori_loop(0, MOE_CHUNKS, rest, 0)
 
     mix_slots = mix_stage.shape[0]
 
@@ -699,6 +704,12 @@
                 for dx in range(mix_slots):
                     mix_copy(0, dx).wait()
                 finish(group_at(g - 1), False)
+
+                @pl.when(g == z_all - 1)
+                def _():
+                    for k in (2, 1):
+                        for dx in range(1, x_all):
+                            m_copy(k, dx).start()
 
             return inner
 
@@ -765,6 +776,76 @@
         return carry
 
     lax.fori_loop(0, z_all, group, 0)
+    for kind, buffer, hbm in (
+        (0, rows, rows_hbm), (1, activated, activated_hbm), (2, grad_expert, grad_out_hbm),
+        (3, grad_gate_up, grad_gate_up_hbm),
+    ):
+        pltpu.make_async_copy(buffer, hbm.at[0, 0], store_sem.at[kind]).wait()
+
+    high_all = z_all * count
+    kinds = []
+    spots = ((hid.at[0], hid.at[1]), (rows, grad_expert))
+    for le in range(local_experts):
+        for dz in range(z_all):
+            keeper = spots[le][dz // 2]
+            r = slice(dz * count, (dz + 1) * count)
+            kinds += [
+                (rows_hbm.at[le, dz], gate_up_w.at[le, r]),
+                (grad_gate_up_hbm.at[le, dz], gate_up_w.at[le, slice(high_all + dz * count, high_all + (dz + 1) * count)]),
+                (grad_out_hbm.at[le, dz], down_w.at[le, r]),
+                (activated_hbm.at[le, dz], keeper.at[:, slice((dz % 2) * half, (dz % 2 + 1) * half)]),
+            ]
+    backs = [pltpu.make_async_copy(a, b, back_sem.at[n]) for n, (a, b) in enumerate(kinds)]
+    for b in backs:
+        b.start()
+    contract = (((0,), (0,)), ((), ()))
+
+    def out_copy(slot, hbm, le, m):
+        return pltpu.make_async_copy(
+            ups.at[slot], hbm.at[le, pl.ds(pl.multiple_of(m * length, length), length)], out_sem.at[slot]
+        )
+
+    for le in range(local_experts):
+        for b in backs[4 * z_all * le : 4 * z_all * (le + 1)]:
+            b.wait()
+
+        def up_weight(m, carry):
+            slot = lax.rem(m, 2)
+            if le == 0:
+                pl.when(m > 1)(out_copy(slot, grad_up_w_hbm, le, m).wait)
+            else:
+                out_copy(slot, grad_up_w_hbm, le, m).wait()
+            left = gate_up_w[le, :high_all, cols(m, length)]
+            for n in range(twice // tile):
+                c = slice(n * tile, (n + 1) * tile)
+                ups[slot, :, c] = lax.dot_general(
+                    left, gate_up_w[le, high_all : 2 * high_all, c], contract, preferred_element_type=f32
+                ).astype(bf16)
+            out_copy(slot, grad_up_w_hbm, le, m).start()
+            return carry
+
+        lax.fori_loop(0, width // length, up_weight, 0)
+
+        def down_weight(m, carry):
+            slot = lax.rem(m, 2)
+            out_copy(slot, grad_down_w_hbm, le, m).wait()
+            for n in range(width // tile):
+                c = slice(n * tile, (n + 1) * tile)
+                total = jnp.zeros((length, tile), f32)
+                for dz in range(z_all):
+                    left = spots[le][dz // 2][
+                        :, pl.ds(pl.multiple_of((dz % 2) * half + m * length, length), length)
+                    ]
+                    total = total + lax.dot_general(
+                        left, down_w[le, dz * count : (dz + 1) * count, c], contract, preferred_element_type=f32
+                    )
+                ups[slot, :, c] = total.astype(bf16)
+            out_copy(slot, grad_down_w_hbm, le, m).start()
+            return carry
+
+        lax.fori_loop(0, half // length, down_weight, 0)
+    for slot in range(2):
+        out_copy(slot, grad_down_w_hbm, 0, 0).wait()
     for dx in range(mix_slots):
         mix_copy(0, dx).wait()
     finish(0, True)
@@ -778,13 +859,11 @@
 
     lax.fori_loop(0, MOE_CHUNKS, total, 0)
 
+    for k in (2, 1):
+        for dx in range(1, x_all):
+            m_copy(k, dx).wait()
     for c in column_copies:
         c.wait()
-    for kind, buffer, hbm in (
-        (0, rows, rows_hbm), (1, activated, activated_hbm), (2, grad_expert, grad_out_hbm),
-        (3, grad_gate_up, grad_gate_up_hbm),
-    ):
-        pltpu.make_async_copy(buffer, hbm.at[0, 0], store_sem.at[kind]).wait()
     for dx in range(1, x_all):
         p_sent(dx)
     for d in range(1, z_all):
@@ -834,12 +913,15 @@
             jax.ShapeDtypeStruct((length, width), f32),
             jax.ShapeDtypeStruct((expert_group, 8, length), f32),
             jax.ShapeDtypeStruct((2, shard_group, length, width // shard_group), bf16),
+            jax.ShapeDtypeStruct(gate_up_weight.shape, bf16),
+            jax.ShapeDtypeStruct(down_weight.shape, bf16),
+            jax.ShapeDtypeStruct((2, x1, length, width), bf16),
             jax.ShapeDtypeStruct((4, x_all, length, width), bf16),
             jax.ShapeDtypeStruct((4, x1, length, width), bf16),
         ]
         + [jax.ShapeDtypeStruct((length, width), bf16)] * (4 * x_all),
         in_specs=[any_spec, any_spec, vmem_spec, vmem_spec, vmem_spec, vmem_spec, any_spec, any_spec, any_spec, any_spec],
-        out_specs=[any_spec] * 4 + [vmem_spec, vmem_spec] + [any_spec] * (3 + 4 * x_all),
+        out_specs=[any_spec] * 4 + [vmem_spec, vmem_spec] + [any_spec] * (6 + 4 * x_all),
         scratch_shapes=[
             pltpu.VMEM(gate_up_weight.shape, bf16),
             pltpu.VMEM(down_weight.shape, bf16),
@@ -868,6 +950,8 @@
             dma((4, x_all)), dma((4, x_all)),
             dma((MOE_CHUNKS,)), dma((min(2, x_all),)),
             dma((2, shard_group - 1)), dma((2, shard_group - 1)), dma((2,)),
+            dma((16 * local_experts,)), dma((2,)),
+            dma((2, x1)), dma((2, x1)),
         ],
         compiler_params=pltpu.CompilerParams(
             collective_id=name_id, has_side_effects=True, vmem_limit_bytes=62 * 1024 * 1024
@@ -880,7 +964,7 @@
         hidden, upstream_all, place, place_t, router_weight, router_weight.T, gate_up_weight, down_weight,
         first, second,
     )
-    return out[:7], out[9:]
+    return out[4:10], out[12:]
 
 
 def start_kernel(
@@ -1211,7 +1295,6 @@
     scaled_two, second_pull = jax.vjp(rms_scale, middle, gain_two)
     hidden_two = scaled_two.astype(bf16)
     router = softmax_rows(jnp.dot(hidden_two, router_full, preferred_element_type=f32))
-    row_count = expert_group * capacity
     done, mixture_parts = moe_layer(
         hidden_two,
         upstream_all,
@@ -1226,12 +1309,16 @@
         capacity,
         2,
     )
-    columns = done[6].reshape(2, shard_group * length, -1).swapaxes(1, 2)
-    expert_rows, activated, grad_expert, grad_gate_up_low = (
-        a.reshape(local_experts, row_count, a.shape[-1]) for a in done[:4]
-    )
-    grad_rows_sum = done[4]
-    grad_router = done[5][:, :local_experts].reshape(experts_all, length).T
+    grad_rows_sum, grad_router, columns, grad_gate_up_full, grad_down_full, came = done
+    columns = columns.reshape(2, shard_group * length, -1).swapaxes(1, 2)
+    grad_router = grad_router[:, :local_experts].reshape(experts_all, length).T
+    grad_gate_up_weight = lax.psum_scatter(
+        grad_gate_up_full, "shard", scatter_dimension=1, tiled=True
+    ).astype(f32)
+    grad_down_weight = lax.psum_scatter(
+        grad_down_full, "shard", scatter_dimension=2, tiled=True
+    ).astype(f32)
+
     parts = dict(enumerate(mixture_parts))
 
     def slot(values, *names):
@@ -1251,32 +1338,15 @@
     )
     grad_middle_norm, grad_gain_two = second_pull(grad_hidden_two)
     grad_middle = upstream + grad_middle_norm
-    two = sum_over_x(parts, 2, expert_group).astype(bf16)
-    grad_middle, expert_rows, two = slot((grad_middle, expert_rows, two), *group(1))
+    two, one = (
+        (mixture_parts[dz * x_all].astype(f32) + jnp.sum(came[dz - 1].astype(f32), axis=0)).astype(bf16)
+        for dz in (2, 1)
+    )
     halves = [two[: length // 2], two[length // 2 :]]
     halves[0] = back_along_z(halves[0], 2, expert_group)
-    one = sum_over_x(parts, 1, expert_group).astype(bf16)
-    grad_gate_up_full = jnp.einsum(
-        "erd,erf->edf", expert_rows, grad_gate_up_low, preferred_element_type=f32
-    ).astype(bf16)
-    grad_middle, grad_gate_up_full, activated, halves, one = slot(
-        (grad_middle, grad_gate_up_full, activated, halves, one), *group(3)
-    )
-    grad_gate_up_weight = lax.psum_scatter(
-        grad_gate_up_full, "shard", scatter_dimension=1, tiled=True
-    ).astype(f32)
+    three = sum_over_x(parts, 3, expert_group).astype(bf16)
+    grad_middle, halves, three = slot((grad_middle, halves, three), *group(0))
     halves[1] = back_along_z(halves[1], 2, expert_group)
-    three = sum_over_x(parts, 3, expert_group).astype(bf16)
-    grad_down_full = jnp.einsum(
-        "erf,erd->efd", activated, grad_expert, preferred_element_type=f32
-    ).astype(bf16)
-    grad_middle, grad_down_full, halves, one, three = slot(
-        (grad_middle, grad_down_full, halves, one, three), *group(0)
-    )
-    grad_down_weight = lax.psum_scatter(
-        grad_down_full, "shard", scatter_dimension=2, tiled=True
-    ).astype(f32)
-    one = back_along_z(one, 1, expert_group)
     here = sum_over_x(parts, 0, expert_group)
     grad_branch_low = grad_middle.astype(bf16)
     grad_attended_low = (
@@ -1284,13 +1354,15 @@
         .astype(bf16)
         .reshape(length, HEADS, HEAD_DIM)
     )
+    grad_attended_low, halves, one, here = slot((grad_attended_low, halves, one, here))
+    one = back_along_z(one, 1, expert_group)
     grad_probs = jnp.einsum(
         "qhd,khd->hqk", grad_attended_low, value_low, preferred_element_type=f32
     )
     grad_scores_low = (
         probs * (grad_probs - jnp.sum(probs * grad_probs, axis=-1, keepdims=True))
     ).astype(bf16)
-    grad_scores_low, one, here, three = slot((grad_scores_low, one, here, three))
+    grad_scores_low, one, three = slot((grad_scores_low, one, three))
     three = back_along_z(three, 3, expert_group)
     grad_queries = (
         jnp.einsum("hqk,khd->qhd", grad_scores_low, key_low, preferred_element_type=f32)

time: 905 us -> 913 us (level)
  matrix products: 103 us -> 58.6 us
  Pallas kernels: 597 us -> 638 us
  waiting for transfers between devices: 50.7 us -> 69.9 us
    dot_general x2 -> x0, matrix products: 41.2 us -> none  [the longest x1 25.8 us: body(): jnp.einsum('erd,erf->edf', expert_rows, grad_gate_up_low, preferred_eleme...]
    pallas_call x1, Pallas kernels: 251 us -> 285 us  [moe_layer(): pl.pallas_call(functools.partial(moe_kernel, (x_all, capacity, shard_grou...]
    ppermute x8 -> x6, waiting for transfers between devices: 35.2 us -> 56 us  [shift(): return lax.ppermute(values, 'expert', pairs)]
    unnamed x114 -> x123, local copies, waits for them, and re-layouts: 19.4 us -> 20.8 us
  transfers between devices with their start and end apart: 11 -> 9, of which waited for: 4 -> 5; matrix products, arithmetic and copies ran while one was open for 21% -> 15% of each run, Pallas kernels for 25% -> 26%
where the time goes in v8:
time: 913 us; the launch traced here: 903 us
  Pallas kernels  638 us (70%)
  waiting for transfers between devices  69.9 us (8%)
  other arithmetic  59.1 us (6%)
  matrix products  58.6 us (6%)
  local copies, waits for them, and re-layouts  54 us (6%)
  between operations  14.8 us (2%)
    pallas_call x1, Pallas kernels, moe_layer(): pl.pallas_call(functools.partial(moe_kernel, (x_all, capacity, shard_grou...  285 us
    pallas_call x1, Pallas kernels, summed_rows(): pl.pallas_call(functools.partial(tail_kernel, (steps, width, x_all, z_all...  234 us
    pallas_call x1, Pallas kernels, start_layer(): pl.pallas_call(functools.partial(start_kernel, (x_all, y_all)), out_shape...  119 us
    ppermute x6, waiting for transfers between devices, shift(): return lax.ppermute(values, 'expert', pairs)  56 us
    unnamed x123, local copies, waits for them, and re-layouts  20.8 us
  transfers between devices with their start and end apart: 9, of which 5 were waited for; matrix products, arithmetic and copies ran while one was open for 15% of the time, Pallas kernels for 26%

profile of v8, /device:TPU:0, one launch (start us, length us, event | category | flops | bytes accessed | tf_op | source)
XLA Modules:
  0.0 902.7 jit_solution(11280069165571031335)
XLA Ops:
  12.8 2.8 copy-done.2
  17.5 118.8 %shard_map.221 = (bf16[2048,6144]{1,0:T(8,128)(2,1)}, bf16[4,2,256,2048]{3,2,1,0:T(8,128)(2,1)S(1)}, bf16[2048,16]{1,0:T(8,128)(2,1)S(1)}, bf16[4,16,512]{2,1,0:...) custom-call(bf16[512,6144]{1,0:T(8,128)(2,1)S(1)} %copy-done.2, ...), custom_call_target="tpu_custom_call" | custom-call | flops 8388608 | bytes 67108864 | tf_op jit(solution)/shard_map/pallas_call | solution.py:1174
  136.3 3.4 copy-done.8
  139.8 13.0 %fusion.73 = f32[256,6144]{1,0:T(8,128)S(1)} fusion(bf16[256,2048]{1,0:T(8,128)(2,1)S(1)} %get-tuple-element.49.second_hbm, bf16[2048,6144]{1,0:T(8,128)(2,1)} %get-tuple-element.50), kind=kOutput, calls=%fused_computation.145 | convolution fusion | flops 6442450944 | bytes 32505856 | tf_op jit(solution)/shard_map/dot_general | solution.py:1263
  155.2 2.4 multiply_multiply_fusion
  157.6 1.9 copy.63
  159.5 2.9 copy.62
  163.7 2.6 constant_dynamic-slice_fusion
  166.3 1.6 copy.64
  170.2 1.4 copy-done.18
  171.8 2.0 fusion.23
  173.8 5.1 fusion.71
  178.9 3.4 convolution_convert_fusion.2
  182.4 1.4 copy.57.first_hbm
  185.7 13.2 %all-gather.2.cloned.1.call-done = bf16[2048,2048]{1,0:T(8,128)(2,1)} async-done(((bf16[512,2048]{1,0:T(8,128)(2,1)}), bf16[2048,2048]{1,0:T(8,128)(2,1)}) %all-gather.2.cloned.1.call-update) | async-done | bytes 8388624 | tf_op jit(solution)/shard_map/all_gather | solution.py:1253
  198.9 5.8 multiply_reduce_fusion.7
  207.2 285.3 %shard_map.222 = (bf16[2,4,256,2048]{3,2,1,0:T(8,128)(2,1)}, bf16[2,4,256,1024]{3,2,1,0:T(8,128)(2,1)}, bf16[2,4,256,2048]{3,2,1,0:T(8,128)(2,1)}, bf16[2,4,256,...) custom-call(bf16[256,2048]{1,0:T(8,128)(2,1)} %multiply_convert_fusi, ...), custom_call_target="tpu_custom_call" | custom-call | flops 103079215104 | bytes 67108864 | tf_op jit(solution)/shard_map/pallas_call | solution.py:906
  494.5 3.6 fusion.24
  499.4 1.5 collective-permute-start.1
  503.4 18.9 %collective-permute-done.1 = bf16[256,2048]{1,0:T(8,128)(2,1)S(1)} collective-permute-done((bf16[256,2048]{1,0:T(8,128)(2,1)S(1)}, bf16[256,2048]{1,0:T(8,128)(2,1)S(1)}, u32[]{:S(2)}, u32[]{:S(2)}) %collective-permute-start.1) | collective-permute-done | bytes 1048608 | tf_op jit(solution)/shard_map/ppermute | solution.py:71
  523.7 1.4 collective-permute-start.3
  525.1 4.0 copy.61
  529.1 1.5 fusion.75
  530.8 6.1 fusion.33
  538.0 2.4 collective-permute-start.2
  540.3 8.0 collective-permute-done.3
  548.4 2.9 convert_add_fusion.3
  551.3 10.0 %collective-permute-done.2 = bf16[128,2048]{1,0:T(8,128)(2,1)S(1)} collective-permute-done((bf16[128,2048]{1,0:T(8,128)(2,1)S(1)}, bf16[128,2048]{1,0:T(8,128)(2,1)S(1)}, u32[]{:S(2)}, u32[]{:S(2)}) %collective-permute-start.2) | collective-permute-done | bytes 524320 | tf_op jit(solution)/shard_map/ppermute | solution.py:71
  562.8 3.0 convolution_convert_fusion.1
  565.9 1.4 copy.60
  567.3 2.6 collective-permute-start.4
  569.9 2.7 fusion.36
  573.7 19.1 %collective-permute-done.4 = bf16[256,2048]{1,0:T(8,128)(2,1)S(1)} collective-permute-done((bf16[256,2048]{1,0:T(8,128)(2,1)}, bf16[256,2048]{1,0:T(8,128)(2,1)S(1)}, u32[]{:S(2)}, u32[]{:S(2)}) %collective-permute-start.4) | collective-permute-done | bytes 1048608 | tf_op jit(solution)/shard_map/ppermute | solution.py:71
  595.6 2.0 fusion.29
  597.6 1.8 copy.58
  599.4 3.0 copy.59
  602.7 4.7 multiply_reduce_fusion.2
  608.7 2.2 fusion.13
  610.9 15.0 %fusion.19 = (f32[2048]{0:T(1024)S(1)}, f32[256]{0:T(256)}, f32[256,2048]{1,0:T(8,128)}) fusion(bf16[256,2048]{1,0:T(8,128)(2,1)S(1)} %copy-done.1, f32[256]{0:T(256)S(1)} %fusion.62, f32[2048]{0:T(1024)S(1)} %bitcast.134, bf16[2048,6144]{1,0:T(8,128)(2,1)} %get-tuple-element.50, bf16[256,2048]{1,0:T(8,128)(2,1)} %copy.60, ...), kind=kOutput, calls=%fused_computation.34 | convolution fusion | flops 6455556096 | bytes 31475712 | tf_op jit(solution)/shard_map/te,de->td/dot_general | solution.py:1384
  626.8 3.6 fusion.15
  631.1 2.2 pad_maximum_fusion.grads_ref
  633.3 233.8 %shard_map.223 = (bf16[512,8192]{1,0:T(8,128)(2,1)}, f32[24,512]{1,0:T(8,128)}) custom-call(bf16[256,8192]{1,0:T(8,128)(2,1)} %pad_maximum_fusion.grads_ref, bf16[2,512,1024]{2,1,0:T(8,128)(2,1)} %bitcast.121, f32[4,24,512]{2,1,0:T(8,128)} %pad_maximum_fusion.1.small_ref), custom_call_target="tpu_custom_call" | custom-call | flops 8589934592 | bytes 16777216 | tf_op jit(solution)/shard_map/pallas_call | solution.py:311
  867.1 1.5 fusion.70
  870.0 4.3 slice_convert_fusion.2
  874.3 3.3 add_convert_fusion
  878.5 6.4 slice_convert_fusion
  884.9 4.2 convert_element_type.152
  889.1 6.7 convert_element_type.151
  (182 shorter events, 37.1 us)
Async XLA Ops:
  7.2 191.7 %all-gather.2.cloned.1.call-start = ((), (), s32[]{:S(2)}) async-start(), calls=%async_computation.2 | async-start | bytes 10485760 | tf_op jit(solution)/shard_map/all_gather | solution.py:1253
  136.3 3.4 copy-start.8
  139.7 13.1 %copy-start.9 = (bf16[256,2048]{1,0:T(8,128)(2,1)}, bf16[256,2048]{1,0:T(8,128)(2,1)S(1)}, u32[]{:S(2)}) copy-start(bf16[256,2048]{1,0:T(8,128)(2,1)S(1)} %get-tuple-element.49.second_hbm) | copy-start | bytes 3145732
  139.7 28.1 %copy-start.3 = (bf16[2048,16]{1,0:T(8,128)(2,1)}, bf16[2048,16]{1,0:T(8,128)(2,1)S(1)}, u32[]{:S(2)}) copy-start(bf16[2048,16]{1,0:T(8,128)(2,1)S(1)} %get-tuple-element.56.router_ref) | copy-start | bytes 196612
  139.7 745.2 %reduce-scatter.5.cloned.1.call-start = ((), (), s32[]{:S(2)}) async-start(), calls=%async_computation.4 | async-start | bytes 10485760 | tf_op jit(solution)/shard_map/reduce_scatter | solution.py:1318
  152.7 4.8 copy-start.10
  153.1 4.4 copy-start.47
  153.9 3.6 copy-start.49
  163.7 6.2 copy-start.55
  173.8 5.1 copy-start.23
  182.3 16.5 %copy-start.1 = (bf16[256,2048]{1,0:T(8,128)(2,1)S(1)}, bf16[256,2048]{1,0:T(8,128)(2,1)}, u32[]{:S(2)}) copy-start(bf16[256,2048]{1,0:T(8,128)(2,1)} %tokens_ref.1) | copy-start | bytes 3145732
  492.6 396.5 %reduce-scatter.3.cloned.1.call-start = ((), (), s32[]{:S(2)}) async-start(), calls=%async_computation.3 | async-start | bytes 20971520 | tf_op jit(solution)/shard_map/reduce_scatter | solution.py:1315
  494.5 4.9 copy-start.56
  494.5 6.4 copy-start.20
  494.5 6.9 copy-start.31
  499.1 24.6 %collective-permute-start = (bf16[128,2048]{1,0:T(8,128)(2,1)S(1)}, bf16[128,2048]{1,0:T(8,128)(2,1)}, u32[]{:S(2)}, u32[]{:S(2)}) collective-permute-start(bf16[128,2048]{1,0:T(8,128)(2,1)S(1)} %get-tuple-element.114), channel_id=1, source_target_pairs={{0,16},{4,20},{8,24},{12,28},{16,0},{20,4},{24,8},{28,12},{1,17},{... | collective-permute-start | bytes 1572872 | tf_op jit(solution)/shard_map/ppermute | solution.py:71
  499.4 22.9 %collective-permute-start.1 = (bf16[256,2048]{1,0:T(8,128)(2,1)S(1)}, bf16[256,2048]{1,0:T(8,128)(2,1)S(1)}, u32[]{:S(2)}, u32[]{:S(2)}) collective-permute-start(bf16[256,2048]{1,0:T(8,128)(2,1)S(1)} %copy-done.56), channel_id=1, source_target_pairs={{0,4},{4,0},{8,12},{12,8},{16,20},{20,16},{24,28},{28,24},{1,5},{5... | collective-permute-start | bytes 3145736 | tf_op jit(solution)/shard_map/ppermute | solution.py:71
  502.8 19.5 %copy-start.33 = (bf16[256,2048]{1,0:T(8,128)(2,1)S(1)}, bf16[256,2048]{1,0:T(8,128)(2,1)}, u32[]{:S(2)}) copy-start(bf16[256,2048]{1,0:T(8,128)(2,1)} %get-tuple-element.61) | copy-start | bytes 3145732
  503.4 27.2 %copy-start.14 = (f32[256,2048]{1,0:T(8,128)}, f32[256,2048]{1,0:T(8,128)S(1)}, u32[]{:S(2)}) copy-start(f32[256,2048]{1,0:T(8,128)S(1)} %fusion.12) | copy-start | bytes 6291460
  523.7 24.7 %collective-permute-start.3 = (bf16[256,2048]{1,0:T(8,128)(2,1)}, bf16[256,2048]{1,0:T(8,128)(2,1)}, u32[]{:S(2)}, u32[]{:S(2)}) collective-permute-start(bf16[256,2048]{1,0:T(8,128)(2,1)} %get-tuple-element.70), channel_id=1, source_target_pairs={{0,4},{4,0},{8,12},{12,8},{16,20},{20,16},{24,28},{28,24},{1,5},{5... | collective-permute-start | bytes 3145736 | tf_op jit(solution)/shard_map/ppermute | solution.py:71
  530.8 6.1 copy-start.26
  536.9 11.4 %copy-start.34 = (bf16[256,2048]{1,0:T(8,128)(2,1)S(1)}, bf16[256,2048]{1,0:T(8,128)(2,1)}, u32[]{:S(2)}) copy-start(bf16[256,2048]{1,0:T(8,128)(2,1)} %get-tuple-element.69) | copy-start | bytes 3145732
  538.0 23.3 %collective-permute-start.2 = (bf16[128,2048]{1,0:T(8,128)(2,1)S(1)}, bf16[128,2048]{1,0:T(8,128)(2,1)S(1)}, u32[]{:S(2)}, u32[]{:S(2)}) collective-permute-start(bf16[128,2048]{1,0:T(8,128)(2,1)S(1)} %copy-done.41), channel_id=1, source_target_pairs={{0,16},{4,20},{8,24},{12,28},{16,0},{20,4},{24,8},{28,12},{1,17},{... | collective-permute-start | bytes 1572872 | tf_op jit(solution)/shard_map/ppermute | solution.py:71
  567.3 5.3 copy-start.57
  567.3 25.5 %collective-permute-start.4 = (bf16[256,2048]{1,0:T(8,128)(2,1)}, bf16[256,2048]{1,0:T(8,128)(2,1)S(1)}, u32[]{:S(2)}, u32[]{:S(2)}) collective-permute-start(bf16[256,2048]{1,0:T(8,128)(2,1)} %get-tuple-element.73), channel_id=1, source_target_pairs={{0,24},{4,28},{8,0},{12,4},{16,8},{20,12},{24,16},{28,20},{1,25},{... | collective-permute-start | bytes 3145736 | tf_op jit(solution)/shard_map/ppermute | solution.py:71
  572.6 20.2 %copy-start.25 = (bf16[256,16,128]{0,2,1:T(8,128)(2,1)S(1)}, bf16[256,16,128]{0,2,1:T(8,128)(2,1)}, u32[]{:S(2)}) copy-start(bf16[256,16,128]{0,2,1:T(8,128)(2,1)} %get-tuple-element.116) | copy-start | bytes 3145732
  573.6 20.1 %copy-start.24 = (bf16[256,16,128]{0,2,1:T(8,128)(2,1)S(1)}, bf16[256,16,128]{0,2,1:T(8,128)(2,1)}, u32[]{:S(2)}) copy-start(bf16[256,16,128]{0,2,1:T(8,128)(2,1)} %copy-done.23) | copy-start | bytes 3145732
  573.6 20.1 %copy-start.38 = (f32[256,128]{0,1:T(8,128)S(1)}, f32[256,128]{0,1:T(8,128)}, u32[]{:S(2)}) copy-start(f32[256,128]{0,1:T(8,128)} %get-tuple-element.130) | copy-start | bytes 393220
  599.4 3.2 copy-start.45
  599.4 3.2 copy-start.48
  599.4 3.2 copy-start.50
  599.4 8.0 slice-start
  602.5 4.9 copy-start.52
  602.5 4.9 copy-start.54
  602.5 4.9 slice-start.1
  602.5 5.5 copy-start.16
  602.5 6.2 copy-start.17
  602.5 30.8 %collective-permute-start.5 = (bf16[256,2048]{1,0:T(8,128)(2,1)}, bf16[256,2048]{1,0:T(8,128)(2,1)}, u32[]{:S(2)}, u32[]{:S(2)}) collective-permute-start(bf16[256,2048]{1,0:T(8,128)(2,1)} %add_convert_fusion.1), channel_id=1, source_target_pairs={{0,8},{4,12},{8,16},{12,20},{16,24},{20,28},{24,0},{28,4},{1,9},{5... | collective-permute-start | bytes 3145736 | tf_op jit(solution)/shard_map/ppermute | solution.py:71
  610.9 15.8 %copy-start.15 = (f32[256,2048]{1,0:T(8,128)S(1)}, f32[256,2048]{1,0:T(8,128)}, u32[]{:S(2)}) copy-start(f32[256,2048]{1,0:T(8,128)} %copy-done.14) | copy-start | bytes 6291460
  626.7 4.4 copy-start.27
  626.8 4.3 copy-start.28
  626.8 4.3 copy-start.29
  626.8 4.3 copy-start.30
  869.9 4.3 copy-start.13
  869.9 4.3 copy-start.22
  869.9 4.3 copy-start.36
  869.9 4.3 copy-start.40
  874.3 4.2 copy-start.21
  (21 other events, 35.6 us)
Sparse Core Ops, SparseCore 0:
  139.8 59.0 all-gather.1
  492.7 69.6 reduce-scatter.4
  565.1 173.8 reduce-scatter.2

commit v9 on v7

--- a/solution.py
+++ b/solution.py
@@ -1343,7 +1343,7 @@
     mixture = sum((a.astype(f32) for a in (one, jnp.concatenate(halves), three)), here)
     block_out = (middle + mixture).astype(bf16)
     grad_rows_kept, small = summed_rows(
-        columns, grads_low, model_width, small, expert_group, shard_group, z_all, 256, 2, 1
+        columns, grads_low, model_width, small, expert_group, shard_group, z_all, 256, 3, 1
     )
     grad_out_weight = grad_rows_kept[:, :model_width].astype(f32)
     grad_qkv_weight = grad_rows_kept[:, model_width:].astype(f32)

time: 905 us -> 919 us (1.015)
  Pallas kernels: 597 us -> 611 us
    pallas_call x1, Pallas kernels: 227 us -> 241 us  [summed_rows(): pl.pallas_call(functools.partial(tail_kernel, (steps, width, x_all, z_all...]
  transfers between devices with their start and end apart: 11 -> 11, of which waited for: 4 -> 4; matrix products, arithmetic and copies ran while one was open for 21% -> 21% of each run, Pallas kernels for 25% -> 27%
where the time goes in v9:
time: 919 us; the launch traced here: 908 us
  Pallas kernels  611 us (66%)
  matrix products  103 us (11%)
  other arithmetic  64.4 us (7%)
  local copies, waits for them, and re-layouts  54.3 us (6%)
  waiting for transfers between devices  50.7 us (6%)
  between operations  14.9 us (2%)
    pallas_call x1, Pallas kernels, moe_layer(): pl.pallas_call(functools.partial(moe_kernel, (x_all, capacity, shard_grou...  251 us
    pallas_call x1, Pallas kernels, summed_rows(): pl.pallas_call(functools.partial(tail_kernel, (steps, width, x_all, z_all...  241 us
    pallas_call x1, Pallas kernels, start_layer(): pl.pallas_call(functools.partial(start_kernel, (x_all, y_all)), out_shape...  119 us
    ppermute x8, waiting for transfers between devices, shift(): return lax.ppermute(values, 'expert', pairs)  35.2 us
    dot_general x1, matrix products, body(): jnp.einsum('erd,erf->edf', expert_rows, grad_gate_up_low, preferred_eleme...  25.8 us
    unnamed x114, local copies, waits for them, and re-layouts  19.4 us
  transfers between devices with their start and end apart: 11, of which 4 were waited for; matrix products, arithmetic and copies ran while one was open for 21% of the time, Pallas kernels for 27%

profile of v9, /device:TPU:0, one launch (start us, length us, event | category | flops | bytes accessed | tf_op | source)
XLA Modules:
  0.0 908.0 jit_solution(1783976720624832055)
XLA Ops:
  12.8 2.8 copy-done.3
  17.5 118.8 %shard_map.221 = (bf16[2048,6144]{1,0:T(8,128)(2,1)}, bf16[4,2,256,2048]{3,2,1,0:T(8,128)(2,1)S(1)}, bf16[2048,16]{1,0:T(8,128)(2,1)S(1)}, bf16[4,16,512]{2,1,0:...) custom-call(bf16[512,6144]{1,0:T(8,128)(2,1)S(1)} %copy-done.3, ...), custom_call_target="tpu_custom_call" | custom-call | flops 8388608 | bytes 67108864 | tf_op jit(solution)/shard_map/pallas_call | solution.py:1090
  136.3 3.4 copy-done.9
  139.8 13.0 %fusion.70 = f32[256,6144]{1,0:T(8,128)S(1)} fusion(bf16[256,2048]{1,0:T(8,128)(2,1)S(1)} %get-tuple-element.63.second_hbm, bf16[2048,6144]{1,0:T(8,128)(2,1)} %get-tuple-element.64), kind=kOutput, calls=%fused_computation.144 | convolution fusion | flops 6442450944 | bytes 32505856 | tf_op jit(solution)/shard_map/dot_general | solution.py:1179
  155.1 2.4 multiply_multiply_fusion
  157.6 1.9 copy.67
  159.5 2.9 copy.66
  164.0 1.5 copy-done.17
  165.7 2.3 fusion.23
  168.0 5.1 fusion.68
  173.1 3.4 convolution_convert_fusion.4
  179.7 1.6 copy.68
  184.1 14.8 %all-gather.2.cloned.1.call-done = bf16[2048,2048]{1,0:T(8,128)(2,1)} async-done(((bf16[512,2048]{1,0:T(8,128)(2,1)}), bf16[2048,2048]{1,0:T(8,128)(2,1)}) %all-gather.2.cloned.1.call-update) | async-done | bytes 8388624 | tf_op jit(solution)/shard_map/all_gather | solution.py:1169
  198.9 6.2 multiply_reduce_fusion.7
  206.7 250.9 %shard_map.222 = (bf16[2,4,256,2048]{3,2,1,0:T(8,128)(2,1)}, bf16[2,4,256,1024]{3,2,1,0:T(8,128)(2,1)}, bf16[2,4,256,2048]{3,2,1,0:T(8,128)(2,1)}, bf16[2,4,256,...) custom-call(bf16[256,2048]{1,0:T(8,128)(2,1)} %copy-done.18, ...), custom_call_target="tpu_custom_call" | custom-call | flops 103079215104 | bytes 67108864 | tf_op jit(solution)/shard_map/pallas_call | solution.py:827
  460.1 3.2 multiply_reduce_fusion.1
  463.9 17.1 %collective-permute-done = bf16[256,2048]{1,0:T(8,128)(2,1)S(1)} collective-permute-done((bf16[256,2048]{1,0:T(8,128)(2,1)}, bf16[256,2048]{1,0:T(8,128)(2,1)S(1)}, u32[]{:S(2)}, u32[]{:S(2)}) %collective-permute-start) | collective-permute-done | bytes 1048608 | tf_op jit(solution)/shard_map/ppermute | solution.py:71
  484.6 25.8 %convolution_convert_fusion = bf16[2,2048,2048]{2,1,0:T(8,128)(2,1)} fusion(bf16[2,1024,2048]{2,1,0:T(8,128)(2,1)} %bitcast.145, bf16[2,1024,2048]{2,1,0:T(8,128)(2,1)} %bitcast.146), kind=kOutput, calls=%fused_computation.2 | convolution fusion | flops 17188257792 | bytes 33554432 | tf_op jit(solution)/shard_map/erd,erf->edf/dot_general | solution.py:1259
  510.3 2.6 add_convert_fusion.2
  513.5 2.4 collective-permute-start.3
  515.9 15.4 %convolution_convert_fusion.1 = bf16[2,1024,2048]{2,1,0:T(8,128)(2,1)} fusion(bf16[2,1024,1024]{2,1,0:T(8,128)(2,1)} %bitcast.147, bf16[2,1024,2048]{2,1,0:T(8,128)(2,1)} %bitcast.144), kind=kOutput, calls=%fused_computation.4 | convolution fusion | flops 8594128896 | bytes 20971520 | tf_op jit(solution)/shard_map/erf,erd->efd/dot_general | solution.py:1270
  531.4 3.7 collective-permute-done.4
  535.1 2.6 add_convert_fusion.1
  539.2 4.0 copy.65
  543.2 1.7 fusion.72
  546.4 8.4 convolution_convert_fusion.2
  554.8 2.3 copy.69
  557.1 2.7 fusion.33
  560.8 2.4 multiply_convert_fusion
  563.2 2.2 collective-permute-start.5
  565.4 1.8 convolution_convert_fusion.3
  567.2 2.5 copy.64
  569.7 3.4 convert_add_fusion.1
  573.1 14.4 %collective-permute-done.5 = bf16[256,2048]{1,0:T(8,128)(2,1)} collective-permute-done((bf16[256,2048]{1,0:T(8,128)(2,1)}, bf16[256,2048]{1,0:T(8,128)(2,1)}, u32[]{:S(2)}, u32[]{:S(2)}) %collective-permute-start.5) | collective-permute-done | bytes 1048608 | tf_op jit(solution)/shard_map/ppermute | solution.py:71
  590.2 2.8 fusion.27
  593.0 2.9 copy.62
  595.9 3.0 copy.63
  599.0 4.7 multiply_reduce_fusion.2
  603.8 3.2 fusion.13
  607.1 14.9 %fusion.19 = (f32[2048]{0:T(1024)S(1)}, f32[256]{0:T(256)}, f32[256,2048]{1,0:T(8,128)}) fusion(bf16[256,2048]{1,0:T(8,128)(2,1)S(1)} %copy-done.2, f32[256]{0:T(256)S(1)} %fusion.59, f32[2048]{0:T(1024)S(1)} %bitcast.133, bf16[2048,6144]{1,0:T(8,128)(2,1)} %get-tuple-element.64, bf16[256,2048]{1,0:T(8,128)(2,1)S(1)} %copy-done.32, ...), kind=kOutput, calls=%fused_computation.36 | convolution fusion | flops 6455556096 | bytes 31475712 | tf_op jit(solution)/shard_map/te,de->td/dot_general | solution.py:1312
  622.8 4.1 fusion.15
  627.8 2.8 pad_maximum_fusion.grads_ref
  630.5 241.4 %shard_map.223 = (bf16[512,8192]{1,0:T(8,128)(2,1)}, f32[24,512]{1,0:T(8,128)}) custom-call(bf16[256,8192]{1,0:T(8,128)(2,1)} %pad_maximum_fusion.grads_ref, bf16[2,512,1024]{2,1,0:T(8,128)(2,1)} %bitcast.120, f32[4,24,512]{2,1,0:T(8,128)} %pad_maximum_fusion.1.small_ref), custom_call_target="tpu_custom_call" | custom-call | flops 8589934592 | bytes 16777216 | tf_op jit(solution)/shard_map/pallas_call | solution.py:311
  874.8 4.3 slice_convert_fusion.2
  879.1 3.8 add_convert_fusion
  883.8 6.4 slice_convert_fusion
  890.2 4.2 convert_element_type.146
  894.4 6.7 convert_element_type.145
  (179 shorter events, 38.4 us)
Async XLA Ops:
  7.2 191.7 %all-gather.2.cloned.1.call-start = ((), (), s32[]{:S(2)}) async-start(), calls=%async_computation.2 | async-start | bytes 10485760 | tf_op jit(solution)/shard_map/all_gather | solution.py:1169
  136.3 3.4 copy-start.9
  139.7 13.1 %copy-start.10 = (bf16[256,2048]{1,0:T(8,128)(2,1)}, bf16[256,2048]{1,0:T(8,128)(2,1)S(1)}, u32[]{:S(2)}) copy-start(bf16[256,2048]{1,0:T(8,128)(2,1)S(1)} %get-tuple-element.63.second_hbm) | copy-start | bytes 3145732
  139.7 65.6 %copy-start.4 = (bf16[2048,16]{1,0:T(8,128)(2,1)}, bf16[2048,16]{1,0:T(8,128)(2,1)S(1)}, u32[]{:S(2)}) copy-start(bf16[2048,16]{1,0:T(8,128)(2,1)S(1)} %get-tuple-element.70.router_ref) | copy-start | bytes 196612
  139.7 750.5 %reduce-scatter.5.cloned.1.call-start = ((), (), s32[]{:S(2)}) async-start(), calls=%async_computation.4 | async-start | bytes 10485760 | tf_op jit(solution)/shard_map/reduce_scatter | solution.py:1276
  152.7 4.8 copy-start.11
  153.1 4.4 copy-start.44
  153.9 3.6 copy-start.46
  159.5 4.2 copy-start.52
  173.1 3.4 copy-start.54
  179.7 19.2 %copy-start.1 = (bf16[256,2048]{1,0:T(8,128)(2,1)S(1)}, bf16[256,2048]{1,0:T(8,128)(2,1)}, u32[]{:S(2)}) copy-start(bf16[256,2048]{1,0:T(8,128)(2,1)} %tokens_ref.1) | copy-start | bytes 3145732
  206.7 253.3 %copy-start.5 = (bf16[2048,16]{1,0:T(8,128)(2,1)S(1)}, bf16[2048,16]{1,0:T(8,128)(2,1)}, u32[]{:S(2)}) copy-start(bf16[2048,16]{1,0:T(8,128)(2,1)} %copy-done.4) | copy-start | bytes 196612
  457.6 23.5 %collective-permute-start = (bf16[256,2048]{1,0:T(8,128)(2,1)}, bf16[256,2048]{1,0:T(8,128)(2,1)S(1)}, u32[]{:S(2)}, u32[]{:S(2)}) collective-permute-start(bf16[256,2048]{1,0:T(8,128)(2,1)} %get-tuple-element.75), channel_id=1, source_target_pairs={{0,4},{4,0},{8,12},{12,8},{16,20},{20,16},{24,28},{28,24},{1,5},{5... | collective-permute-start | bytes 3145736 | tf_op jit(solution)/shard_map/ppermute | solution.py:71
  460.1 3.2 copy-start.7
  460.1 3.2 copy-start.13
  463.3 17.7 %copy-start.36 = (bf16[256,2048]{1,0:T(8,128)(2,1)S(1)}, bf16[256,2048]{1,0:T(8,128)(2,1)}, u32[]{:S(2)}) copy-start(bf16[256,2048]{1,0:T(8,128)(2,1)} %get-tuple-element.74) | copy-start | bytes 3145732
  481.5 28.9 %collective-permute-start.2 = (bf16[256,2048]{1,0:T(8,128)(2,1)}, bf16[256,2048]{1,0:T(8,128)(2,1)}, u32[]{:S(2)}, u32[]{:S(2)}) collective-permute-start(bf16[256,2048]{1,0:T(8,128)(2,1)} %get-tuple-element.84), channel_id=1, source_target_pairs={{0,4},{4,0},{8,12},{12,8},{16,20},{20,16},{24,28},{28,24},{1,5},{5... | collective-permute-start | bytes 3145736 | tf_op jit(solution)/shard_map/ppermute | solution.py:71
  484.0 29.0 %collective-permute-start.1 = (bf16[128,2048]{1,0:T(8,128)(2,1)}, bf16[128,2048]{1,0:T(8,128)(2,1)}, u32[]{:S(2)}, u32[]{:S(2)}) collective-permute-start(bf16[128,2048]{1,0:T(8,128)(2,1)} %get-tuple-element.140), channel_id=1, source_target_pairs={{0,16},{4,20},{8,24},{12,28},{16,0},{20,4},{24,8},{28,12},{1,17},{... | collective-permute-start | bytes 1572872 | tf_op jit(solution)/shard_map/ppermute | solution.py:71
  484.6 25.8 %copy-start.35 = (bf16[256,2048]{1,0:T(8,128)(2,1)S(1)}, bf16[256,2048]{1,0:T(8,128)(2,1)}, u32[]{:S(2)}) copy-start(bf16[256,2048]{1,0:T(8,128)(2,1)} %get-tuple-element.83) | copy-start | bytes 3145732
  513.0 22.1 %collective-permute-start.4 = (bf16[256,2048]{1,0:T(8,128)(2,1)}, bf16[256,2048]{1,0:T(8,128)(2,1)}, u32[]{:S(2)}, u32[]{:S(2)}) collective-permute-start(bf16[256,2048]{1,0:T(8,128)(2,1)} %get-tuple-element.94), channel_id=1, source_target_pairs={{0,4},{4,0},{8,12},{12,8},{16,20},{20,16},{24,28},{28,24},{1,5},{5... | collective-permute-start | bytes 3145736 | tf_op jit(solution)/shard_map/ppermute | solution.py:71
  513.5 24.1 %collective-permute-start.3 = (bf16[128,2048]{1,0:T(8,128)(2,1)}, bf16[128,2048]{1,0:T(8,128)(2,1)}, u32[]{:S(2)}, u32[]{:S(2)}) collective-permute-start(bf16[128,2048]{1,0:T(8,128)(2,1)} %get-tuple-element.91), channel_id=1, source_target_pairs={{0,16},{4,20},{8,24},{12,28},{16,0},{20,4},{24,8},{28,12},{1,17},{... | collective-permute-start | bytes 1572872 | tf_op jit(solution)/shard_map/ppermute | solution.py:71
  515.9 19.1 %copy-start.34 = (bf16[256,2048]{1,0:T(8,128)(2,1)S(1)}, bf16[256,2048]{1,0:T(8,128)(2,1)}, u32[]{:S(2)}) copy-start(bf16[256,2048]{1,0:T(8,128)(2,1)} %get-tuple-element.93) | copy-start | bytes 3145732
  537.7 356.7 %reduce-scatter.3.cloned.1.call-start = ((), (), s32[]{:S(2)}) async-start(), calls=%async_computation.3 | async-start | bytes 20971520 | tf_op jit(solution)/shard_map/reduce_scatter | solution.py:1265
  545.0 24.7 %collective-permute-start.6 = (bf16[256,2048]{1,0:T(8,128)(2,1)}, bf16[256,2048]{1,0:T(8,128)(2,1)}, u32[]{:S(2)}, u32[]{:S(2)}) collective-permute-start(bf16[256,2048]{1,0:T(8,128)(2,1)} %get-tuple-element.100), channel_id=1, source_target_pairs={{0,4},{4,0},{8,12},{12,8},{16,20},{20,16},{24,28},{28,24},{1,5},{5... | collective-permute-start | bytes 3145736 | tf_op jit(solution)/shard_map/ppermute | solution.py:71
  557.1 3.7 copy-start.53
  557.1 3.7 copy-start.55
  560.8 4.6 copy-start.23
  563.2 24.4 %collective-permute-start.5 = (bf16[256,2048]{1,0:T(8,128)(2,1)}, bf16[256,2048]{1,0:T(8,128)(2,1)}, u32[]{:S(2)}, u32[]{:S(2)}) collective-permute-start(bf16[256,2048]{1,0:T(8,128)(2,1)} %add_convert_fusion.2), channel_id=1, source_target_pairs={{0,24},{4,28},{8,0},{12,4},{16,8},{20,12},{24,16},{28,20},{1,25},{... | collective-permute-start | bytes 3145736 | tf_op jit(solution)/shard_map/ppermute | solution.py:71
  569.7 17.9 %copy-start.21 = (bf16[16,256,256]{1,2,0:T(8,128)(2,1)S(1)}, bf16[16,256,256]{1,2,0:T(8,128)(2,1)}, u32[]{:S(2)}) copy-start(bf16[16,256,256]{1,2,0:T(8,128)(2,1)} %multiply_convert_fusion) | copy-start | bytes 6291460
  569.7 17.9 %copy-start.25 = (bf16[256,16,128]{0,2,1:T(8,128)(2,1)S(1)}, bf16[256,16,128]{0,2,1:T(8,128)(2,1)}, u32[]{:S(2)}) copy-start(bf16[256,16,128]{0,2,1:T(8,128)(2,1)} %get-tuple-element.142) | copy-start | bytes 3145732
  573.1 15.3 %copy-start.24 = (bf16[256,16,128]{0,2,1:T(8,128)(2,1)S(1)}, bf16[256,16,128]{0,2,1:T(8,128)(2,1)}, u32[]{:S(2)}) copy-start(bf16[256,16,128]{0,2,1:T(8,128)(2,1)} %get-tuple-element.141) | copy-start | bytes 3145732
  573.1 15.3 %copy-start.38 = (f32[256,128]{0,1:T(8,128)S(1)}, f32[256,128]{0,1:T(8,128)}, u32[]{:S(2)}) copy-start(f32[256,128]{0,1:T(8,128)} %get-tuple-element.156) | copy-start | bytes 393220
  598.9 4.8 copy-start.49
  598.9 4.8 copy-start.51
  598.9 4.9 copy-start.15
  598.9 4.9 copy-start.16
  598.9 31.6 %collective-permute-start.7 = (bf16[256,2048]{1,0:T(8,128)(2,1)}, bf16[256,2048]{1,0:T(8,128)(2,1)}, u32[]{:S(2)}, u32[]{:S(2)}) collective-permute-start(bf16[256,2048]{1,0:T(8,128)(2,1)} %add_convert_fusion.1), channel_id=1, source_target_pairs={{0,8},{4,12},{8,16},{12,20},{16,24},{20,28},{24,0},{28,4},{1,9},{5... | collective-permute-start | bytes 3145736 | tf_op jit(solution)/shard_map/ppermute | solution.py:71
  603.8 3.3 copy-start.32
  603.8 3.3 copy-start.43
  607.0 14.9 %copy-start.28 = (bf16[256,2048]{1,0:T(8,128)(2,1)}, bf16[256,2048]{1,0:T(8,128)(2,1)S(1)}, u32[]{:S(2)}) copy-start(bf16[256,2048]{1,0:T(8,128)(2,1)S(1)} %get-tuple-element.127) | copy-start | bytes 3145732
  607.0 14.9 %copy-start.30 = (bf16[256,2048]{1,0:T(8,128)(2,1)}, bf16[256,2048]{1,0:T(8,128)(2,1)S(1)}, u32[]{:S(2)}) copy-start(bf16[256,2048]{1,0:T(8,128)(2,1)S(1)} %get-tuple-element.128) | copy-start | bytes 3145732
  622.8 4.9 copy-start.27
  622.8 4.9 copy-start.29
  622.8 4.8 copy-start.31
  622.8 5.0 copy-start.33
  874.8 4.3 copy-start.14
  874.8 4.3 copy-start.20
  879.1 4.7 copy-start.19
  (19 other events, 33.9 us)
Sparse Core Ops, SparseCore 0:
  139.8 59.0 all-gather.1
  537.8 70.1 reduce-scatter.4
  610.7 210.3 reduce-scatter.2
